TPU v7x, 256 devices: a whole 4x4x8 slice. The times are simulated.
256 devices in a mesh: grp: 8 (over y, core), dev: 32 (over z, x).
Axes of the slice: x: 4, y: 4, z: 8, core: 2. Of those that a mesh axis runs over, the one named last changes fastest.
Arguments:
- fine_input: bfloat16 [512, 64, 4096], P(('grp', 'dev')), may hold values from -6 to 6
- conv_weight: bfloat16 [27, 64, 64], replicated, may hold values from -0.15625 to 0.15625
- down_weight: bfloat16 [8, 128, 64], replicated, may hold values from -0.25 to 0.25
- coarse_cot: bfloat16 [256, 128, 4096], P(('grp', 'dev')), may hold values from -6 to 6
- neighbours: int32 [512, 26], P(('grp', 'dev')), may hold values from -1 to 511, as said below
- children: int32 [256, 8], P(('grp', 'dev')), may hold values from -1 to 511, as said below
Outputs:
- coarse_features: bfloat16 [256, 128, 4096], P(('grp', 'dev'))
- input_grad: bfloat16 [512, 64, 4096], P(('grp', 'dev'))
- conv_grad: float32 [27, 64, 64], replicated
- down_grad: float32 [8, 128, 64], replicated
Inputs may be any that keep to these rules, and one draw needn't show every extreme that they name: `neighbours`: entry -1 means no brick at that offset. A brick named for offset (dx, dy, dz) of a brick on device (g, d) lies on device (g, d + dy); the relation is symmetric. Entry -1 means no child. The children of a coarse slot on device (g, d) lie on devices (g, 2 (d // 2)) and (g, 2 (d // 2) + 1), the child of octant (ox, oy, oz) on the one with dev index 2 (d // 2) + oy. Every fine brick is the child of exactly one coarse slot and octant.
All inputs are finite; a program needn't handle non-finite values.
Results may differ from a plain program's by a relative error of at most 0.005.
Values may be sent and summed in bfloat16 or wider, within the bound.
No kernel may reach another device: no remote copies, remote signals or barrier semaphores. Data moves between devices by JAX's collectives and lax.ppermute only.
A program may use at most 128 MiB of HBM per device.

v0:
```python
import jax
import jax.numpy as jnp
from jax import lax
from jax.sharding import PartitionSpec as P

SIDE = 16


def extended(array, sides, width):
    for axis, dim in sides:
        peers, length = (lax.axis_size(axis), array.shape[dim])
        up = [(i, (i + 1) % peers) for i in range(peers - 1)]
        down = [(j, i) for i, j in up]
        last = lax.slice_in_dim(array, length - width, length, axis=dim)
        initial = lax.slice_in_dim(array, 0, width, axis=dim)
        before = lax.ppermute(last, axis, up)
        after = lax.ppermute(initial, axis, down)
        array = jnp.concatenate([before, array, after], axis=dim)
    return array


def from_partner(array, axis, stride):
    return lax.ppermute(array, axis, [(i, i ^ 1 << stride) for i in range(lax.axis_size(axis))])


def face_sets(bricks_in):
    last = bricks_in.shape[-1] - 1
    x_faces = jnp.stack([bricks_in[:, :, 0], bricks_in[:, :, last]], axis=1)
    y_faces = jnp.stack([bricks_in[:, :, :, 0], bricks_in[:, :, :, last]], axis=1)
    z_faces = jnp.stack([bricks_in[..., 0], bricks_in[..., last]], axis=1)
    return (x_faces, y_faces, z_faces)


def ranges(offset, edge):
    if offset == 0:
        return slice(0, edge)
    if offset == 1:
        return slice(0, 1)
    return slice(edge - 1, edge)


def assemble(bricks_in, lookup):
    pieces_by_offset = {(0, 0, 0): bricks_in}
    column = 0
    edge = bricks_in.shape[2]
    for step_x in (-1, 0, 1):
        for step_y in (-1, 0, 1):
            for step_z in (-1, 0, 1):
                if step_x == 0 and step_y == 0 and (step_z == 0):
                    continue
                take_x = ranges(step_x, edge)
                take_y = ranges(step_y, edge)
                take_z = ranges(step_z, edge)
                if step_y != 0:
                    plane = lookup(1, step_y, column)
                    block = plane[:, :, take_x, take_z][:, :, :, None, :]
                elif step_x != 0:
                    plane = lookup(0, step_x, column)
                    block = plane[:, :, take_y, take_z][:, :, None, :, :]
                else:
                    plane = lookup(2, step_z, column)
                    block = plane[:, :, :, :, None]
                pieces_by_offset[step_x, step_y, step_z] = block
                column += 1
    slabs = []
    for step_x in (-1, 0, 1):
        lines = []
        for step_y in (-1, 0, 1):
            lines.append(
                jnp.concatenate(
                    [pieces_by_offset[step_x, step_y, step_z] for step_z in (-1, 0, 1)], axis=4
                )
            )
        slabs.append(jnp.concatenate(lines, axis=3))
    return jnp.concatenate(slabs, axis=2)


def make_lookup(x_faces, z_faces, row_table, near):
    brick_count = x_faces.shape[0]

    def lookup(face_axis, offset, column):
        entry = near[:, column]
        slot = jnp.remainder(entry, brick_count)
        facing = 0 if offset == 1 else 1
        if face_axis == 1:
            plane = row_table[offset + 1][slot, facing]
        elif face_axis == 0:
            plane = x_faces[slot, facing]
        else:
            plane = z_faces[slot, facing]
        return jnp.where((entry >= 0)[:, None, None, None], plane, jnp.zeros_like(plane))

    return lookup


def conv_taps(padded, weights):
    number = padded.shape[0]
    edge = padded.shape[2] - 2
    outs, channels = (weights.shape[1], weights.shape[2])
    kernel = weights.reshape(3, 3, 3, outs, channels).transpose(3, 4, 0, 1, 2)
    result = lax.conv_general_dilated(
        padded,
        kernel,
        (1, 1, 1),
        "VALID",
        dimension_numbers=("NCDHW", "OIDHW", "NCDHW"),
        preferred_element_type=jnp.float32,
    )
    return result.reshape(number, outs, edge**3)


def tap_grads(padded, grads):
    number, channels = (padded.shape[0], padded.shape[1])
    edge = padded.shape[2] - 2
    outs = grads.shape[1]
    shaped = grads.reshape(number, outs, edge, edge, edge)
    result = lax.conv_general_dilated(
        padded,
        shaped,
        (1, 1, 1),
        "VALID",
        dimension_numbers=("CNDHW", "IODHW", "NCDHW"),
        preferred_element_type=jnp.float32,
    )
    return result.transpose(2, 3, 4, 1, 0).reshape(27, outs, channels)


def to_octants(bricks_in):
    number, channels, edge = (bricks_in.shape[0], bricks_in.shape[1], bricks_in.shape[2])
    half_side = edge // 2
    shaped = bricks_in.reshape(number, channels, half_side, 2, half_side, 2, half_side, 2)
    return shaped.transpose(0, 3, 5, 7, 1, 2, 4, 6).reshape(number, 8 * channels, half_side**3)


def from_octants(parts, channels, edge):
    number = parts.shape[0]
    half_side = edge // 2
    shaped = parts.reshape(number, 2, 2, 2, channels, half_side, half_side, half_side)
    return shaped.transpose(0, 4, 5, 1, 6, 2, 7, 3).reshape(number, channels, edge**3)


def body(fine_input, conv_weight, down_weight, coarse_cot, neighbours, children):
    brick_count, channels = (fine_input.shape[0], fine_input.shape[1])
    coarse_count, coarse_width = (coarse_cot.shape[0], coarse_cot.shape[1])
    half_side = SIDE // 2
    bricks_in = fine_input.reshape(brick_count, channels, SIDE, SIDE, SIDE)
    my_rank = lax.axis_index("grp") * lax.axis_size("dev") + lax.axis_index("dev")
    partner = jnp.bitwise_xor(my_rank, 1)
    down_flat = down_weight.transpose(1, 0, 2).reshape(coarse_width, 8 * channels)
    x_faces, y_faces, z_faces = face_sets(bricks_in)
    sent_rows = y_faces.reshape(1, brick_count, 2, channels, SIDE * SIDE)
    got_rows = extended(sent_rows, (("dev", 0),), 1)
    row_table = got_rows.reshape(3, brick_count, 2, channels, SIDE, SIDE)
    padded = assemble(bricks_in, make_lookup(x_faces, z_faces, row_table, neighbours))
    preact = conv_taps(padded, conv_weight)
    active = jax.nn.silu(preact).astype(jnp.bfloat16)
    parts_own = to_octants(active.reshape(brick_count, channels, SIDE, SIDE, SIDE))
    octant_mine = jnp.einsum(
        "ok,bkv->bov", down_flat, parts_own, preferred_element_type=jnp.float32
    ).astype(jnp.bfloat16)
    octant_theirs = from_partner(octant_mine, "dev", 0)
    octant_table = jnp.concatenate([octant_mine, octant_theirs], axis=0)
    child_list = children.reshape(-1)
    holder = jnp.floor_divide(child_list, brick_count)
    position = jnp.where(
        holder == my_rank,
        jnp.remainder(child_list, brick_count),
        brick_count + jnp.remainder(child_list, brick_count),
    )
    picked = octant_table[position]
    picked = jnp.where((child_list >= 0)[:, None, None], picked, jnp.zeros_like(picked))
    picked = picked.reshape(coarse_count, 2, 2, 2, coarse_width, half_side, half_side, half_side)
    coarse_features = picked.transpose(0, 4, 1, 5, 2, 6, 3, 7).reshape(
        coarse_count, coarse_width, SIDE**3
    )
    cot_parts = coarse_cot.reshape(
        coarse_count, coarse_width, 2, half_side, 2, half_side, 2, half_side
    )
    cot_parts = cot_parts.transpose(0, 2, 4, 6, 1, 3, 5, 7).reshape(
        coarse_count * 8, coarse_width * half_side**3
    )
    slots = jnp.arange(brick_count, dtype=jnp.int32)
    wanted = jnp.concatenate([my_rank * brick_count + slots, partner * brick_count + slots])
    selector = (child_list[None, :] == wanted[:, None]).astype(jnp.bfloat16)
    routed = jnp.dot(selector, cot_parts, preferred_element_type=jnp.float32).astype(jnp.bfloat16)
    routed = routed.reshape(2 * brick_count, coarse_width, half_side**3)
    incoming = from_partner(routed[brick_count:], "dev", 0)
    octant_grad = (routed[:brick_count].astype(jnp.float32) + incoming.astype(jnp.float32)).astype(
        jnp.bfloat16
    )
    down_part = jnp.einsum(
        "bov,bkv->ok", octant_grad, parts_own, preferred_element_type=jnp.float32
    )
    active_grad = from_octants(
        jnp.einsum("ok,bov->bkv", down_flat, octant_grad, preferred_element_type=jnp.float32),
        channels,
        SIDE,
    )
    sigmoid_pre = jax.nn.sigmoid(preact)
    preact_grad = (active_grad * sigmoid_pre * (1.0 + preact * (1.0 - sigmoid_pre))).astype(
        jnp.bfloat16
    )
    conv_part = tap_grads(padded, preact_grad)
    conv_grad, down_sum = lax.psum((conv_part, down_part), ("grp", "dev"))
    grad_bricks = preact_grad.reshape(brick_count, channels, SIDE, SIDE, SIDE)
    grad_x, grad_y, grad_z = face_sets(grad_bricks)
    grad_sent = grad_y.reshape(1, brick_count, 2, channels, SIDE * SIDE)
    grad_got = extended(grad_sent, (("dev", 0),), 1)
    grad_table = grad_got.reshape(3, brick_count, 2, channels, SIDE, SIDE)
    grad_padded = assemble(grad_bricks, make_lookup(grad_x, grad_z, grad_table, neighbours))
    flipped = conv_weight[::-1].transpose(0, 2, 1)
    input_grad = conv_taps(grad_padded, flipped).astype(jnp.bfloat16)
    down_grad = down_sum.reshape(coarse_width, 8, channels).transpose(1, 0, 2)
    return (coarse_features, input_grad, conv_grad, down_grad)


def solution(mesh):
    in_specs = (
        P(("grp", "dev"), None, None),
        P(),
        P(),
        P(("grp", "dev"), None, None),
        P(("grp", "dev"), None),
        P(("grp", "dev"), None),
    )
    out_specs = (P(("grp", "dev"), None, None), P(("grp", "dev"), None, None), P(), P())
    return jax.shard_map(body, mesh=mesh, in_specs=in_specs, out_specs=out_specs, check_vma=False)
```

profile of v0, /device:TPU:1, one launch (start us, length us, event | category | flops | bytes accessed | tf_op | source)
XLA Modules:
  0.0 649.8 jit_solution(7037276240856005606)
XLA Ops:
  7.2 5.0 copy.397
  14.9 5.3 collective-permute-start
  21.8 23.0 %copy.453 = bf16[1,2,2,2,128,8,8,8]{7,6,5,4,3,2,1,0:T(8,128)(2,1)} copy(bf16[1,2,2,2,128,8,8,8]{4,7,3,6,2,5,1,0:T(8,128)(2,1)S(1)} %bitcast.337) | data formatting | bytes 2097152 | tf_op jit(solution)/shard_map/transpose | solution.py:179
  44.8 42.5 %reshape.489 = bf16[8,65536]{1,0:T(8,128)(2,1)S(1)} reshape(bf16[1,2,2,2,128,8,8,8]{7,6,5,4,3,2,1,0:T(8,128)(2,1)} %copy.453) | data formatting | bytes 2097152 | tf_op jit(solution)/shard_map/reshape | solution.py:179
  106.8 1.8 rev.3
  136.2 56.0 %fusion.204 = bf16[64,18,18,2,18]{0,3,4,2,1:T(2,128)(2,1)S(1)} fusion(bf16[2,64,1,1,1]{1,0,4,3,2:T(2,128)(2,1)S(1)} %get-tuple-element.96, bf16[2,64,1,1,16]{1,0,4,3,2:T(2,128)(2,1)S(1)} %get-tuple-element.92, bf16[2,64,1,1,1]{1,0,4,3,2:T(2,128)(2,1)S(1)} %get-tuple-element.114, bf16[2,64,1,16,1]{1,0,4,3,2:T(2,128)(2,1)} %get-tuple-element.108, ...), kind=kLoop, calls=%fused_computation.476 | loop fusion | flops 19408896 | bytes 2985984 | tf_op jit(solution)/shard_map/concatenate | solution.py:75
  192.3 57.3 %fusion.208 = bf16[2,64,18,18,18]{1,0,4,3,2:T(2,128)(2,1)} fusion(bf16[2,64,1,1,1]{1,0,4,3,2:T(2,128)(2,1)S(1)} %get-tuple-element.96, bf16[2,64,1,1,16]{1,0,4,3,2:T(2,128)(2,1)S(1)} %get-tuple-element.92, bf16[2,64,1,1,1]{1,0,4,3,2:T(2,128)(2,1)S(1)} %get-tuple-element.114, bf16[2,64,1,16,1]{1,0,4,3,2:T(2,128)(2,1)S(1)} %copy-done.17, ...), kind=kLoop, calls=%bitcast_fusion.clone.1 | loop fusion | flops 19408896 | bytes 2985984 | tf_op jit(solution)/shard_map/transpose | solution.py:125
  249.6 3.6 pad.26
  254.9 25.8 %add_divide_fusion = (f32[16,16,16,3,64]{4,2,3,1,0:T(8,128)S(1)}, f32[16,16,16,3,64]{4,2,3,1,0:T(8,128)S(1)}, f32[16,16,16,3,64]{4,2,3,1,0:T(8,128)S(1)}) fusion(bf16[3,3,3,64,64]{4,3,2,1,0:T(8,128)(2,1)S(1)} %bitcast.349, bf16[64,18,18,2,7,2]{0,4,3,5,2,1:T(8,128)(2,1)S(1)} %slice.529, bf16[64,18,18,2,8,3]{0,4,3,5,2,1:T(8,128)(2,1)S(1)} %copy.444, ...), kind=kOutput, calls=%fused_computation.69 | convolution fusion | flops 2733367296 | bytes 12810288 | tf_op jit(solution)/shard_map/conv_general_dilated | solution.py:101
  280.7 2.0 copy.445
  283.1 1.7 copy.446
  286.0 2.0 copy.457
  288.0 2.4 slice.533
  290.4 2.0 copy.459
  292.4 2.4 slice.534
  294.8 2.5 copy.449
  302.1 4.3 reshape.490
  306.5 4.7 copy.456
  311.2 4.2 fusion.13
  324.5 5.1 collective-permute-start.4
  332.8 30.9 %fusion.21 = f32[3,3,3,64,64]{4,3,2,1,0:T(8,128)} fusion(bf16[2,64,16,16,16]{1,4,3,0,2:T(8,128)(2,1)S(1)} %fusion.13, bf16[2,64,18,18,18]{1,0,4,3,2:T(2,128)(2,1)} %fusion.208), kind=kOutput, calls=%fused_computation.83 | convolution fusion | flops 1811939328 | bytes 2983936 | tf_op jit(solution)/shard_map/transpose | solution.py:125
  372.5 2.2 fusion.189
  415.7 4.2 maximum_bitcast_fusion
  419.9 3.1 copy.529
  423.0 3.6 pad.28.clone
  428.2 8.0 %fusion.5 = bf16[64,18,18,2,8,5]{0,3,5,4,2,1:T(2,128)(2,1)} fusion(bf16[64,18,18,2,7,2]{0,3,5,4,2,1:T(2,128)(2,1)S(1)} %slice.561, bf16[64,18,18,2,8,3]{0,3,5,4,2,1:T(2,128)(2,1)S(1)} %bitcast.320), kind=kLoop, calls=%fused_computation.60 | loop fusion | flops 9953280 | bytes 6469632 | tf_op jit(solution)/shard_map/conv_general_dilated | solution.py:101
  438.2 15.4 %select_convert_fusion = bf16[16,16,16,3,64]{4,2,3,1,0:T(8,128)(2,1)} fusion(pred[16,3]{0,1:T(4,128)(4,1)S(1)} %copy-done.81, bf16[3,3,3,64,64]{3,4,2,1,0:T(8,128)(2,1)S(1)} %bitcast.350, bf16[64,18,18,2,8,5]{0,3,5,4,2,1:T(2,128)(2,1)} %fusion.5), kind=kOutput, calls=%fused_computation.67 | convolution fusion | flops 2719481856 | bytes 5111856 | tf_op jit(solution)/shard_map/conv_general_dilated | solution.py:101
  455.2 2.7 copy.510
  458.9 1.6 copy.517
  460.5 178.4 %all-reduce.29.cloned.1.call-done = (f32[27,64,64]{2,1,0:T(8,128)}, f32[8,128,64]{1,2,0:T(8,128)}) async-done(((f32[27,64,64]{2,1,0:T(8,128)}, f32[8,128,64]{1,2,0:T(8,128)}), (f32[27,64,64]{2,1,0:T(8,128)}, f32[8,128,64]{1,2,0:T(8,128)})) %all-reduce.29.cloned.1.call-update) | async-done | bytes 704528 | tf_op jit(solution)/shard_map/psum | solution.py:204
  638.9 2.2 copy.738
  641.1 1.7 copy.739
  (370 shorter events, 126.3 us)
Async XLA Ops:
  7.2 291.6 %copy-start = (bf16[8,128,64]{1,2,0:T(8,128)(2,1)S(1)}, bf16[8,128,64]{1,2,0:T(8,128)(2,1)}, u32[]{:S(2)}) copy-start(bf16[8,128,64]{1,2,0:T(8,128)(2,1)} %param.8) | copy-start | bytes 393220
  7.2 631.7 %all-reduce.29.cloned.1.call-start = ((), (), s32[]{:S(2)}) async-start(), calls=%async_computation | async-start | bytes 2293760 | tf_op jit(solution)/shard_map/psum | solution.py:204
  13.6 96.2 %collective-permute-start.1 = (bf16[1,2,2,64,256]{3,1,4,2,0:T(2,128)(2,1)}, bf16[1,2,2,64,256]{3,1,4,2,0:T(2,128)(2,1)}, u32[]{:S(2)}, u32[]{:S(2)}) collective-permute-start(bf16[1,2,2,64,256]{3,1,4,2,0:T(2,128)(2,1)} %pad_maximum_fusion.1), channel_id=1, source_target_pairs={{1,0},{2,1},{3,2},{4,3},{5,4},{6,5},{7,6},{8,7},{9,8},{10,9},{11,1... | collective-permute-start | bytes 393224 | tf_op jit(solution)/shard_map/ppermute | solution.py:17
  14.9 105.3 %collective-permute-start = (bf16[1,2,2,64,256]{3,1,4,2,0:T(2,128)(2,1)}, bf16[1,2,2,64,256]{3,1,4,2,0:T(2,128)(2,1)}, u32[]{:S(2)}, u32[]{:S(2)}) collective-permute-start(bf16[1,2,2,64,256]{3,1,4,2,0:T(2,128)(2,1)} %pad_maximum_fusion.1), channel_id=1, source_target_pairs={{0,1},{1,2},{2,3},{3,4},{4,5},{5,6},{6,7},{7,8},{8,9},{9,10},{10,1... | collective-permute-start | bytes 393224 | tf_op jit(solution)/shard_map/ppermute | solution.py:16
  44.8 42.6 %copy-start.79 = (s32[1,8]{1,0:T(1,128)S(1)}, s32[1,8]{1,0:T(1,128)}, u32[]{:S(2)}) copy-start(s32[1,8]{1,0:T(1,128)} %param.11) | copy-start | bytes 100
  90.8 209.8 %collective-permute-start.3 = (bf16[2,128,512]{2,1,0:T(8,128)(2,1)}, bf16[2,128,512]{2,1,0:T(8,128)(2,1)}, u32[]{:S(2)}, u32[]{:S(2)}) collective-permute-start(bf16[2,128,512]{2,1,0:T(8,128)(2,1)} %bitcast.278), channel_id=1, source_target_pairs={{0,1},{1,0},{2,3},{3,2},{4,5},{5,4},{6,7},{7,6},{8,9},{9,8},{10,11... | collective-permute-start | bytes 786440 | tf_op jit(solution)/shard_map/ppermute | solution.py:23
  103.8 11.7 %copy-start.42 = (s32[2]{0:T(128)S(1)}, s32[2]{0:T(128)}, u32[]{:S(2)}) copy-start(s32[2]{0:T(128)} %get-tuple-element.54) | copy-start | bytes 28
  136.2 56.1 %copy-start.11 = (bf16[2,64,16,16,1]{1,0,4,3,2:T(2,128)(2,1)S(1)}, bf16[2,64,16,16,1]{1,0,4,3,2:T(2,128)(2,1)}, u32[]{:S(2)}) copy-start(bf16[2,64,16,16,1]{1,0,4,3,2:T(2,128)(2,1)} %get-tuple-element.100) | copy-start | bytes 196612
  136.2 56.1 %copy-start.17 = (bf16[2,64,1,16,1]{1,0,4,3,2:T(2,128)(2,1)S(1)}, bf16[2,64,1,16,1]{1,0,4,3,2:T(2,128)(2,1)}, u32[]{:S(2)}) copy-start(bf16[2,64,1,16,1]{1,0,4,3,2:T(2,128)(2,1)} %get-tuple-element.108) | copy-start | bytes 12292
  136.2 56.1 %copy-start.18 = (bf16[2,64,1,16,1]{1,0,4,3,2:T(2,128)(2,1)S(1)}, bf16[2,64,1,16,1]{1,0,4,3,2:T(2,128)(2,1)}, u32[]{:S(2)}) copy-start(bf16[2,64,1,16,1]{1,0,4,3,2:T(2,128)(2,1)} %get-tuple-element.93) | copy-start | bytes 12292
  136.2 56.1 %copy-start.19 = (bf16[2,64,1,16,1]{1,0,4,3,2:T(2,128)(2,1)S(1)}, bf16[2,64,1,16,1]{1,0,4,3,2:T(2,128)(2,1)}, u32[]{:S(2)}) copy-start(bf16[2,64,1,16,1]{1,0,4,3,2:T(2,128)(2,1)} %get-tuple-element.94) | copy-start | bytes 12292
  299.9 136.3 %collective-permute-start.2 = (bf16[2,128,512]{1,2,0:T(8,128)(2,1)}, bf16[2,128,512]{1,2,0:T(8,128)(2,1)}, u32[]{:S(2)}, u32[]{:S(2)}) collective-permute-start(bf16[2,128,512]{1,2,0:T(8,128)(2,1)} %fusion.23), channel_id=1, source_target_pairs={{0,1},{1,0},{2,3},{3,2},{4,5},{5,4},{6,7},{7,6},{8,9},{9,8},{10,11... | collective-permute-start | bytes 786440 | tf_op jit(solution)/shard_map/ppermute | solution.py:23
  323.2 52.2 %collective-permute-start.5 = (bf16[1,2,2,64,256]{3,4,1,2,0:T(8,128)(2,1)}, bf16[1,2,2,64,256]{3,4,1,2,0:T(8,128)(2,1)}, u32[]{:S(2)}, u32[]{:S(2)}) collective-permute-start(bf16[1,2,2,64,256]{3,4,1,2,0:T(8,128)(2,1)} %pad_maximum_fusion.4), channel_id=1, source_target_pairs={{1,0},{2,1},{3,2},{4,3},{5,4},{6,5},{7,6},{8,7},{9,8},{10,9},{11,1... | collective-permute-start | bytes 393224 | tf_op jit(solution)/shard_map/ppermute | solution.py:17
  324.5 60.4 %collective-permute-start.4 = (bf16[1,2,2,64,256]{3,4,1,2,0:T(8,128)(2,1)}, bf16[1,2,2,64,256]{3,4,1,2,0:T(8,128)(2,1)}, u32[]{:S(2)}, u32[]{:S(2)}) collective-permute-start(bf16[1,2,2,64,256]{3,4,1,2,0:T(8,128)(2,1)} %pad_maximum_fusion.4), channel_id=1, source_target_pairs={{0,1},{1,2},{2,3},{3,4},{4,5},{5,6},{6,7},{7,8},{8,9},{9,10},{10,1... | collective-permute-start | bytes 393224 | tf_op jit(solution)/shard_map/ppermute | solution.py:16
  332.7 31.9 %copy-start.67 = (pred[2]{0:T(512)(128)(4,1)S(1)}, pred[2]{0:T(512)(128)(4,1)}, u32[]{:S(2)}) copy-start(pred[2]{0:T(512)(128)(4,1)} %copy-done.66) | copy-start | bytes 10
  332.7 32.5 %copy-start.5 = (bf16[2,64,16,16]{1,3,2,0:T(8,128)(2,1)S(1)}, bf16[2,64,16,16]{1,3,2,0:T(8,128)(2,1)}, u32[]{:S(2)}) copy-start(bf16[2,64,16,16]{1,3,2,0:T(8,128)(2,1)} %gather_fusion.48) | copy-start | bytes 196612
  332.7 32.5 %copy-start.75 = (pred[2]{0:T(512)(128)(4,1)S(1)}, pred[2]{0:T(512)(128)(4,1)}, u32[]{:S(2)}) copy-start(pred[2]{0:T(512)(128)(4,1)} %copy-done.74) | copy-start | bytes 10
  332.7 34.2 %copy-start.65 = (pred[2]{0:T(512)(128)(4,1)S(1)}, pred[2]{0:T(512)(128)(4,1)}, u32[]{:S(2)}) copy-start(pred[2]{0:T(512)(128)(4,1)} %copy-done.64) | copy-start | bytes 10
  332.7 35.7 %copy-start.71 = (pred[2]{0:T(512)(128)(4,1)S(1)}, pred[2]{0:T(512)(128)(4,1)}, u32[]{:S(2)}) copy-start(pred[2]{0:T(512)(128)(4,1)} %copy-done.70) | copy-start | bytes 10
  332.8 36.7 %copy-start.77 = (pred[2]{0:T(512)(128)(4,1)S(1)}, pred[2]{0:T(512)(128)(4,1)}, u32[]{:S(2)}) copy-start(pred[2]{0:T(512)(128)(4,1)} %copy-done.76) | copy-start | bytes 10
  332.8 37.5 %copy-start.7 = (bf16[2,64,16,16]{1,3,2,0:T(8,128)(2,1)S(1)}, bf16[2,64,16,16]{1,3,2,0:T(8,128)(2,1)}, u32[]{:S(2)}) copy-start(bf16[2,64,16,16]{1,3,2,0:T(8,128)(2,1)} %gather_fusion.39) | copy-start | bytes 196612
  332.8 37.5 %copy-start.73 = (pred[2]{0:T(512)(128)(4,1)S(1)}, pred[2]{0:T(512)(128)(4,1)}, u32[]{:S(2)}) copy-start(pred[2]{0:T(512)(128)(4,1)} %get-tuple-element.32) | copy-start | bytes 10
  332.8 37.7 %copy-start.6 = (bf16[2,64,16,16]{1,3,2,0:T(8,128)(2,1)S(1)}, bf16[2,64,16,16]{1,3,2,0:T(8,128)(2,1)}, u32[]{:S(2)}) copy-start(bf16[2,64,16,16]{1,3,2,0:T(8,128)(2,1)} %gather_fusion.40) | copy-start | bytes 196612
  332.8 37.7 %copy-start.72 = (pred[2]{0:T(512)(128)(4,1)S(1)}, pred[2]{0:T(512)(128)(4,1)}, u32[]{:S(2)}) copy-start(pred[2]{0:T(512)(128)(4,1)} %get-tuple-element.31) | copy-start | bytes 10
  332.8 39.7 %copy-start.4 = (f32[2,65536]{1,0:T(2,128)S(1)}, f32[2,65536]{1,0:T(2,128)}, u32[]{:S(2)}) copy-start(f32[2,65536]{1,0:T(2,128)} %get-tuple-element.89) | copy-start | bytes 1572868
  363.7 11.0 %copy-start.69 = (pred[2]{0:T(512)(128)(4,1)S(1)}, pred[2]{0:T(512)(128)(4,1)}, u32[]{:S(2)}) copy-start(pred[2]{0:T(512)(128)(4,1)} %copy-done.68) | copy-start | bytes 10
  363.7 12.7 %copy-start.59 = (s32[2]{0:T(128)S(1)}, s32[2]{0:T(128)}, u32[]{:S(2)}) copy-start(s32[2]{0:T(128)} %get-tuple-element.71) | copy-start | bytes 28
  394.0 20.6 %copy-start.14 = (bf16[2,64,1,16,16]{1,0,4,3,2:T(2,128)(2,1)S(1)}, bf16[2,64,1,16,16]{1,0,4,3,2:T(2,128)(2,1)}, u32[]{:S(2)}) copy-start(bf16[2,64,1,16,16]{1,0,4,3,2:T(2,128)(2,1)} %broadcast_select_fusion.11) | copy-start | bytes 196612
  394.0 21.7 %copy-start.12 = (bf16[2,64,16,16,1]{1,4,3,0,2:T(2,128)(2,1)S(1)}, bf16[2,64,16,16,1]{1,4,3,0,2:T(2,128)(2,1)}, u32[]{:S(2)}) copy-start(bf16[2,64,16,16,1]{1,4,3,0,2:T(2,128)(2,1)} %copy.487) | copy-start | bytes 196612
  394.0 21.7 %copy-start.13 = (bf16[2,64,16,16,1]{1,4,3,0,2:T(2,128)(2,1)S(1)}, bf16[2,64,16,16,1]{1,4,3,0,2:T(2,128)(2,1)}, u32[]{:S(2)}) copy-start(bf16[2,64,16,16,1]{1,4,3,0,2:T(2,128)(2,1)} %copy.486) | copy-start | bytes 196612
  438.2 15.4 %copy-start.78 = (pred[2,2,2]{2,1,0:T(4,128)(4,1)S(1)}, pred[2,2,2]{2,1,0:T(4,128)(4,1)}, u32[]{:S(2)}) copy-start(pred[2,2,2]{2,1,0:T(4,128)(4,1)} %ge.297) | copy-start | bytes 28
  458.3 184.5 %copy-start.1 = (bf16[8,128,64]{1,2,0:T(8,128)(2,1)S(1)}, bf16[8,128,64]{1,2,0:T(8,128)(2,1)}, u32[]{:S(2)}) copy-start(bf16[8,128,64]{1,2,0:T(8,128)(2,1)} %param.8) | copy-start | bytes 393220
  (60 other events, 352.6 us)
Sparse Core Ops, SparseCore 0:
  374.8 264.0 all-reduce.28
where the time goes:
time: 654 us; the launch traced here: 650 us
  local copies, waits for them, and re-layouts  190 us (29%)
  waiting for transfers between devices  178 us (27%)
  other arithmetic  173 us (26%)
  matrix products  78.5 us (12%)
  between operations  15.8 us (2%)
  starting transfers between devices  14.4 us (2%)
    psum x1, waiting for transfers between devices, body(): conv_grad, down_sum = lax.psum((conv_part, down_part), ('grp', 'dev'))  178 us
    concatenate x2, other arithmetic, assemble(): return jnp.concatenate(slabs, axis=2)  60.3 us
    transpose x1, other arithmetic, tap_grads(): return result.transpose(2, 3, 4, 1, 0).reshape(27, outs, channels)  57.3 us
    reshape x1, local copies, waits for them, and re-layouts, body(): cot_parts.transpose(0, 2, 4, 6, 1, 3, 5, 7)  42.5 us
    conv_general_dilated x2, matrix products, conv_taps(): lax.conv_general_dilated(padded, kernel, (1, 1, 1), 'VALID', dimension_nu...  41.3 us
    transpose x1, matrix products, tap_grads(): return result.transpose(2, 3, 4, 1, 0).reshape(27, outs, channels)  30.9 us
    gather x36, local copies, waits for them, and re-layouts, lookup(): plane = row_table[offset + 1][slot, facing]  27.5 us
    transpose x1, local copies, waits for them, and re-layouts, body(): cot_parts.transpose(0, 2, 4, 6, 1, 3, 5, 7)  23 us
  transfers between devices with their start and end apart: 7, of which 1 were waited for; matrix products, arithmetic and copies ran while one was open for 66% of the time, Pallas kernels for 0%

commit v1 on v0

v1 whole, which is shorter than its diff:
```python
import functools

import jax
import jax.numpy as jnp
from jax import lax
from jax.experimental import pallas as pl
from jax.experimental.pallas import tpu as pltpu
from jax.sharding import PartitionSpec as P

SIDE = 16
HALF = 8
LANES = 128
F32 = jnp.float32
BF16 = jnp.bfloat16
CONV_ROWS = 960
DOWN_ROWS = 512
SHARE = 8

VMEM_SPEC = pl.BlockSpec(memory_space=pltpu.VMEM)
SMEM_SPEC = pl.BlockSpec(memory_space=pltpu.SMEM)


def params(mib):
    return pltpu.CompilerParams(vmem_limit_bytes=mib * 1024 * 1024)


def low_half(shape):
    return lax.broadcasted_iota(jnp.int32, shape, len(shape) - 1) < 64


def swap_halves(x):
    return pltpu.roll(x, 64, x.ndim - 1)


def faces_kernel(x_ref, v_ref, low_ref, high_ref):
    def plane(i, carry):
        columns = pl.ds(pl.multiple_of(i * 256, 256), 256)
        turned = x_ref[:, columns].astype(F32).T.astype(BF16).reshape(SIDE, SIDE, LANES)
        v_ref[i] = turned
        low_ref[i] = turned[0]
        high_ref[i] = turned[SIDE - 1]
        return carry

    lax.fori_loop(0, SIDE, plane, 0)


def faces_call(x):
    face = jax.ShapeDtypeStruct((SIDE, SIDE, LANES), BF16)
    return pl.pallas_call(
        faces_kernel,
        out_shape=(jax.ShapeDtypeStruct((SIDE, SIDE, SIDE, LANES), BF16), face, face),
        in_specs=[VMEM_SPEC],
        out_specs=(VMEM_SPEC,) * 3,
        compiler_params=params(16),
        cost_estimate=pl.CostEstimate(flops=0, bytes_accessed=4_000_000, transcendentals=0),
        name="faces",
    )(x)


def find_octant(child_ref, wanted):
    place = jnp.int32(0)
    found = jnp.int32(0)
    for o in range(8):
        hit = (child_ref[0, o] == wanted).astype(jnp.int32)
        place = place + hit * o
        found = found + hit
    return place, found


def cot_kernel(child_ref, rank_ref, cot_ref, own_ref, send_ref, turned_ref):
    def plane(i, carry):
        columns = pl.ds(pl.multiple_of(i * 256, 256), 256)
        turned = cot_ref[:, columns].astype(F32).T
        turned_ref[i // HALF, i % HALF] = turned.reshape(2, HALF, 2, HALF, LANES)
        return carry

    lax.fori_loop(0, SIDE, plane, 0)
    rank = rank_ref[0]
    for out_ref, holder in ((own_ref, rank), (send_ref, rank ^ 1)):
        for slot in range(2):
            place, found = find_octant(child_ref, holder * 2 + slot)
            block = turned_ref[place // 4, :, place // 2 % 2, :, place % 2]
            block = jnp.where(found > 0, block, jnp.zeros_like(block))
            out_ref[slot] = block.reshape(512, LANES).astype(BF16)


def cot_call(children, rank, cot):
    blocks = jax.ShapeDtypeStruct((2, 512, LANES), BF16)
    return pl.pallas_call(
        cot_kernel,
        out_shape=(blocks, blocks),
        in_specs=[SMEM_SPEC, SMEM_SPEC, VMEM_SPEC],
        out_specs=(VMEM_SPEC,) * 2,
        scratch_shapes=[pltpu.VMEM((2, HALF, 2, HALF, 2, HALF, LANES), F32)],
        compiler_params=params(20),
        cost_estimate=pl.CostEstimate(flops=0, bytes_accessed=4_000_000, transcendentals=0),
        name="cot",
    )(children, rank, cot)


def coarse_kernel(child_ref, rank_ref, mine_ref, theirs_ref, out_ref, whole_ref):
    rank = rank_ref[0]
    for o in range(8):
        entry = child_ref[0, o]
        slot = jnp.maximum(entry, 0) % 2
        here = jnp.maximum(entry, 0) // 2 == rank
        mine = mine_ref[slot].astype(F32)
        theirs = theirs_ref[slot].astype(F32)
        block = jnp.where(here, mine, theirs)
        block = jnp.where(entry >= 0, block, jnp.zeros_like(block))
        whole_ref[o // 4, :, o // 2 % 2, :, o % 2] = block.reshape(HALF, HALF, HALF, LANES)

    def plane(i, carry):
        columns = pl.ds(pl.multiple_of(i * 256, 256), 256)
        turned = whole_ref[i // HALF, i % HALF].reshape(256, LANES).T
        out_ref[:, columns] = turned.astype(BF16)
        return carry

    lax.fori_loop(0, SIDE, plane, 0)


def coarse_call(children, rank, mine, theirs):
    return pl.pallas_call(
        coarse_kernel,
        out_shape=jax.ShapeDtypeStruct((LANES, SIDE**3), BF16),
        in_specs=[SMEM_SPEC, SMEM_SPEC, VMEM_SPEC, VMEM_SPEC],
        out_specs=VMEM_SPEC,
        scratch_shapes=[pltpu.VMEM((2, HALF, 2, HALF, 2, HALF, LANES), F32)],
        compiler_params=params(20),
        cost_estimate=pl.CostEstimate(flops=0, bytes_accessed=4_000_000, transcendentals=0),
        name="coarse",
    )(children, rank, mine, theirs)


def spans(step):
    if step == 0:
        return slice(1, SIDE + 1), slice(0, SIDE)
    if step == 1:
        return slice(SIDE + 1, SIDE + 2), slice(0, 1)
    return slice(0, 1), slice(SIDE - 1, SIDE)


def shifted(span):
    return slice(span.start + 1, span.stop + 1)


def assemble(near_ref, v_ref, before_ref, after_ref, face_ref, pad_ref):
    def clear(i, carry):
        pad_ref[i, :, 0:8] = jnp.zeros((SIDE + 2, 8, LANES), F32)
        pad_ref[i, :, 16:24] = jnp.zeros((SIDE + 2, 8, LANES), F32)
        return carry

    lax.fori_loop(0, SIDE + 2, clear, 0)

    def core(i, carry):
        pad_ref[i + 1, 1 : SIDE + 1, 1 : SIDE + 1] = v_ref[i].astype(F32)
        return carry

    lax.fori_loop(0, SIDE, core, 0)
    face_ref[0] = before_ref[...].astype(F32)
    face_ref[1] = after_ref[...].astype(F32)
    lower = low_half((1, LANES))
    column = 0
    for step_x in (-1, 0, 1):
        for step_y in (-1, 0, 1):
            for step_z in (-1, 0, 1):
                if step_x == 0 and step_y == 0 and step_z == 0:
                    continue
                first, second = near_ref[0, column], near_ref[1, column]
                column += 1
                straight = [
                    jnp.logical_and(e >= 0, jnp.maximum(e, 0) % 2 == n).astype(F32)
                    for n, e in enumerate((first, second))
                ]
                crossed = [
                    jnp.logical_and(e >= 0, jnp.maximum(e, 0) % 2 != n).astype(F32)
                    for n, e in enumerate((first, second))
                ]
                keep = jnp.where(lower, straight[0], straight[1])
                cross = jnp.where(lower, crossed[0], crossed[1])
                put_x, take_x = spans(step_x)
                put_y, take_y = spans(step_y)
                put_z, take_z = spans(step_z)

                def choose(x):
                    shape = (1,) * (x.ndim - 1) + (LANES,)
                    return x * keep.reshape(shape) + swap_halves(x) * cross.reshape(shape)

                if step_y != 0:
                    side = 0 if step_y < 0 else 1
                    pad_ref[put_x, put_y.start, put_z] = choose(face_ref[side, take_x, take_z])
                elif step_x != 0:
                    pad_ref[put_x.start, put_y, put_z] = choose(
                        pad_ref[take_x.start + 1, shifted(take_y), shifted(take_z)]
                    )
                else:

                    def line(i, carry):
                        pad_ref[i + 1, put_y, put_z] = choose(
                            pad_ref[i + 1, shifted(take_y), shifted(take_z)]
                        )
                        return carry

                    lax.fori_loop(0, SIDE, line, 0)


def gather_taps(pad_ref, a0_ref, a1_ref):
    lower = low_half((SIDE, LANES))

    def plane(i, carry):
        for j in range(SIDE + 2):
            for pair in range(2):
                near = pad_ref[i, j, 2 * pair : 2 * pair + SIDE]
                far = pad_ref[i, j, 2 * pair + 1 : 2 * pair + 1 + SIDE]
                lanes = slice(pair * LANES, (pair + 1) * LANES)
                a0_ref[i, j, :, lanes] = jnp.where(lower, near, swap_halves(far)).astype(BF16)
                a1_ref[i, j, :, lanes] = jnp.where(lower, swap_halves(near), far).astype(BF16)
        return carry

    lax.fori_loop(0, SIDE + 2, plane, 0)


def convolve(a_refs, w_ref, acc_ref, group=2):
    rows = group * 256

    def clear(i, carry):
        acc_ref[i] = jnp.zeros((256, LANES), F32)
        return carry

    lax.fori_loop(0, SIDE + 4, clear, 0)
    lower = low_half((256, LANES))

    def planes(g, carry):
        start = g * group
        results = []
        for n in range(2):
            total = None
            for b in range(3):
                lhs = a_refs[n][pl.ds(start, group), b : b + SIDE].reshape(rows, 256)
                part = jnp.dot(lhs, w_ref[n, b], preferred_element_type=F32)
                total = part if total is None else total + part
            results.append(total)
        zero, one = results
        for p in range(group):
            own = slice(p * 256, (p + 1) * 256)
            z, o = zero[own], one[own]
            acc_ref[start + p + 2] += jnp.where(lower, z[:, :LANES], o[:, :LANES])
            acc_ref[start + p + 1] += swap_halves(jnp.where(lower, o[:, :LANES], z[:, :LANES]))
            acc_ref[start + p] += z[:, LANES:] + o[:, LANES:]
        return carry

    lax.fori_loop(0, (SIDE + 2) // group, planes, 0)


def taps():
    return [(t, t // 4, t // 2 % 2, t % 2) for t in range(8)]


def middle_kernel(
    near_ref,
    v_ref,
    before_ref,
    after_ref,
    w_ref,
    down_ref,
    down_t_ref,
    own_ref,
    came_ref,
    oct_ref,
    g_ref,
    low_ref,
    high_ref,
    sums_ref,
    face_ref,
    pad_ref,
    a0_ref,
    a1_ref,
    acc_ref,
    fine_ref,
    act_ref,
    turned_ref,
    cg_ref,
):
    assemble(near_ref, v_ref, before_ref, after_ref, face_ref, pad_ref)
    gather_taps(pad_ref, a0_ref, a1_ref)
    convolve((a0_ref, a1_ref), w_ref, acc_ref)

    def activate(i, carry):
        preact = acc_ref[i + 2]
        gate = 1.0 / (1.0 + jnp.exp(-preact))
        fine_ref[i // 2, i % 2] = (preact * gate).reshape(HALF, 2, SIDE, LANES)
        acc_ref[i + 2] = gate * (1.0 + preact * (1.0 - gate))
        return carry

    lax.fori_loop(0, SIDE, activate, 0)
    for t, a, b, c in taps():
        picked = fine_ref[:, a, :, b, pl.ds(c, HALF, stride=2), :]
        act_ref[:, t * LANES : (t + 1) * LANES] = picked.reshape(512, LANES).astype(BF16)
    octants = jnp.dot(act_ref[...], down_ref[...], preferred_element_type=F32).astype(BF16)
    oct_ref[0] = octants[:, :LANES]
    oct_ref[1] = octants[:, LANES:]

    grads = [own_ref[n].astype(F32) + came_ref[n].astype(F32) for n in range(2)]
    lower = low_half((LANES, LANES))
    turned_grads = [grad.T.astype(BF16) for grad in grads]
    grads = jnp.concatenate([grad.astype(BF16) for grad in grads], axis=1)
    folded = []
    for t, a, b, c in taps():
        lanes = slice(t * LANES, (t + 1) * LANES)
        spread = jnp.dot(grads, down_t_ref[:, lanes], preferred_element_type=F32)
        fine_ref[:, a, :, b, pl.ds(c, HALF, stride=2), :] = spread.reshape(HALF, HALF, HALF, LANES)
        parts = [
            jnp.dot(turned, act_ref[:, lanes], preferred_element_type=F32)
            for turned in turned_grads
        ]
        both = jnp.where(lower, parts[0], parts[1])
        folded.append(both + swap_halves(both))
    for t in range(4):
        rows = slice(CONV_ROWS + t * LANES, CONV_ROWS + (t + 1) * LANES)
        sums_ref[rows] = jnp.where(lower, folded[t], folded[t + 4]).astype(BF16)

    for p in (0, 1, SIDE + 2, SIDE + 3):
        turned_ref[p] = jnp.zeros((LANES, 256), BF16)

    def back(i, carry):
        grad = fine_ref[i // 2, i % 2].reshape(256, LANES) * acc_ref[i + 2]
        turned_ref[i + 2] = grad.T.astype(BF16)
        rounded = grad.astype(BF16).reshape(SIDE, SIDE, LANES)
        g_ref[i] = rounded
        low_ref[i] = rounded[0]
        high_ref[i] = rounded[SIDE - 1]
        return carry

    lax.fori_loop(0, SIDE, back, 0)

    cg_ref[...] = jnp.zeros_like(cg_ref)

    def weigh(i, carry):
        lhs = [
            jnp.concatenate(
                [turned_ref[i + 2 - a, n * 64 : (n + 1) * 64] for a in range(3)], axis=0
            )
            for n in range(2)
        ]
        for b in range(3):
            total = cg_ref[b]
            for n, a_ref in enumerate((a0_ref, a1_ref)):
                rhs = a_ref[i, b : b + SIDE].reshape(256, 256)
                total += jnp.dot(lhs[n], rhs, preferred_element_type=F32)
            cg_ref[b] = total
        return carry

    lax.fori_loop(0, SIDE + 2, weigh, 0)
    lower = low_half((192, LANES))
    for b in range(3):
        sums_ref[b * 192 : (b + 1) * 192] = cg_ref[b, :, :LANES].astype(BF16)
    last = [cg_ref[b, :, LANES:] for b in range(3)]
    sums_ref[576:768] = jnp.where(lower, last[0], swap_halves(last[1])).astype(BF16)
    sums_ref[768:960] = jnp.where(lower, last[2], 0.0).astype(BF16)
    sums_ref[CONV_ROWS + DOWN_ROWS :] = jnp.zeros(
        (sums_ref.shape[0] - CONV_ROWS - DOWN_ROWS, LANES), BF16
    )


def tap_scratch():
    return [
        pltpu.VMEM((2, SIDE, SIDE, LANES), F32),
        pltpu.VMEM((SIDE + 2, SIDE + 2, 24, LANES), F32),
        pltpu.VMEM((SIDE + 2, SIDE + 2, SIDE, 256), BF16),
        pltpu.VMEM((SIDE + 2, SIDE + 2, SIDE, 256), BF16),
        pltpu.VMEM((SIDE + 4, 256, LANES), F32),
    ]


def middle_call(near, v, before, after, weights, down, down_t, own, came, rows):
    face = jax.ShapeDtypeStruct((SIDE, SIDE, LANES), BF16)
    return pl.pallas_call(
        middle_kernel,
        out_shape=(
            jax.ShapeDtypeStruct((2, 512, LANES), BF16),
            jax.ShapeDtypeStruct((SIDE, SIDE, SIDE, LANES), BF16),
            face,
            face,
            jax.ShapeDtypeStruct((rows, LANES), BF16),
        ),
        in_specs=[SMEM_SPEC] + [VMEM_SPEC] * 8,
        out_specs=(VMEM_SPEC,) * 5,
        scratch_shapes=tap_scratch()
        + [
            pltpu.VMEM((HALF, 2, HALF, 2, SIDE, LANES), F32),
            pltpu.VMEM((512, 8 * LANES), BF16),
            pltpu.VMEM((SIDE + 4, LANES, 256), BF16),
            pltpu.VMEM((3, 192, 256), F32),
        ],
        compiler_params=params(44),
        cost_estimate=pl.CostEstimate(
            flops=8_000_000_000, bytes_accessed=6_000_000, transcendentals=600_000
        ),
        name="middle",
    )(near, v, before, after, weights, down, down_t, own, came)


def input_kernel(
    near_ref,
    g_ref,
    before_ref,
    after_ref,
    w_ref,
    out_ref,
    face_ref,
    pad_ref,
    a0_ref,
    a1_ref,
    acc_ref,
):
    assemble(near_ref, g_ref, before_ref, after_ref, face_ref, pad_ref)
    gather_taps(pad_ref, a0_ref, a1_ref)
    convolve((a0_ref, a1_ref), w_ref, acc_ref)

    def plane(i, carry):
        columns = pl.ds(pl.multiple_of(i * 256, 256), 256)
        out_ref[:, columns] = acc_ref[i + 2].T.astype(BF16)
        return carry

    lax.fori_loop(0, SIDE, plane, 0)


def input_call(near, g, before, after, weights):
    return pl.pallas_call(
        input_kernel,
        out_shape=jax.ShapeDtypeStruct((LANES, SIDE**3), BF16),
        in_specs=[SMEM_SPEC] + [VMEM_SPEC] * 4,
        out_specs=VMEM_SPEC,
        scratch_shapes=tap_scratch(),
        compiler_params=params(32),
        cost_estimate=pl.CostEstimate(
            flops=4_000_000_000, bytes_accessed=3_000_000, transcendentals=0
        ),
        name="input_grad",
    )(near, g, before, after, weights)


def split_kernel(sums_ref, conv_ref, down_ref):
    for a in range(3):
        rows = slice(a * 64, (a + 1) * 64)
        for b in range(3):
            for c in range(3):
                chunk, upper = (b, c) if c < 2 else ((3, b) if b < 2 else (4, 0))
                base = chunk * 192
                block = sums_ref[base + rows.start : base + rows.stop].astype(F32)
                block = swap_halves(block) if upper else block
                conv_ref[9 * a + 3 * b + c] = block[:, :64]
    for t in range(4):
        block = sums_ref[CONV_ROWS + t * LANES : CONV_ROWS + (t + 1) * LANES].astype(F32)
        down_ref[t] = block[:, :64]
        down_ref[t + 4] = swap_halves(block)[:, :64]


def split_call(sums):
    return pl.pallas_call(
        split_kernel,
        out_shape=(
            jax.ShapeDtypeStruct((27, 64, 64), F32),
            jax.ShapeDtypeStruct((8, LANES, 64), F32),
        ),
        in_specs=[VMEM_SPEC],
        out_specs=(VMEM_SPEC,) * 2,
        compiler_params=params(16),
        name="split",
    )(sums)


def tap_weights(weights):
    shaped = weights.transpose(1, 2, 3, 0, 4)
    shaped = jnp.pad(shaped, ((0, 0), (0, 1), (0, 0), (0, 1), (0, 0)))
    first = shaped.reshape(3, 256, 256)
    second = shaped[:, :, :, jnp.array([1, 0, 3, 2])].reshape(3, 256, 256)
    return jnp.stack([first, second])


def both_ways(array, axis):
    peers = lax.axis_size(axis)
    up = [(i, i + 1) for i in range(peers - 1)]
    down = [(j, i) for i, j in up]
    low, high = array
    return lax.ppermute(high, axis, up), lax.ppermute(low, axis, down)


def from_partner(array, axis):
    return lax.ppermute(array, axis, [(i, i ^ 1) for i in range(lax.axis_size(axis))])


def total_sums(sums):
    axes = ("grp", "dev")
    peers = lax.axis_size("grp") * lax.axis_size("dev")
    shares = lax.all_to_all(sums.reshape(peers, SHARE, LANES), axes, 0, 0)
    mine = jnp.sum(shares.astype(F32), axis=0).astype(BF16)
    return lax.all_gather(mine, axes, axis=0, tiled=True)


def body(fine_input, conv_weight, down_weight, coarse_cot, neighbours, children):
    rank = lax.axis_index("grp") * lax.axis_size("dev") + lax.axis_index("dev")
    rank = rank.reshape(1).astype(jnp.int32)
    peers = lax.axis_size("grp") * lax.axis_size("dev")

    own, send = cot_call(children, rank, coarse_cot.reshape(LANES, SIDE**3))
    came = from_partner(send, "dev")
    voxels, low, high = faces_call(fine_input.reshape(LANES, SIDE**3))
    before, after = both_ways((low, high), "dev")

    taps_in = conv_weight.reshape(3, 3, 3, 64, 64)
    forward = tap_weights(taps_in.transpose(0, 1, 2, 4, 3))
    backward = tap_weights(taps_in[::-1, ::-1, ::-1])
    eye = jnp.eye(2, dtype=BF16)
    down_t = (
        down_weight.transpose(1, 0, 2)[None, :, :, None, :] * eye[:, None, None, :, None]
    ).reshape(256, 8 * LANES)
    down = down_t.T

    octants, grads, grad_low, grad_high, sums = middle_call(
        neighbours, voxels, before, after, forward, down, down_t, own, came, peers * SHARE
    )
    grad_before, grad_after = both_ways((grad_low, grad_high), "dev")
    theirs = from_partner(octants, "dev")
    gathered = total_sums(sums)
    coarse = coarse_call(children, rank, octants, theirs)
    input_grad = input_call(neighbours, grads, grad_before, grad_after, backward)
    conv_grad, down_grad = split_call(gathered)
    return (
        coarse.reshape(1, LANES, SIDE**3),
        input_grad.reshape(2, 64, SIDE**3),
        conv_grad,
        down_grad,
    )


def solution(mesh):
    in_specs = (
        P(("grp", "dev"), None, None),
        P(),
        P(),
        P(("grp", "dev"), None, None),
        P(("grp", "dev"), None),
        P(("grp", "dev"), None),
    )
    out_specs = (P(("grp", "dev"), None, None), P(("grp", "dev"), None, None), P(), P())
    return jax.shard_map(body, mesh=mesh, in_specs=in_specs, out_specs=out_specs, check_vma=False)
```

time: 654 us -> 181 us (0.28)
  waiting for transfers between devices: 178 us -> 2.11 us
  other arithmetic: 173 us -> 1.97 us
  local copies, waits for them, and re-layouts: 190 us -> 20.2 us
  matrix products: 78.5 us -> 0 us
  blocking collectives: 0 us -> 73.4 us
  Pallas kernels: 0 us -> 48.9 us
  starting transfers between devices: 14.4 us -> 31.8 us
  between operations: 15.8 us -> 0.9 us
    psum x1 -> x0, waiting for transfers between devices: 178 us -> none  [body(): conv_grad, down_sum = lax.psum((conv_part, down_part), ('grp', 'dev'))]
    all_gather x0 -> x1, blocking collectives: none -> 73.4 us  [total_sums(): return lax.all_gather(mine, axes, axis=0, tiled=True)]
    concatenate x10 -> x0, other arithmetic: 66.2 us -> none  [the longest x2 60.3 us: assemble(): return jnp.concatenate(slabs, axis=2)]
    transpose x2 -> x0, other arithmetic: 58.4 us -> none  [the longest x1 57.3 us: tap_grads(): return result.transpose(2, 3, 4, 1, 0).reshape(27, outs, channels)]
    pallas_call x0 -> x6, Pallas kernels: none -> 48.9 us  [the longest x1 23.7 us: middle_call(): pl.pallas_call(middle_kernel, out_shape=(jax.ShapeDtypeStruct((2, 512, LA...]
    reshape x3 -> x2, local copies, waits for them, and re-layouts: 48.4 us -> 1.01 us  [body(): taps_in = conv_weight.reshape(3, 3, 3, 64, 64)]
    conv_general_dilated x2 -> x0, matrix products: 41.3 us -> none  [conv_taps(): lax.conv_general_dilated(padded, kernel, (1, 1, 1), 'VALID', dimension_nu...]
    gather x53 -> x4, local copies, waits for them, and re-layouts: 42.3 us -> 4.59 us  [tap_weights(): second = shaped[:, :, :, jnp.array([1, 0, 3, 2])].reshape(3, 256, 256)]
  transfers between devices with their start and end apart: 7 -> 7, of which waited for: 1 -> 1; matrix products, arithmetic and copies ran while one was open for 66% -> 7% of each run, Pallas kernels for 0% -> 12%
where the time goes in v1:
time: 181 us; the launch traced here: 179 us
  blocking collectives  73.4 us (41%)
  Pallas kernels  48.9 us (27%)
  starting transfers between devices  31.8 us (18%)
  local copies, waits for them, and re-layouts  20.2 us (11%)
  waiting for transfers between devices  2.11 us (1%)
  other arithmetic  1.97 us (1%)
    all_gather x1, blocking collectives, total_sums(): return lax.all_gather(mine, axes, axis=0, tiled=True)  73.4 us
    pallas_call x1, Pallas kernels, middle_call(): pl.pallas_call(middle_kernel, out_shape=(jax.ShapeDtypeStruct((2, 512, LA...  23.7 us
    all_to_all x1, starting transfers between devices, total_sums(): shares = lax.all_to_all(sums.reshape(peers, SHARE, LANES), axes, 0, 0)  19.6 us
    pallas_call x1, Pallas kernels, input_call(): pl.pallas_call(input_kernel, out_shape=jax.ShapeDtypeStruct((LANES, SIDE...  15.3 us
    unnamed x36, local copies, waits for them, and re-layouts  9.1 us
    ppermute x4, starting transfers between devices, both_ways(): return (lax.ppermute(high, axis, up), lax.ppermute(low, axis, down))  7.77 us
    gather x4, local copies, waits for them, and re-layouts, tap_weights(): second = shaped[:, :, :, jnp.array([1, 0, 3, 2])].reshape(3, 256, 256)  4.59 us
    ppermute x2, starting transfers between devices, from_partner(): lax.ppermute(array, axis, [(i, i ^ 1) for i in range(lax.axis_size(axis))])  4.39 us
  transfers between devices with their start and end apart: 7, of which 1 were waited for; matrix products, arithmetic and copies ran while one was open for 7% of the time, Pallas kernels for 12%

profile of v1, /device:TPU:1, one launch (start us, length us, event | category | flops | bytes accessed | tf_op | source)
XLA Modules:
  0.0 179.3 jit_solution(16930333924733417342)
XLA Ops:
  0.6 0.6 copy-done.2
  1.3 1.2 copy-done
  2.5 3.0 %cot.1 = (bf16[2,512,128]{2,1,0:T(8,128)(2,1)S(1)}, bf16[2,512,128]{2,1,0:T(8,128)(2,1)}) custom-call(s32[1,8]{1,0:T(1,128)S(1)} %copy-done.2, s32[1]{0:T(128)} %bitcast.rank_ref, bf16[128,4096]{1,0:T(8,128)(2,1)S(1)} %bitcast.26), custom_call_target="tpu_custom_call" | custom-call | bytes 4000000 | tf_op jit(solution)/shard_map/cot/pallas_call | solution.py:89
  5.6 2.0 %collective-permute-start.2 = (bf16[2,512,128]{2,1,0:T(8,128)(2,1)}, bf16[2,512,128]{2,1,0:T(8,128)(2,1)S(1)}, u32[]{:S(2)}, u32[]{:S(2)}) collective-permute-start(bf16[2,512,128]{2,1,0:T(8,128)(2,1)} %get-tuple-element.20), channel_id=1, source_target_pairs={{0,1},{1,0},{2,3},{3,2},{4,5},{5,4},{6,7},{7,6},{8,9},{9,8},{10,11... | collective-permute-start | bytes 786440 | tf_op jit(solution)/shard_map/ppermute | solution.py:490
  7.6 2.3 %faces.1 = (bf16[16,16,16,128]{3,2,1,0:T(8,128)(2,1)S(1)}, bf16[16,16,128]{2,1,0:T(8,128)(2,1)}, bf16[16,16,128]{2,1,0:T(8,128)(2,1)}) custom-call(bf16[128,4096]{1,0:T(8,128)(2,1)S(1)} %bitcast.27), custom_call_target="tpu_custom_call" | custom-call | bytes 4000000 | tf_op jit(solution)/shard_map/faces/pallas_call | solution.py:49
  9.9 1.9 %collective-permute-start = (bf16[16,16,128]{2,1,0:T(8,128)(2,1)}, bf16[16,16,128]{2,1,0:T(8,128)(2,1)S(1)}, u32[]{:S(2)}, u32[]{:S(2)}) collective-permute-start(bf16[16,16,128]{2,1,0:T(8,128)(2,1)} %get-tuple-element.17), channel_id=1, source_target_pairs={{0,1},{1,2},{2,3},{3,4},{4,5},{5,6},{6,7},{7,8},{8,9},{9,10},{10,1... | collective-permute-start | bytes 196616 | tf_op jit(solution)/shard_map/ppermute | solution.py:486
  11.8 1.3 collective-permute-start.1
  13.2 1.0 copy.24
  14.1 1.2 pad.7
  16.0 1.5 gather_fusion
  17.5 1.8 copy.26
  19.3 1.2 stack_reshape.13
  22.4 0.6 copy-done.7
  23.0 0.7 copy-done.3
  23.7 0.7 copy-done.9
  24.4 0.9 copy-done.4
  25.4 0.8 copy-done.8
  26.2 23.7 %middle.1 = (bf16[2,512,128]{2,1,0:T(8,128)(2,1)S(1)}, bf16[16,16,16,128]{3,2,1,0:T(8,128)(2,1)S(1)}, bf16[16,16,128]{2,1,0:T(8,128)(2,1)S(1)}, bf16[16,16,128]{2,1,0:T(8,128)(2,1)S(1)}, bf16[2048,128]{1,0:T(8,128)(2,1)}) custom-call(s32[2,26]{1,0:T(2,128)S(1)} %copy-done.9, bf16[16,16,16,128]{3,2,1,0:T(8,128)(2,1)S(1)} %get-tuple-element.16.v_ref, ...), custom_call_target="tpu_custom_call" | custom-call | flops 8000000000 | bytes 6000000 | tf_op jit(solution)/shard_map/middle/pallas_call | solution.py:377
  50.0 0.6 copy-done.5
  50.6 1.0 copy-done.10
  51.5 19.6 %all-to-all-start = ((bf16[256,8,128]{2,1,0:T(8,128)(2,1)}), bf16[256,8,128]{2,1,0:T(8,128)(2,1)}, u32[]{:S(2)}, u32[]{:S(2)}) async-start(bf16[256,8,128]{2,1,0:T(8,128)(2,1)} %bitcast.12), calls=%async_computation | async-start | bytes 1048576 | tf_op jit(solution)/shard_map/all_to_all | solution.py:496
  71.4 0.7 gather_fusion.1
  74.7 3.3 %collective-permute-start.4 = (bf16[16,16,128]{2,1,0:T(8,128)(2,1)S(1)}, bf16[16,16,128]{2,1,0:T(8,128)(2,1)S(1)}, u32[]{:S(2)}, u32[]{:S(2)}) collective-permute-start(bf16[16,16,128]{2,1,0:T(8,128)(2,1)S(1)} %copy-done.6), channel_id=1, source_target_pairs={{0,1},{1,2},{2,3},{3,4},{4,5},{5,6},{6,7},{7,8},{8,9},{9,10},{10,1... | collective-permute-start | bytes 196616 | tf_op jit(solution)/shard_map/ppermute | solution.py:486
  78.0 1.3 collective-permute-start.5
  79.4 2.3 %collective-permute-start.3 = (bf16[2,512,128]{2,1,0:T(8,128)(2,1)S(1)}, bf16[2,512,128]{2,1,0:T(8,128)(2,1)S(1)}, u32[]{:S(2)}, u32[]{:S(2)}) collective-permute-start(bf16[2,512,128]{2,1,0:T(8,128)(2,1)S(1)} %get-tuple-element.21.mine_ref), channel_id=1, source_target_pairs={{0,1},{1,0},{2,3},{3,2},{4,5},{5,4},{6,7},{7,6},{8,9},{9,8},{10,11... | collective-permute-start | bytes 786440 | tf_op jit(solution)/shard_map/ppermute | solution.py:490
  81.7 2.1 %collective-permute-done.5.after_ref = bf16[16,16,128]{2,1,0:T(8,128)(2,1)S(1)} collective-permute-done((bf16[16,16,128]{2,1,0:T(8,128)(2,1)S(1)}, bf16[16,16,128]{2,1,0:T(8,128)(2,1)S(1)}, u32[]{:S(2)}, u32[]{:S(2)}) %collective-permute-start.5) | collective-permute-done | bytes 65568 | tf_op jit(solution)/shard_map/ppermute | solution.py:486
  83.8 15.3 %input_grad.1 = bf16[128,4096]{1,0:T(8,128)(2,1)} custom-call(s32[2,26]{1,0:T(2,128)S(1)} %copy-done.9, bf16[16,16,16,128]{3,2,1,0:T(8,128)(2,1)S(1)} %copy-done.11, bf16[16,16,128]{2,1,0:T(8,128)(2,1)S(1)} %collective-permute-done.4.before_ref, bf16[16,16,128]{2,1,0:T(8,128)(2,1)S(1)} %collective-permute-done.5.after_ref, ...), custom_call_target="tpu_custom_call" | custom-call | flops 4000000000 | bytes 3000000 | tf_op jit(solution)/shard_map/input_grad/pallas_call | solution.py:429
  99.2 3.5 %coarse.1 = bf16[128,4096]{1,0:T(8,128)(2,1)} custom-call(s32[1,8]{1,0:T(1,128)S(1)} %copy-done.2, s32[1]{0:T(128)} %bitcast.rank_ref, bf16[2,512,128]{2,1,0:T(8,128)(2,1)S(1)} %get-tuple-element.21.mine_ref, bf16[2,512,128]{2,1,0:T(8,128)(2,1)S(1)} %collective-permute-done.3.theirs_ref), custom_call_target="tpu_custom_call" | custom-call | bytes 4000000 | tf_op jit(solution)/shard_map/coarse/pallas_call | solution.py:123
  102.7 1.3 reduce_sum.12
  104.0 73.4 %all_gather.3.sums_ref = bf16[2048,128]{1,0:T(8,128)(2,1)S(1)} all-gather(bf16[8,128]{1,0:T(8,128)(2,1)S(1)} %reduce_sum.12), channel_id=1, replica_groups=mesh['grp'=8,'dev'=32] {'grp','dev'}, dimensions={0}, use_global_device_ids=true | all-gather | bytes 526336 | tf_op jit(solution)/shard_map/all_gather | solution.py:498
  177.3 1.0 split.1
  178.4 0.9 copy.31
  (47 shorter events, 5.4 us)
Async XLA Ops:
  0.6 0.7 copy-start.2
  1.3 1.2 copy-start
  2.5 5.1 %copy-start.1 = (bf16[2,64,4096]{2,1,0:T(8,128)(2,1)S(1)}, bf16[2,64,4096]{2,1,0:T(8,128)(2,1)}, u32[]{:S(2)}) copy-start(bf16[2,64,4096]{2,1,0:T(8,128)(2,1)} %param.8) | copy-start | bytes 3145732
  5.6 17.5 %collective-permute-start.2 = (bf16[2,512,128]{2,1,0:T(8,128)(2,1)}, bf16[2,512,128]{2,1,0:T(8,128)(2,1)S(1)}, u32[]{:S(2)}, u32[]{:S(2)}) collective-permute-start(bf16[2,512,128]{2,1,0:T(8,128)(2,1)} %get-tuple-element.20), channel_id=1, source_target_pairs={{0,1},{1,0},{2,3},{3,2},{4,5},{5,4},{6,7},{7,6},{8,9},{9,8},{10,11... | collective-permute-start | bytes 786440 | tf_op jit(solution)/shard_map/ppermute | solution.py:490
  7.6 5.5 %copy-start.12 = (bf16[27,64,64]{2,1,0:T(8,128)(2,1)S(1)}, bf16[27,64,64]{2,1,0:T(8,128)(2,1)}, u32[]{:S(2)}) copy-start(bf16[27,64,64]{2,1,0:T(8,128)(2,1)} %param.9) | copy-start | bytes 663556
  9.9 12.5 %collective-permute-start = (bf16[16,16,128]{2,1,0:T(8,128)(2,1)}, bf16[16,16,128]{2,1,0:T(8,128)(2,1)S(1)}, u32[]{:S(2)}, u32[]{:S(2)}) collective-permute-start(bf16[16,16,128]{2,1,0:T(8,128)(2,1)} %get-tuple-element.17), channel_id=1, source_target_pairs={{0,1},{1,2},{2,3},{3,4},{4,5},{5,6},{6,7},{7,8},{8,9},{9,10},{10,1... | collective-permute-start | bytes 196616 | tf_op jit(solution)/shard_map/ppermute | solution.py:486
  11.8 10.6 %collective-permute-start.1 = (bf16[16,16,128]{2,1,0:T(8,128)(2,1)}, bf16[16,16,128]{2,1,0:T(8,128)(2,1)S(1)}, u32[]{:S(2)}, u32[]{:S(2)}) collective-permute-start(bf16[16,16,128]{2,1,0:T(8,128)(2,1)} %get-tuple-element.18), channel_id=1, source_target_pairs={{1,0},{2,1},{3,2},{4,3},{5,4},{6,5},{7,6},{8,7},{9,8},{10,9},{11,1... | collective-permute-start | bytes 196616 | tf_op jit(solution)/shard_map/ppermute | solution.py:486
  13.1 1.0 copy-start.16
  20.5 0.9 copy-start.15
  21.0 1.0 copy-start.14
  22.4 0.6 copy-start.7
  23.0 0.7 copy-start.3
  23.7 0.7 copy-start.9
  24.4 0.9 copy-start.4
  25.4 0.8 copy-start.8
  49.9 0.6 copy-start.5
  50.6 1.0 copy-start.10
  51.5 19.6 %copy-start.13 = (bf16[27,64,64]{2,1,0:T(8,128)(2,1)S(1)}, bf16[27,64,64]{2,1,0:T(8,128)(2,1)}, u32[]{:S(2)}) copy-start(bf16[27,64,64]{2,1,0:T(8,128)(2,1)} %param.9) | copy-start | bytes 663556
  51.5 51.1 %all-to-all-start = ((bf16[256,8,128]{2,1,0:T(8,128)(2,1)}), bf16[256,8,128]{2,1,0:T(8,128)(2,1)}, u32[]{:S(2)}, u32[]{:S(2)}) async-start(bf16[256,8,128]{2,1,0:T(8,128)(2,1)} %bitcast.12), calls=%async_computation | async-start | bytes 1048576 | tf_op jit(solution)/shard_map/all_to_all | solution.py:496
  73.9 0.8 copy-start.6
  74.4 9.5 %copy-start.11 = (bf16[16,16,16,128]{3,2,1,0:T(8,128)(2,1)S(1)}, bf16[16,16,16,128]{3,2,1,0:T(8,128)(2,1)}, u32[]{:S(2)}) copy-start(bf16[16,16,16,128]{3,2,1,0:T(8,128)(2,1)} %copy-done.10) | copy-start | bytes 3145732
  74.7 7.0 %collective-permute-start.4 = (bf16[16,16,128]{2,1,0:T(8,128)(2,1)S(1)}, bf16[16,16,128]{2,1,0:T(8,128)(2,1)S(1)}, u32[]{:S(2)}, u32[]{:S(2)}) collective-permute-start(bf16[16,16,128]{2,1,0:T(8,128)(2,1)S(1)} %copy-done.6), channel_id=1, source_target_pairs={{0,1},{1,2},{2,3},{3,4},{4,5},{5,6},{6,7},{7,8},{8,9},{9,10},{10,1... | collective-permute-start | bytes 196616 | tf_op jit(solution)/shard_map/ppermute | solution.py:486
  78.0 5.8 %collective-permute-start.5 = (bf16[16,16,128]{2,1,0:T(8,128)(2,1)S(1)}, bf16[16,16,128]{2,1,0:T(8,128)(2,1)S(1)}, u32[]{:S(2)}, u32[]{:S(2)}) collective-permute-start(bf16[16,16,128]{2,1,0:T(8,128)(2,1)S(1)} %get-tuple-element.24), channel_id=1, source_target_pairs={{1,0},{2,1},{3,2},{4,3},{5,4},{6,5},{7,6},{8,7},{9,8},{10,9},{11,1... | collective-permute-start | bytes 196616 | tf_op jit(solution)/shard_map/ppermute | solution.py:486
  79.4 19.8 %collective-permute-start.3 = (bf16[2,512,128]{2,1,0:T(8,128)(2,1)S(1)}, bf16[2,512,128]{2,1,0:T(8,128)(2,1)S(1)}, u32[]{:S(2)}, u32[]{:S(2)}) collective-permute-start(bf16[2,512,128]{2,1,0:T(8,128)(2,1)S(1)} %get-tuple-element.21.mine_ref), channel_id=1, source_target_pairs={{0,1},{1,0},{2,3},{3,2},{4,5},{5,4},{6,7},{7,6},{8,9},{9,8},{10,11... | collective-permute-start | bytes 786440 | tf_op jit(solution)/shard_map/ppermute | solution.py:490

commit v2 on v1

v2 whole, which is shorter than its diff:
```python
import jax
import jax.numpy as jnp
from jax import lax
from jax.experimental import pallas as pl
from jax.experimental.pallas import tpu as pltpu
from jax.sharding import PartitionSpec as P

SIDE = 16
HALF = 8
LANES = 128
F32 = jnp.float32
BF16 = jnp.bfloat16
CONV_ROWS = 960
DOWN_ROWS = 512
SHARE = 8

VMEM_SPEC = pl.BlockSpec(memory_space=pltpu.VMEM)
SMEM_SPEC = pl.BlockSpec(memory_space=pltpu.SMEM)


def params(mib):
    return pltpu.CompilerParams(vmem_limit_bytes=mib * 1024 * 1024)


def low_half(shape):
    return lax.broadcasted_iota(jnp.int32, shape, len(shape) - 1) < 64


def swap_halves(x):
    return pltpu.roll(x, 64, x.ndim - 1)


def place_faces(rank_ref, i, planes, pair_ref, other_ref):
    even = rank_ref[0] % 2 == 0
    low, high = planes[0], planes[SIDE - 1]
    pair_ref[pl.ds(pl.multiple_of(1024 + i * SIDE, SIDE), SIDE)] = jnp.where(even, high, low)
    other_ref[pl.ds(pl.multiple_of(i * SIDE, SIDE), SIDE)] = jnp.where(even, low, high)


def find_octant(child_ref, wanted):
    place = jnp.int32(0)
    found = jnp.int32(0)
    for o in range(8):
        hit = (child_ref[0, o] == wanted).astype(jnp.int32)
        place = place + hit * o
        found = found + hit
    return place, found


def first_kernel(
    child_ref, rank_ref, cot_ref, x_ref, own_ref, v_ref, pair_ref, other_ref, turned_ref
):
    def plane(i, carry):
        columns = pl.ds(pl.multiple_of(i * 256, 256), 256)
        turned = cot_ref[:, columns].astype(F32).T
        turned_ref[i // HALF, i % HALF] = turned.reshape(2, HALF, 2, HALF, LANES)
        voxels = x_ref[:, columns].astype(F32).T.astype(BF16).reshape(SIDE, SIDE, LANES)
        v_ref[i] = voxels
        place_faces(rank_ref, i, voxels, pair_ref, other_ref)
        return carry

    lax.fori_loop(0, SIDE, plane, 0)
    rank = rank_ref[0]
    for out_ref, holder in ((own_ref, rank), (pair_ref, rank ^ 1)):
        for slot in range(2):
            place, found = find_octant(child_ref, holder * 2 + slot)
            block = turned_ref[place // 4, :, place // 2 % 2, :, place % 2]
            block = jnp.where(found > 0, block, jnp.zeros_like(block))
            out_ref[slot * 512 : (slot + 1) * 512] = block.reshape(512, LANES).astype(BF16)


def first_call(children, rank, cot, x):
    return pl.pallas_call(
        first_kernel,
        out_shape=(
            jax.ShapeDtypeStruct((1024, LANES), BF16),
            jax.ShapeDtypeStruct((SIDE, SIDE, SIDE, LANES), BF16),
            jax.ShapeDtypeStruct((1280, LANES), BF16),
            jax.ShapeDtypeStruct((256, LANES), BF16),
        ),
        in_specs=[SMEM_SPEC, SMEM_SPEC, VMEM_SPEC, VMEM_SPEC],
        out_specs=(VMEM_SPEC,) * 4,
        scratch_shapes=[pltpu.VMEM((2, HALF, 2, HALF, 2, HALF, LANES), F32)],
        compiler_params=params(20),
        cost_estimate=pl.CostEstimate(flops=0, bytes_accessed=8_000_000, transcendentals=0),
        name="first",
    )(children, rank, cot, x)


def weights_kernel(
    conv_ref, down_in_ref, forward_ref, backward_ref, down_ref, down_t_ref
):
    blank = jnp.zeros((64, 64), F32)
    for b in range(3):
        for c in range(4):
            rows = slice(b * 256 + c * 64, b * 256 + (c + 1) * 64)
            if c == 3:
                for n in range(2):
                    forward_ref[n, rows] = jnp.zeros((64, 256), BF16)
                    backward_ref[n, rows] = jnp.zeros((64, 256), BF16)
                continue
            ahead = [conv_ref[9 * a + 3 * b + c].astype(F32) for a in range(3)]
            behind = [conv_ref[26 - (9 * a + 3 * b + c)].astype(F32) for a in range(3)]
            for n in range(2):
                order = (0, 1, 2, None) if n == 0 else (1, 0, None, 2)
                for half in range(2):
                    pair = order[2 * half : 2 * half + 2]
                    lanes = slice(half * LANES, (half + 1) * LANES)
                    taps = [blank if a is None else ahead[a] for a in pair]
                    forward_ref[n, rows, lanes] = jnp.concatenate(taps, axis=0).T.astype(BF16)
                    taps = [blank if a is None else behind[a] for a in pair]
                    backward_ref[n, rows, lanes] = jnp.concatenate(taps, axis=1).astype(BF16)
    for t in range(8):
        tap = down_in_ref[t]
        blank = jnp.zeros((64, LANES), BF16)
        rows = [jnp.concatenate([tap, blank], axis=1), jnp.concatenate([blank, tap], axis=1)]
        block = jnp.concatenate(rows, axis=0)
        down_ref[t * LANES : (t + 1) * LANES] = block
        down_t_ref[:, t * LANES : (t + 1) * LANES] = block.astype(F32).T.astype(BF16)


def weights_call(conv_weight, down_weight):
    conv = jax.ShapeDtypeStruct((2, 768, 256), BF16)
    return pl.pallas_call(
        weights_kernel,
        out_shape=(
            conv,
            conv,
            jax.ShapeDtypeStruct((8 * LANES, 256), BF16),
            jax.ShapeDtypeStruct((256, 8 * LANES), BF16),
        ),
        in_specs=[VMEM_SPEC] * 2,
        out_specs=(VMEM_SPEC,) * 4,
        compiler_params=params(16),
        cost_estimate=pl.CostEstimate(flops=0, bytes_accessed=8_000_000, transcendentals=0),
        name="weights",
    )(conv_weight, down_weight)


def coarse_kernel(child_ref, rank_ref, mine_ref, theirs_ref, out_ref, whole_ref):
    rank = rank_ref[0]
    for o in range(8):
        entry = child_ref[0, o]
        slot = jnp.maximum(entry, 0) % 2
        here = jnp.maximum(entry, 0) // 2 == rank
        rows = pl.ds(pl.multiple_of(slot * 512, 512), 512)
        mine = mine_ref[rows].astype(F32)
        theirs = theirs_ref[rows].astype(F32)
        block = jnp.where(here, mine, theirs)
        block = jnp.where(entry >= 0, block, jnp.zeros_like(block))
        whole_ref[o // 4, :, o // 2 % 2, :, o % 2] = block.reshape(HALF, HALF, HALF, LANES)

    def plane(i, carry):
        columns = pl.ds(pl.multiple_of(i * 256, 256), 256)
        turned = whole_ref[i // HALF, i % HALF].reshape(256, LANES).T
        out_ref[:, columns] = turned.astype(BF16)
        return carry

    lax.fori_loop(0, SIDE, plane, 0)


def coarse_call(children, rank, mine, theirs):
    return pl.pallas_call(
        coarse_kernel,
        out_shape=jax.ShapeDtypeStruct((LANES, SIDE**3), BF16),
        in_specs=[SMEM_SPEC, SMEM_SPEC, VMEM_SPEC, VMEM_SPEC],
        out_specs=VMEM_SPEC,
        scratch_shapes=[pltpu.VMEM((2, HALF, 2, HALF, 2, HALF, LANES), F32)],
        compiler_params=params(20),
        cost_estimate=pl.CostEstimate(flops=0, bytes_accessed=4_000_000, transcendentals=0),
        name="coarse",
    )(children, rank, mine, theirs)


def spans(step):
    if step == 0:
        return slice(1, SIDE + 1), slice(0, SIDE)
    if step == 1:
        return slice(SIDE + 1, SIDE + 2), slice(0, 1)
    return slice(0, 1), slice(SIDE - 1, SIDE)


def shifted(span):
    return slice(span.start + 1, span.stop + 1)


def assemble(near_ref, rank_ref, v_ref, pair_ref, other_ref, face_ref, pad_ref):
    def core(i, carry):
        pad_ref[i, :, 16:24] = jnp.zeros((SIDE + 2, 8, LANES), F32)

        @pl.when(jnp.logical_and(i >= 1, i <= SIDE))
        def _():
            pad_ref[i, 1 : SIDE + 1, 1 : SIDE + 1] = v_ref[i - 1].astype(F32)

        return carry

    lax.fori_loop(0, SIDE + 2, core, 0)
    even = rank_ref[0] % 2 == 0
    pair = pair_ref[1024:1280].astype(F32).reshape(SIDE, SIDE, LANES)
    other = other_ref[...].astype(F32).reshape(SIDE, SIDE, LANES)
    face_ref[0] = jnp.where(even, other, pair)
    face_ref[1] = jnp.where(even, pair, other)
    lower = low_half((1, LANES))
    column = 0
    ends = []
    for step_x in (-1, 0, 1):
        for step_y in (-1, 0, 1):
            for step_z in (-1, 0, 1):
                if step_x == 0 and step_y == 0 and step_z == 0:
                    continue
                entries = near_ref[0, column], near_ref[1, column]
                column += 1
                straight = [
                    jnp.logical_and(e >= 0, jnp.maximum(e, 0) % 2 == n).astype(F32)
                    for n, e in enumerate(entries)
                ]
                crossed = [
                    jnp.logical_and(e >= 0, jnp.maximum(e, 0) % 2 != n).astype(F32)
                    for n, e in enumerate(entries)
                ]
                keep = jnp.where(lower, straight[0], straight[1])
                cross = jnp.where(lower, crossed[0], crossed[1])
                put_x, take_x = spans(step_x)
                put_y, take_y = spans(step_y)
                put_z, take_z = spans(step_z)

                def choose(x, keep=keep, cross=cross):
                    shape = (1,) * (x.ndim - 1) + (LANES,)
                    return x * keep.reshape(shape) + swap_halves(x) * cross.reshape(shape)

                if step_y != 0:
                    side = 0 if step_y < 0 else 1
                    pad_ref[put_x, put_y.start, put_z] = choose(face_ref[side, take_x, take_z])
                elif step_x != 0:
                    pad_ref[put_x.start, put_y, put_z] = choose(
                        pad_ref[take_x.start + 1, shifted(take_y), shifted(take_z)]
                    )
                else:
                    ends.append((choose, put_z, shifted(take_z)))

    def line(i, carry):
        for choose, put_z, take_z in ends:
            pad_ref[i + 1, 1 : SIDE + 1, put_z] = choose(pad_ref[i + 1, 1 : SIDE + 1, take_z])
        return carry

    lax.fori_loop(0, SIDE, line, 0)


def gather_taps(pad_ref, a0_ref, a1_ref):
    lower = low_half((SIDE, LANES))

    def plane(i, carry):
        for j in range(SIDE + 2):
            for pair in range(2):
                near = pad_ref[i, j, 2 * pair : 2 * pair + SIDE]
                far = pad_ref[i, j, 2 * pair + 1 : 2 * pair + 1 + SIDE]
                lanes = slice(pair * LANES, (pair + 1) * LANES)
                a0_ref[i, j, :, lanes] = jnp.where(lower, near, swap_halves(far)).astype(BF16)
                a1_ref[i, j, :, lanes] = jnp.where(lower, swap_halves(near), far).astype(BF16)
        return carry

    lax.fori_loop(0, SIDE + 2, plane, 0)


def convolve(a_refs, w_ref, acc_ref, group=3):
    rows = group * 256

    def clear(i, carry):
        acc_ref[i] = jnp.zeros((256, LANES), F32)
        return carry

    lax.fori_loop(0, SIDE + 4, clear, 0)
    lower = low_half((256, LANES))

    def planes(g, carry):
        start = g * group
        results = []
        for n in range(2):
            lhs = [
                a_refs[n][pl.ds(start, group), b : b + SIDE].reshape(rows, 256) for b in range(3)
            ]
            lhs = jnp.concatenate(lhs, axis=1)
            results.append(jnp.dot(lhs, w_ref[n], preferred_element_type=F32))
        zero, one = results
        for p in range(group):
            own = slice(p * 256, (p + 1) * 256)
            z, o = zero[own], one[own]
            acc_ref[start + p + 2] += jnp.where(lower, z[:, :LANES], o[:, :LANES])
            acc_ref[start + p + 1] += swap_halves(jnp.where(lower, o[:, :LANES], z[:, :LANES]))
            acc_ref[start + p] += z[:, LANES:] + o[:, LANES:]
        return carry

    lax.fori_loop(0, (SIDE + 2) // group, planes, 0)


def taps():
    return [(t, t // 4, t // 2 % 2, t % 2) for t in range(8)]


def middle_kernel(
    near_ref,
    rank_ref,
    v_ref,
    pair_ref,
    other_ref,
    w_ref,
    down_ref,
    down_t_ref,
    own_ref,
    pair_out_ref,
    other_out_ref,
    g_ref,
    a0_ref,
    a1_ref,
    act_ref,
    turned_ref,
    spun_ref,
    face_ref,
    pad_ref,
    acc_ref,
    fine_ref,
):
    assemble(near_ref, rank_ref, v_ref, pair_ref, other_ref, face_ref, pad_ref)
    gather_taps(pad_ref, a0_ref, a1_ref)
    convolve((a0_ref, a1_ref), w_ref, acc_ref)

    def activate(i, carry):
        preact = acc_ref[i + 2]
        gate = 1.0 / (1.0 + jnp.exp(-preact))
        fine_ref[i // 2, i % 2] = (preact * gate).reshape(HALF, 2, SIDE, LANES)
        acc_ref[i + 2] = gate * (1.0 + preact * (1.0 - gate))
        return carry

    lax.fori_loop(0, SIDE, activate, 0)
    for t, a, b, c in taps():
        picked = fine_ref[:, a, :, b, pl.ds(c, HALF, stride=2), :]
        act_ref[:, t * LANES : (t + 1) * LANES] = picked.reshape(512, LANES).astype(BF16)
    octants = jnp.dot(act_ref[...], down_ref[...], preferred_element_type=F32).astype(BF16)
    pair_out_ref[0:512] = octants[:, :LANES]
    pair_out_ref[512:1024] = octants[:, LANES:]

    grads = []
    for n in range(2):
        rows = slice(n * 512, (n + 1) * 512)
        grad = own_ref[rows].astype(F32) + pair_ref[rows].astype(F32)
        spun_ref[n] = grad.T.astype(BF16)
        grads.append(grad.astype(BF16))
    grads = jnp.concatenate(grads, axis=1)
    for pair in range(4):
        lanes = slice(pair * 256, (pair + 1) * 256)
        spread = jnp.dot(grads, down_t_ref[:, lanes], preferred_element_type=F32)
        for c in range(2):
            part = spread[:, c * LANES : (c + 1) * LANES].reshape(HALF, HALF, HALF, LANES)
            fine_ref[:, pair // 2, :, pair % 2, pl.ds(c, HALF, stride=2), :] = part

    for p in (0, 1, SIDE + 2, SIDE + 3):
        turned_ref[p] = jnp.zeros((LANES, 256), BF16)

    def back(i, carry):
        grad = fine_ref[i // 2, i % 2].reshape(256, LANES) * acc_ref[i + 2]
        turned_ref[i + 2] = grad.T.astype(BF16)
        rounded = grad.astype(BF16).reshape(SIDE, SIDE, LANES)
        g_ref[i] = rounded
        place_faces(rank_ref, i, rounded, pair_out_ref, other_out_ref)
        return carry

    lax.fori_loop(0, SIDE, back, 0)


def weigh_kernel(a0_ref, a1_ref, act_ref, turned_ref, spun_ref, sums_ref, cg_ref):
    lower = low_half((LANES, LANES))
    whole = [jnp.dot(spun_ref[n], act_ref[...], preferred_element_type=F32) for n in range(2)]
    folded = []
    for t in range(8):
        lanes = slice(t * LANES, (t + 1) * LANES)
        both = jnp.where(lower, whole[0][:, lanes], whole[1][:, lanes])
        folded.append(both + swap_halves(both))
    for t in range(4):
        rows = slice(CONV_ROWS + t * LANES, CONV_ROWS + (t + 1) * LANES)
        sums_ref[rows] = jnp.where(lower, folded[t], folded[t + 4]).astype(BF16)

    cg_ref[...] = jnp.zeros_like(cg_ref)

    def weigh(g, carry):
        lhs = []
        for i in (2 * g, 2 * g + 1):
            for n in range(2):
                own = slice(n * 64, (n + 1) * 64)
                lhs.append(
                    jnp.concatenate([turned_ref[i + 2 - a, own] for a in range(3)], axis=0)
                )
        lhs = jnp.concatenate(lhs, axis=1)
        for b in range(3):
            rhs = []
            for i in (2 * g, 2 * g + 1):
                for a_ref in (a0_ref, a1_ref):
                    rhs.append(a_ref[i, b : b + SIDE].reshape(256, 256))
            rhs = jnp.concatenate(rhs, axis=0)
            cg_ref[b] += jnp.dot(lhs, rhs, preferred_element_type=F32)
        return carry

    lax.fori_loop(0, SIDE // 2 + 1, weigh, 0)
    lower = low_half((192, LANES))
    for b in range(3):
        sums_ref[b * 192 : (b + 1) * 192] = cg_ref[b, :, :LANES].astype(BF16)
    last = [cg_ref[b, :, LANES:] for b in range(3)]
    sums_ref[576:768] = jnp.where(lower, last[0], swap_halves(last[1])).astype(BF16)
    sums_ref[768:960] = jnp.where(lower, last[2], 0.0).astype(BF16)
    sums_ref[CONV_ROWS + DOWN_ROWS :] = jnp.zeros(
        (sums_ref.shape[0] - CONV_ROWS - DOWN_ROWS, LANES), BF16
    )


TAPPED = (SIDE + 2, SIDE + 2, SIDE, 256)
PAD_SCRATCH = [
    pltpu.VMEM((2, SIDE, SIDE, LANES), F32),
    pltpu.VMEM((SIDE + 2, SIDE + 2, 24, LANES), F32),
    pltpu.VMEM((SIDE + 4, 256, LANES), F32),
]


def middle_call(near, rank, v, pair, other, weights, down, down_t, own):
    return pl.pallas_call(
        middle_kernel,
        out_shape=(
            jax.ShapeDtypeStruct((1280, LANES), BF16),
            jax.ShapeDtypeStruct((256, LANES), BF16),
            jax.ShapeDtypeStruct((SIDE, SIDE, SIDE, LANES), BF16),
            jax.ShapeDtypeStruct(TAPPED, BF16),
            jax.ShapeDtypeStruct(TAPPED, BF16),
            jax.ShapeDtypeStruct((512, 8 * LANES), BF16),
            jax.ShapeDtypeStruct((SIDE + 4, LANES, 256), BF16),
            jax.ShapeDtypeStruct((2, LANES, 512), BF16),
        ),
        in_specs=[SMEM_SPEC] * 2 + [VMEM_SPEC] * 7,
        out_specs=(VMEM_SPEC,) * 8,
        scratch_shapes=PAD_SCRATCH + [pltpu.VMEM((HALF, 2, HALF, 2, SIDE, LANES), F32)],
        compiler_params=params(32),
        cost_estimate=pl.CostEstimate(
            flops=4_000_000_000, bytes_accessed=16_000_000, transcendentals=600_000
        ),
        name="middle",
    )(near, rank, v, pair, other, weights, down, down_t, own)


def weigh_call(a0, a1, act, turned, spun, rows):
    return pl.pallas_call(
        weigh_kernel,
        out_shape=jax.ShapeDtypeStruct((rows, LANES), BF16),
        in_specs=[VMEM_SPEC] * 5,
        out_specs=VMEM_SPEC,
        scratch_shapes=[pltpu.VMEM((3, 192, 256), F32)],
        compiler_params=params(20),
        cost_estimate=pl.CostEstimate(
            flops=4_000_000_000, bytes_accessed=10_000_000, transcendentals=0
        ),
        name="weigh",
    )(a0, a1, act, turned, spun)


def input_kernel(
    near_ref,
    rank_ref,
    g_ref,
    pair_ref,
    other_ref,
    w_ref,
    out_ref,
    face_ref,
    pad_ref,
    acc_ref,
    a0_ref,
    a1_ref,
):
    assemble(near_ref, rank_ref, g_ref, pair_ref, other_ref, face_ref, pad_ref)
    gather_taps(pad_ref, a0_ref, a1_ref)
    convolve((a0_ref, a1_ref), w_ref, acc_ref)

    def plane(i, carry):
        columns = pl.ds(pl.multiple_of(i * 256, 256), 256)
        out_ref[:, columns] = acc_ref[i + 2].T.astype(BF16)
        return carry

    lax.fori_loop(0, SIDE, plane, 0)


def input_call(near, rank, g, pair, other, weights):
    return pl.pallas_call(
        input_kernel,
        out_shape=jax.ShapeDtypeStruct((LANES, SIDE**3), BF16),
        in_specs=[SMEM_SPEC] * 2 + [VMEM_SPEC] * 4,
        out_specs=VMEM_SPEC,
        scratch_shapes=PAD_SCRATCH + [pltpu.VMEM(TAPPED, BF16)] * 2,
        compiler_params=params(28),
        cost_estimate=pl.CostEstimate(
            flops=4_000_000_000, bytes_accessed=3_000_000, transcendentals=0
        ),
        name="input_grad",
    )(near, rank, g, pair, other, weights)


def add_kernel(shares_ref, out_ref):
    peers = shares_ref.shape[0]
    lanes = 16
    total = jnp.sum(shares_ref[0:lanes].astype(F32), axis=0)
    for start in range(lanes, peers, lanes):
        total = total + jnp.sum(shares_ref[start : start + lanes].astype(F32), axis=0)
    total = total.astype(BF16)
    for start in range(0, peers, lanes):
        out_ref[start : start + lanes] = jnp.broadcast_to(total[None], (lanes, SHARE, LANES))


def add_call(shares):
    return pl.pallas_call(
        add_kernel,
        out_shape=jax.ShapeDtypeStruct(shares.shape, BF16),
        in_specs=[VMEM_SPEC],
        out_specs=VMEM_SPEC,
        compiler_params=params(16),
        cost_estimate=pl.CostEstimate(flops=0, bytes_accessed=2_000_000, transcendentals=0),
        name="add",
    )(shares)


def split_kernel(sums_ref, conv_ref, down_ref):
    for a in range(3):
        for b in range(3):
            for c in range(3):
                chunk, upper = (b, c) if c < 2 else ((3, b) if b < 2 else (4, 0))
                base = chunk * 192 + a * 64
                block = sums_ref[base : base + 64].astype(F32)
                block = swap_halves(block) if upper else block
                conv_ref[9 * a + 3 * b + c] = block[:, :64]
    for t in range(4):
        block = sums_ref[CONV_ROWS + t * LANES : CONV_ROWS + (t + 1) * LANES].astype(F32).T
        down_ref[t] = block[:64]
        down_ref[t + 4] = block[64:]


def split_call(sums):
    return pl.pallas_call(
        split_kernel,
        out_shape=(
            jax.ShapeDtypeStruct((27, 64, 64), F32),
            jax.ShapeDtypeStruct((8, 64, LANES), F32),
        ),
        in_specs=[VMEM_SPEC],
        out_specs=(VMEM_SPEC,) * 2,
        compiler_params=params(16),
        name="split",
    )(sums)


def exchange(pair, other, axis):
    peers = lax.axis_size(axis)
    across = [(i, i + 1) for i in range(1, peers - 1, 2)]
    return (
        lax.ppermute(pair, axis, [(i, i ^ 1) for i in range(peers)]),
        lax.ppermute(other, axis, across + [(j, i) for i, j in across]),
    )


def total_sums(sums):
    axes = ("grp", "dev")
    peers = lax.axis_size("grp") * lax.axis_size("dev")
    shares = lax.all_to_all(sums.reshape(peers, SHARE, LANES), axes, 0, 0)
    return lax.all_to_all(add_call(shares), axes, 0, 0).reshape(peers * SHARE, LANES)


def body(fine_input, conv_weight, down_weight, coarse_cot, neighbours, children):
    rank = lax.axis_index("grp") * lax.axis_size("dev") + lax.axis_index("dev")
    rank = rank.reshape(1).astype(jnp.int32)
    peers = lax.axis_size("grp") * lax.axis_size("dev")

    own, voxels, pair, other = first_call(
        children, rank, coarse_cot.reshape(LANES, SIDE**3), fine_input.reshape(LANES, SIDE**3)
    )
    pair, other = exchange(pair, other, "dev")
    forward, backward, down, down_t = weights_call(conv_weight, down_weight.transpose(0, 2, 1))
    mine, other_out, grads, a0, a1, act, turned, spun = middle_call(
        neighbours, rank, voxels, pair, other, forward, down, down_t, own
    )
    theirs, grad_other = exchange(mine, other_out, "dev")
    sums = weigh_call(a0, a1, act, turned, spun, peers * SHARE)
    gathered = total_sums(sums)
    coarse = coarse_call(children, rank, mine, theirs)
    input_grad = input_call(neighbours, rank, grads, theirs, grad_other, backward)
    conv_grad, down_grad = split_call(gathered)
    return (
        coarse.reshape(1, LANES, SIDE**3),
        input_grad.reshape(2, 64, SIDE**3),
        conv_grad,
        down_grad.transpose(0, 2, 1),
    )


def solution(mesh):
    in_specs = (
        P(("grp", "dev"), None, None),
        P(),
        P(),
        P(("grp", "dev"), None, None),
        P(("grp", "dev"), None),
        P(("grp", "dev"), None),
    )
    out_specs = (P(("grp", "dev"), None, None), P(("grp", "dev"), None, None), P(), P())
    return jax.shard_map(body, mesh=mesh, in_specs=in_specs, out_specs=out_specs, check_vma=False)
```

time: 181 us -> 110 us (0.61)
  blocking collectives: 73.4 us -> 36.9 us
  starting transfers between devices: 31.8 us -> 11.2 us
  local copies, waits for them, and re-layouts: 20.2 us -> 5.02 us
  waiting for transfers between devices: 2.11 us -> 13 us
  Pallas kernels: 48.9 us -> 41.2 us
  other arithmetic: 1.97 us -> 0 us
    all_gather x1 -> x0, blocking collectives: 73.4 us -> none  [total_sums(): return lax.all_gather(mine, axes, axis=0, tiled=True)]
    all_to_all x0 -> x1, blocking collectives: none -> 36.9 us  [total_sums(): shares = lax.all_to_all(sums.reshape(peers, SHARE, LANES), axes, 0, 0)]
    all_to_all x1, starting transfers between devices: 19.6 us -> 6.32 us  [total_sums(): lax.all_to_all(add_call(shares), axes, 0, 0).reshape(peers * SHARE, LANES)]
    ppermute x6 -> x4, waiting for transfers between devices: 2.1 us -> 13 us  [the longest x2 13 us: exchange(): lax.ppermute(pair, axis, [(i, i ^ 1) for i in range(peers)])]
    ppermute x6 -> x4, starting transfers between devices: 12.2 us -> 4.91 us  [the longest x2 3.61 us: exchange(): lax.ppermute(pair, axis, [(i, i ^ 1) for i in range(peers)])]
    pallas_call x3 -> x5, Pallas kernels: 29.1 us -> 23.2 us  [the longest x1 14.2 us: middle_call(): pl.pallas_call(middle_kernel, out_shape=(jax.ShapeDtypeStruct((1280, LANE...]
    gather x4 -> x0, local copies, waits for them, and re-layouts: 4.59 us -> none  [tap_weights(): second = shaped[:, :, :, jnp.array([1, 0, 3, 2])].reshape(3, 256, 256)]
    unnamed x36 -> x14, local copies, waits for them, and re-layouts: 9.1 us -> 5.02 us
  transfers between devices with their start and end apart: 7 -> 5, of which waited for: 1 -> 2; matrix products, arithmetic and copies ran while one was open for 7% -> 0% of each run, Pallas kernels for 12% -> 16%
where the time goes in v2:
time: 110 us; the launch traced here: 108 us
  Pallas kernels  41.2 us (37%)
  blocking collectives  36.9 us (34%)
  waiting for transfers between devices  13 us (12%)
  starting transfers between devices  11.2 us (10%)
  local copies, waits for them, and re-layouts  5.02 us (5%)
    all_to_all x1, blocking collectives, total_sums(): shares = lax.all_to_all(sums.reshape(peers, SHARE, LANES), axes, 0, 0)  36.9 us
    pallas_call x1, Pallas kernels, middle_call(): pl.pallas_call(middle_kernel, out_shape=(jax.ShapeDtypeStruct((1280, LANE...  14.2 us
    pallas_call x1, Pallas kernels, input_call(): pl.pallas_call(input_kernel, out_shape=jax.ShapeDtypeStruct((LANES, SIDE...  13.4 us
    ppermute x2, waiting for transfers between devices, exchange(): lax.ppermute(pair, axis, [(i, i ^ 1) for i in range(peers)])  13 us
    all_to_all x1, starting transfers between devices, total_sums(): lax.all_to_all(add_call(shares), axes, 0, 0).reshape(peers * SHARE, LANES)  6.32 us
    pallas_call x1, Pallas kernels, weigh_call(): pl.pallas_call(weigh_kernel, out_shape=jax.ShapeDtypeStruct((rows, LANES)...  5.04 us
    unnamed x14, local copies, waits for them, and re-layouts  5.02 us
    ppermute x2, starting transfers between devices, exchange(): lax.ppermute(pair, axis, [(i, i ^ 1) for i in range(peers)])  3.61 us
  transfers between devices with their start and end apart: 5, of which 2 were waited for; matrix products, arithmetic and copies ran while one was open for 0% of the time, Pallas kernels for 16%

profile of v2, /device:TPU:1, one launch (start us, length us, event | category | flops | bytes accessed | tf_op | source)
XLA Modules:
  0.0 108.0 jit_solution(1177633398630884709)
XLA Ops:
  0.6 0.0 copy-start.6
  0.6 0.0 copy-start
  0.7 1.2 %copy-done = bf16[1,128,4096]{2,1,0:T(8,128)(2,1)S(1)} copy-done((bf16[1,128,4096]{2,1,0:T(8,128)(2,1)S(1)}, bf16[1,128,4096]{2,1,0:T(8,128)(2,1)}, u32[]{:S(2)}) %copy-start) | copy-done | bytes 1048600
  1.9 0.0 copy-start.1
  1.9 1.2 %copy-done.1 = bf16[2,64,4096]{2,1,0:T(8,128)(2,1)S(1)} copy-done((bf16[2,64,4096]{2,1,0:T(8,128)(2,1)S(1)}, bf16[2,64,4096]{2,1,0:T(8,128)(2,1)}, u32[]{:S(2)}) %copy-start.1) | copy-done | bytes 1048600
  3.1 0.0 copy-start.4
  3.1 0.7 copy-done.4
  3.8 2.4 %first.1 = (bf16[1024,128]{1,0:T(8,128)(2,1)S(1)}, bf16[16,16,16,128]{3,2,1,0:T(8,128)(2,1)S(1)}, bf16[1280,128]{1,0:T(8,128)(2,1)S(1)}, bf16[256,128]{1,0:T(8,128)(2,1)S(1)}) custom-call(s32[1,8]{1,0:T(1,128)S(1)} %copy-done.4, s32[1]{0:T(128)} %bitcast.rank_ref, bf16[128,4096]{1,0:T(8,128)(2,1)S(1)} %bitcast.10, bf16[128,4096]{1,0:T(8,128)(2,1)S(1)} %bitcast.11), custom_call_target="tpu_custom_call" | custom-call | bytes 8000000 | tf_op jit(solution)/shard_map/first/pallas_call | solution.py:73
  6.2 2.1 %collective-permute-start = (bf16[1280,128]{1,0:T(8,128)(2,1)S(1)}, bf16[1280,128]{1,0:T(8,128)(2,1)S(1)}, u32[]{:S(2)}, u32[]{:S(2)}) collective-permute-start(bf16[1280,128]{1,0:T(8,128)(2,1)S(1)} %get-tuple-element.23), channel_id=1, source_target_pairs={{0,1},{1,0},{2,3},{3,2},{4,5},{5,4},{6,7},{7,6},{8,9},{9,8},{10,11... | collective-permute-start | bytes 983048 | tf_op jit(solution)/shard_map/ppermute | solution.py:558
  8.3 0.7 collective-permute-start.1
  9.0 0.0 copy-start.2
  9.0 1.0 copy-done.2
  10.0 0.9 copy-done.3
  10.9 0.6 weights.1
  11.5 0.0 collective-permute-done.1.other_ref
  11.5 2.9 %collective-permute-done.pair_ref = bf16[1280,128]{1,0:T(8,128)(2,1)S(1)} collective-permute-done((bf16[1280,128]{1,0:T(8,128)(2,1)S(1)}, bf16[1280,128]{1,0:T(8,128)(2,1)S(1)}, u32[]{:S(2)}, u32[]{:S(2)}) %collective-permute-start) | collective-permute-done | bytes 327712 | tf_op jit(solution)/shard_map/ppermute | solution.py:558
  14.4 0.0 copy-done.6
  14.4 14.2 %middle.1 = (bf16[1280,128]{1,0:T(8,128)(2,1)S(1)}, bf16[256,128]{1,0:T(8,128)(2,1)S(1)}, bf16[16,16,16,128]{3,2,1,0:T(8,128)(2,1)S(1)}, bf16[18,18,16,256]{3,2,...) custom-call(s32[2,26]{1,0:T(2,128)S(1)} %copy-done.6, ...), custom_call_target="tpu_custom_call" | custom-call | flops 4000000000 | bytes 16000000 | tf_op jit(solution)/shard_map/middle/pallas_call | solution.py:423
  28.6 5.0 %weigh.1 = bf16[2048,128]{1,0:T(8,128)(2,1)S(1)} custom-call(bf16[18,18,16,256]{3,2,1,0:T(8,128)(2,1)S(1)} %get-tuple-element.33.a0_ref, bf16[18,18,16,256]{3,2,1,0:T(8,128)(2,1)S(1)} %get-tuple-element.34.a1_ref, bf16[512,1024]{1,0:T(8,128)(2,1)S(1)} %get-tuple-element.35.act_ref, bf16[20,128,256]{2,1,0:T(8,128)(2,1)S(1)} %get-tuple-element.36.turned_ref, ...), custom_call_target="tpu_custom_call" | custom-call | flops 4000000000 | bytes 10000000 | tf_op jit(solution)/shard_map/weigh/pallas_call | solution.py:447
  33.6 0.0 copy-start.5
  33.6 36.9 %all_to_all.10.shares_ref = bf16[256,8,128]{2,1,0:T(8,128)(2,1)S(1)} all-to-all(bf16[256,8,128]{2,1,0:T(8,128)(2,1)S(1)} %bitcast.12), channel_id=1, replica_groups=mesh['grp'=8,'dev'=32] {'grp','dev'}, dimensions={0} | all-to-all | bytes 1048576 | tf_op jit(solution)/shard_map/all_to_all | solution.py:566
  70.5 0.9 add.5
  71.4 6.3 %all-to-all-start.1 = ((bf16[256,8,128]{2,1,0:T(8,128)(2,1)}), bf16[256,8,128]{2,1,0:T(8,128)(2,1)S(1)}, u32[]{:S(2)}, u32[]{:S(2)}) async-start(bf16[256,8,128]{2,1,0:T(8,128)(2,1)} %add.5), calls=%async_computation.1 | async-start | bytes 1048576 | tf_op jit(solution)/shard_map/all_to_all | solution.py:567
  77.8 1.5 %collective-permute-start.2 = (bf16[1280,128]{1,0:T(8,128)(2,1)S(1)}, bf16[1280,128]{1,0:T(8,128)(2,1)S(1)}, u32[]{:S(2)}, u32[]{:S(2)}) collective-permute-start(bf16[1280,128]{1,0:T(8,128)(2,1)S(1)} %get-tuple-element.29.mine_ref), channel_id=1, source_target_pairs={{0,1},{1,0},{2,3},{3,2},{4,5},{5,4},{6,7},{7,6},{8,9},{9,8},{10,11... | collective-permute-start | bytes 983048 | tf_op jit(solution)/shard_map/ppermute | solution.py:558
  79.2 0.7 collective-permute-start.3
  79.9 10.1 %collective-permute-done.2.theirs_ref.pair_ref = bf16[1280,128]{1,0:T(8,128)(2,1)S(1)} collective-permute-done((bf16[1280,128]{1,0:T(8,128)(2,1)S(1)}, bf16[1280,128]{1,0:T(8,128)(2,1)S(1)}, u32[]{:S(2)}, u32[]{:S(2)}) %collective-permute-start.2) | collective-permute-done | bytes 327712 | tf_op jit(solution)/shard_map/ppermute | solution.py:558
  90.0 0.0 copy-done.5
  90.0 3.5 %coarse.1 = bf16[128,4096]{1,0:T(8,128)(2,1)} custom-call(s32[1,8]{1,0:T(1,128)S(1)} %copy-done.5, s32[1]{0:T(128)} %bitcast.rank_ref, bf16[1280,128]{1,0:T(8,128)(2,1)S(1)} %get-tuple-element.29.mine_ref, bf16[1280,128]{1,0:T(8,128)(2,1)S(1)} %collective-permute-done.2.theirs_ref.pair_ref), custom_call_target="tpu_custom_call" | custom-call | bytes 4000000 | tf_op jit(solution)/shard_map/coarse/pallas_call | solution.py:163
  93.5 0.0 collective-permute-done.3.other_ref
  93.5 13.4 %input_grad.1 = bf16[128,4096]{1,0:T(8,128)(2,1)} custom-call(s32[2,26]{1,0:T(2,128)S(1)} %copy-done.6, s32[1]{0:T(128)} %bitcast.rank_ref, bf16[16,16,16,128]{3,2,1,0:T(8,128)(2,1)S(1)} %get-tuple-element.30.g_ref, bf16[1280,128]{1,0:T(8,128)(2,1)S(1)} %collective-permute-done.2.theirs_ref.pair_ref, bf16[256,128]{1,0:T(8,128)(2,1)S(1)} %collective-permute-done.3.other_ref, ...), custom_call_target="tpu_custom_call" | custom-call | flops 4000000000 | bytes 3000000 | tf_op jit(solution)/shard_map/input_grad/pallas_call | solution.py:488
  106.9 0.0 all-to-all-done.1
  106.9 1.1 %split.1 = (f32[27,64,64]{2,1,0:T(8,128)}, f32[8,64,128]{2,1,0:T(8,128)}) custom-call(bf16[2048,128]{1,0:T(8,128)(2,1)S(1)} %bitcast.9), custom_call_target="tpu_custom_call" | custom-call | tf_op jit(solution)/shard_map/split/pallas_call | solution.py:541
  (1 shorter events, 0.0 us)
Async XLA Ops:
  0.6 13.8 %copy-start.6 = (s32[2,26]{1,0:T(2,128)S(1)}, s32[2,26]{1,0:T(2,128)}, u32[]{:S(2)}) copy-start(s32[2,26]{1,0:T(2,128)} %near_ref.3) | copy-start | bytes 628
  0.6 1.2 %copy-start = (bf16[1,128,4096]{2,1,0:T(8,128)(2,1)S(1)}, bf16[1,128,4096]{2,1,0:T(8,128)(2,1)}, u32[]{:S(2)}) copy-start(bf16[1,128,4096]{2,1,0:T(8,128)(2,1)} %param.9) | copy-start | bytes 3145732
  1.9 1.2 %copy-start.1 = (bf16[2,64,4096]{2,1,0:T(8,128)(2,1)S(1)}, bf16[2,64,4096]{2,1,0:T(8,128)(2,1)}, u32[]{:S(2)}) copy-start(bf16[2,64,4096]{2,1,0:T(8,128)(2,1)} %param.6) | copy-start | bytes 3145732
  3.1 0.7 copy-start.4
  6.2 8.2 %collective-permute-start = (bf16[1280,128]{1,0:T(8,128)(2,1)S(1)}, bf16[1280,128]{1,0:T(8,128)(2,1)S(1)}, u32[]{:S(2)}, u32[]{:S(2)}) collective-permute-start(bf16[1280,128]{1,0:T(8,128)(2,1)S(1)} %get-tuple-element.23), channel_id=1, source_target_pairs={{0,1},{1,0},{2,3},{3,2},{4,5},{5,4},{6,7},{7,6},{8,9},{9,8},{10,11... | collective-permute-start | bytes 983048 | tf_op jit(solution)/shard_map/ppermute | solution.py:558
  8.3 3.2 %collective-permute-start.1 = (bf16[256,128]{1,0:T(8,128)(2,1)S(1)}, bf16[256,128]{1,0:T(8,128)(2,1)S(1)}, u32[]{:S(2)}, u32[]{:S(2)}) collective-permute-start(bf16[256,128]{1,0:T(8,128)(2,1)S(1)} %get-tuple-element.24), channel_id=1, source_target_pairs={{1,2},{3,4},{5,6},{7,8},{9,10},{11,12},{13,14},{15,16},{17,18},{19... | collective-permute-start | bytes 196616 | tf_op jit(solution)/shard_map/ppermute | solution.py:559
  9.0 1.0 copy-start.2
  10.0 0.9 copy-start.3
  33.6 56.4 %copy-start.5 = (s32[1,8]{1,0:T(1,128)S(1)}, s32[1,8]{1,0:T(1,128)}, u32[]{:S(2)}) copy-start(s32[1,8]{1,0:T(1,128)} %child_ref.3) | copy-start | bytes 100
  71.4 35.5 %all-to-all-start.1 = ((bf16[256,8,128]{2,1,0:T(8,128)(2,1)}), bf16[256,8,128]{2,1,0:T(8,128)(2,1)S(1)}, u32[]{:S(2)}, u32[]{:S(2)}) async-start(bf16[256,8,128]{2,1,0:T(8,128)(2,1)} %add.5), calls=%async_computation.1 | async-start | bytes 1048576 | tf_op jit(solution)/shard_map/all_to_all | solution.py:567
  77.8 12.3 %collective-permute-start.2 = (bf16[1280,128]{1,0:T(8,128)(2,1)S(1)}, bf16[1280,128]{1,0:T(8,128)(2,1)S(1)}, u32[]{:S(2)}, u32[]{:S(2)}) collective-permute-start(bf16[1280,128]{1,0:T(8,128)(2,1)S(1)} %get-tuple-element.29.mine_ref), channel_id=1, source_target_pairs={{0,1},{1,0},{2,3},{3,2},{4,5},{5,4},{6,7},{7,6},{8,9},{9,8},{10,11... | collective-permute-start | bytes 983048 | tf_op jit(solution)/shard_map/ppermute | solution.py:558
  79.2 14.3 %collective-permute-start.3 = (bf16[256,128]{1,0:T(8,128)(2,1)S(1)}, bf16[256,128]{1,0:T(8,128)(2,1)S(1)}, u32[]{:S(2)}, u32[]{:S(2)}) collective-permute-start(bf16[256,128]{1,0:T(8,128)(2,1)S(1)} %get-tuple-element.31), channel_id=1, source_target_pairs={{1,2},{3,4},{5,6},{7,8},{9,10},{11,12},{13,14},{15,16},{17,18},{19... | collective-permute-start | bytes 196616 | tf_op jit(solution)/shard_map/ppermute | solution.py:559

commit v3 on v2

v3 whole, which is shorter than its diff:
```python
import functools

import jax
import jax.numpy as jnp
from jax import lax
from jax.experimental import pallas as pl
from jax.experimental.pallas import tpu as pltpu
from jax.sharding import PartitionSpec as P

SIDE = 16
HALF = 8
LANES = 128
F32 = jnp.float32
BF16 = jnp.bfloat16
CONV_ROWS = 960
DOWN_ROWS = 512
GROUPS = 8
SHARE = (CONV_ROWS + DOWN_ROWS) // GROUPS

VMEM_SPEC = pl.BlockSpec(memory_space=pltpu.VMEM)
SMEM_SPEC = pl.BlockSpec(memory_space=pltpu.SMEM)
ANY_SPEC = pl.BlockSpec(memory_space=pl.ANY)
TOKEN = jax.ShapeDtypeStruct((8, LANES), F32)


def params(mib):
    return pltpu.CompilerParams(vmem_limit_bytes=mib * 1024 * 1024)


def loop(count, body, unroll):
    def step(g, carry):
        for p in range(unroll):
            body(g * unroll + p)
        return carry

    lax.fori_loop(0, count // unroll, step, 0)


def low_half(shape):
    return lax.broadcasted_iota(jnp.int32, shape, len(shape) - 1) < 64


def swap_halves(x):
    return pltpu.roll(x, 64, x.ndim - 1)


def place_faces(info_ref, i, planes, pair_ref, other_ref, first=0):
    even = info_ref[0] % 2 == 0
    low, high = planes[0], planes[SIDE - 1]
    pair_ref[pl.ds(pl.multiple_of(first + i * SIDE, SIDE), SIDE)] = jnp.where(even, high, low)
    other_ref[pl.ds(pl.multiple_of(i * SIDE, SIDE), SIDE)] = jnp.where(even, low, high)


def faces_kernel(info_ref, x_ref, v_ref, pair_ref, other_ref, token_ref):
    def plane(i):
        columns = pl.ds(pl.multiple_of(i * 256, 256), 256)
        voxels = x_ref[:, columns].astype(F32).T.astype(BF16).reshape(SIDE, SIDE, LANES)
        v_ref[i] = voxels
        place_faces(info_ref, i, voxels, pair_ref, other_ref)

    loop(SIDE, plane, 4)
    token_ref[...] = jnp.zeros_like(token_ref)


def faces_call(info, x):
    face = jax.ShapeDtypeStruct((256, LANES), BF16)
    return pl.pallas_call(
        faces_kernel,
        out_shape=(jax.ShapeDtypeStruct((SIDE, SIDE, SIDE, LANES), BF16), face, face, TOKEN),
        in_specs=[SMEM_SPEC, VMEM_SPEC],
        out_specs=(VMEM_SPEC,) * 4,
        compiler_params=params(16),
        cost_estimate=pl.CostEstimate(flops=0, bytes_accessed=4_000_000, transcendentals=0),
        name="faces",
    )(info, x)


def find_octant(info_ref, wanted):
    place = jnp.int32(0)
    found = jnp.int32(0)
    for o in range(8):
        hit = (info_ref[2 + o] == wanted).astype(jnp.int32)
        place = place + hit * o
        found = found + hit
    return place, found


def cot_kernel(after_ref, info_ref, cot_ref, own_ref, send_ref, turned_ref):
    def plane(i):
        columns = pl.ds(pl.multiple_of(i * 256, 256), 256)
        turned = cot_ref[:, columns].astype(F32).T
        turned_ref[i // HALF, i % HALF] = turned.reshape(2, HALF, 2, HALF, LANES)

    loop(SIDE, plane, 4)
    rank = info_ref[0]
    for out_ref, holder in ((own_ref, rank), (send_ref, rank ^ 1)):
        for slot in range(2):
            place, found = find_octant(info_ref, holder * 2 + slot)
            block = turned_ref[place // 4, :, place // 2 % 2, :, place % 2]
            block = jnp.where(found > 0, block, jnp.zeros_like(block))
            out_ref[slot * 512 : (slot + 1) * 512] = block.reshape(512, LANES).astype(BF16)


def cot_call(after, info, cot):
    blocks = jax.ShapeDtypeStruct((1024, LANES), BF16)
    return pl.pallas_call(
        cot_kernel,
        out_shape=(blocks, blocks),
        in_specs=[ANY_SPEC, SMEM_SPEC, VMEM_SPEC],
        out_specs=(VMEM_SPEC,) * 2,
        scratch_shapes=[pltpu.VMEM((2, HALF, 2, HALF, 2, HALF, LANES), F32)],
        compiler_params=params(20),
        cost_estimate=pl.CostEstimate(flops=0, bytes_accessed=8_000_000, transcendentals=0),
        name="cot",
    )(after, info, cot)


def weights_kernel(
    conv_ref, down_in_ref, forward_ref, backward_ref, down_ref, down_t_ref
):
    blank = jnp.zeros((64, 64), F32)
    for b in range(3):
        for c in range(3):
            rows = slice(b * 256 + c * 64, b * 256 + (c + 1) * 64)
            ahead = [conv_ref[9 * a + 3 * b + c].astype(F32) for a in range(3)]
            behind = [conv_ref[26 - (9 * a + 3 * b + c)].astype(F32) for a in range(3)]
            for n in range(2):
                order = (0, 1, 2, None) if n == 0 else (1, 0, None, 2)
                if c == 2:
                    rows = slice(b * 256 + 128 + n * 64, b * 256 + 192 + n * 64)
                    unused = slice(b * 256 + 192 - n * 64, b * 256 + 256 - n * 64)
                    forward_ref[n, unused] = jnp.zeros((64, 256), BF16)
                    backward_ref[n, unused] = jnp.zeros((64, 256), BF16)
                for half in range(2):
                    pair = order[2 * half : 2 * half + 2]
                    lanes = slice(half * LANES, (half + 1) * LANES)
                    taps = [blank if a is None else ahead[a] for a in pair]
                    forward_ref[n, rows, lanes] = jnp.concatenate(taps, axis=0).T.astype(BF16)
                    taps = [blank if a is None else behind[a] for a in pair]
                    backward_ref[n, rows, lanes] = jnp.concatenate(taps, axis=1).astype(BF16)
    for t in range(8):
        tap = down_in_ref[t]
        blank = jnp.zeros((64, LANES), BF16)
        rows = [jnp.concatenate([tap, blank], axis=1), jnp.concatenate([blank, tap], axis=1)]
        block = jnp.concatenate(rows, axis=0)
        down_ref[t * LANES : (t + 1) * LANES] = block
        down_t_ref[:, t * LANES : (t + 1) * LANES] = block.astype(F32).T.astype(BF16)


def weights_call(conv_weight, down_weight):
    conv = jax.ShapeDtypeStruct((2, 768, 256), BF16)
    return pl.pallas_call(
        weights_kernel,
        out_shape=(
            conv,
            conv,
            jax.ShapeDtypeStruct((8 * LANES, 256), BF16),
            jax.ShapeDtypeStruct((256, 8 * LANES), BF16),
        ),
        in_specs=[VMEM_SPEC] * 2,
        out_specs=(VMEM_SPEC,) * 4,
        compiler_params=params(16),
        cost_estimate=pl.CostEstimate(flops=0, bytes_accessed=8_000_000, transcendentals=0),
        name="weights",
    )(conv_weight, down_weight)


def coarse_half_kernel(half, *refs):
    _, info_ref, mine_ref, theirs_ref = refs[:4]
    out_ref, token_ref, whole_ref = refs[-3:]
    token_ref[...] = jnp.zeros_like(token_ref)
    for o in range(4):
        entry = info_ref[2 + half * 4 + o]
        slot = jnp.maximum(entry, 0) % 2
        here = jnp.maximum(entry, 0) // 2 == info_ref[0]
        rows = pl.ds(pl.multiple_of(slot * 512, 512), 512)
        block = jnp.where(here, mine_ref[rows], theirs_ref[rows])
        block = jnp.where(entry >= 0, block, jnp.zeros_like(block)).astype(F32)
        whole_ref[:, o // 2, :, o % 2] = block.reshape(HALF, HALF, HALF, LANES)

    for i in range(HALF):
        turned = whole_ref[i].reshape(256, LANES).T
        out_ref[:, i * 256 : (i + 1) * 256] = turned.astype(BF16)


def coarse_half_call(after, info, mine, theirs, half, begun=()):
    return pl.pallas_call(
        functools.partial(coarse_half_kernel, half),
        grid=(1,),
        out_shape=(jax.ShapeDtypeStruct((LANES, SIDE**3), BF16), TOKEN),
        in_specs=[ANY_SPEC, SMEM_SPEC, VMEM_SPEC, VMEM_SPEC] + [ANY_SPEC] * len(begun),
        out_specs=(
            pl.BlockSpec((LANES, SIDE**3 // 2), lambda g: (0, half)),
            pl.BlockSpec((8, LANES), lambda g: (0, 0)),
        ),
        input_output_aliases={4: 0} if begun else {},
        scratch_shapes=[pltpu.VMEM((HALF, 2, HALF, 2, HALF, LANES), F32)],
        compiler_params=params(16),
        cost_estimate=pl.CostEstimate(flops=0, bytes_accessed=4_000_000, transcendentals=0),
        name="coarse_half",
    )(after, info, mine, theirs, *begun)


def spans(step):
    if step == 0:
        return slice(1, SIDE + 1), slice(0, SIDE)
    if step == 1:
        return slice(SIDE + 1, SIDE + 2), slice(0, 1)
    return slice(0, 1), slice(SIDE - 1, SIDE)


def assemble(info_ref, v_ref, pair_ref, other_ref, face_ref, core_ref, ends_ref):
    def fill(i):
        core_ref[i + 1, SIDE : 17 * SIDE] = v_ref[i].astype(F32).reshape(256, LANES)

    loop(SIDE, fill, 4)
    even = info_ref[0] % 2 == 0
    pair = pair_ref[pair_ref.shape[0] - 256 :].astype(F32).reshape(SIDE, SIDE, LANES)
    other = other_ref[...].astype(F32).reshape(SIDE, SIDE, LANES)
    face_ref[0] = jnp.where(even, other, pair)
    face_ref[1] = jnp.where(even, pair, other)
    lower = low_half((1, LANES))
    column = 0
    lines = []
    for step_x in (-1, 0, 1):
        for step_y in (-1, 0, 1):
            for step_z in (-1, 0, 1):
                if step_x == 0 and step_y == 0 and step_z == 0:
                    continue
                entries = info_ref[10 + column], info_ref[36 + column]
                column += 1
                straight = [
                    jnp.logical_and(e >= 0, jnp.maximum(e, 0) % 2 == n).astype(F32)
                    for n, e in enumerate(entries)
                ]
                crossed = [
                    jnp.logical_and(e >= 0, jnp.maximum(e, 0) % 2 != n).astype(F32)
                    for n, e in enumerate(entries)
                ]
                keep = jnp.where(lower, straight[0], straight[1])
                cross = jnp.where(lower, crossed[0], crossed[1])
                put_x, take_x = spans(step_x)

                def choose(x, keep=keep, cross=cross):
                    shape = (1,) * (x.ndim - 1) + (LANES,)
                    return x * keep.reshape(shape) + swap_halves(x) * cross.reshape(shape)

                end = 0 if step_z < 0 else 1
                row = SIDE - 1 if step_z < 0 else 0
                strided = pl.ds(SIDE + row, SIDE, stride=SIDE)
                if step_y != 0:
                    side = 0 if step_y < 0 else 1
                    y = 0 if step_y < 0 else SIDE + 1
                    if step_z == 0:
                        core_ref[put_x, y * SIDE : (y + 1) * SIDE] = choose(face_ref[side, take_x])
                    else:
                        ends_ref[end, put_x, y : y + 1] = choose(
                            face_ref[side, take_x, row : row + 1]
                        )
                elif step_x != 0:
                    taken = take_x.start + 1
                    if step_z == 0:
                        core_ref[put_x.start, SIDE : 17 * SIDE] = choose(
                            core_ref[taken, SIDE : 17 * SIDE]
                        )
                    else:
                        ends_ref[end, put_x.start, 1 : SIDE + 1] = choose(core_ref[taken, strided])
                else:
                    lines.append((choose, end, strided))

    def line(i):
        for choose, end, strided in lines:
            ends_ref[end, i + 1, 1 : SIDE + 1] = choose(core_ref[i + 1, strided])

    loop(SIDE, line, 4)


def gather_taps(core_ref, ends_ref, tap_refs):
    lower = low_half((SIDE, LANES))
    rows = lax.broadcasted_iota(jnp.int32, (8, LANES), 0)
    top, bottom = rows == 0, rows == 7

    def plane(i):
        for j in range(SIDE + 2):
            first = core_ref[i, j * SIDE : j * SIDE + 8]
            second = core_ref[i, j * SIDE + 8 : (j + 1) * SIDE]
            down_first, down_second = pltpu.roll(first, 1, 0), pltpu.roll(second, 1, 0)
            up_first, up_second = pltpu.roll(first, 7, 0), pltpu.roll(second, 7, 0)
            before = jnp.concatenate(
                [
                    jnp.where(top, ends_ref[0, i, j : j + 1], down_first),
                    jnp.where(top, down_first, down_second),
                ],
                axis=0,
            )
            after = jnp.concatenate(
                [
                    jnp.where(bottom, up_second, up_first),
                    jnp.where(bottom, ends_ref[1, i, j : j + 1], up_second),
                ],
                axis=0,
            )
            here = jnp.concatenate([first, second], axis=0)
            tap_refs[0][i, j] = jnp.where(lower, before, swap_halves(here)).astype(BF16)
            tap_refs[1][i, j] = jnp.where(lower, swap_halves(before), here).astype(BF16)
            tap_refs[2][i, j] = after.astype(BF16)

    loop(SIDE + 2, plane, 3)


def convolve(tap_refs, w_ref, acc_ref, first=0, planes=SIDE + 2, group=6):
    rows = group * 256

    def clear(i):
        acc_ref[i] = jnp.zeros((256, LANES), F32)

    loop(planes + 2, clear, 4)
    lower = low_half((256, LANES))

    def step(g, carry):
        start = g * group
        results = []
        for n in range(2):
            lhs = [
                tap_refs[chunk][pl.ds(first + start, group), b : b + SIDE].reshape(rows, LANES)
                for b in range(3)
                for chunk in (n, 2)
            ]
            lhs = jnp.concatenate(lhs, axis=1)
            results.append(jnp.dot(lhs, w_ref[n], preferred_element_type=F32))
        zero, one = results
        for p in range(group):
            own = slice(p * 256, (p + 1) * 256)
            z, o = zero[own], one[own]
            acc_ref[start + p + 2] += jnp.where(lower, z[:, :LANES], o[:, :LANES])
            acc_ref[start + p + 1] += swap_halves(jnp.where(lower, o[:, :LANES], z[:, :LANES]))
            acc_ref[start + p] += z[:, LANES:] + o[:, LANES:]
        return carry

    lax.fori_loop(0, planes // group, step, 0)


def taps():
    return [(t, t // 4, t // 2 % 2, t % 2) for t in range(8)]


def forward_kernel(
    info_ref,
    v_ref,
    pair_ref,
    other_ref,
    w_ref,
    down_ref,
    oct_ref,
    slope_ref,
    act_ref,
    zero_ref,
    one_ref,
    both_ref,
    face_ref,
    core_ref,
    ends_ref,
    acc_ref,
    fine_ref,
):
    tap_refs = (zero_ref, one_ref, both_ref)
    assemble(info_ref, v_ref, pair_ref, other_ref, face_ref, core_ref, ends_ref)
    gather_taps(core_ref, ends_ref, tap_refs)
    convolve(tap_refs, w_ref, acc_ref)

    def activate(i):
        preact = acc_ref[i + 2]
        gate = 1.0 / (1.0 + jnp.exp(-preact))
        fine_ref[i // 2, i % 2] = (preact * gate).reshape(HALF, 2, SIDE, LANES)
        slope_ref[i] = gate * (1.0 + preact * (1.0 - gate))

    loop(SIDE, activate, 4)
    for t, a, b, c in taps():
        picked = fine_ref[:, a, :, b, pl.ds(c, HALF, stride=2), :]
        act_ref[:, t * LANES : (t + 1) * LANES] = picked.reshape(512, LANES).astype(BF16)
    octants = jnp.dot(act_ref[...], down_ref[...], preferred_element_type=F32).astype(BF16)
    oct_ref[0:512] = octants[:, :LANES]
    oct_ref[512:1024] = octants[:, LANES:]


def back_kernel(
    info_ref,
    own_ref,
    came_ref,
    down_t_ref,
    slope_ref,
    oct_ref,
    pair_ref,
    other_ref,
    g_ref,
    turned_ref,
    spun_ref,
    fine_ref,
):
    pair_ref[0:1024] = oct_ref[...]
    grads = []
    for n in range(2):
        rows = slice(n * 512, (n + 1) * 512)
        grad = own_ref[rows].astype(F32) + came_ref[rows].astype(F32)
        spun_ref[n] = grad.T.astype(BF16)
        grads.append(grad.astype(BF16))
    grads = jnp.concatenate(grads, axis=1)
    for pair in range(4):
        lanes = slice(pair * 256, (pair + 1) * 256)
        spread = jnp.dot(grads, down_t_ref[:, lanes], preferred_element_type=F32)
        for c in range(2):
            part = spread[:, c * LANES : (c + 1) * LANES].reshape(HALF, HALF, HALF, LANES)
            fine_ref[:, pair // 2, :, pair % 2, pl.ds(c, HALF, stride=2), :] = part

    for p in (0, 1, SIDE + 2, SIDE + 3):
        turned_ref[p] = jnp.zeros((LANES, 256), BF16)

    def back(i):
        grad = fine_ref[i // 2, i % 2].reshape(256, LANES) * slope_ref[i]
        turned_ref[i + 2] = grad.T.astype(BF16)
        rounded = grad.astype(BF16).reshape(SIDE, SIDE, LANES)
        g_ref[i] = rounded
        place_faces(info_ref, i, rounded, pair_ref, other_ref, 1024)

    loop(SIDE, back, 4)


def weigh_kernel(info_ref, zero_ref, one_ref, both_ref, act_ref, turned_ref, spun_ref, *refs):
    kept_ref, sent_ref, token_ref, sums_ref, total_ref = refs
    token_ref[...] = jnp.zeros_like(token_ref)
    lower = low_half((LANES, LANES))
    whole = [jnp.dot(spun_ref[n], act_ref[...], preferred_element_type=F32) for n in range(2)]
    folded = []
    for t in range(8):
        lanes = slice(t * LANES, (t + 1) * LANES)
        both = jnp.where(lower, whole[0][:, lanes], whole[1][:, lanes])
        folded.append(both + swap_halves(both))
    for t in range(4):
        rows = slice(CONV_ROWS + t * LANES, CONV_ROWS + (t + 1) * LANES)
        sums_ref[rows] = jnp.where(lower, folded[t], folded[t + 4])

    total_ref[...] = jnp.zeros_like(total_ref)

    def weigh(g, carry):
        planes = [3 * g + p for p in range(3)]
        for n, brick_ref in enumerate((zero_ref, one_ref)):
            lhs = [
                jnp.concatenate(
                    [turned_ref[i + 2 - a, n * 64 : (n + 1) * 64] for a in range(3)], axis=0
                )
                for i in planes
            ]
            rhs = [
                jnp.concatenate(
                    [
                        ref[i, b : b + SIDE].reshape(256, LANES)
                        for ref in (brick_ref, both_ref)
                        for b in range(3)
                    ],
                    axis=1,
                )
                for i in planes
            ]
            total_ref[n] += jnp.dot(
                jnp.concatenate(lhs, axis=1),
                jnp.concatenate(rhs, axis=0),
                preferred_element_type=F32,
            )
        return carry

    lax.fori_loop(0, (SIDE + 2) // 3, weigh, 0)
    lower = low_half((192, LANES))
    last = []
    for b in range(3):
        lanes = slice(b * LANES, (b + 1) * LANES)
        sums_ref[b * 192 : (b + 1) * 192] = total_ref[0, :, lanes] + total_ref[1, :, lanes]
        lanes = slice((3 + b) * LANES, (4 + b) * LANES)
        both = jnp.where(lower, total_ref[0, :, lanes], total_ref[1, :, lanes])
        last.append(both + swap_halves(both))
    sums_ref[576:768] = jnp.where(lower, last[0], last[1])
    sums_ref[768:960] = jnp.where(lower, last[2], 0.0)
    core = info_ref[1] % 2
    for y in range(GROUPS // 2):
        kept_ref[y] = sums_ref[share_rows(2 * y + core)]
        sent_ref[y] = sums_ref[share_rows(2 * y + 1 - core)].astype(BF16)


def share_rows(group):
    return pl.ds(pl.multiple_of(group * SHARE, 8), SHARE)


TAPPED = (SIDE + 2, SIDE + 2, SIDE, LANES)
PAD_SCRATCH = [
    pltpu.VMEM((2, SIDE, SIDE, LANES), F32),
    pltpu.VMEM((SIDE + 2, 18 * SIDE, LANES), F32),
    pltpu.VMEM((2, SIDE + 2, 24, LANES), F32),
    pltpu.VMEM((SIDE + 4, 256, LANES), F32),
]
FINE_SCRATCH = pltpu.VMEM((HALF, 2, HALF, 2, SIDE, LANES), F32)


def forward_call(info, v, pair, other, weights, down):
    return pl.pallas_call(
        forward_kernel,
        out_shape=(
            jax.ShapeDtypeStruct((1024, LANES), BF16),
            jax.ShapeDtypeStruct((SIDE, 256, LANES), F32),
            jax.ShapeDtypeStruct((512, 8 * LANES), BF16),
        )
        + (jax.ShapeDtypeStruct(TAPPED, BF16),) * 3,
        in_specs=[SMEM_SPEC] + [VMEM_SPEC] * 5,
        out_specs=(VMEM_SPEC,) * 6,
        scratch_shapes=PAD_SCRATCH + [FINE_SCRATCH],
        compiler_params=params(28),
        cost_estimate=pl.CostEstimate(
            flops=4_000_000_000, bytes_accessed=16_000_000, transcendentals=600_000
        ),
        name="forward",
    )(info, v, pair, other, weights, down)


def back_call(info, own, came, down_t, slope, octants):
    return pl.pallas_call(
        back_kernel,
        out_shape=(
            jax.ShapeDtypeStruct((1280, LANES), BF16),
            jax.ShapeDtypeStruct((256, LANES), BF16),
            jax.ShapeDtypeStruct((SIDE, SIDE, SIDE, LANES), BF16),
            jax.ShapeDtypeStruct((SIDE + 4, LANES, 256), BF16),
            jax.ShapeDtypeStruct((2, LANES, 512), BF16),
        ),
        in_specs=[SMEM_SPEC] + [VMEM_SPEC] * 5,
        out_specs=(VMEM_SPEC,) * 5,
        scratch_shapes=[FINE_SCRATCH],
        compiler_params=params(24),
        cost_estimate=pl.CostEstimate(
            flops=300_000_000, bytes_accessed=8_000_000, transcendentals=0
        ),
        name="back",
    )(info, own, came, down_t, slope, octants)


def weigh_call(info, zero, one, both, act, turned, spun):
    return pl.pallas_call(
        weigh_kernel,
        out_shape=(
            jax.ShapeDtypeStruct((GROUPS // 2, SHARE, LANES), F32),
            jax.ShapeDtypeStruct((GROUPS // 2, SHARE, LANES), BF16),
            TOKEN,
        ),
        in_specs=[SMEM_SPEC] + [VMEM_SPEC] * 6,
        out_specs=(VMEM_SPEC,) * 3,
        scratch_shapes=[
            pltpu.VMEM((CONV_ROWS + DOWN_ROWS, LANES), F32),
            pltpu.VMEM((2, 192, 768), F32),
        ],
        compiler_params=params(20),
        cost_estimate=pl.CostEstimate(
            flops=4_000_000_000, bytes_accessed=10_000_000, transcendentals=0
        ),
        name="weigh",
    )(info, zero, one, both, act, turned, spun)


def input_taps_kernel(
    after_ref,
    info_ref,
    g_ref,
    pair_ref,
    other_ref,
    zero_ref,
    one_ref,
    both_ref,
    token_ref,
    face_ref,
    core_ref,
    ends_ref,
):
    assemble(info_ref, g_ref, pair_ref, other_ref, face_ref, core_ref, ends_ref)
    gather_taps(core_ref, ends_ref, (zero_ref, one_ref, both_ref))
    token_ref[...] = jnp.zeros_like(token_ref)


def input_taps_call(after, info, g, pair, other):
    return pl.pallas_call(
        input_taps_kernel,
        out_shape=(jax.ShapeDtypeStruct(TAPPED, BF16),) * 3 + (TOKEN,),
        in_specs=[ANY_SPEC, SMEM_SPEC] + [VMEM_SPEC] * 3,
        out_specs=(VMEM_SPEC,) * 4,
        scratch_shapes=PAD_SCRATCH[:3],
        compiler_params=params(20),
        cost_estimate=pl.CostEstimate(
            flops=2_000_000_000, bytes_accessed=8_000_000, transcendentals=0
        ),
        name="input_taps",
    )(after, info, g, pair, other)


def input_half_kernel(half, *refs):
    _, zero_ref, one_ref, both_ref, w_ref = refs[:5]
    out_ref, token_ref, acc_ref = refs[-3:]
    convolve((zero_ref, one_ref, both_ref), w_ref, acc_ref, half * HALF, HALF + 2, 5)

    for i in range(HALF):
        out_ref[:, i * 256 : (i + 1) * 256] = acc_ref[i + 2].T.astype(BF16)
    token_ref[...] = jnp.zeros_like(token_ref)


def input_half_call(after, taps, weights, half, begun=()):
    return pl.pallas_call(
        functools.partial(input_half_kernel, half),
        grid=(1,),
        out_shape=(jax.ShapeDtypeStruct((LANES, SIDE**3), BF16), TOKEN),
        in_specs=[ANY_SPEC] + [VMEM_SPEC] * 4 + [ANY_SPEC] * len(begun),
        out_specs=(
            pl.BlockSpec((LANES, SIDE**3 // 2), lambda g: (0, half)),
            pl.BlockSpec((8, LANES), lambda g: (0, 0)),
        ),
        input_output_aliases={5: 0} if begun else {},
        scratch_shapes=[pltpu.VMEM((HALF + 4, 256, LANES), F32)],
        compiler_params=params(16),
        cost_estimate=pl.CostEstimate(
            flops=2_500_000_000, bytes_accessed=6_000_000, transcendentals=0
        ),
        name="input_half",
    )(after, *taps, weights, *begun)


def deal_kernel(after_ref, info_ref, kept_ref, came_ref, own_ref, *refs):
    share_refs, total_ref = refs[:-1], refs[-1]
    total_ref[...] = kept_ref[...] + came_ref[...].astype(F32)
    y = info_ref[1] // 2
    own_ref[...] = total_ref[y]
    for s, share_ref in enumerate(share_refs):
        share_ref[...] = total_ref[y ^ (s + 1)].astype(BF16)


def deal_call(after, info, kept, came):
    return pl.pallas_call(
        deal_kernel,
        out_shape=(jax.ShapeDtypeStruct((SHARE, LANES), F32),)
        + (jax.ShapeDtypeStruct((SHARE, LANES), BF16),) * 3,
        in_specs=[ANY_SPEC, SMEM_SPEC, VMEM_SPEC, VMEM_SPEC],
        out_specs=(VMEM_SPEC,) * 4,
        scratch_shapes=[pltpu.VMEM((GROUPS // 2, SHARE, LANES), F32)],
        compiler_params=params(16),
        cost_estimate=pl.CostEstimate(flops=0, bytes_accessed=500_000, transcendentals=0),
        name="deal",
    )(after, info, kept, came)


def add_kernel(after_ref, *refs):
    parts = [ref[...].astype(F32) for ref in refs[:-1]]
    while len(parts) > 1:
        parts = [first + second for first, second in zip(parts[::2], parts[1::2])]
    refs[-1][...] = parts[0].astype(refs[-1].dtype)


def add_call(after, parts, dtype=BF16):
    return pl.pallas_call(
        add_kernel,
        out_shape=jax.ShapeDtypeStruct(parts[0].shape, dtype),
        in_specs=[ANY_SPEC] + [VMEM_SPEC] * len(parts),
        out_specs=VMEM_SPEC,
        compiler_params=params(16),
        cost_estimate=pl.CostEstimate(flops=0, bytes_accessed=500_000, transcendentals=0),
        name="add",
    )(after, *parts)


def collect_kernel(info_ref, *refs):
    y = info_ref[1] // 2
    for s, share_ref in enumerate(refs[:-1]):
        refs[-1][y ^ s] = share_ref[...]


def collect_call(info, shares):
    return pl.pallas_call(
        collect_kernel,
        out_shape=jax.ShapeDtypeStruct((GROUPS // 2, SHARE, LANES), BF16),
        in_specs=[SMEM_SPEC] + [VMEM_SPEC] * len(shares),
        out_specs=VMEM_SPEC,
        compiler_params=params(16),
        cost_estimate=pl.CostEstimate(flops=0, bytes_accessed=500_000, transcendentals=0),
        name="collect",
    )(info, *shares)


def split_kernel(after_ref, info_ref, mine_ref, theirs_ref, conv_ref, down_ref, sums_ref):
    core = info_ref[1] % 2
    for y in range(GROUPS // 2):
        sums_ref[share_rows(2 * y + core)] = mine_ref[y].astype(F32)
        sums_ref[share_rows(2 * y + 1 - core)] = theirs_ref[y].astype(F32)
    for a in range(3):
        for b in range(3):
            for c in range(3):
                chunk, upper = (b, c) if c < 2 else ((3, b) if b < 2 else (4, 0))
                base = chunk * 192 + a * 64
                block = sums_ref[base : base + 64]
                block = swap_halves(block) if upper else block
                conv_ref[9 * a + 3 * b + c] = block[:, :64]
    for t in range(4):
        block = sums_ref[CONV_ROWS + t * LANES : CONV_ROWS + (t + 1) * LANES].T
        down_ref[t] = block[:64]
        down_ref[t + 4] = block[64:]


def split_call(after, info, mine, theirs):
    return pl.pallas_call(
        split_kernel,
        out_shape=(
            jax.ShapeDtypeStruct((27, 64, 64), F32),
            jax.ShapeDtypeStruct((8, 64, LANES), F32),
        ),
        in_specs=[ANY_SPEC, SMEM_SPEC] + [VMEM_SPEC] * 2,
        out_specs=(VMEM_SPEC,) * 2,
        scratch_shapes=[pltpu.VMEM((CONV_ROWS + DOWN_ROWS, LANES), F32)],
        compiler_params=params(16),
        name="split",
    )(after, info, mine, theirs)


def swaps(axis, step=1):
    return [(i, i ^ step) for i in range(lax.axis_size(axis))]


def swapped(array, axis, steps):
    return [lax.ppermute(array, axis, swaps(axis, step)) for step in steps]


def exchange(pair, other, axis):
    peers = lax.axis_size(axis)
    across = [(i, (i + 1) % peers) for i in range(1, peers, 2)]
    return (
        lax.ppermute(pair, axis, swaps(axis)),
        lax.ppermute(other, axis, across + [(j, i) for i, j in across]),
    )


def body(fine_input, conv_weight, down_weight, coarse_cot, neighbours, children):
    rank = lax.axis_index("grp") * lax.axis_size("dev") + lax.axis_index("dev")
    info = [rank.reshape(1), lax.axis_index("grp").reshape(1), children.reshape(8)]
    info = jnp.concatenate([part.astype(jnp.int32) for part in info + [neighbours.reshape(52)]])

    voxels, pair, other, token = faces_call(info, fine_input.reshape(LANES, SIDE**3))
    own, send = cot_call(token, info, coarse_cot.reshape(LANES, SIDE**3))
    pair, other = exchange(pair, other, "dev")
    came = lax.ppermute(send, "dev", swaps("dev"))
    forward, backward, down, down_t = weights_call(conv_weight, down_weight.transpose(0, 2, 1))
    octants, slope, act, zero, one, both = forward_call(
        info, voxels, pair, other, forward, down
    )
    mine, other_out, grads, turned, spun = back_call(info, own, came, down_t, slope, octants)
    theirs, grad_other = exchange(mine, other_out, "dev")
    kept, sent, token = weigh_call(info, zero, one, both, act, turned, spun)

    (came,) = swapped(sent, "grp", (1,))
    coarse, token = coarse_half_call(token, info, mine, theirs, 0)
    own, *shares = deal_call(token, info, kept, came)
    came = [lax.ppermute(share, "grp", swaps("grp", 2 * s + 2)) for s, share in enumerate(shares)]
    *input_taps, token = input_taps_call(own, info, grads, theirs, grad_other)
    part = add_call(token, [own, *came], F32)
    came = swapped(part, "dev", (1, 2, 3))
    input_grad, token = input_half_call(part, input_taps, backward, 0)
    part = add_call(token, [part, *came])
    came = swapped(part, "dev", (4, 8, 12))
    input_grad, token = input_half_call(part, input_taps, backward, 1, (input_grad,))
    part = add_call(token, [part, *came])
    came = swapped(part, "dev", (16,))
    coarse, token = coarse_half_call(part, info, mine, theirs, 1, (coarse,))
    part = add_call(token, [part, *came])
    shares = collect_call(info, [part, *swapped(part, "grp", (2, 4, 6))])
    (came,) = swapped(shares, "grp", (1,))
    conv_grad, down_grad = split_call(token, info, shares, came)
    return (
        coarse.reshape(1, LANES, SIDE**3),
        input_grad.reshape(2, 64, SIDE**3),
        conv_grad,
        down_grad.transpose(0, 2, 1),
    )


def solution(mesh):
    in_specs = (
        P(("grp", "dev"), None, None),
        P(),
        P(),
        P(("grp", "dev"), None, None),
        P(("grp", "dev"), None),
        P(("grp", "dev"), None),
    )
    out_specs = (P(("grp", "dev"), None, None), P(("grp", "dev"), None, None), P(), P())
    return jax.shard_map(body, mesh=mesh, in_specs=in_specs, out_specs=out_specs, check_vma=False)
```

time: 110 us -> 84.7 us (0.77); the launches traced: 108 us -> 84.5 us
  blocking collectives: 36.9 us -> 0 us
  starting transfers between devices: 11.2 us -> 37.5 us
  Pallas kernels: 41.2 us -> 34.3 us
  waiting for transfers between devices: 13 us -> 9.16 us
  local copies, waits for them, and re-layouts: 5.02 us -> 2 us
    all_to_all x1 -> x0, blocking collectives: 36.9 us -> none  [total_sums(): shares = lax.all_to_all(sums.reshape(peers, SHARE, LANES), axes, 0, 0)]
    ppermute x2 -> x18, starting transfers between devices: 3.61 us -> 27.2 us  [the longest x12 19.4 us: swapped(): return [lax.ppermute(array, axis, swaps(axis, step)) for step in steps]]
    ppermute x2, starting transfers between devices: 1.31 us -> 10.4 us  [exchange(): lax.ppermute(other, axis, across + [(j, i) for i, j in across])]
    pallas_call x6 -> x16, Pallas kernels: 39.4 us -> 31.9 us  [the longest x1 8.38 us: forward_call(): pl.pallas_call(forward_kernel, out_shape=(jax.ShapeDtypeStruct((1024, LAN...]
    all_to_all x1 -> x0, starting transfers between devices: 6.32 us -> none  [total_sums(): lax.all_to_all(add_call(shares), axes, 0, 0).reshape(peers * SHARE, LANES)]
    ppermute x2 -> x18, waiting for transfers between devices: 13 us -> 9.16 us  [the longest x12 7.55 us: swapped(): return [lax.ppermute(array, axis, swaps(axis, step)) for step in steps]]
    unnamed x14 -> x8, local copies, waits for them, and re-layouts: 5.02 us -> 1.24 us
  transfers between devices with their start and end apart: 5 -> 20, of which waited for: 2 -> 5; matrix products, arithmetic and copies ran while one was open for 0% -> 0% of each run, Pallas kernels for 16% -> 34%
where the time goes in v3:
time: 84.7 us; the launch traced here: 84.5 us
  starting transfers between devices  37.5 us (44%)
  Pallas kernels  34.3 us (40%)
  waiting for transfers between devices  9.16 us (11%)
  local copies, waits for them, and re-layouts  2 us (2%)
    ppermute x12, starting transfers between devices, swapped(): return [lax.ppermute(array, axis, swaps(axis, step)) for step in steps]  19.4 us
    ppermute x2, starting transfers between devices, exchange(): lax.ppermute(other, axis, across + [(j, i) for i, j in across])  10.4 us
    pallas_call x1, Pallas kernels, forward_call(): pl.pallas_call(forward_kernel, out_shape=(jax.ShapeDtypeStruct((1024, LAN...  8.38 us
    ppermute x12, waiting for transfers between devices, swapped(): return [lax.ppermute(array, axis, swaps(axis, step)) for step in steps]  7.55 us
    pallas_call x2, Pallas kernels, input_half_call(): pl.pallas_call(functools.partial(input_half_kernel, half), grid=(1,), out...  7.25 us
    pallas_call x1, Pallas kernels, weigh_call(): pl.pallas_call(weigh_kernel, out_shape=(jax.ShapeDtypeStruct((GROUPS // 2...  5.24 us
    ppermute x3, starting transfers between devices, body(): lax.ppermute(share, 'grp', swaps('grp', 2 * s + 2))  4.02 us
    ppermute x2, starting transfers between devices, exchange(): lax.ppermute(pair, axis, swaps(axis))  3.65 us
  transfers between devices with their start and end apart: 20, of which 5 were waited for; matrix products, arithmetic and copies ran while one was open for 0% of the time, Pallas kernels for 34%

profile of v3, /device:TPU:1, one launch (start us, length us, event | category | flops | bytes accessed | tf_op | source)
XLA Modules:
  0.0 84.5 jit_solution(6498655864433785282)
XLA Ops:
  0.6 0.8 reshape.35
  1.4 0.7 pad_add_fusion.info_ref.refs_1_
  2.1 1.2 %copy-done = bf16[2,64,4096]{2,1,0:T(8,128)(2,1)S(1)} copy-done((bf16[2,64,4096]{2,1,0:T(8,128)(2,1)S(1)}, bf16[2,64,4096]{2,1,0:T(8,128)(2,1)}, u32[]{:S(2)}) %copy-start) | copy-done | bytes 1048600
  3.4 1.1 %faces.1 = (bf16[16,16,16,128]{3,2,1,0:T(8,128)(2,1)S(1)}, bf16[256,128]{1,0:T(8,128)(2,1)S(1)}, bf16[256,128]{1,0:T(8,128)(2,1)S(1)}, f32[8,128]{1,0:T(8,128)S(1)}) custom-call(s32[62]{0:T(128)S(1)} %pad_add_fusion.info_ref.refs_1_, bf16[128,4096]{1,0:T(8,128)(2,1)S(1)} %bitcast.9), custom_call_target="tpu_custom_call" | custom-call | bytes 4000000 | tf_op jit(solution)/shard_map/faces/pallas_call | solution.py:67
  4.5 2.1 %collective-permute-start = (bf16[256,128]{1,0:T(8,128)(2,1)S(1)}, bf16[256,128]{1,0:T(8,128)(2,1)S(1)}, u32[]{:S(2)}, u32[]{:S(2)}) collective-permute-start(bf16[256,128]{1,0:T(8,128)(2,1)S(1)} %get-tuple-element.47), channel_id=1, source_target_pairs={{0,1},{1,0},{2,3},{3,2},{4,5},{5,4},{6,7},{7,6},{8,9},{9,8},{10,11... | collective-permute-start | bytes 196616 | tf_op jit(solution)/shard_map/ppermute | solution.py:735
  6.6 7.1 %collective-permute-start.1 = (bf16[256,128]{1,0:T(8,128)(2,1)S(1)}, bf16[256,128]{1,0:T(8,128)(2,1)S(1)}, u32[]{:S(2)}, u32[]{:S(2)}) collective-permute-start(bf16[256,128]{1,0:T(8,128)(2,1)S(1)} %get-tuple-element.48), channel_id=1, source_target_pairs={{1,2},{3,4},{5,6},{7,8},{9,10},{11,12},{13,14},{15,16},{17,18},{19... | collective-permute-start | bytes 196616 | tf_op jit(solution)/shard_map/ppermute | solution.py:736
  13.7 1.3 %cot.1 = (bf16[1024,128]{1,0:T(8,128)(2,1)S(1)}, bf16[1024,128]{1,0:T(8,128)(2,1)S(1)}) custom-call(f32[8,128]{1,0:T(8,128)S(1)} %get-tuple-element.55.after_ref, s32[62]{0:T(128)S(1)} %pad_add_fusion.info_ref.refs_1_, bf16[128,4096]{1,0:T(8,128)(2,1)S(1)} %bitcast.10), custom_call_target="tpu_custom_call" | custom-call | bytes 8000000 | tf_op jit(solution)/shard_map/cot/pallas_call | solution.py:106
  15.8 8.4 %forward.1 = (bf16[1024,128]{1,0:T(8,128)(2,1)S(1)}, f32[16,256,128]{2,1,0:T(8,128)S(1)}, bf16[512,1024]{1,0:T(8,128)(2,1)S(1)}, bf16[18,18,16,128]{3,2,1,0:T(8,...) custom-call(s32[62]{0:T(128)S(1)} %pad_add_fusion.info_ref.refs_1_, ...), custom_call_target="tpu_custom_call" | custom-call | flops 4000000000 | bytes 16000000 | tf_op jit(solution)/shard_map/forward/pallas_call | solution.py:503
  24.2 1.7 %back.1 = (bf16[1280,128]{1,0:T(8,128)(2,1)S(1)}, bf16[256,128]{1,0:T(8,128)(2,1)S(1)}, bf16[16,16,16,128]{3,2,1,0:T(8,128)(2,1)S(1)}, bf16[20,128,256]{2,1,0:T(8,128)(2,1)S(1)}, bf16[2,128,512]{2,1,0:T(8,128)(2,1)S(1)}) custom-call(s32[62]{0:T(128)S(1)} %pad_add_fusion.info_ref.refs_1_, bf16[1024,128]{1,0:T(8,128)(2,1)S(1)} %get-tuple-element.56.own_ref, ...), custom_call_target="tpu_custom_call" | custom-call | flops 300000000 | bytes 8000000 | tf_op jit(solution)/shard_map/back/pallas_call | solution.py:523
  25.9 1.5 %collective-permute-start.3 = (bf16[1280,128]{1,0:T(8,128)(2,1)S(1)}, bf16[1280,128]{1,0:T(8,128)(2,1)S(1)}, u32[]{:S(2)}, u32[]{:S(2)}) collective-permute-start(bf16[1280,128]{1,0:T(8,128)(2,1)S(1)} %get-tuple-element.64.refs_2_), channel_id=1, source_target_pairs={{0,1},{1,0},{2,3},{3,2},{4,5},{5,4},{6,7},{7,6},{8,9},{9,8},{10,11... | collective-permute-start | bytes 983048 | tf_op jit(solution)/shard_map/ppermute | solution.py:735
  27.4 5.2 %weigh.1 = (f32[4,184,128]{2,1,0:T(8,128)S(1)}, bf16[4,184,128]{2,1,0:T(8,128)(2,1)S(1)}, f32[8,128]{1,0:T(8,128)S(1)}) custom-call(s32[62]{0:T(128)S(1)} %pad_add_fusion.info_ref.refs_1_, bf16[18,18,16,128]{3,2,1,0:T(8,128)(2,1)S(1)} %get-tuple-element.51.zero_ref, bf16[18,18,16,128]{3,2,1,0:T(8,128)(2,1)S(1)} %get-tuple-element.52.one_ref, ...), custom_call_target="tpu_custom_call" | custom-call | flops 4000000000 | bytes 10000000 | tf_op jit(solution)/shard_map/weigh/pallas_call | solution.py:544
  32.6 1.9 %collective-permute-start.4 = (bf16[4,184,128]{2,1,0:T(8,128)(2,1)S(1)}, bf16[4,184,128]{2,1,0:T(8,128)(2,1)S(1)}, u32[]{:S(2)}, u32[]{:S(2)}) collective-permute-start(bf16[4,184,128]{2,1,0:T(8,128)(2,1)S(1)} %get-tuple-element.67), channel_id=1, source_target_pairs={{0,32},{32,0},{64,96},{96,64},{128,160},{160,128},{192,224},{224,1... | collective-permute-start | bytes 565256 | tf_op jit(solution)/shard_map/ppermute | solution.py:728
  34.5 3.2 %collective-permute-start.5 = (bf16[256,128]{1,0:T(8,128)(2,1)S(1)}, bf16[256,128]{1,0:T(8,128)(2,1)S(1)}, u32[]{:S(2)}, u32[]{:S(2)}) collective-permute-start(bf16[256,128]{1,0:T(8,128)(2,1)S(1)} %get-tuple-element.70), channel_id=1, source_target_pairs={{1,2},{3,4},{5,6},{7,8},{9,10},{11,12},{13,14},{15,16},{17,18},{19... | collective-permute-start | bytes 196616 | tf_op jit(solution)/shard_map/ppermute | solution.py:736
  37.8 1.6 %coarse_half.2 = (bf16[128,4096]{1,0:T(8,128)(2,1)}, f32[8,128]{1,0:T(8,128)S(1)}) custom-call(f32[8,128]{1,0:T(8,128)S(1)} %get-tuple-element.63.refs_0_, s32[62]{0:T(128)S(1)} %pad_add_fusion.info_ref.refs_1_, bf16[1280,128]{1,0:T(8,128)(2,1)S(1)} %get-tuple-element.64.refs_2_, bf16[1280,128]{1,0:T(8,128)(2,1)S(1)} %collective-permute-done.3.refs_3_.pair_ref), custom_call_target="tpu_custom_call" | custom-call | bytes 4000000 | tf_op jit(solution)/shard_map/coarse_half/pallas_call | solution.py:187
  40.0 1.4 %collective-permute-start.6 = (bf16[184,128]{1,0:T(8,128)(2,1)S(1)}, bf16[184,128]{1,0:T(8,128)(2,1)S(1)}, u32[]{:S(2)}, u32[]{:S(2)}) collective-permute-start(bf16[184,128]{1,0:T(8,128)(2,1)S(1)} %get-tuple-element.72), channel_id=1, source_target_pairs={{0,64},{32,96},{64,0},{96,32},{128,192},{160,224},{192,128},{224,1... | collective-permute-start | bytes 141320 | tf_op jit(solution)/shard_map/ppermute | solution.py:760
  41.3 2.6 %collective-permute-start.7 = (bf16[184,128]{1,0:T(8,128)(2,1)S(1)}, bf16[184,128]{1,0:T(8,128)(2,1)S(1)}, u32[]{:S(2)}, u32[]{:S(2)}) collective-permute-start(bf16[184,128]{1,0:T(8,128)(2,1)S(1)} %get-tuple-element.73), channel_id=1, source_target_pairs={{0,128},{32,160},{64,192},{96,224},{128,0},{160,32},{192,64},{224,... | collective-permute-start | bytes 141320 | tf_op jit(solution)/shard_map/ppermute | solution.py:760
  44.0 2.5 %input_taps.1 = (bf16[18,18,16,128]{3,2,1,0:T(8,128)(2,1)S(1)}, bf16[18,18,16,128]{3,2,1,0:T(8,128)(2,1)S(1)}, bf16[18,18,16,128]{3,2,1,0:T(8,128)(2,1)S(1)}, f32[8,128]{1,0:T(8,128)S(1)}) custom-call(f32[184,128]{1,0:T(8,128)S(1)} %get-tuple-element.68.after_ref.refs_0_, s32[62]{0:T(128)S(1)} %pad_add_fusion.info_ref.refs_1_, ...), custom_call_target="tpu_custom_call" | custom-call | flops 2000000000 | bytes 8000000 | tf_op jit(solution)/shard_map/input_taps/pallas_call | solution.py:585
  46.5 1.6 %collective-permute-done.8.refs_3_ = bf16[184,128]{1,0:T(8,128)(2,1)S(1)} collective-permute-done((bf16[184,128]{1,0:T(8,128)(2,1)S(1)}, bf16[184,128]{1,0:T(8,128)(2,1)S(1)}, u32[]{:S(2)}, u32[]{:S(2)}) %collective-permute-start.8) | collective-permute-done | bytes 47136 | tf_op jit(solution)/shard_map/ppermute | solution.py:760
  48.5 3.0 %collective-permute-start.9 = (f32[184,128]{1,0:T(8,128)S(1)}, f32[184,128]{1,0:T(8,128)S(1)}, u32[]{:S(2)}, u32[]{:S(2)}) collective-permute-start(f32[184,128]{1,0:T(8,128)S(1)} %add.14.refs_0_), channel_id=1, source_target_pairs={{0,1},{1,0},{2,3},{3,2},{4,5},{5,4},{6,7},{7,6},{8,9},{9,8},{10,11... | collective-permute-start | bytes 282632 | tf_op jit(solution)/shard_map/ppermute | solution.py:728
  51.5 3.6 %input_half.2 = (bf16[128,4096]{1,0:T(8,128)(2,1)}, f32[8,128]{1,0:T(8,128)S(1)}) custom-call(f32[184,128]{1,0:T(8,128)S(1)} %add.14.refs_0_, bf16[18,18,16,128]{3,2,1,0:T(8,128)(2,1)S(1)} %get-tuple-element.75.refs_1_, bf16[18,18,16,128]{3,2,1,0:T(8,128)(2,1)S(1)} %get-tuple-element.76.refs_2_, bf16[18,18,16,128]{3,2,1,0:T(8,128)(2,1)S(1)} %get-tuple-element.77.refs_3_, ...), custom_call_target="tpu_custom_call" | custom-call | flops 2500000000 | bytes 6000000 | tf_op jit(solution)/shard_map/input_half/pallas_call | solution.py:610
  55.9 2.9 %collective-permute-start.12 = (bf16[184,128]{1,0:T(8,128)(2,1)S(1)}, bf16[184,128]{1,0:T(8,128)(2,1)S(1)}, u32[]{:S(2)}, u32[]{:S(2)}) collective-permute-start(bf16[184,128]{1,0:T(8,128)(2,1)S(1)} %add.15.refs_0_), channel_id=1, source_target_pairs={{0,4},{1,5},{2,6},{3,7},{4,0},{5,1},{6,2},{7,3},{8,12},{9,13},{10,... | collective-permute-start | bytes 141320 | tf_op jit(solution)/shard_map/ppermute | solution.py:728
  58.8 3.6 %input_half.3 = (bf16[128,4096]{1,0:T(8,128)(2,1)}, f32[8,128]{1,0:T(8,128)S(1)}) custom-call(bf16[184,128]{1,0:T(8,128)(2,1)S(1)} %add.15.refs_0_, bf16[18,18,16,128]{3,2,1,0:T(8,128)(2,1)S(1)} %get-tuple-element.75.refs_1_, bf16[18,18,16,128]{3,2,1,0:T(8,128)(2,1)S(1)} %get-tuple-element.76.refs_2_, ...), custom_call_target="tpu_custom_call", output_to_operand_aliasing={{0}: (5, {})} | custom-call | flops 2500000000 | bytes 6000000 | tf_op jit(solution)/shard_map/input_half/pallas_call | solution.py:610
  62.5 1.4 %collective-permute-start.15 = (bf16[184,128]{1,0:T(8,128)(2,1)S(1)}, bf16[184,128]{1,0:T(8,128)(2,1)S(1)}, u32[]{:S(2)}, u32[]{:S(2)}) collective-permute-start(bf16[184,128]{1,0:T(8,128)(2,1)S(1)} %add.16.refs_0_), channel_id=1, source_target_pairs={{0,16},{1,17},{2,18},{3,19},{4,20},{5,21},{6,22},{7,23},{8,24},{9,... | collective-permute-start | bytes 141320 | tf_op jit(solution)/shard_map/ppermute | solution.py:728
  63.9 1.6 %coarse_half.3 = (bf16[128,4096]{1,0:T(8,128)(2,1)}, f32[8,128]{1,0:T(8,128)S(1)}) custom-call(bf16[184,128]{1,0:T(8,128)(2,1)S(1)} %add.16.refs_0_, s32[62]{0:T(128)S(1)} %pad_add_fusion.info_ref.refs_1_, bf16[1280,128]{1,0:T(8,128)(2,1)S(1)} %get-tuple-element.64.refs_2_, ...), custom_call_target="tpu_custom_call", output_to_operand_aliasing={{0}: (4, {})} | custom-call | bytes 4000000 | tf_op jit(solution)/shard_map/coarse_half/pallas_call | solution.py:187
  65.5 3.9 %collective-permute-done.15.refs_1_ = bf16[184,128]{1,0:T(8,128)(2,1)S(1)} collective-permute-done((bf16[184,128]{1,0:T(8,128)(2,1)S(1)}, bf16[184,128]{1,0:T(8,128)(2,1)S(1)}, u32[]{:S(2)}, u32[]{:S(2)}) %collective-permute-start.15) | collective-permute-done | bytes 47136 | tf_op jit(solution)/shard_map/ppermute | solution.py:728
  69.4 1.5 %collective-permute-start.18 = (bf16[184,128]{1,0:T(8,128)(2,1)S(1)}, bf16[184,128]{1,0:T(8,128)(2,1)S(1)}, u32[]{:S(2)}, u32[]{:S(2)}) collective-permute-start(bf16[184,128]{1,0:T(8,128)(2,1)S(1)} %add.17.refs_0_), channel_id=1, source_target_pairs={{0,192},{32,224},{64,128},{96,160},{128,64},{160,96},{192,0},{224,... | collective-permute-start | bytes 141320 | tf_op jit(solution)/shard_map/ppermute | solution.py:728
  70.9 1.8 %collective-permute-start.16 = (bf16[184,128]{1,0:T(8,128)(2,1)S(1)}, bf16[184,128]{1,0:T(8,128)(2,1)S(1)}, u32[]{:S(2)}, u32[]{:S(2)}) collective-permute-start(bf16[184,128]{1,0:T(8,128)(2,1)S(1)} %add.17.refs_0_), channel_id=1, source_target_pairs={{0,64},{32,96},{64,0},{96,32},{128,192},{160,224},{192,128},{224,1... | collective-permute-start | bytes 141320 | tf_op jit(solution)/shard_map/ppermute | solution.py:728
  72.7 1.1 %collective-permute-done.18.refs_3_ = bf16[184,128]{1,0:T(8,128)(2,1)S(1)} collective-permute-done((bf16[184,128]{1,0:T(8,128)(2,1)S(1)}, bf16[184,128]{1,0:T(8,128)(2,1)S(1)}, u32[]{:S(2)}, u32[]{:S(2)}) %collective-permute-start.18) | collective-permute-done | bytes 47136 | tf_op jit(solution)/shard_map/ppermute | solution.py:728
  73.9 1.4 %collective-permute-done.17.refs_2_ = bf16[184,128]{1,0:T(8,128)(2,1)S(1)} collective-permute-done((bf16[184,128]{1,0:T(8,128)(2,1)S(1)}, bf16[184,128]{1,0:T(8,128)(2,1)S(1)}, u32[]{:S(2)}, u32[]{:S(2)}) %collective-permute-start.17) | collective-permute-done | bytes 47136 | tf_op jit(solution)/shard_map/ppermute | solution.py:728
  75.9 5.8 %collective-permute-start.19 = (bf16[4,184,128]{2,1,0:T(8,128)(2,1)S(1)}, bf16[4,184,128]{2,1,0:T(8,128)(2,1)S(1)}, u32[]{:S(2)}, u32[]{:S(2)}) collective-permute-start(bf16[4,184,128]{2,1,0:T(8,128)(2,1)S(1)} %collect.1.mine_ref), channel_id=1, source_target_pairs={{0,32},{32,0},{64,96},{96,64},{128,160},{160,128},{192,224},{224,1... | collective-permute-start | bytes 565256 | tf_op jit(solution)/shard_map/ppermute | solution.py:728
  81.7 1.1 %collective-permute-done.19.theirs_ref = bf16[4,184,128]{2,1,0:T(8,128)(2,1)S(1)} collective-permute-done((bf16[4,184,128]{2,1,0:T(8,128)(2,1)S(1)}, bf16[4,184,128]{2,1,0:T(8,128)(2,1)S(1)}, u32[]{:S(2)}, u32[]{:S(2)}) %collective-permute-start.19) | collective-permute-done | bytes 188448 | tf_op jit(solution)/shard_map/ppermute | solution.py:728
  82.7 1.8 %split.1 = (f32[27,64,64]{2,1,0:T(8,128)}, f32[8,64,128]{2,1,0:T(8,128)}) custom-call(f32[8,128]{1,0:T(8,128)S(1)} %get-tuple-element.85.after_ref, s32[62]{0:T(128)S(1)} %pad_add_fusion.info_ref.refs_1_, bf16[4,184,128]{2,1,0:T(8,128)(2,1)S(1)} %collect.1.mine_ref, bf16[4,184,128]{2,1,0:T(8,128)(2,1)S(1)} %collective-permute-done.19.theirs_ref), custom_call_target="tpu_custom_call" | custom-call | tf_op jit(solution)/shard_map/split/pallas_call | solution.py:709
  (36 shorter events, 3.1 us)
Async XLA Ops:
  2.1 1.2 %copy-start = (bf16[2,64,4096]{2,1,0:T(8,128)(2,1)S(1)}, bf16[2,64,4096]{2,1,0:T(8,128)(2,1)}, u32[]{:S(2)}) copy-start(bf16[2,64,4096]{2,1,0:T(8,128)(2,1)} %param.6) | copy-start | bytes 3145732
  3.4 10.4 %copy-start.1 = (bf16[1,128,4096]{2,1,0:T(8,128)(2,1)S(1)}, bf16[1,128,4096]{2,1,0:T(8,128)(2,1)}, u32[]{:S(2)}) copy-start(bf16[1,128,4096]{2,1,0:T(8,128)(2,1)} %param.9) | copy-start | bytes 3145732
  3.4 11.8 %copy-start.2 = (bf16[27,64,64]{2,1,0:T(8,128)(2,1)S(1)}, bf16[27,64,64]{2,1,0:T(8,128)(2,1)}, u32[]{:S(2)}) copy-start(bf16[27,64,64]{2,1,0:T(8,128)(2,1)} %conv_ref.1) | copy-start | bytes 663556
  3.4 11.8 %copy-start.3 = (bf16[8,128,64]{1,2,0:T(8,128)(2,1)S(1)}, bf16[8,128,64]{1,2,0:T(8,128)(2,1)}, u32[]{:S(2)}) copy-start(bf16[8,128,64]{1,2,0:T(8,128)(2,1)} %param.8) | copy-start | bytes 393220
  4.5 11.3 %collective-permute-start = (bf16[256,128]{1,0:T(8,128)(2,1)S(1)}, bf16[256,128]{1,0:T(8,128)(2,1)S(1)}, u32[]{:S(2)}, u32[]{:S(2)}) collective-permute-start(bf16[256,128]{1,0:T(8,128)(2,1)S(1)} %get-tuple-element.47), channel_id=1, source_target_pairs={{0,1},{1,0},{2,3},{3,2},{4,5},{5,4},{6,7},{7,6},{8,9},{9,8},{10,11... | collective-permute-start | bytes 196616 | tf_op jit(solution)/shard_map/ppermute | solution.py:735
  6.6 9.2 %collective-permute-start.1 = (bf16[256,128]{1,0:T(8,128)(2,1)S(1)}, bf16[256,128]{1,0:T(8,128)(2,1)S(1)}, u32[]{:S(2)}, u32[]{:S(2)}) collective-permute-start(bf16[256,128]{1,0:T(8,128)(2,1)S(1)} %get-tuple-element.48), channel_id=1, source_target_pairs={{1,2},{3,4},{5,6},{7,8},{9,10},{11,12},{13,14},{15,16},{17,18},{19... | collective-permute-start | bytes 196616 | tf_op jit(solution)/shard_map/ppermute | solution.py:736
  15.0 9.2 %collective-permute-start.2 = (bf16[1024,128]{1,0:T(8,128)(2,1)S(1)}, bf16[1024,128]{1,0:T(8,128)(2,1)S(1)}, u32[]{:S(2)}, u32[]{:S(2)}) collective-permute-start(bf16[1024,128]{1,0:T(8,128)(2,1)S(1)} %get-tuple-element.57), channel_id=1, source_target_pairs={{0,1},{1,0},{2,3},{3,2},{4,5},{5,4},{6,7},{7,6},{8,9},{9,8},{10,11... | collective-permute-start | bytes 786440 | tf_op jit(solution)/shard_map/ppermute | solution.py:748
  25.9 11.9 %collective-permute-start.3 = (bf16[1280,128]{1,0:T(8,128)(2,1)S(1)}, bf16[1280,128]{1,0:T(8,128)(2,1)S(1)}, u32[]{:S(2)}, u32[]{:S(2)}) collective-permute-start(bf16[1280,128]{1,0:T(8,128)(2,1)S(1)} %get-tuple-element.64.refs_2_), channel_id=1, source_target_pairs={{0,1},{1,0},{2,3},{3,2},{4,5},{5,4},{6,7},{7,6},{8,9},{9,8},{10,11... | collective-permute-start | bytes 983048 | tf_op jit(solution)/shard_map/ppermute | solution.py:735
  32.6 6.7 %collective-permute-start.4 = (bf16[4,184,128]{2,1,0:T(8,128)(2,1)S(1)}, bf16[4,184,128]{2,1,0:T(8,128)(2,1)S(1)}, u32[]{:S(2)}, u32[]{:S(2)}) collective-permute-start(bf16[4,184,128]{2,1,0:T(8,128)(2,1)S(1)} %get-tuple-element.67), channel_id=1, source_target_pairs={{0,32},{32,0},{64,96},{96,64},{128,160},{160,128},{192,224},{224,1... | collective-permute-start | bytes 565256 | tf_op jit(solution)/shard_map/ppermute | solution.py:728
  34.5 9.5 %collective-permute-start.5 = (bf16[256,128]{1,0:T(8,128)(2,1)S(1)}, bf16[256,128]{1,0:T(8,128)(2,1)S(1)}, u32[]{:S(2)}, u32[]{:S(2)}) collective-permute-start(bf16[256,128]{1,0:T(8,128)(2,1)S(1)} %get-tuple-element.70), channel_id=1, source_target_pairs={{1,2},{3,4},{5,6},{7,8},{9,10},{11,12},{13,14},{15,16},{17,18},{19... | collective-permute-start | bytes 196616 | tf_op jit(solution)/shard_map/ppermute | solution.py:736
  40.0 6.5 %collective-permute-start.6 = (bf16[184,128]{1,0:T(8,128)(2,1)S(1)}, bf16[184,128]{1,0:T(8,128)(2,1)S(1)}, u32[]{:S(2)}, u32[]{:S(2)}) collective-permute-start(bf16[184,128]{1,0:T(8,128)(2,1)S(1)} %get-tuple-element.72), channel_id=1, source_target_pairs={{0,64},{32,96},{64,0},{96,32},{128,192},{160,224},{192,128},{224,1... | collective-permute-start | bytes 141320 | tf_op jit(solution)/shard_map/ppermute | solution.py:760
  41.3 5.2 %collective-permute-start.7 = (bf16[184,128]{1,0:T(8,128)(2,1)S(1)}, bf16[184,128]{1,0:T(8,128)(2,1)S(1)}, u32[]{:S(2)}, u32[]{:S(2)}) collective-permute-start(bf16[184,128]{1,0:T(8,128)(2,1)S(1)} %get-tuple-element.73), channel_id=1, source_target_pairs={{0,128},{32,160},{64,192},{96,224},{128,0},{160,32},{192,64},{224,... | collective-permute-start | bytes 141320 | tf_op jit(solution)/shard_map/ppermute | solution.py:760
  44.0 4.1 %collective-permute-start.8 = (bf16[184,128]{1,0:T(8,128)(2,1)S(1)}, bf16[184,128]{1,0:T(8,128)(2,1)S(1)}, u32[]{:S(2)}, u32[]{:S(2)}) collective-permute-start(bf16[184,128]{1,0:T(8,128)(2,1)S(1)} %get-tuple-element.74), channel_id=1, source_target_pairs={{0,192},{32,224},{64,128},{96,160},{128,64},{160,96},{192,0},{224,... | collective-permute-start | bytes 141320 | tf_op jit(solution)/shard_map/ppermute | solution.py:760
  48.1 7.0 %collective-permute-start.11 = (f32[184,128]{1,0:T(8,128)S(1)}, f32[184,128]{1,0:T(8,128)S(1)}, u32[]{:S(2)}, u32[]{:S(2)}) collective-permute-start(f32[184,128]{1,0:T(8,128)S(1)} %add.14.refs_0_), channel_id=1, source_target_pairs={{0,3},{1,2},{2,1},{3,0},{4,7},{5,6},{6,5},{7,4},{8,11},{9,10},{10,... | collective-permute-start | bytes 282632 | tf_op jit(solution)/shard_map/ppermute | solution.py:728
  48.2 6.9 %collective-permute-start.10 = (f32[184,128]{1,0:T(8,128)S(1)}, f32[184,128]{1,0:T(8,128)S(1)}, u32[]{:S(2)}, u32[]{:S(2)}) collective-permute-start(f32[184,128]{1,0:T(8,128)S(1)} %add.14.refs_0_), channel_id=1, source_target_pairs={{0,2},{1,3},{2,0},{3,1},{4,6},{5,7},{6,4},{7,5},{8,10},{9,11},{10,... | collective-permute-start | bytes 282632 | tf_op jit(solution)/shard_map/ppermute | solution.py:728
  48.5 6.6 %collective-permute-start.9 = (f32[184,128]{1,0:T(8,128)S(1)}, f32[184,128]{1,0:T(8,128)S(1)}, u32[]{:S(2)}, u32[]{:S(2)}) collective-permute-start(f32[184,128]{1,0:T(8,128)S(1)} %add.14.refs_0_), channel_id=1, source_target_pairs={{0,1},{1,0},{2,3},{3,2},{4,5},{5,4},{6,7},{7,6},{8,9},{9,8},{10,11... | collective-permute-start | bytes 282632 | tf_op jit(solution)/shard_map/ppermute | solution.py:728
  55.1 7.3 %collective-permute-start.14 = (bf16[184,128]{1,0:T(8,128)(2,1)S(1)}, bf16[184,128]{1,0:T(8,128)(2,1)S(1)}, u32[]{:S(2)}, u32[]{:S(2)}) collective-permute-start(bf16[184,128]{1,0:T(8,128)(2,1)S(1)} %add.15.refs_0_), channel_id=1, source_target_pairs={{0,12},{1,13},{2,14},{3,15},{4,8},{5,9},{6,10},{7,11},{8,4},{9,5},... | collective-permute-start | bytes 141320 | tf_op jit(solution)/shard_map/ppermute | solution.py:728
  55.9 6.6 %collective-permute-start.13 = (bf16[184,128]{1,0:T(8,128)(2,1)S(1)}, bf16[184,128]{1,0:T(8,128)(2,1)S(1)}, u32[]{:S(2)}, u32[]{:S(2)}) collective-permute-start(bf16[184,128]{1,0:T(8,128)(2,1)S(1)} %add.15.refs_0_), channel_id=1, source_target_pairs={{0,8},{1,9},{2,10},{3,11},{4,12},{5,13},{6,14},{7,15},{8,0},{9,1},... | collective-permute-start | bytes 141320 | tf_op jit(solution)/shard_map/ppermute | solution.py:728
  55.9 6.6 %collective-permute-start.12 = (bf16[184,128]{1,0:T(8,128)(2,1)S(1)}, bf16[184,128]{1,0:T(8,128)(2,1)S(1)}, u32[]{:S(2)}, u32[]{:S(2)}) collective-permute-start(bf16[184,128]{1,0:T(8,128)(2,1)S(1)} %add.15.refs_0_), channel_id=1, source_target_pairs={{0,4},{1,5},{2,6},{3,7},{4,0},{5,1},{6,2},{7,3},{8,12},{9,13},{10,... | collective-permute-start | bytes 141320 | tf_op jit(solution)/shard_map/ppermute | solution.py:728
  62.5 6.9 %collective-permute-start.15 = (bf16[184,128]{1,0:T(8,128)(2,1)S(1)}, bf16[184,128]{1,0:T(8,128)(2,1)S(1)}, u32[]{:S(2)}, u32[]{:S(2)}) collective-permute-start(bf16[184,128]{1,0:T(8,128)(2,1)S(1)} %add.16.refs_0_), channel_id=1, source_target_pairs={{0,16},{1,17},{2,18},{3,19},{4,20},{5,21},{6,22},{7,23},{8,24},{9,... | collective-permute-start | bytes 141320 | tf_op jit(solution)/shard_map/ppermute | solution.py:728
  69.4 4.5 %collective-permute-start.18 = (bf16[184,128]{1,0:T(8,128)(2,1)S(1)}, bf16[184,128]{1,0:T(8,128)(2,1)S(1)}, u32[]{:S(2)}, u32[]{:S(2)}) collective-permute-start(bf16[184,128]{1,0:T(8,128)(2,1)S(1)} %add.17.refs_0_), channel_id=1, source_target_pairs={{0,192},{32,224},{64,128},{96,160},{128,64},{160,96},{192,0},{224,... | collective-permute-start | bytes 141320 | tf_op jit(solution)/shard_map/ppermute | solution.py:728
  70.9 4.4 %collective-permute-start.17 = (bf16[184,128]{1,0:T(8,128)(2,1)S(1)}, bf16[184,128]{1,0:T(8,128)(2,1)S(1)}, u32[]{:S(2)}, u32[]{:S(2)}) collective-permute-start(bf16[184,128]{1,0:T(8,128)(2,1)S(1)} %add.17.refs_0_), channel_id=1, source_target_pairs={{0,128},{32,160},{64,192},{96,224},{128,0},{160,32},{192,64},{224,... | collective-permute-start | bytes 141320 | tf_op jit(solution)/shard_map/ppermute | solution.py:728
  70.9 4.4 %collective-permute-start.16 = (bf16[184,128]{1,0:T(8,128)(2,1)S(1)}, bf16[184,128]{1,0:T(8,128)(2,1)S(1)}, u32[]{:S(2)}, u32[]{:S(2)}) collective-permute-start(bf16[184,128]{1,0:T(8,128)(2,1)S(1)} %add.17.refs_0_), channel_id=1, source_target_pairs={{0,64},{32,96},{64,0},{96,32},{128,192},{160,224},{192,128},{224,1... | collective-permute-start | bytes 141320 | tf_op jit(solution)/shard_map/ppermute | solution.py:728
  75.9 6.8 %collective-permute-start.19 = (bf16[4,184,128]{2,1,0:T(8,128)(2,1)S(1)}, bf16[4,184,128]{2,1,0:T(8,128)(2,1)S(1)}, u32[]{:S(2)}, u32[]{:S(2)}) collective-permute-start(bf16[4,184,128]{2,1,0:T(8,128)(2,1)S(1)} %collect.1.mine_ref), channel_id=1, source_target_pairs={{0,32},{32,0},{64,96},{96,64},{128,160},{160,128},{192,224},{224,1... | collective-permute-start | bytes 565256 | tf_op jit(solution)/shard_map/ppermute | solution.py:728

commit v4 on v3

--- a/solution.py
+++ b/solution.py
@@ -1,5 +1,3 @@
-import functools
-
 import jax
 import jax.numpy as jnp
 from jax import lax
@@ -14,8 +12,8 @@
 BF16 = jnp.bfloat16
 CONV_ROWS = 960
 DOWN_ROWS = 512
-GROUPS = 8
-SHARE = (CONV_ROWS + DOWN_ROWS) // GROUPS
+SHARE = 96
+PIECE = 8
 
 VMEM_SPEC = pl.BlockSpec(memory_space=pltpu.VMEM)
 SMEM_SPEC = pl.BlockSpec(memory_space=pltpu.SMEM)
@@ -44,75 +42,75 @@
     return pltpu.roll(x, 64, x.ndim - 1)
 
 
-def place_faces(info_ref, i, planes, pair_ref, other_ref, first=0):
-    even = info_ref[0] % 2 == 0
+def place_faces(rank_ref, i, planes, pair_ref, other_ref, first=0):
+    even = rank_ref[0] % 2 == 0
     low, high = planes[0], planes[SIDE - 1]
     pair_ref[pl.ds(pl.multiple_of(first + i * SIDE, SIDE), SIDE)] = jnp.where(even, high, low)
     other_ref[pl.ds(pl.multiple_of(i * SIDE, SIDE), SIDE)] = jnp.where(even, low, high)
 
 
-def faces_kernel(info_ref, x_ref, v_ref, pair_ref, other_ref, token_ref):
+def faces_kernel(rank_ref, child_ref, near_ref, x_ref, v_ref, pair_ref, other_ref, token_ref):
     def plane(i):
         columns = pl.ds(pl.multiple_of(i * 256, 256), 256)
         voxels = x_ref[:, columns].astype(F32).T.astype(BF16).reshape(SIDE, SIDE, LANES)
         v_ref[i] = voxels
-        place_faces(info_ref, i, voxels, pair_ref, other_ref)
+        place_faces(rank_ref, i, voxels, pair_ref, other_ref)
 
     loop(SIDE, plane, 4)
     token_ref[...] = jnp.zeros_like(token_ref)
 
 
-def faces_call(info, x):
+def faces_call(rank, children, near, x):
     face = jax.ShapeDtypeStruct((256, LANES), BF16)
     return pl.pallas_call(
         faces_kernel,
         out_shape=(jax.ShapeDtypeStruct((SIDE, SIDE, SIDE, LANES), BF16), face, face, TOKEN),
-        in_specs=[SMEM_SPEC, VMEM_SPEC],
+        in_specs=[SMEM_SPEC] * 3 + [VMEM_SPEC],
         out_specs=(VMEM_SPEC,) * 4,
         compiler_params=params(16),
         cost_estimate=pl.CostEstimate(flops=0, bytes_accessed=4_000_000, transcendentals=0),
         name="faces",
-    )(info, x)
-
-
-def find_octant(info_ref, wanted):
+    )(rank, children, near, x)
+
+
+def find_octant(child_ref, wanted):
     place = jnp.int32(0)
     found = jnp.int32(0)
     for o in range(8):
-        hit = (info_ref[2 + o] == wanted).astype(jnp.int32)
+        hit = (child_ref[0, o] == wanted).astype(jnp.int32)
         place = place + hit * o
         found = found + hit
     return place, found
 
 
-def cot_kernel(after_ref, info_ref, cot_ref, own_ref, send_ref, turned_ref):
+def cot_kernel(after_ref, child_ref, rank_ref, cot_ref, own_ref, send_ref, turned_ref):
     def plane(i):
         columns = pl.ds(pl.multiple_of(i * 256, 256), 256)
         turned = cot_ref[:, columns].astype(F32).T
         turned_ref[i // HALF, i % HALF] = turned.reshape(2, HALF, 2, HALF, LANES)
 
     loop(SIDE, plane, 4)
-    rank = info_ref[0]
+    rank = rank_ref[0]
     for out_ref, holder in ((own_ref, rank), (send_ref, rank ^ 1)):
         for slot in range(2):
-            place, found = find_octant(info_ref, holder * 2 + slot)
+            place, found = find_octant(child_ref, holder * 2 + slot)
             block = turned_ref[place // 4, :, place // 2 % 2, :, place % 2]
             block = jnp.where(found > 0, block, jnp.zeros_like(block))
             out_ref[slot * 512 : (slot + 1) * 512] = block.reshape(512, LANES).astype(BF16)
 
 
-def cot_call(after, info, cot):
+def cot_call(after, children, rank, cot):
     blocks = jax.ShapeDtypeStruct((1024, LANES), BF16)
     return pl.pallas_call(
         cot_kernel,
         out_shape=(blocks, blocks),
-        in_specs=[ANY_SPEC, SMEM_SPEC, VMEM_SPEC],
+        in_specs=[ANY_SPEC, SMEM_SPEC, SMEM_SPEC, VMEM_SPEC],
         out_specs=(VMEM_SPEC,) * 2,
         scratch_shapes=[pltpu.VMEM((2, HALF, 2, HALF, 2, HALF, LANES), F32)],
         compiler_params=params(20),
         cost_estimate=pl.CostEstimate(flops=0, bytes_accessed=8_000_000, transcendentals=0),
         name="cot",
-    )(after, info, cot)
+    )(after, children, rank, cot)
 
 
 def weights_kernel(
@@ -165,40 +163,35 @@
     )(conv_weight, down_weight)
 
 
-def coarse_half_kernel(half, *refs):
-    _, info_ref, mine_ref, theirs_ref = refs[:4]
-    out_ref, token_ref, whole_ref = refs[-3:]
-    token_ref[...] = jnp.zeros_like(token_ref)
-    for o in range(4):
-        entry = info_ref[2 + half * 4 + o]
+def coarse_kernel(after_ref, child_ref, rank_ref, mine_ref, theirs_ref, out_ref, whole_ref):
+    for o in range(8):
+        entry = child_ref[0, o]
         slot = jnp.maximum(entry, 0) % 2
-        here = jnp.maximum(entry, 0) // 2 == info_ref[0]
+        here = jnp.maximum(entry, 0) // 2 == rank_ref[0]
         rows = pl.ds(pl.multiple_of(slot * 512, 512), 512)
         block = jnp.where(here, mine_ref[rows], theirs_ref[rows])
         block = jnp.where(entry >= 0, block, jnp.zeros_like(block)).astype(F32)
-        whole_ref[:, o // 2, :, o % 2] = block.reshape(HALF, HALF, HALF, LANES)
-
-    for i in range(HALF):
-        turned = whole_ref[i].reshape(256, LANES).T
-        out_ref[:, i * 256 : (i + 1) * 256] = turned.astype(BF16)
-
-
-def coarse_half_call(after, info, mine, theirs, half, begun=()):
-    return pl.pallas_call(
-        functools.partial(coarse_half_kernel, half),
-        grid=(1,),
-        out_shape=(jax.ShapeDtypeStruct((LANES, SIDE**3), BF16), TOKEN),
-        in_specs=[ANY_SPEC, SMEM_SPEC, VMEM_SPEC, VMEM_SPEC] + [ANY_SPEC] * len(begun),
-        out_specs=(
-            pl.BlockSpec((LANES, SIDE**3 // 2), lambda g: (0, half)),
-            pl.BlockSpec((8, LANES), lambda g: (0, 0)),
-        ),
-        input_output_aliases={4: 0} if begun else {},
-        scratch_shapes=[pltpu.VMEM((HALF, 2, HALF, 2, HALF, LANES), F32)],
-        compiler_params=params(16),
+        whole_ref[o // 4, :, o // 2 % 2, :, o % 2] = block.reshape(HALF, HALF, HALF, LANES)
+
+    def plane(i):
+        columns = pl.ds(pl.multiple_of(i * 256, 256), 256)
+        turned = whole_ref[i // HALF, i % HALF].reshape(256, LANES).T
+        out_ref[:, columns] = turned.astype(BF16)
+
+    loop(SIDE, plane, 4)
+
+
+def coarse_call(after, children, rank, mine, theirs):
+    return pl.pallas_call(
+        coarse_kernel,
+        out_shape=jax.ShapeDtypeStruct((LANES, SIDE**3), BF16),
+        in_specs=[ANY_SPEC, SMEM_SPEC, SMEM_SPEC, VMEM_SPEC, VMEM_SPEC],
+        out_specs=VMEM_SPEC,
+        scratch_shapes=[pltpu.VMEM((2, HALF, 2, HALF, 2, HALF, LANES), F32)],
+        compiler_params=params(20),
         cost_estimate=pl.CostEstimate(flops=0, bytes_accessed=4_000_000, transcendentals=0),
-        name="coarse_half",
-    )(after, info, mine, theirs, *begun)
+        name="coarse",
+    )(after, children, rank, mine, theirs)
 
 
 def spans(step):
@@ -209,12 +202,12 @@
     return slice(0, 1), slice(SIDE - 1, SIDE)
 
 
-def assemble(info_ref, v_ref, pair_ref, other_ref, face_ref, core_ref, ends_ref):
+def assemble(near_ref, rank_ref, v_ref, pair_ref, other_ref, face_ref, core_ref, ends_ref):
     def fill(i):
         core_ref[i + 1, SIDE : 17 * SIDE] = v_ref[i].astype(F32).reshape(256, LANES)
 
     loop(SIDE, fill, 4)
-    even = info_ref[0] % 2 == 0
+    even = rank_ref[0] % 2 == 0
     pair = pair_ref[pair_ref.shape[0] - 256 :].astype(F32).reshape(SIDE, SIDE, LANES)
     other = other_ref[...].astype(F32).reshape(SIDE, SIDE, LANES)
     face_ref[0] = jnp.where(even, other, pair)
@@ -227,7 +220,7 @@
             for step_z in (-1, 0, 1):
                 if step_x == 0 and step_y == 0 and step_z == 0:
                     continue
-                entries = info_ref[10 + column], info_ref[36 + column]
+                entries = near_ref[0, column], near_ref[1, column]
                 column += 1
                 straight = [
                     jnp.logical_and(e >= 0, jnp.maximum(e, 0) % 2 == n).astype(F32)
@@ -345,7 +338,8 @@
 
 
 def forward_kernel(
-    info_ref,
+    near_ref,
+    rank_ref,
     v_ref,
     pair_ref,
     other_ref,
@@ -364,7 +358,7 @@
     fine_ref,
 ):
     tap_refs = (zero_ref, one_ref, both_ref)
-    assemble(info_ref, v_ref, pair_ref, other_ref, face_ref, core_ref, ends_ref)
+    assemble(near_ref, rank_ref, v_ref, pair_ref, other_ref, face_ref, core_ref, ends_ref)
     gather_taps(core_ref, ends_ref, tap_refs)
     convolve(tap_refs, w_ref, acc_ref)
 
@@ -384,7 +378,7 @@
 
 
 def back_kernel(
-    info_ref,
+    rank_ref,
     own_ref,
     came_ref,
     down_t_ref,
@@ -420,14 +414,14 @@
         turned_ref[i + 2] = grad.T.astype(BF16)
         rounded = grad.astype(BF16).reshape(SIDE, SIDE, LANES)
         g_ref[i] = rounded
-        place_faces(info_ref, i, rounded, pair_ref, other_ref, 1024)
+        place_faces(rank_ref, i, rounded, pair_ref, other_ref, 1024)
 
     loop(SIDE, back, 4)
 
 
-def weigh_kernel(info_ref, zero_ref, one_ref, both_ref, act_ref, turned_ref, spun_ref, *refs):
-    kept_ref, sent_ref, token_ref, sums_ref, total_ref = refs
-    token_ref[...] = jnp.zeros_like(token_ref)
+def weigh_kernel(
+    zero_ref, one_ref, both_ref, act_ref, turned_ref, spun_ref, sums_ref, total_ref
+):
     lower = low_half((LANES, LANES))
     whole = [jnp.dot(spun_ref[n], act_ref[...], preferred_element_type=F32) for n in range(2)]
     folded = []
@@ -437,7 +431,7 @@
         folded.append(both + swap_halves(both))
     for t in range(4):
         rows = slice(CONV_ROWS + t * LANES, CONV_ROWS + (t + 1) * LANES)
-        sums_ref[rows] = jnp.where(lower, folded[t], folded[t + 4])
+        sums_ref[rows] = jnp.where(lower, folded[t], folded[t + 4]).astype(BF16)
 
     total_ref[...] = jnp.zeros_like(total_ref)
 
@@ -473,20 +467,17 @@
     last = []
     for b in range(3):
         lanes = slice(b * LANES, (b + 1) * LANES)
-        sums_ref[b * 192 : (b + 1) * 192] = total_ref[0, :, lanes] + total_ref[1, :, lanes]
+        sums_ref[b * 192 : (b + 1) * 192] = (total_ref[0, :, lanes] + total_ref[1, :, lanes]).astype(
+            BF16
+        )
         lanes = slice((3 + b) * LANES, (4 + b) * LANES)
         both = jnp.where(lower, total_ref[0, :, lanes], total_ref[1, :, lanes])
         last.append(both + swap_halves(both))
-    sums_ref[576:768] = jnp.where(lower, last[0], last[1])
-    sums_ref[768:960] = jnp.where(lower, last[2], 0.0)
-    core = info_ref[1] % 2
-    for y in range(GROUPS // 2):
-        kept_ref[y] = sums_ref[share_rows(2 * y + core)]
-        sent_ref[y] = sums_ref[share_rows(2 * y + 1 - core)].astype(BF16)
-
-
-def share_rows(group):
-    return pl.ds(pl.multiple_of(group * SHARE, 8), SHARE)
+    sums_ref[576:768] = jnp.where(lower, last[0], last[1]).astype(BF16)
+    sums_ref[768:960] = jnp.where(lower, last[2], 0.0).astype(BF16)
+    sums_ref[CONV_ROWS + DOWN_ROWS :] = jnp.zeros(
+        (sums_ref.shape[0] - CONV_ROWS - DOWN_ROWS, LANES), BF16
+    )
 
 
 TAPPED = (SIDE + 2, SIDE + 2, SIDE, LANES)
@@ -499,7 +490,7 @@
 FINE_SCRATCH = pltpu.VMEM((HALF, 2, HALF, 2, SIDE, LANES), F32)
 
 
-def forward_call(info, v, pair, other, weights, down):
+def forward_call(near, rank, v, pair, other, weights, down):
     return pl.pallas_call(
         forward_kernel,
         out_shape=(
@@ -508,7 +499,7 @@
             jax.ShapeDtypeStruct((512, 8 * LANES), BF16),
         )
         + (jax.ShapeDtypeStruct(TAPPED, BF16),) * 3,
-        in_specs=[SMEM_SPEC] + [VMEM_SPEC] * 5,
+        in_specs=[SMEM_SPEC] * 2 + [VMEM_SPEC] * 5,
         out_specs=(VMEM_SPEC,) * 6,
         scratch_shapes=PAD_SCRATCH + [FINE_SCRATCH],
         compiler_params=params(28),
@@ -516,10 +507,10 @@
             flops=4_000_000_000, bytes_accessed=16_000_000, transcendentals=600_000
         ),
         name="forward",
-    )(info, v, pair, other, weights, down)
-
-
-def back_call(info, own, came, down_t, slope, octants):
+    )(near, rank, v, pair, other, weights, down)
+
+
+def back_call(rank, own, came, down_t, slope, octants):
     return pl.pallas_call(
         back_kernel,
         out_shape=(
@@ -537,195 +528,187 @@
             flops=300_000_000, bytes_accessed=8_000_000, transcendentals=0
         ),
         name="back",
-    )(info, own, came, down_t, slope, octants)
-
-
-def weigh_call(info, zero, one, both, act, turned, spun):
+    )(rank, own, came, down_t, slope, octants)
+
+
+def weigh_call(zero, one, both, act, turned, spun, rows):
     return pl.pallas_call(
         weigh_kernel,
-        out_shape=(
-            jax.ShapeDtypeStruct((GROUPS // 2, SHARE, LANES), F32),
-            jax.ShapeDtypeStruct((GROUPS // 2, SHARE, LANES), BF16),
-            TOKEN,
-        ),
-        in_specs=[SMEM_SPEC] + [VMEM_SPEC] * 6,
-        out_specs=(VMEM_SPEC,) * 3,
-        scratch_shapes=[
-            pltpu.VMEM((CONV_ROWS + DOWN_ROWS, LANES), F32),
-            pltpu.VMEM((2, 192, 768), F32),
-        ],
+        out_shape=jax.ShapeDtypeStruct((rows, LANES), BF16),
+        in_specs=[VMEM_SPEC] * 6,
+        out_specs=VMEM_SPEC,
+        scratch_shapes=[pltpu.VMEM((2, 192, 768), F32)],
         compiler_params=params(20),
         cost_estimate=pl.CostEstimate(
             flops=4_000_000_000, bytes_accessed=10_000_000, transcendentals=0
         ),
         name="weigh",
-    )(info, zero, one, both, act, turned, spun)
-
-
-def input_taps_kernel(
+    )(zero, one, both, act, turned, spun)
+
+
+def input_kernel(
     after_ref,
-    info_ref,
+    near_ref,
+    rank_ref,
     g_ref,
     pair_ref,
     other_ref,
-    zero_ref,
-    one_ref,
-    both_ref,
+    w_ref,
+    out_ref,
     token_ref,
     face_ref,
     core_ref,
     ends_ref,
+    acc_ref,
+    *tap_refs,
 ):
-    assemble(info_ref, g_ref, pair_ref, other_ref, face_ref, core_ref, ends_ref)
-    gather_taps(core_ref, ends_ref, (zero_ref, one_ref, both_ref))
+    assemble(near_ref, rank_ref, g_ref, pair_ref, other_ref, face_ref, core_ref, ends_ref)
+    gather_taps(core_ref, ends_ref, tap_refs)
+    convolve(tap_refs, w_ref, acc_ref)
+
+    def plane(i):
+        columns = pl.ds(pl.multiple_of(i * 256, 256), 256)
+        out_ref[:, columns] = acc_ref[i + 2].T.astype(BF16)
+
+    loop(SIDE, plane, 4)
     token_ref[...] = jnp.zeros_like(token_ref)
 
 
-def input_taps_call(after, info, g, pair, other):
-    return pl.pallas_call(
-        input_taps_kernel,
-        out_shape=(jax.ShapeDtypeStruct(TAPPED, BF16),) * 3 + (TOKEN,),
-        in_specs=[ANY_SPEC, SMEM_SPEC] + [VMEM_SPEC] * 3,
-        out_specs=(VMEM_SPEC,) * 4,
-        scratch_shapes=PAD_SCRATCH[:3],
-        compiler_params=params(20),
+def input_call(after, near, rank, g, pair, other, weights):
+    return pl.pallas_call(
+        input_kernel,
+        out_shape=(jax.ShapeDtypeStruct((LANES, SIDE**3), BF16), TOKEN),
+        in_specs=[ANY_SPEC] + [SMEM_SPEC] * 2 + [VMEM_SPEC] * 4,
+        out_specs=(VMEM_SPEC,) * 2,
+        scratch_shapes=PAD_SCRATCH + [pltpu.VMEM(TAPPED, BF16)] * 3,
+        compiler_params=params(28),
         cost_estimate=pl.CostEstimate(
-            flops=2_000_000_000, bytes_accessed=8_000_000, transcendentals=0
+            flops=4_000_000_000, bytes_accessed=3_000_000, transcendentals=0
         ),
-        name="input_taps",
-    )(after, info, g, pair, other)
-
-
-def input_half_kernel(half, *refs):
-    _, zero_ref, one_ref, both_ref, w_ref = refs[:5]
-    out_ref, token_ref, acc_ref = refs[-3:]
-    convolve((zero_ref, one_ref, both_ref), w_ref, acc_ref, half * HALF, HALF + 2, 5)
-
-    for i in range(HALF):
-        out_ref[:, i * 256 : (i + 1) * 256] = acc_ref[i + 2].T.astype(BF16)
+        name="input_grad",
+    )(after, near, rank, g, pair, other, weights)
+
+
+def add_shares_kernel(after_ref, shares_ref, out_ref, token_ref):
+    total = shares_ref[0].astype(F32)
+    for peer in range(1, shares_ref.shape[0]):
+        total = total + shares_ref[peer].astype(F32)
+    out_ref[0:SHARE] = total
+    out_ref[SHARE:] = jnp.zeros((out_ref.shape[0] - SHARE, LANES), F32)
     token_ref[...] = jnp.zeros_like(token_ref)
 
 
-def input_half_call(after, taps, weights, half, begun=()):
-    return pl.pallas_call(
-        functools.partial(input_half_kernel, half),
-        grid=(1,),
-        out_shape=(jax.ShapeDtypeStruct((LANES, SIDE**3), BF16), TOKEN),
-        in_specs=[ANY_SPEC] + [VMEM_SPEC] * 4 + [ANY_SPEC] * len(begun),
-        out_specs=(
-            pl.BlockSpec((LANES, SIDE**3 // 2), lambda g: (0, half)),
-            pl.BlockSpec((8, LANES), lambda g: (0, 0)),
-        ),
-        input_output_aliases={5: 0} if begun else {},
-        scratch_shapes=[pltpu.VMEM((HALF + 4, 256, LANES), F32)],
-        compiler_params=params(16),
-        cost_estimate=pl.CostEstimate(
-            flops=2_500_000_000, bytes_accessed=6_000_000, transcendentals=0
-        ),
-        name="input_half",
-    )(after, *taps, weights, *begun)
-
-
-def deal_kernel(after_ref, info_ref, kept_ref, came_ref, own_ref, *refs):
-    share_refs, total_ref = refs[:-1], refs[-1]
-    total_ref[...] = kept_ref[...] + came_ref[...].astype(F32)
-    y = info_ref[1] // 2
-    own_ref[...] = total_ref[y]
-    for s, share_ref in enumerate(share_refs):
-        share_ref[...] = total_ref[y ^ (s + 1)].astype(BF16)
-
-
-def deal_call(after, info, kept, came):
-    return pl.pallas_call(
-        deal_kernel,
-        out_shape=(jax.ShapeDtypeStruct((SHARE, LANES), F32),)
-        + (jax.ShapeDtypeStruct((SHARE, LANES), BF16),) * 3,
-        in_specs=[ANY_SPEC, SMEM_SPEC, VMEM_SPEC, VMEM_SPEC],
-        out_specs=(VMEM_SPEC,) * 4,
-        scratch_shapes=[pltpu.VMEM((GROUPS // 2, SHARE, LANES), F32)],
+def add_shares_call(after, shares, rows):
+    return pl.pallas_call(
+        add_shares_kernel,
+        out_shape=(jax.ShapeDtypeStruct((rows, LANES), F32), TOKEN),
+        in_specs=[ANY_SPEC, VMEM_SPEC],
+        out_specs=(VMEM_SPEC,) * 2,
         compiler_params=params(16),
         cost_estimate=pl.CostEstimate(flops=0, bytes_accessed=500_000, transcendentals=0),
-        name="deal",
-    )(after, info, kept, came)
-
-
-def add_kernel(after_ref, *refs):
-    parts = [ref[...].astype(F32) for ref in refs[:-1]]
-    while len(parts) > 1:
-        parts = [first + second for first, second in zip(parts[::2], parts[1::2])]
-    refs[-1][...] = parts[0].astype(refs[-1].dtype)
-
-
-def add_call(after, parts, dtype=BF16):
-    return pl.pallas_call(
-        add_kernel,
-        out_shape=jax.ShapeDtypeStruct(parts[0].shape, dtype),
-        in_specs=[ANY_SPEC] + [VMEM_SPEC] * len(parts),
+        name="add_shares",
+    )(after, shares)
+
+
+def add_pieces_kernel(after_ref, pieces_ref, out_ref, token_ref):
+    total = jnp.sum(pieces_ref[...], axis=0).astype(BF16)
+    out_ref[...] = jnp.broadcast_to(total[None], out_ref.shape)
+    token_ref[...] = jnp.zeros_like(token_ref)
+
+
+def add_pieces_call(after, pieces):
+    return pl.pallas_call(
+        add_pieces_kernel,
+        out_shape=(jax.ShapeDtypeStruct(pieces.shape, BF16), TOKEN),
+        in_specs=[ANY_SPEC, VMEM_SPEC],
+        out_specs=(VMEM_SPEC,) * 2,
+        compiler_params=params(16),
+        cost_estimate=pl.CostEstimate(flops=0, bytes_accessed=500_000, transcendentals=0),
+        name="add_pieces",
+    )(after, pieces)
+
+
+def spread_kernel(after_ref, rows_ref, out_ref, token_ref):
+    kept = rows_ref[0:SHARE]
+    for peer in range(out_ref.shape[0]):
+        out_ref[peer] = kept
+    token_ref[...] = jnp.zeros_like(token_ref)
+
+
+def spread_call(after, rows, peers):
+    return pl.pallas_call(
+        spread_kernel,
+        out_shape=(jax.ShapeDtypeStruct((peers, SHARE, LANES), BF16), TOKEN),
+        in_specs=[ANY_SPEC, VMEM_SPEC],
+        out_specs=(VMEM_SPEC,) * 2,
+        compiler_params=params(16),
+        cost_estimate=pl.CostEstimate(flops=0, bytes_accessed=500_000, transcendentals=0),
+        name="spread",
+    )(after, rows)
+
+
+def pass_kernel(token_ref, out_ref):
+    out_ref[...] = token_ref[...]
+
+
+def pass_call(token):
+    return pl.pallas_call(
+        pass_kernel,
+        out_shape=TOKEN,
+        in_specs=[VMEM_SPEC],
         out_specs=VMEM_SPEC,
         compiler_params=params(16),
-        cost_estimate=pl.CostEstimate(flops=0, bytes_accessed=500_000, transcendentals=0),
-        name="add",
-    )(after, *parts)
-
-
-def collect_kernel(info_ref, *refs):
-    y = info_ref[1] // 2
-    for s, share_ref in enumerate(refs[:-1]):
-        refs[-1][y ^ s] = share_ref[...]
-
-
-def collect_call(info, shares):
-    return pl.pallas_call(
-        collect_kernel,
-        out_shape=jax.ShapeDtypeStruct((GROUPS // 2, SHARE, LANES), BF16),
-        in_specs=[SMEM_SPEC] + [VMEM_SPEC] * len(shares),
-        out_specs=VMEM_SPEC,
+        name="pass",
+    )(token)
+
+
+def stamp_kernel(sums_ref, pair_ref, other_ref, out_ref):
+    pass
+
+
+def stamp_call(sums, pair, other):
+    return pl.pallas_call(
+        stamp_kernel,
+        out_shape=jax.ShapeDtypeStruct(sums.shape, sums.dtype),
+        in_specs=[ANY_SPEC] * 3,
+        out_specs=ANY_SPEC,
+        input_output_aliases={0: 0},
         compiler_params=params(16),
-        cost_estimate=pl.CostEstimate(flops=0, bytes_accessed=500_000, transcendentals=0),
-        name="collect",
-    )(info, *shares)
-
-
-def split_kernel(after_ref, info_ref, mine_ref, theirs_ref, conv_ref, down_ref, sums_ref):
-    core = info_ref[1] % 2
-    for y in range(GROUPS // 2):
-        sums_ref[share_rows(2 * y + core)] = mine_ref[y].astype(F32)
-        sums_ref[share_rows(2 * y + 1 - core)] = theirs_ref[y].astype(F32)
+        name="stamp",
+    )(sums, pair, other)
+
+
+def split_kernel(sums_ref, conv_ref, down_ref):
     for a in range(3):
         for b in range(3):
             for c in range(3):
                 chunk, upper = (b, c) if c < 2 else ((3, b) if b < 2 else (4, 0))
                 base = chunk * 192 + a * 64
-                block = sums_ref[base : base + 64]
+                block = sums_ref[base : base + 64].astype(F32)
                 block = swap_halves(block) if upper else block
                 conv_ref[9 * a + 3 * b + c] = block[:, :64]
     for t in range(4):
-        block = sums_ref[CONV_ROWS + t * LANES : CONV_ROWS + (t + 1) * LANES].T
+        block = sums_ref[CONV_ROWS + t * LANES : CONV_ROWS + (t + 1) * LANES].astype(F32).T
         down_ref[t] = block[:64]
         down_ref[t + 4] = block[64:]
 
 
-def split_call(after, info, mine, theirs):
+def split_call(sums):
     return pl.pallas_call(
         split_kernel,
         out_shape=(
             jax.ShapeDtypeStruct((27, 64, 64), F32),
             jax.ShapeDtypeStruct((8, 64, LANES), F32),
         ),
-        in_specs=[ANY_SPEC, SMEM_SPEC] + [VMEM_SPEC] * 2,
+        in_specs=[VMEM_SPEC],
         out_specs=(VMEM_SPEC,) * 2,
-        scratch_shapes=[pltpu.VMEM((CONV_ROWS + DOWN_ROWS, LANES), F32)],
         compiler_params=params(16),
         name="split",
-    )(after, info, mine, theirs)
-
-
-def swaps(axis, step=1):
-    return [(i, i ^ step) for i in range(lax.axis_size(axis))]
-
-
-def swapped(array, axis, steps):
-    return [lax.ppermute(array, axis, swaps(axis, step)) for step in steps]
+    )(sums)
+
+
+def swaps(axis):
+    return [(i, i ^ 1) for i in range(lax.axis_size(axis))]
 
 
 def exchange(pair, other, axis):
@@ -738,40 +721,36 @@
 
 
 def body(fine_input, conv_weight, down_weight, coarse_cot, neighbours, children):
-    rank = lax.axis_index("grp") * lax.axis_size("dev") + lax.axis_index("dev")
-    info = [rank.reshape(1), lax.axis_index("grp").reshape(1), children.reshape(8)]
-    info = jnp.concatenate([part.astype(jnp.int32) for part in info + [neighbours.reshape(52)]])
-
-    voxels, pair, other, token = faces_call(info, fine_input.reshape(LANES, SIDE**3))
-    own, send = cot_call(token, info, coarse_cot.reshape(LANES, SIDE**3))
-    pair, other = exchange(pair, other, "dev")
-    came = lax.ppermute(send, "dev", swaps("dev"))
+    dev = ("z", "x")
+    rank = lax.axis_index(("y", "core", "z", "x")).reshape(1).astype(jnp.int32)
+
+    voxels, pair, other, token = faces_call(
+        rank, children, neighbours, fine_input.reshape(LANES, SIDE**3)
+    )
+    own, send = cot_call(token, children, rank, coarse_cot.reshape(LANES, SIDE**3))
+    pair, other = exchange(pair, other, dev)
+    came = lax.ppermute(send, dev, swaps(dev))
     forward, backward, down, down_t = weights_call(conv_weight, down_weight.transpose(0, 2, 1))
     octants, slope, act, zero, one, both = forward_call(
-        info, voxels, pair, other, forward, down
+        neighbours, rank, voxels, pair, other, forward, down
     )
-    mine, other_out, grads, turned, spun = back_call(info, own, came, down_t, slope, octants)
-    theirs, grad_other = exchange(mine, other_out, "dev")
-    kept, sent, token = weigh_call(info, zero, one, both, act, turned, spun)
-
-    (came,) = swapped(sent, "grp", (1,))
-    coarse, token = coarse_half_call(token, info, mine, theirs, 0)
-    own, *shares = deal_call(token, info, kept, came)
-    came = [lax.ppermute(share, "grp", swaps("grp", 2 * s + 2)) for s, share in enumerate(shares)]
-    *input_taps, token = input_taps_call(own, info, grads, theirs, grad_other)
-    part = add_call(token, [own, *came], F32)
-    came = swapped(part, "dev", (1, 2, 3))
-    input_grad, token = input_half_call(part, input_taps, backward, 0)
-    part = add_call(token, [part, *came])
-    came = swapped(part, "dev", (4, 8, 12))
-    input_grad, token = input_half_call(part, input_taps, backward, 1, (input_grad,))
-    part = add_call(token, [part, *came])
-    came = swapped(part, "dev", (16,))
-    coarse, token = coarse_half_call(part, info, mine, theirs, 1, (coarse,))
-    part = add_call(token, [part, *came])
-    shares = collect_call(info, [part, *swapped(part, "grp", (2, 4, 6))])
-    (came,) = swapped(shares, "grp", (1,))
-    conv_grad, down_grad = split_call(token, info, shares, came)
+    mine, other_out, grads, turned, spun = back_call(rank, own, came, down_t, slope, octants)
+    theirs, grad_other = exchange(mine, other_out, dev)
+
+    outer, inner = ("y", "x"), ("core", "z")
+    shares, pieces = lax.axis_size(outer), lax.axis_size(inner)
+    sums = weigh_call(zero, one, both, act, turned, spun, shares * SHARE)
+    sums = stamp_call(sums, theirs, grad_other)
+    came = lax.all_to_all(sums.reshape(shares, SHARE, LANES), outer, 0, 0)
+    input_grad, token = input_call(sums, neighbours, rank, grads, theirs, grad_other, backward)
+    part, token = add_shares_call(token, came, pieces * PIECE)
+    came = lax.all_to_all(part.reshape(pieces, PIECE, LANES), inner, 0, 0)
+    part, token = add_pieces_call(pass_call(token), came)
+    came = lax.all_to_all(part, inner, 0, 0).reshape(pieces * PIECE, LANES)
+    spread, token = spread_call(pass_call(token), came, shares)
+    gathered = lax.all_to_all(spread, outer, 0, 0).reshape(shares * SHARE, LANES)
+    coarse = coarse_call(token, children, rank, mine, theirs)
+    conv_grad, down_grad = split_call(gathered)
     return (
         coarse.reshape(1, LANES, SIDE**3),
         input_grad.reshape(2, 64, SIDE**3),
@@ -781,13 +760,11 @@
 
 
 def solution(mesh):
-    in_specs = (
-        P(("grp", "dev"), None, None),
-        P(),
-        P(),
-        P(("grp", "dev"), None, None),
-        P(("grp", "dev"), None),
-        P(("grp", "dev"), None),
+    grp, dev = mesh.devices.shape
+    mesh = jax.sharding.Mesh(
+        mesh.devices.reshape(grp // 2, 2, dev // 4, 4), ("y", "core", "z", "x")
     )
-    out_specs = (P(("grp", "dev"), None, None), P(("grp", "dev"), None, None), P(), P())
+    bricks = ("y", "core", "z", "x")
+    in_specs = (P(bricks, None, None), P(), P(), P(bricks, None, None), P(bricks, None), P(bricks, None))
+    out_specs = (P(bricks, None, None), P(bricks, None, None), P(), P())
     return jax.shard_map(body, mesh=mesh, in_specs=in_specs, out_specs=out_specs, check_vma=False)

time: 84.7 us -> 95.1 us (1.12)
  waiting for transfers between devices: 9.16 us -> 22.3 us
  Pallas kernels: 34.3 us -> 32.3 us
  starting transfers between devices: 37.5 us -> 35.9 us
  local copies, waits for them, and re-layouts: 2 us -> 3.31 us
    ppermute x16 -> x1, starting transfers between devices: 23.5 us -> 0.09 us  [body(): came = lax.ppermute(send, dev, swaps(dev))]
    all_to_all x0 -> x4, starting transfers between devices: none -> 22.8 us  [the longest x1 8.1 us: body(): came = lax.all_to_all(part.reshape(pieces, PIECE, LANES), inner, 0, 0)]
    all_to_all x0 -> x4, waiting for transfers between devices: none -> 20.8 us  [the longest x1 7.16 us: body(): came = lax.all_to_all(part.reshape(pieces, PIECE, LANES), inner, 0, 0)]
    ppermute x16 -> x1, waiting for transfers between devices: 9.15 us -> 0.01 us  [body(): came = lax.ppermute(send, dev, swaps(dev))]
    unnamed x8 -> x18, local copies, waits for them, and re-layouts: 1.24 us -> 3.31 us
    ppermute x2, starting transfers between devices: 3.65 us -> 2.13 us  [exchange(): lax.ppermute(pair, axis, swaps(axis))]
    ppermute x2, waiting for transfers between devices: 0.01 us -> 1.47 us  [exchange(): lax.ppermute(pair, axis, swaps(axis))]
    pallas_call x12 -> x9, Pallas kernels: 19.4 us -> 18.5 us  [the longest x1 8.64 us: input_call(): pl.pallas_call(input_kernel, out_shape=(jax.ShapeDtypeStruct((LANES, SIDE...]
  transfers between devices with their start and end apart: 20 -> 9, of which waited for: 5 -> 4; matrix products, arithmetic and copies ran while one was open for 0% -> 0% of each run, Pallas kernels for 34% -> 28%
where the time goes in v4:
time: 95.1 us; the launch traced here: 94.6 us
  starting transfers between devices  35.9 us (38%)
  Pallas kernels  32.3 us (34%)
  waiting for transfers between devices  22.3 us (23%)
  local copies, waits for them, and re-layouts  3.31 us (3%)
    ppermute x2, starting transfers between devices, exchange(): lax.ppermute(other, axis, across + [(j, i) for i, j in across])  10.9 us
    pallas_call x1, Pallas kernels, input_call(): pl.pallas_call(input_kernel, out_shape=(jax.ShapeDtypeStruct((LANES, SIDE...  8.64 us
    pallas_call x1, Pallas kernels, forward_call(): pl.pallas_call(forward_kernel, out_shape=(jax.ShapeDtypeStruct((1024, LAN...  8.4 us
    all_to_all x1, starting transfers between devices, body(): came = lax.all_to_all(part.reshape(pieces, PIECE, LANES), inner, 0, 0)  8.1 us
    all_to_all x1, waiting for transfers between devices, body(): came = lax.all_to_all(part.reshape(pieces, PIECE, LANES), inner, 0, 0)  7.16 us
    all_to_all x1, waiting for transfers between devices, body(): came = lax.all_to_all(part, inner, 0, 0).reshape(pieces * PIECE, LANES)  7 us
    all_to_all x1, waiting for transfers between devices, body(): lax.all_to_all(spread, outer, 0, 0).reshape(shares * SHARE, LANES)  6.68 us
    all_to_all x1, starting transfers between devices, body(): lax.all_to_all(spread, outer, 0, 0).reshape(shares * SHARE, LANES)  6.19 us
  transfers between devices with their start and end apart: 9, of which 4 were waited for; matrix products, arithmetic and copies ran while one was open for 0% of the time, Pallas kernels for 28%

profile of v4, /device:TPU:1, one launch (start us, length us, event | category | flops | bytes accessed | tf_op | source)
XLA Modules:
  0.0 94.6 jit_solution(6173052610998142973)
XLA Ops:
  0.7 1.3 %copy-done.1 = bf16[2,64,4096]{2,1,0:T(8,128)(2,1)S(1)} copy-done((bf16[2,64,4096]{2,1,0:T(8,128)(2,1)S(1)}, bf16[2,64,4096]{2,1,0:T(8,128)(2,1)}, u32[]{:S(2)}) %copy-start.1) | copy-done | bytes 1048600
  2.0 0.7 copy-done.4
  2.6 0.7 copy-done.7
  3.3 1.1 %faces.1 = (bf16[16,16,16,128]{3,2,1,0:T(8,128)(2,1)S(1)}, bf16[256,128]{1,0:T(8,128)(2,1)S(1)}, bf16[256,128]{1,0:T(8,128)(2,1)S(1)}, f32[8,128]{1,0:T(8,128)S(1)}) custom-call(s32[1]{0:T(128)} %bitcast.rank_ref, s32[1,8]{1,0:T(1,128)S(1)} %copy-done.4, s32[2,26]{1,0:T(2,128)S(1)} %copy-done.7, bf16[128,4096]{1,0:T(8,128)(2,1)S(1)} %bitcast.13), custom_call_target="tpu_custom_call" | custom-call | bytes 4000000 | tf_op jit(solution)/shard_map/faces/pallas_call | solution.py:65
  4.4 2.1 %collective-permute-start = (bf16[256,128]{1,0:T(8,128)(2,1)S(1)}, bf16[256,128]{1,0:T(8,128)(2,1)S(1)}, u32[]{:S(2)}, u32[]{:S(2)}) collective-permute-start(bf16[256,128]{1,0:T(8,128)(2,1)S(1)} %get-tuple-element.36), channel_id=1, source_target_pairs={{0,1},{1,0},{2,3},{3,2},{4,5},{5,4},{6,7},{7,6},{8,9},{9,8},{10,11... | collective-permute-start | bytes 196616 | tf_op jit(solution)/shard_map/ppermute | solution.py:718
  6.6 7.1 %collective-permute-start.1 = (bf16[256,128]{1,0:T(8,128)(2,1)S(1)}, bf16[256,128]{1,0:T(8,128)(2,1)S(1)}, u32[]{:S(2)}, u32[]{:S(2)}) collective-permute-start(bf16[256,128]{1,0:T(8,128)(2,1)S(1)} %get-tuple-element.37), channel_id=1, source_target_pairs={{1,2},{3,4},{5,6},{7,8},{9,10},{11,12},{13,14},{15,16},{17,18},{19... | collective-permute-start | bytes 196616 | tf_op jit(solution)/shard_map/ppermute | solution.py:719
  13.7 0.7 copy-done.5
  14.3 1.3 %cot.1 = (bf16[1024,128]{1,0:T(8,128)(2,1)S(1)}, bf16[1024,128]{1,0:T(8,128)(2,1)S(1)}) custom-call(f32[8,128]{1,0:T(8,128)S(1)} %get-tuple-element.44.after_ref, s32[1,8]{1,0:T(1,128)S(1)} %copy-done.5, s32[1]{0:T(128)} %bitcast.rank_ref, bf16[128,4096]{1,0:T(8,128)(2,1)S(1)} %bitcast.12), custom_call_target="tpu_custom_call" | custom-call | bytes 8000000 | tf_op jit(solution)/shard_map/cot/pallas_call | solution.py:104
  15.6 0.1 collective-permute-start.2
  15.7 0.6 weights.1
  16.4 0.0 collective-permute-done.pair_ref
  16.4 0.0 collective-permute-done.1.other_ref
  16.4 8.4 %forward.1 = (bf16[1024,128]{1,0:T(8,128)(2,1)S(1)}, f32[16,256,128]{2,1,0:T(8,128)S(1)}, bf16[512,1024]{1,0:T(8,128)(2,1)S(1)}, bf16[18,18,16,128]{3,2,1,0:T(8,...) custom-call(s32[2,26]{1,0:T(2,128)S(1)} %copy-done.8, s32[1]{0:T(128)} %bitcast.rank_ref, ...), custom_call_target="tpu_custom_call" | custom-call | flops 4000000000 | bytes 16000000 | tf_op jit(solution)/shard_map/forward/pallas_call | solution.py:494
  24.8 0.0 collective-permute-done.2.came_ref
  24.8 1.2 %back.1 = (bf16[1280,128]{1,0:T(8,128)(2,1)S(1)}, bf16[256,128]{1,0:T(8,128)(2,1)S(1)}, bf16[16,16,16,128]{3,2,1,0:T(8,128)(2,1)S(1)}, bf16[20,128,256]{2,1,0:T(8,128)(2,1)S(1)}, bf16[2,128,512]{2,1,0:T(8,128)(2,1)S(1)}) custom-call(s32[1]{0:T(128)} %bitcast.rank_ref, bf16[1024,128]{1,0:T(8,128)(2,1)S(1)} %get-tuple-element.45.own_ref, ...), custom_call_target="tpu_custom_call" | custom-call | flops 300000000 | bytes 8000000 | tf_op jit(solution)/shard_map/back/pallas_call | solution.py:514
  26.0 3.8 %collective-permute-start.4 = (bf16[256,128]{1,0:T(8,128)(2,1)S(1)}, bf16[256,128]{1,0:T(8,128)(2,1)S(1)}, u32[]{:S(2)}, u32[]{:S(2)}) collective-permute-start(bf16[256,128]{1,0:T(8,128)(2,1)S(1)} %get-tuple-element.53), channel_id=1, source_target_pairs={{1,2},{3,4},{5,6},{7,8},{9,10},{11,12},{13,14},{15,16},{17,18},{19... | collective-permute-start | bytes 196616 | tf_op jit(solution)/shard_map/ppermute | solution.py:719
  29.8 5.3 %weigh.1.sums_ref = bf16[1536,128]{1,0:T(8,128)(2,1)} custom-call(bf16[18,18,16,128]{3,2,1,0:T(8,128)(2,1)S(1)} %get-tuple-element.40.zero_ref, bf16[18,18,16,128]{3,2,1,0:T(8,128)(2,1)S(1)} %get-tuple-element.41.one_ref, bf16[18,18,16,128]{3,2,1,0:T(8,128)(2,1)S(1)} %get-tuple-element.42.both_ref, bf16[512,1024]{1,0:T(8,128)(2,1)S(1)} %get-tuple-element.43.act_ref, ...), custom_call_target="tpu_custom_call" | custom-call | flops 4000000000 | bytes 10000000 | tf_op jit(solution)/shard_map/weigh/pallas_call | solution.py:535
  35.1 1.5 %collective-permute-done.3.pair_ref.theirs_ref = bf16[1280,128]{1,0:T(8,128)(2,1)S(1)} collective-permute-done((bf16[1280,128]{1,0:T(8,128)(2,1)S(1)}, bf16[1280,128]{1,0:T(8,128)(2,1)S(1)}, u32[]{:S(2)}, u32[]{:S(2)}) %collective-permute-start.3) | collective-permute-done | bytes 327712 | tf_op jit(solution)/shard_map/ppermute | solution.py:718
  36.6 4.3 %all-to-all-start = ((bf16[16,96,128]{2,1,0:T(8,128)(2,1)}), bf16[16,96,128]{2,1,0:T(8,128)(2,1)S(1)}, u32[]{:S(2)}, u32[]{:S(2)}) async-start(bf16[16,96,128]{2,1,0:T(8,128)(2,1)} %bitcast.4), calls=%async_computation | async-start | bytes 786432 | tf_op jit(solution)/shard_map/all_to_all | solution.py:744
  40.9 8.6 %input_grad.1 = (bf16[128,4096]{1,0:T(8,128)(2,1)}, f32[8,128]{1,0:T(8,128)S(1)}) custom-call(bf16[1536,128]{1,0:T(8,128)(2,1)} %stamp.1.after_ref, s32[2,26]{1,0:T(2,128)S(1)} %copy-done.8, s32[1]{0:T(128)} %bitcast.rank_ref, bf16[16,16,16,128]{3,2,1,0:T(8,128)(2,1)S(1)} %get-tuple-element.54.g_ref, ...), custom_call_target="tpu_custom_call" | custom-call | flops 4000000000 | bytes 3000000 | tf_op jit(solution)/shard_map/input_grad/pallas_call | solution.py:578
  49.5 0.0 all-to-all-done.shares_ref
  49.5 0.7 add_shares.1
  50.2 8.1 %all-to-all-start.1 = ((f32[16,8,128]{2,1,0:T(8,128)}), f32[16,8,128]{2,1,0:T(8,128)S(1)}, u32[]{:S(2)}, u32[]{:S(2)}) async-start(f32[16,8,128]{2,1,0:T(8,128)} %bitcast.5), calls=%async_computation.1 | async-start | bytes 131072 | tf_op jit(solution)/shard_map/all_to_all | solution.py:747
  58.3 7.2 %all-to-all-done.1.pieces_ref = f32[16,8,128]{2,1,0:T(8,128)S(1)} async-done(((f32[16,8,128]{2,1,0:T(8,128)}), f32[16,8,128]{2,1,0:T(8,128)S(1)}, u32[]{:S(2)}, u32[]{:S(2)}) %all-to-all-start.1) | async-done | bytes 65568 | tf_op jit(solution)/shard_map/all_to_all | solution.py:747
  65.5 0.6 add_pieces.1
  66.1 4.2 %all-to-all-start.2 = ((bf16[16,8,128]{2,1,0:T(8,128)(2,1)}), bf16[16,8,128]{2,1,0:T(8,128)(2,1)S(1)}, u32[]{:S(2)}, u32[]{:S(2)}) async-start(bf16[16,8,128]{2,1,0:T(8,128)(2,1)} %get-tuple-element.60), calls=%async_computation.2 | async-start | bytes 65536 | tf_op jit(solution)/shard_map/all_to_all | solution.py:749
  70.4 7.0 %all-to-all-done.2 = bf16[16,8,128]{2,1,0:T(8,128)(2,1)S(1)} async-done(((bf16[16,8,128]{2,1,0:T(8,128)(2,1)}), bf16[16,8,128]{2,1,0:T(8,128)(2,1)S(1)}, u32[]{:S(2)}, u32[]{:S(2)}) %all-to-all-start.2) | async-done | bytes 32800 | tf_op jit(solution)/shard_map/all_to_all | solution.py:749
  77.4 0.8 spread.1
  78.2 6.2 %all-to-all-start.3 = ((bf16[16,96,128]{2,1,0:T(8,128)(2,1)}), bf16[16,96,128]{2,1,0:T(8,128)(2,1)S(1)}, u32[]{:S(2)}, u32[]{:S(2)}) async-start(bf16[16,96,128]{2,1,0:T(8,128)(2,1)} %get-tuple-element.63), calls=%async_computation.3 | async-start | bytes 786432 | tf_op jit(solution)/shard_map/all_to_all | solution.py:751
  84.4 2.4 %coarse.1 = bf16[128,4096]{1,0:T(8,128)(2,1)} custom-call(f32[8,128]{1,0:T(8,128)S(1)} %get-tuple-element.61.after_ref, s32[1,8]{1,0:T(1,128)S(1)} %copy-done.6, s32[1]{0:T(128)} %bitcast.rank_ref, bf16[1280,128]{1,0:T(8,128)(2,1)S(1)} %get-tuple-element.52.mine_ref, bf16[1280,128]{1,0:T(8,128)(2,1)S(1)} %collective-permute-done.3.pair_ref.theirs_ref), custom_call_target="tpu_custom_call" | custom-call | bytes 4000000 | tf_op jit(solution)/shard_map/coarse/pallas_call | solution.py:185
  86.8 6.7 %all-to-all-done.3 = bf16[16,96,128]{2,1,0:T(8,128)(2,1)S(1)} async-done(((bf16[16,96,128]{2,1,0:T(8,128)(2,1)}), bf16[16,96,128]{2,1,0:T(8,128)(2,1)S(1)}, u32[]{:S(2)}, u32[]{:S(2)}) %all-to-all-start.3) | async-done | bytes 393248 | tf_op jit(solution)/shard_map/all_to_all | solution.py:751
  93.5 1.1 %split.1 = (f32[27,64,64]{2,1,0:T(8,128)}, f32[8,64,128]{2,1,0:T(8,128)}) custom-call(bf16[1536,128]{1,0:T(8,128)(2,1)S(1)} %bitcast.11), custom_call_target="tpu_custom_call" | custom-call | tf_op jit(solution)/shard_map/split/pallas_call | solution.py:697
  (19 shorter events, 0.0 us)
Async XLA Ops:
  0.6 13.0 %copy-start = (bf16[1,128,4096]{2,1,0:T(8,128)(2,1)S(1)}, bf16[1,128,4096]{2,1,0:T(8,128)(2,1)}, u32[]{:S(2)}) copy-start(bf16[1,128,4096]{2,1,0:T(8,128)(2,1)} %param.9) | copy-start | bytes 3145732
  0.7 1.3 %copy-start.1 = (bf16[2,64,4096]{2,1,0:T(8,128)(2,1)S(1)}, bf16[2,64,4096]{2,1,0:T(8,128)(2,1)}, u32[]{:S(2)}) copy-start(bf16[2,64,4096]{2,1,0:T(8,128)(2,1)} %param.6) | copy-start | bytes 3145732
  2.0 0.7 copy-start.4
  2.6 0.7 copy-start.7
  3.3 12.4 %copy-start.2 = (bf16[27,64,64]{2,1,0:T(8,128)(2,1)S(1)}, bf16[27,64,64]{2,1,0:T(8,128)(2,1)}, u32[]{:S(2)}) copy-start(bf16[27,64,64]{2,1,0:T(8,128)(2,1)} %conv_ref.1) | copy-start | bytes 663556
  3.3 12.4 %copy-start.3 = (bf16[8,128,64]{1,2,0:T(8,128)(2,1)S(1)}, bf16[8,128,64]{1,2,0:T(8,128)(2,1)}, u32[]{:S(2)}) copy-start(bf16[8,128,64]{1,2,0:T(8,128)(2,1)} %param.8) | copy-start | bytes 393220
  4.4 12.0 %collective-permute-start = (bf16[256,128]{1,0:T(8,128)(2,1)S(1)}, bf16[256,128]{1,0:T(8,128)(2,1)S(1)}, u32[]{:S(2)}, u32[]{:S(2)}) collective-permute-start(bf16[256,128]{1,0:T(8,128)(2,1)S(1)} %get-tuple-element.36), channel_id=1, source_target_pairs={{0,1},{1,0},{2,3},{3,2},{4,5},{5,4},{6,7},{7,6},{8,9},{9,8},{10,11... | collective-permute-start | bytes 196616 | tf_op jit(solution)/shard_map/ppermute | solution.py:718
  6.6 9.8 %collective-permute-start.1 = (bf16[256,128]{1,0:T(8,128)(2,1)S(1)}, bf16[256,128]{1,0:T(8,128)(2,1)S(1)}, u32[]{:S(2)}, u32[]{:S(2)}) collective-permute-start(bf16[256,128]{1,0:T(8,128)(2,1)S(1)} %get-tuple-element.37), channel_id=1, source_target_pairs={{1,2},{3,4},{5,6},{7,8},{9,10},{11,12},{13,14},{15,16},{17,18},{19... | collective-permute-start | bytes 196616 | tf_op jit(solution)/shard_map/ppermute | solution.py:719
  13.7 0.7 copy-start.5
  14.3 2.1 %copy-start.8 = (s32[2,26]{1,0:T(2,128)S(1)}, s32[2,26]{1,0:T(2,128)}, u32[]{:S(2)}) copy-start(s32[2,26]{1,0:T(2,128)} %near_ref.5) | copy-start | bytes 628
  15.6 9.2 %collective-permute-start.2 = (bf16[1024,128]{1,0:T(8,128)(2,1)S(1)}, bf16[1024,128]{1,0:T(8,128)(2,1)S(1)}, u32[]{:S(2)}, u32[]{:S(2)}) collective-permute-start(bf16[1024,128]{1,0:T(8,128)(2,1)S(1)} %get-tuple-element.46), channel_id=1, source_target_pairs={{0,1},{1,0},{2,3},{3,2},{4,5},{5,4},{6,7},{7,6},{8,9},{9,8},{10,11... | collective-permute-start | bytes 786440 | tf_op jit(solution)/shard_map/ppermute | solution.py:732
  26.0 9.1 %collective-permute-start.4 = (bf16[256,128]{1,0:T(8,128)(2,1)S(1)}, bf16[256,128]{1,0:T(8,128)(2,1)S(1)}, u32[]{:S(2)}, u32[]{:S(2)}) collective-permute-start(bf16[256,128]{1,0:T(8,128)(2,1)S(1)} %get-tuple-element.53), channel_id=1, source_target_pairs={{1,2},{3,4},{5,6},{7,8},{9,10},{11,12},{13,14},{15,16},{17,18},{19... | collective-permute-start | bytes 196616 | tf_op jit(solution)/shard_map/ppermute | solution.py:719
  29.8 6.8 %collective-permute-start.3 = (bf16[1280,128]{1,0:T(8,128)(2,1)S(1)}, bf16[1280,128]{1,0:T(8,128)(2,1)S(1)}, u32[]{:S(2)}, u32[]{:S(2)}) collective-permute-start(bf16[1280,128]{1,0:T(8,128)(2,1)S(1)} %get-tuple-element.52.mine_ref), channel_id=1, source_target_pairs={{0,1},{1,0},{2,3},{3,2},{4,5},{5,4},{6,7},{7,6},{8,9},{9,8},{10,11... | collective-permute-start | bytes 983048 | tf_op jit(solution)/shard_map/ppermute | solution.py:718
  36.6 13.0 %all-to-all-start = ((bf16[16,96,128]{2,1,0:T(8,128)(2,1)}), bf16[16,96,128]{2,1,0:T(8,128)(2,1)S(1)}, u32[]{:S(2)}, u32[]{:S(2)}) async-start(bf16[16,96,128]{2,1,0:T(8,128)(2,1)} %bitcast.4), calls=%async_computation | async-start | bytes 786432 | tf_op jit(solution)/shard_map/all_to_all | solution.py:744
  49.5 34.8 %copy-start.6 = (s32[1,8]{1,0:T(1,128)S(1)}, s32[1,8]{1,0:T(1,128)}, u32[]{:S(2)}) copy-start(s32[1,8]{1,0:T(1,128)} %child_ref.5) | copy-start | bytes 100
  50.2 15.3 %all-to-all-start.1 = ((f32[16,8,128]{2,1,0:T(8,128)}), f32[16,8,128]{2,1,0:T(8,128)S(1)}, u32[]{:S(2)}, u32[]{:S(2)}) async-start(f32[16,8,128]{2,1,0:T(8,128)} %bitcast.5), calls=%async_computation.1 | async-start | bytes 131072 | tf_op jit(solution)/shard_map/all_to_all | solution.py:747
  66.1 11.2 %all-to-all-start.2 = ((bf16[16,8,128]{2,1,0:T(8,128)(2,1)}), bf16[16,8,128]{2,1,0:T(8,128)(2,1)S(1)}, u32[]{:S(2)}, u32[]{:S(2)}) async-start(bf16[16,8,128]{2,1,0:T(8,128)(2,1)} %get-tuple-element.60), calls=%async_computation.2 | async-start | bytes 65536 | tf_op jit(solution)/shard_map/all_to_all | solution.py:749
  78.2 15.3 %all-to-all-start.3 = ((bf16[16,96,128]{2,1,0:T(8,128)(2,1)}), bf16[16,96,128]{2,1,0:T(8,128)(2,1)S(1)}, u32[]{:S(2)}, u32[]{:S(2)}) async-start(bf16[16,96,128]{2,1,0:T(8,128)(2,1)} %get-tuple-element.63), calls=%async_computation.3 | async-start | bytes 786432 | tf_op jit(solution)/shard_map/all_to_all | solution.py:751

commit v5 on v3

--- a/solution.py
+++ b/solution.py
@@ -15,6 +15,7 @@
 CONV_ROWS = 960
 DOWN_ROWS = 512
 GROUPS = 8
+ROWS = 32
 SHARE = (CONV_ROWS + DOWN_ROWS) // GROUPS
 
 VMEM_SPEC = pl.BlockSpec(memory_space=pltpu.VMEM)
@@ -44,25 +45,25 @@
     return pltpu.roll(x, 64, x.ndim - 1)
 
 
-def place_faces(info_ref, i, planes, pair_ref, other_ref, first=0):
-    even = info_ref[0] % 2 == 0
+def place_faces(rank_ref, i, planes, pair_ref, other_ref, first=0):
+    even = rank_ref[0] % 2 == 0
     low, high = planes[0], planes[SIDE - 1]
     pair_ref[pl.ds(pl.multiple_of(first + i * SIDE, SIDE), SIDE)] = jnp.where(even, high, low)
     other_ref[pl.ds(pl.multiple_of(i * SIDE, SIDE), SIDE)] = jnp.where(even, low, high)
 
 
-def faces_kernel(info_ref, x_ref, v_ref, pair_ref, other_ref, token_ref):
+def faces_kernel(rank_ref, x_ref, v_ref, pair_ref, other_ref, token_ref):
     def plane(i):
         columns = pl.ds(pl.multiple_of(i * 256, 256), 256)
         voxels = x_ref[:, columns].astype(F32).T.astype(BF16).reshape(SIDE, SIDE, LANES)
         v_ref[i] = voxels
-        place_faces(info_ref, i, voxels, pair_ref, other_ref)
+        place_faces(rank_ref, i, voxels, pair_ref, other_ref)
 
     loop(SIDE, plane, 4)
     token_ref[...] = jnp.zeros_like(token_ref)
 
 
-def faces_call(info, x):
+def faces_call(rank, x):
     face = jax.ShapeDtypeStruct((256, LANES), BF16)
     return pl.pallas_call(
         faces_kernel,
@@ -72,47 +73,47 @@
         compiler_params=params(16),
         cost_estimate=pl.CostEstimate(flops=0, bytes_accessed=4_000_000, transcendentals=0),
         name="faces",
-    )(info, x)
-
-
-def find_octant(info_ref, wanted):
+    )(rank, x)
+
+
+def find_octant(child_ref, wanted):
     place = jnp.int32(0)
     found = jnp.int32(0)
     for o in range(8):
-        hit = (info_ref[2 + o] == wanted).astype(jnp.int32)
+        hit = (child_ref[0, o] == wanted).astype(jnp.int32)
         place = place + hit * o
         found = found + hit
     return place, found
 
 
-def cot_kernel(after_ref, info_ref, cot_ref, own_ref, send_ref, turned_ref):
+def cot_kernel(after_ref, child_ref, rank_ref, cot_ref, own_ref, send_ref, turned_ref):
     def plane(i):
         columns = pl.ds(pl.multiple_of(i * 256, 256), 256)
         turned = cot_ref[:, columns].astype(F32).T
         turned_ref[i // HALF, i % HALF] = turned.reshape(2, HALF, 2, HALF, LANES)
 
     loop(SIDE, plane, 4)
-    rank = info_ref[0]
+    rank = rank_ref[0]
     for out_ref, holder in ((own_ref, rank), (send_ref, rank ^ 1)):
         for slot in range(2):
-            place, found = find_octant(info_ref, holder * 2 + slot)
+            place, found = find_octant(child_ref, holder * 2 + slot)
             block = turned_ref[place // 4, :, place // 2 % 2, :, place % 2]
             block = jnp.where(found > 0, block, jnp.zeros_like(block))
             out_ref[slot * 512 : (slot + 1) * 512] = block.reshape(512, LANES).astype(BF16)
 
 
-def cot_call(after, info, cot):
+def cot_call(after, children, rank, cot):
     blocks = jax.ShapeDtypeStruct((1024, LANES), BF16)
     return pl.pallas_call(
         cot_kernel,
         out_shape=(blocks, blocks),
-        in_specs=[ANY_SPEC, SMEM_SPEC, VMEM_SPEC],
+        in_specs=[ANY_SPEC, SMEM_SPEC, SMEM_SPEC, VMEM_SPEC],
         out_specs=(VMEM_SPEC,) * 2,
         scratch_shapes=[pltpu.VMEM((2, HALF, 2, HALF, 2, HALF, LANES), F32)],
         compiler_params=params(20),
         cost_estimate=pl.CostEstimate(flops=0, bytes_accessed=8_000_000, transcendentals=0),
         name="cot",
-    )(after, info, cot)
+    )(after, children, rank, cot)
 
 
 def weights_kernel(
@@ -166,13 +167,13 @@
 
 
 def coarse_half_kernel(half, *refs):
-    _, info_ref, mine_ref, theirs_ref = refs[:4]
+    _, child_ref, rank_ref, mine_ref, theirs_ref = refs[:5]
     out_ref, token_ref, whole_ref = refs[-3:]
     token_ref[...] = jnp.zeros_like(token_ref)
     for o in range(4):
-        entry = info_ref[2 + half * 4 + o]
+        entry = child_ref[0, half * 4 + o]
         slot = jnp.maximum(entry, 0) % 2
-        here = jnp.maximum(entry, 0) // 2 == info_ref[0]
+        here = jnp.maximum(entry, 0) // 2 == rank_ref[0]
         rows = pl.ds(pl.multiple_of(slot * 512, 512), 512)
         block = jnp.where(here, mine_ref[rows], theirs_ref[rows])
         block = jnp.where(entry >= 0, block, jnp.zeros_like(block)).astype(F32)
@@ -183,22 +184,22 @@
         out_ref[:, i * 256 : (i + 1) * 256] = turned.astype(BF16)
 
 
-def coarse_half_call(after, info, mine, theirs, half, begun=()):
+def coarse_half_call(after, children, rank, mine, theirs, half, begun=()):
     return pl.pallas_call(
         functools.partial(coarse_half_kernel, half),
         grid=(1,),
         out_shape=(jax.ShapeDtypeStruct((LANES, SIDE**3), BF16), TOKEN),
-        in_specs=[ANY_SPEC, SMEM_SPEC, VMEM_SPEC, VMEM_SPEC] + [ANY_SPEC] * len(begun),
+        in_specs=[ANY_SPEC, SMEM_SPEC, SMEM_SPEC, VMEM_SPEC, VMEM_SPEC] + [ANY_SPEC] * len(begun),
         out_specs=(
             pl.BlockSpec((LANES, SIDE**3 // 2), lambda g: (0, half)),
             pl.BlockSpec((8, LANES), lambda g: (0, 0)),
         ),
-        input_output_aliases={4: 0} if begun else {},
+        input_output_aliases={5: 0} if begun else {},
         scratch_shapes=[pltpu.VMEM((HALF, 2, HALF, 2, HALF, LANES), F32)],
         compiler_params=params(16),
         cost_estimate=pl.CostEstimate(flops=0, bytes_accessed=4_000_000, transcendentals=0),
         name="coarse_half",
-    )(after, info, mine, theirs, *begun)
+    )(after, children, rank, mine, theirs, *begun)
 
 
 def spans(step):
@@ -209,79 +210,88 @@
     return slice(0, 1), slice(SIDE - 1, SIDE)
 
 
-def assemble(info_ref, v_ref, pair_ref, other_ref, face_ref, core_ref, ends_ref):
+def chooser(near_ref, column):
+    lower = low_half((1, LANES))
+    entries = near_ref[0, column], near_ref[1, column]
+    straight = [
+        jnp.logical_and(e >= 0, jnp.maximum(e, 0) % 2 == n).astype(F32)
+        for n, e in enumerate(entries)
+    ]
+    crossed = [
+        jnp.logical_and(e >= 0, jnp.maximum(e, 0) % 2 != n).astype(F32)
+        for n, e in enumerate(entries)
+    ]
+    keep = jnp.where(lower, straight[0], straight[1])
+    cross = jnp.where(lower, crossed[0], crossed[1])
+
+    def choose(x):
+        shape = (1,) * (x.ndim - 1) + (LANES,)
+        return x * keep.reshape(shape) + swap_halves(x) * cross.reshape(shape)
+
+    return choose
+
+
+def offsets():
+    steps = [(x, y, z) for x in (-1, 0, 1) for y in (-1, 0, 1) for z in (-1, 0, 1)]
+    steps.remove((0, 0, 0))
+    return list(enumerate(steps))
+
+
+def assemble_inner(near_ref, v_ref, core_ref, ends_ref):
     def fill(i):
-        core_ref[i + 1, SIDE : 17 * SIDE] = v_ref[i].astype(F32).reshape(256, LANES)
+        core_ref[i + 1] = v_ref[i].astype(F32).reshape(256, LANES)
 
     loop(SIDE, fill, 4)
-    even = info_ref[0] % 2 == 0
+    lines = []
+    for column, (step_x, step_y, step_z) in offsets():
+        if step_y != 0:
+            continue
+        choose = chooser(near_ref, column)
+        put_x, take_x = spans(step_x)
+        end = 0 if step_z < 0 else 1
+        strided = pl.ds(SIDE - 1 if step_z < 0 else 0, SIDE, stride=SIDE)
+        if step_x == 0:
+            lines.append((choose, end, strided))
+        elif step_z == 0:
+            core_ref[put_x.start] = choose(core_ref[take_x.start + 1])
+        else:
+            ends_ref[end, put_x.start] = choose(core_ref[take_x.start + 1, strided])
+
+    def line(i):
+        for choose, end, strided in lines:
+            ends_ref[end, i + 1] = choose(core_ref[i + 1, strided])
+
+    loop(SIDE, line, 4)
+
+
+def assemble_edges(near_ref, rank_ref, pair_ref, other_ref, face_ref, core_ref, ends_ref):
+    even = rank_ref[0] % 2 == 0
     pair = pair_ref[pair_ref.shape[0] - 256 :].astype(F32).reshape(SIDE, SIDE, LANES)
     other = other_ref[...].astype(F32).reshape(SIDE, SIDE, LANES)
     face_ref[0] = jnp.where(even, other, pair)
     face_ref[1] = jnp.where(even, pair, other)
-    lower = low_half((1, LANES))
-    column = 0
-    lines = []
-    for step_x in (-1, 0, 1):
-        for step_y in (-1, 0, 1):
-            for step_z in (-1, 0, 1):
-                if step_x == 0 and step_y == 0 and step_z == 0:
-                    continue
-                entries = info_ref[10 + column], info_ref[36 + column]
-                column += 1
-                straight = [
-                    jnp.logical_and(e >= 0, jnp.maximum(e, 0) % 2 == n).astype(F32)
-                    for n, e in enumerate(entries)
-                ]
-                crossed = [
-                    jnp.logical_and(e >= 0, jnp.maximum(e, 0) % 2 != n).astype(F32)
-                    for n, e in enumerate(entries)
-                ]
-                keep = jnp.where(lower, straight[0], straight[1])
-                cross = jnp.where(lower, crossed[0], crossed[1])
-                put_x, take_x = spans(step_x)
-
-                def choose(x, keep=keep, cross=cross):
-                    shape = (1,) * (x.ndim - 1) + (LANES,)
-                    return x * keep.reshape(shape) + swap_halves(x) * cross.reshape(shape)
-
-                end = 0 if step_z < 0 else 1
-                row = SIDE - 1 if step_z < 0 else 0
-                strided = pl.ds(SIDE + row, SIDE, stride=SIDE)
-                if step_y != 0:
-                    side = 0 if step_y < 0 else 1
-                    y = 0 if step_y < 0 else SIDE + 1
-                    if step_z == 0:
-                        core_ref[put_x, y * SIDE : (y + 1) * SIDE] = choose(face_ref[side, take_x])
-                    else:
-                        ends_ref[end, put_x, y : y + 1] = choose(
-                            face_ref[side, take_x, row : row + 1]
-                        )
-                elif step_x != 0:
-                    taken = take_x.start + 1
-                    if step_z == 0:
-                        core_ref[put_x.start, SIDE : 17 * SIDE] = choose(
-                            core_ref[taken, SIDE : 17 * SIDE]
-                        )
-                    else:
-                        ends_ref[end, put_x.start, 1 : SIDE + 1] = choose(core_ref[taken, strided])
-                else:
-                    lines.append((choose, end, strided))
-
-    def line(i):
-        for choose, end, strided in lines:
-            ends_ref[end, i + 1, 1 : SIDE + 1] = choose(core_ref[i + 1, strided])
-
-    loop(SIDE, line, 4)
-
-
-def gather_taps(core_ref, ends_ref, tap_refs):
+    for column, (step_x, step_y, step_z) in offsets():
+        if step_y == 0:
+            continue
+        choose = chooser(near_ref, column)
+        put_x, take_x = spans(step_x)
+        side = 0 if step_y < 0 else 1
+        if step_z == 0:
+            core_ref[put_x, side * SIDE : (side + 1) * SIDE] = choose(face_ref[side, take_x])
+        else:
+            end, row = (0, SIDE - 1) if step_z < 0 else (1, 0)
+            ends_ref[end, put_x, side : side + 1] = choose(
+                face_ref[side, take_x, row : row + 1]
+            )
+
+
+def gather_taps(core_ref, ends_ref, tap_refs, unroll):
     lower = low_half((SIDE, LANES))
     rows = lax.broadcasted_iota(jnp.int32, (8, LANES), 0)
     top, bottom = rows == 0, rows == 7
 
     def plane(i):
-        for j in range(SIDE + 2):
+        for j in range(tap_refs[0].shape[1]):
             first = core_ref[i, j * SIDE : j * SIDE + 8]
             second = core_ref[i, j * SIDE + 8 : (j + 1) * SIDE]
             down_first, down_second = pltpu.roll(first, 1, 0), pltpu.roll(second, 1, 0)
@@ -305,7 +315,18 @@
             tap_refs[1][i, j] = jnp.where(lower, swap_halves(before), here).astype(BF16)
             tap_refs[2][i, j] = after.astype(BF16)
 
-    loop(SIDE + 2, plane, 3)
+    loop(SIDE + 2, plane, unroll)
+
+
+def window(refs, planes, b):
+    inner_ref, edge_ref = refs
+    if b == 0:
+        parts = [edge_ref[planes, 0:1], inner_ref[planes, 0 : SIDE - 1]]
+    elif b == 1:
+        parts = [inner_ref[planes]]
+    else:
+        parts = [inner_ref[planes, 1:SIDE], edge_ref[planes, 1:2]]
+    return jnp.concatenate(parts, axis=1).reshape(-1, LANES)
 
 
 def convolve(tap_refs, w_ref, acc_ref, first=0, planes=SIDE + 2, group=6):
@@ -322,7 +343,7 @@
         results = []
         for n in range(2):
             lhs = [
-                tap_refs[chunk][pl.ds(first + start, group), b : b + SIDE].reshape(rows, LANES)
+                window(tap_refs[chunk], pl.ds(first + start, group), b)
                 for b in range(3)
                 for chunk in (n, 2)
             ]
@@ -344,29 +365,37 @@
     return [(t, t // 4, t // 2 % 2, t % 2) for t in range(8)]
 
 
+def inner_kernel(near_ref, v_ref, zero_ref, one_ref, both_ref, core_ref, ends_ref):
+    assemble_inner(near_ref, v_ref, core_ref, ends_ref)
+    gather_taps(core_ref, ends_ref, (zero_ref, one_ref, both_ref), 3)
+
+
 def forward_kernel(
-    info_ref,
-    v_ref,
+    near_ref,
+    rank_ref,
     pair_ref,
     other_ref,
+    zero_ref,
+    one_ref,
+    both_ref,
     w_ref,
     down_ref,
     oct_ref,
     slope_ref,
     act_ref,
-    zero_ref,
-    one_ref,
-    both_ref,
+    zero_edge_ref,
+    one_edge_ref,
+    both_edge_ref,
     face_ref,
     core_ref,
     ends_ref,
     acc_ref,
     fine_ref,
 ):
-    tap_refs = (zero_ref, one_ref, both_ref)
-    assemble(info_ref, v_ref, pair_ref, other_ref, face_ref, core_ref, ends_ref)
-    gather_taps(core_ref, ends_ref, tap_refs)
-    convolve(tap_refs, w_ref, acc_ref)
+    edges = (zero_edge_ref, one_edge_ref, both_edge_ref)
+    assemble_edges(near_ref, rank_ref, pair_ref, other_ref, face_ref, core_ref, ends_ref)
+    gather_taps(core_ref, ends_ref, edges, 9)
+    convolve(tuple(zip((zero_ref, one_ref, both_ref), edges)), w_ref, acc_ref)
 
     def activate(i):
         preact = acc_ref[i + 2]
@@ -384,7 +413,7 @@
 
 
 def back_kernel(
-    info_ref,
+    rank_ref,
     own_ref,
     came_ref,
     down_t_ref,
@@ -420,14 +449,15 @@
         turned_ref[i + 2] = grad.T.astype(BF16)
         rounded = grad.astype(BF16).reshape(SIDE, SIDE, LANES)
         g_ref[i] = rounded
-        place_faces(info_ref, i, rounded, pair_ref, other_ref, 1024)
+        place_faces(rank_ref, i, rounded, pair_ref, other_ref, 1024)
 
     loop(SIDE, back, 4)
 
 
-def weigh_kernel(info_ref, zero_ref, one_ref, both_ref, act_ref, turned_ref, spun_ref, *refs):
-    kept_ref, sent_ref, token_ref, sums_ref, total_ref = refs
-    token_ref[...] = jnp.zeros_like(token_ref)
+def weigh_kernel(*refs):
+    rank_ref, inner, edges = refs[0], refs[1:4], refs[4:7]
+    act_ref, turned_ref, spun_ref, kept_ref, sent_ref, sums_ref, total_ref = refs[7:]
+    zero, one, both_taps = zip(inner, edges)
     lower = low_half((LANES, LANES))
     whole = [jnp.dot(spun_ref[n], act_ref[...], preferred_element_type=F32) for n in range(2)]
     folded = []
@@ -443,7 +473,7 @@
 
     def weigh(g, carry):
         planes = [3 * g + p for p in range(3)]
-        for n, brick_ref in enumerate((zero_ref, one_ref)):
+        for n, brick in enumerate((zero, one)):
             lhs = [
                 jnp.concatenate(
                     [turned_ref[i + 2 - a, n * 64 : (n + 1) * 64] for a in range(3)], axis=0
@@ -453,8 +483,8 @@
             rhs = [
                 jnp.concatenate(
                     [
-                        ref[i, b : b + SIDE].reshape(256, LANES)
-                        for ref in (brick_ref, both_ref)
+                        window(refs, pl.ds(i, 1), b)
+                        for refs in (brick, both_taps)
                         for b in range(3)
                     ],
                     axis=1,
@@ -479,27 +509,55 @@
         last.append(both + swap_halves(both))
     sums_ref[576:768] = jnp.where(lower, last[0], last[1])
     sums_ref[768:960] = jnp.where(lower, last[2], 0.0)
-    core = info_ref[1] % 2
+    core = core_of(rank_ref)
     for y in range(GROUPS // 2):
         kept_ref[y] = sums_ref[share_rows(2 * y + core)]
         sent_ref[y] = sums_ref[share_rows(2 * y + 1 - core)].astype(BF16)
 
 
+def core_of(rank_ref):
+    return rank_ref[0] // ROWS % 2
+
+
+def y_of(rank_ref):
+    return rank_ref[0] // (2 * ROWS)
+
+
 def share_rows(group):
     return pl.ds(pl.multiple_of(group * SHARE, 8), SHARE)
 
 
-TAPPED = (SIDE + 2, SIDE + 2, SIDE, LANES)
-PAD_SCRATCH = [
+INNER_TAPS = jax.ShapeDtypeStruct((SIDE + 2, SIDE, SIDE, LANES), BF16)
+EDGE_TAPS = jax.ShapeDtypeStruct((SIDE + 2, 2, SIDE, LANES), BF16)
+INNER_SCRATCH = [
+    pltpu.VMEM((SIDE + 2, 256, LANES), F32),
+    pltpu.VMEM((2, SIDE + 2, SIDE, LANES), F32),
+]
+EDGE_SCRATCH = [
     pltpu.VMEM((2, SIDE, SIDE, LANES), F32),
-    pltpu.VMEM((SIDE + 2, 18 * SIDE, LANES), F32),
-    pltpu.VMEM((2, SIDE + 2, 24, LANES), F32),
-    pltpu.VMEM((SIDE + 4, 256, LANES), F32),
+    pltpu.VMEM((SIDE + 2, 2 * SIDE, LANES), F32),
+    pltpu.VMEM((2, SIDE + 2, 8, LANES), F32),
 ]
+ACC_SCRATCH = pltpu.VMEM((SIDE + 4, 256, LANES), F32)
 FINE_SCRATCH = pltpu.VMEM((HALF, 2, HALF, 2, SIDE, LANES), F32)
 
 
-def forward_call(info, v, pair, other, weights, down):
+def inner_call(near, v):
+    return pl.pallas_call(
+        inner_kernel,
+        out_shape=(INNER_TAPS,) * 3,
+        in_specs=[SMEM_SPEC, VMEM_SPEC],
+        out_specs=(VMEM_SPEC,) * 3,
+        scratch_shapes=INNER_SCRATCH,
+        compiler_params=params(20),
+        cost_estimate=pl.CostEstimate(
+            flops=1_000_000_000, bytes_accessed=8_000_000, transcendentals=0
+        ),
+        name="inner",
+    )(near, v)
+
+
+def forward_call(near, rank, pair, other, inner, weights, down):
     return pl.pallas_call(
         forward_kernel,
         out_shape=(
@@ -507,19 +565,19 @@
             jax.ShapeDtypeStruct((SIDE, 256, LANES), F32),
             jax.ShapeDtypeStruct((512, 8 * LANES), BF16),
         )
-        + (jax.ShapeDtypeStruct(TAPPED, BF16),) * 3,
-        in_specs=[SMEM_SPEC] + [VMEM_SPEC] * 5,
+        + (EDGE_TAPS,) * 3,
+        in_specs=[SMEM_SPEC] * 2 + [VMEM_SPEC] * 7,
         out_specs=(VMEM_SPEC,) * 6,
-        scratch_shapes=PAD_SCRATCH + [FINE_SCRATCH],
+        scratch_shapes=EDGE_SCRATCH + [ACC_SCRATCH, FINE_SCRATCH],
         compiler_params=params(28),
         cost_estimate=pl.CostEstimate(
             flops=4_000_000_000, bytes_accessed=16_000_000, transcendentals=600_000
         ),
         name="forward",
-    )(info, v, pair, other, weights, down)
-
-
-def back_call(info, own, came, down_t, slope, octants):
+    )(near, rank, pair, other, *inner, weights, down)
+
+
+def back_call(rank, own, came, down_t, slope, octants):
     return pl.pallas_call(
         back_kernel,
         out_shape=(
@@ -537,19 +595,18 @@
             flops=300_000_000, bytes_accessed=8_000_000, transcendentals=0
         ),
         name="back",
-    )(info, own, came, down_t, slope, octants)
-
-
-def weigh_call(info, zero, one, both, act, turned, spun):
+    )(rank, own, came, down_t, slope, octants)
+
+
+def weigh_call(rank, inner, edges, act, turned, spun):
     return pl.pallas_call(
         weigh_kernel,
         out_shape=(
             jax.ShapeDtypeStruct((GROUPS // 2, SHARE, LANES), F32),
             jax.ShapeDtypeStruct((GROUPS // 2, SHARE, LANES), BF16),
-            TOKEN,
-        ),
-        in_specs=[SMEM_SPEC] + [VMEM_SPEC] * 6,
-        out_specs=(VMEM_SPEC,) * 3,
+        ),
+        in_specs=[SMEM_SPEC] + [VMEM_SPEC] * 9,
+        out_specs=(VMEM_SPEC,) * 2,
         scratch_shapes=[
             pltpu.VMEM((CONV_ROWS + DOWN_ROWS, LANES), F32),
             pltpu.VMEM((2, 192, 768), F32),
@@ -559,47 +616,40 @@
             flops=4_000_000_000, bytes_accessed=10_000_000, transcendentals=0
         ),
         name="weigh",
-    )(info, zero, one, both, act, turned, spun)
-
-
-def input_taps_kernel(
-    after_ref,
-    info_ref,
-    g_ref,
-    pair_ref,
-    other_ref,
-    zero_ref,
-    one_ref,
-    both_ref,
-    token_ref,
-    face_ref,
-    core_ref,
-    ends_ref,
-):
-    assemble(info_ref, g_ref, pair_ref, other_ref, face_ref, core_ref, ends_ref)
-    gather_taps(core_ref, ends_ref, (zero_ref, one_ref, both_ref))
+    )(rank, *inner, *edges, act, turned, spun)
+
+
+def input_taps_kernel(after_ref, near_ref, rank_ref, g_ref, pair_ref, other_ref, *refs):
+    inner, edges, token_ref = refs[:3], refs[3:6], refs[6]
+    core_ref, ends_ref, face_ref, edge_core_ref, edge_ends_ref = refs[7:]
+    assemble_inner(near_ref, g_ref, core_ref, ends_ref)
+    gather_taps(core_ref, ends_ref, inner, 3)
+    assemble_edges(
+        near_ref, rank_ref, pair_ref, other_ref, face_ref, edge_core_ref, edge_ends_ref
+    )
+    gather_taps(edge_core_ref, edge_ends_ref, edges, 9)
     token_ref[...] = jnp.zeros_like(token_ref)
 
 
-def input_taps_call(after, info, g, pair, other):
+def input_taps_call(after, near, rank, g, pair, other):
     return pl.pallas_call(
         input_taps_kernel,
-        out_shape=(jax.ShapeDtypeStruct(TAPPED, BF16),) * 3 + (TOKEN,),
-        in_specs=[ANY_SPEC, SMEM_SPEC] + [VMEM_SPEC] * 3,
-        out_specs=(VMEM_SPEC,) * 4,
-        scratch_shapes=PAD_SCRATCH[:3],
+        out_shape=(INNER_TAPS,) * 3 + (EDGE_TAPS,) * 3 + (TOKEN,),
+        in_specs=[ANY_SPEC] + [SMEM_SPEC] * 2 + [VMEM_SPEC] * 3,
+        out_specs=(VMEM_SPEC,) * 7,
+        scratch_shapes=INNER_SCRATCH + EDGE_SCRATCH,
         compiler_params=params(20),
         cost_estimate=pl.CostEstimate(
-            flops=2_000_000_000, bytes_accessed=8_000_000, transcendentals=0
+            flops=1_000_000_000, bytes_accessed=8_000_000, transcendentals=0
         ),
         name="input_taps",
-    )(after, info, g, pair, other)
+    )(after, near, rank, g, pair, other)
 
 
 def input_half_kernel(half, *refs):
-    _, zero_ref, one_ref, both_ref, w_ref = refs[:5]
+    inner, edges, w_ref = refs[1:4], refs[4:7], refs[7]
     out_ref, token_ref, acc_ref = refs[-3:]
-    convolve((zero_ref, one_ref, both_ref), w_ref, acc_ref, half * HALF, HALF + 2, 5)
+    convolve(tuple(zip(inner, edges)), w_ref, acc_ref, half * HALF, HALF + 2, 5)
 
     for i in range(HALF):
         out_ref[:, i * 256 : (i + 1) * 256] = acc_ref[i + 2].T.astype(BF16)
@@ -611,12 +661,12 @@
         functools.partial(input_half_kernel, half),
         grid=(1,),
         out_shape=(jax.ShapeDtypeStruct((LANES, SIDE**3), BF16), TOKEN),
-        in_specs=[ANY_SPEC] + [VMEM_SPEC] * 4 + [ANY_SPEC] * len(begun),
+        in_specs=[ANY_SPEC] + [VMEM_SPEC] * 7 + [ANY_SPEC] * len(begun),
         out_specs=(
             pl.BlockSpec((LANES, SIDE**3 // 2), lambda g: (0, half)),
             pl.BlockSpec((8, LANES), lambda g: (0, 0)),
         ),
-        input_output_aliases={5: 0} if begun else {},
+        input_output_aliases={8: 0} if begun else {},
         scratch_shapes=[pltpu.VMEM((HALF + 4, 256, LANES), F32)],
         compiler_params=params(16),
         cost_estimate=pl.CostEstimate(
@@ -626,27 +676,27 @@
     )(after, *taps, weights, *begun)
 
 
-def deal_kernel(after_ref, info_ref, kept_ref, came_ref, own_ref, *refs):
+def deal_kernel(rank_ref, kept_ref, came_ref, own_ref, *refs):
     share_refs, total_ref = refs[:-1], refs[-1]
     total_ref[...] = kept_ref[...] + came_ref[...].astype(F32)
-    y = info_ref[1] // 2
+    y = y_of(rank_ref)
     own_ref[...] = total_ref[y]
     for s, share_ref in enumerate(share_refs):
         share_ref[...] = total_ref[y ^ (s + 1)].astype(BF16)
 
 
-def deal_call(after, info, kept, came):
+def deal_call(rank, kept, came):
     return pl.pallas_call(
         deal_kernel,
         out_shape=(jax.ShapeDtypeStruct((SHARE, LANES), F32),)
         + (jax.ShapeDtypeStruct((SHARE, LANES), BF16),) * 3,
-        in_specs=[ANY_SPEC, SMEM_SPEC, VMEM_SPEC, VMEM_SPEC],
+        in_specs=[SMEM_SPEC, VMEM_SPEC, VMEM_SPEC],
         out_specs=(VMEM_SPEC,) * 4,
         scratch_shapes=[pltpu.VMEM((GROUPS // 2, SHARE, LANES), F32)],
         compiler_params=params(16),
         cost_estimate=pl.CostEstimate(flops=0, bytes_accessed=500_000, transcendentals=0),
         name="deal",
-    )(after, info, kept, came)
+    )(rank, kept, came)
 
 
 def add_kernel(after_ref, *refs):
@@ -668,26 +718,26 @@
     )(after, *parts)
 
 
-def collect_kernel(info_ref, *refs):
-    y = info_ref[1] // 2
+def collect_kernel(after_ref, rank_ref, *refs):
+    y = y_of(rank_ref)
     for s, share_ref in enumerate(refs[:-1]):
         refs[-1][y ^ s] = share_ref[...]
 
 
-def collect_call(info, shares):
+def collect_call(after, rank, shares):
     return pl.pallas_call(
         collect_kernel,
         out_shape=jax.ShapeDtypeStruct((GROUPS // 2, SHARE, LANES), BF16),
-        in_specs=[SMEM_SPEC] + [VMEM_SPEC] * len(shares),
+        in_specs=[ANY_SPEC, SMEM_SPEC] + [VMEM_SPEC] * len(shares),
         out_specs=VMEM_SPEC,
         compiler_params=params(16),
         cost_estimate=pl.CostEstimate(flops=0, bytes_accessed=500_000, transcendentals=0),
         name="collect",
-    )(info, *shares)
-
-
-def split_kernel(after_ref, info_ref, mine_ref, theirs_ref, conv_ref, down_ref, sums_ref):
-    core = info_ref[1] % 2
+    )(after, rank, *shares)
+
+
+def split_kernel(rank_ref, mine_ref, theirs_ref, conv_ref, down_ref, sums_ref):
+    core = core_of(rank_ref)
     for y in range(GROUPS // 2):
         sums_ref[share_rows(2 * y + core)] = mine_ref[y].astype(F32)
         sums_ref[share_rows(2 * y + 1 - core)] = theirs_ref[y].astype(F32)
@@ -705,19 +755,19 @@
         down_ref[t + 4] = block[64:]
 
 
-def split_call(after, info, mine, theirs):
+def split_call(rank, mine, theirs):
     return pl.pallas_call(
         split_kernel,
         out_shape=(
             jax.ShapeDtypeStruct((27, 64, 64), F32),
             jax.ShapeDtypeStruct((8, 64, LANES), F32),
         ),
-        in_specs=[ANY_SPEC, SMEM_SPEC] + [VMEM_SPEC] * 2,
+        in_specs=[SMEM_SPEC] + [VMEM_SPEC] * 2,
         out_specs=(VMEM_SPEC,) * 2,
         scratch_shapes=[pltpu.VMEM((CONV_ROWS + DOWN_ROWS, LANES), F32)],
         compiler_params=params(16),
         name="split",
-    )(after, info, mine, theirs)
+    )(rank, mine, theirs)
 
 
 def swaps(axis, step=1):
@@ -738,40 +788,41 @@
 
 
 def body(fine_input, conv_weight, down_weight, coarse_cot, neighbours, children):
-    rank = lax.axis_index("grp") * lax.axis_size("dev") + lax.axis_index("dev")
-    info = [rank.reshape(1), lax.axis_index("grp").reshape(1), children.reshape(8)]
-    info = jnp.concatenate([part.astype(jnp.int32) for part in info + [neighbours.reshape(52)]])
-
-    voxels, pair, other, token = faces_call(info, fine_input.reshape(LANES, SIDE**3))
-    own, send = cot_call(token, info, coarse_cot.reshape(LANES, SIDE**3))
-    pair, other = exchange(pair, other, "dev")
-    came = lax.ppermute(send, "dev", swaps("dev"))
+    dev = ("z", "x")
+    rank = lax.axis_index(("y", "core", "z", "x")).reshape(1).astype(jnp.int32)
+
+    voxels, pair, other, token = faces_call(rank, fine_input.reshape(LANES, SIDE**3))
+    own, send = cot_call(token, children, rank, coarse_cot.reshape(LANES, SIDE**3))
+    pair, other = exchange(pair, other, dev)
+    came = lax.ppermute(send, dev, swaps(dev))
     forward, backward, down, down_t = weights_call(conv_weight, down_weight.transpose(0, 2, 1))
-    octants, slope, act, zero, one, both = forward_call(
-        info, voxels, pair, other, forward, down
+    inner = inner_call(neighbours, voxels)
+    octants, slope, act, *edges = forward_call(
+        neighbours, rank, pair, other, inner, forward, down
     )
-    mine, other_out, grads, turned, spun = back_call(info, own, came, down_t, slope, octants)
-    theirs, grad_other = exchange(mine, other_out, "dev")
-    kept, sent, token = weigh_call(info, zero, one, both, act, turned, spun)
-
-    (came,) = swapped(sent, "grp", (1,))
-    coarse, token = coarse_half_call(token, info, mine, theirs, 0)
-    own, *shares = deal_call(token, info, kept, came)
-    came = [lax.ppermute(share, "grp", swaps("grp", 2 * s + 2)) for s, share in enumerate(shares)]
-    *input_taps, token = input_taps_call(own, info, grads, theirs, grad_other)
+    mine, other_out, grads, turned, spun = back_call(rank, own, came, down_t, slope, octants)
+    theirs, grad_other = exchange(mine, other_out, dev)
+
+    kept, sent = weigh_call(rank, inner, edges, act, turned, spun)
+    (came,) = swapped(sent, "core", (1,))
+    own, *shares = deal_call(rank, kept, came)
+    came = [lax.ppermute(share, "y", swaps("y", s + 1)) for s, share in enumerate(shares)]
+    *taps_in, token = input_taps_call(own, neighbours, rank, grads, theirs, grad_other)
     part = add_call(token, [own, *came], F32)
-    came = swapped(part, "dev", (1, 2, 3))
-    input_grad, token = input_half_call(part, input_taps, backward, 0)
+    came = swapped(part, "x", (1, 2, 3))
+    input_grad, token = input_half_call(part, taps_in, backward, 0)
     part = add_call(token, [part, *came])
-    came = swapped(part, "dev", (4, 8, 12))
-    input_grad, token = input_half_call(part, input_taps, backward, 1, (input_grad,))
+    came = swapped(part, "z", (1, 2, 3))
+    input_grad, token = input_half_call(part, taps_in, backward, 1, (input_grad,))
     part = add_call(token, [part, *came])
-    came = swapped(part, "dev", (16,))
-    coarse, token = coarse_half_call(part, info, mine, theirs, 1, (coarse,))
+    came = swapped(part, "z", (4,))
+    coarse, token = coarse_half_call(part, children, rank, mine, theirs, 0)
     part = add_call(token, [part, *came])
-    shares = collect_call(info, [part, *swapped(part, "grp", (2, 4, 6))])
-    (came,) = swapped(shares, "grp", (1,))
-    conv_grad, down_grad = split_call(token, info, shares, came)
+    came = swapped(part, "y", (1, 2, 3))
+    coarse, token = coarse_half_call(part, children, rank, mine, theirs, 1, (coarse,))
+    shares = collect_call(token, rank, [part, *came])
+    (came,) = swapped(shares, "core", (1,))
+    conv_grad, down_grad = split_call(rank, shares, came)
     return (
         coarse.reshape(1, LANES, SIDE**3),
         input_grad.reshape(2, 64, SIDE**3),
@@ -781,13 +832,11 @@
 
 
 def solution(mesh):
-    in_specs = (
-        P(("grp", "dev"), None, None),
-        P(),
-        P(),
-        P(("grp", "dev"), None, None),
-        P(("grp", "dev"), None),
-        P(("grp", "dev"), None),
+    grp, dev = mesh.devices.shape
+    mesh = jax.sharding.Mesh(
+        mesh.devices.reshape(grp // 2, 2, dev // 4, 4), ("y", "core", "z", "x")
     )
-    out_specs = (P(("grp", "dev"), None, None), P(("grp", "dev"), None, None), P(), P())
+    bricks = ("y", "core", "z", "x")
+    in_specs = (P(bricks, None, None), P(), P(), P(bricks, None, None), P(bricks, None), P(bricks, None))
+    out_specs = (P(bricks, None, None), P(bricks, None, None), P(), P())
     return jax.shard_map(body, mesh=mesh, in_specs=in_specs, out_specs=out_specs, check_vma=False)

time: 84.7 us -> 79.3 us (0.936)
  Pallas kernels: 34.3 us -> 32.1 us
  starting transfers between devices: 37.5 us -> 36.2 us
  waiting for transfers between devices: 9.16 us -> 8.04 us
    ppermute x2, starting transfers between devices: 10.4 us -> 7.42 us  [exchange(): lax.ppermute(other, axis, across + [(j, i) for i, j in across])]
    pallas_call x1 -> x2, Pallas kernels: 2.5 us -> 4.98 us  [the longest x1 2.71 us: input_taps_call(): pl.pallas_call(input_taps_kernel, out_shape=(INNER_TAPS,) * 3 + (EDGE_TAP...]
    ppermute x2, waiting for transfers between devices: 0.01 us -> 1.85 us  [exchange(): lax.ppermute(other, axis, across + [(j, i) for i, j in across])]
    ppermute x12, starting transfers between devices: 19.4 us -> 21 us  [swapped(): return [lax.ppermute(array, axis, swaps(axis, step)) for step in steps]]
    ppermute x4, waiting for transfers between devices: 1.6 us -> 0.01 us  [the longest x3 0.01 us: body(): lax.ppermute(share, 'y', swaps('y', s + 1))]
    pallas_call x1, Pallas kernels: 8.38 us -> 6.89 us  [forward_call(): pl.pallas_call(forward_kernel, out_shape=(jax.ShapeDtypeStruct((1024, LAN...]
    ppermute x12, waiting for transfers between devices: 7.55 us -> 6.18 us  [swapped(): return [lax.ppermute(array, axis, swaps(axis, step)) for step in steps]]
    unnamed x8 -> x14, local copies, waits for them, and re-layouts: 1.24 us -> 1.98 us
  transfers between devices with their start and end apart: 20 -> 20, of which waited for: 5 -> 5; matrix products, arithmetic and copies ran while one was open for 0% -> 0% of each run, Pallas kernels for 34% -> 37%
where the time goes in v5:
time: 79.3 us; the launch traced here: 79.1 us
  starting transfers between devices  36.2 us (46%)
  Pallas kernels  32.1 us (40%)
  waiting for transfers between devices  8.04 us (10%)
  local copies, waits for them, and re-layouts  1.98 us (2%)
  between operations  0.85 us (1%)
    ppermute x12, starting transfers between devices, swapped(): return [lax.ppermute(array, axis, swaps(axis, step)) for step in steps]  21 us
    ppermute x2, starting transfers between devices, exchange(): lax.ppermute(other, axis, across + [(j, i) for i, j in across])  7.42 us
    pallas_call x2, Pallas kernels, input_half_call(): pl.pallas_call(functools.partial(input_half_kernel, half), grid=(1,), out...  7.27 us
    pallas_call x1, Pallas kernels, forward_call(): pl.pallas_call(forward_kernel, out_shape=(jax.ShapeDtypeStruct((1024, LAN...  6.89 us
    ppermute x12, waiting for transfers between devices, swapped(): return [lax.ppermute(array, axis, swaps(axis, step)) for step in steps]  6.18 us
    pallas_call x1, Pallas kernels, weigh_call(): pl.pallas_call(weigh_kernel, out_shape=(jax.ShapeDtypeStruct((GROUPS // 2...  4.71 us
    ppermute x3, starting transfers between devices, body(): lax.ppermute(share, 'y', swaps('y', s + 1))  4 us
    ppermute x2, starting transfers between devices, exchange(): lax.ppermute(pair, axis, swaps(axis))  3.65 us
  transfers between devices with their start and end apart: 20, of which 5 were waited for; matrix products, arithmetic and copies ran while one was open for 0% of the time, Pallas kernels for 37%

profile of v5, /device:TPU:1, one launch (start us, length us, event | category | flops | bytes accessed | tf_op | source)
XLA Modules:
  0.0 79.1 jit_solution(14806115795040592886)
XLA Ops:
  0.7 1.3 %copy-done.1 = bf16[2,64,4096]{2,1,0:T(8,128)(2,1)S(1)} copy-done((bf16[2,64,4096]{2,1,0:T(8,128)(2,1)S(1)}, bf16[2,64,4096]{2,1,0:T(8,128)(2,1)}, u32[]{:S(2)}) %copy-start.1) | copy-done | bytes 1048600
  2.5 2.1 %collective-permute-start = (bf16[256,128]{1,0:T(8,128)(2,1)S(1)}, bf16[256,128]{1,0:T(8,128)(2,1)S(1)}, u32[]{:S(2)}, u32[]{:S(2)}) collective-permute-start(bf16[256,128]{1,0:T(8,128)(2,1)S(1)} %get-tuple-element.55), channel_id=1, source_target_pairs={{0,1},{1,0},{2,3},{3,2},{4,5},{5,4},{6,7},{7,6},{8,9},{9,8},{10,11... | collective-permute-start | bytes 196616 | tf_op jit(solution)/shard_map/ppermute | solution.py:785
  4.7 7.1 %collective-permute-start.1 = (bf16[256,128]{1,0:T(8,128)(2,1)S(1)}, bf16[256,128]{1,0:T(8,128)(2,1)S(1)}, u32[]{:S(2)}, u32[]{:S(2)}) collective-permute-start(bf16[256,128]{1,0:T(8,128)(2,1)S(1)} %get-tuple-element.56), channel_id=1, source_target_pairs={{1,2},{3,4},{5,6},{7,8},{9,10},{11,12},{13,14},{15,16},{17,18},{19... | collective-permute-start | bytes 196616 | tf_op jit(solution)/shard_map/ppermute | solution.py:786
  11.8 0.7 copy-done.4
  12.4 1.3 %cot.1 = (bf16[1024,128]{1,0:T(8,128)(2,1)S(1)}, bf16[1024,128]{1,0:T(8,128)(2,1)S(1)}) custom-call(f32[8,128]{1,0:T(8,128)S(1)} %get-tuple-element.63.after_ref, s32[1,8]{1,0:T(1,128)S(1)} %copy-done.4, s32[1]{0:T(128)} %bitcast.rank_ref.refs_0_.refs_2_, bf16[128,4096]{1,0:T(8,128)(2,1)S(1)} %bitcast.7), custom_call_target="tpu_custom_call" | custom-call | bytes 8000000 | tf_op jit(solution)/shard_map/cot/pallas_call | solution.py:107
  13.9 0.6 weights.1
  14.5 2.3 %inner.1 = (bf16[18,16,16,128]{3,2,1,0:T(8,128)(2,1)S(1)}, bf16[18,16,16,128]{3,2,1,0:T(8,128)(2,1)S(1)}, bf16[18,16,16,128]{3,2,1,0:T(8,128)(2,1)S(1)}) custom-call(s32[2,26]{1,0:T(2,128)S(1)} %copy-done.6, bf16[16,16,16,128]{3,2,1,0:T(8,128)(2,1)S(1)} %get-tuple-element.51.v_ref), custom_call_target="tpu_custom_call" | custom-call | flops 1000000000 | bytes 8000000 | tf_op jit(solution)/shard_map/inner/pallas_call | solution.py:546
  16.8 6.9 %forward.1 = (bf16[1024,128]{1,0:T(8,128)(2,1)S(1)}, f32[16,256,128]{2,1,0:T(8,128)S(1)}, bf16[512,1024]{1,0:T(8,128)(2,1)S(1)}, bf16[18,2,16,128]{3,2,1,0:T(8,1...) custom-call(s32[2,26]{1,0:T(2,128)S(1)} %copy-done.6, ...), custom_call_target="tpu_custom_call" | custom-call | flops 4000000000 | bytes 16000000 | tf_op jit(solution)/shard_map/forward/pallas_call | solution.py:561
  23.7 1.2 %back.1 = (bf16[1280,128]{1,0:T(8,128)(2,1)S(1)}, bf16[256,128]{1,0:T(8,128)(2,1)S(1)}, bf16[16,16,16,128]{3,2,1,0:T(8,128)(2,1)S(1)}, bf16[20,128,256]{2,1,0:T(8,128)(2,1)S(1)}, bf16[2,128,512]{2,1,0:T(8,128)(2,1)S(1)}) custom-call(s32[1]{0:T(128)} %bitcast.rank_ref.refs_0_.refs_2_, bf16[1024,128]{1,0:T(8,128)(2,1)S(1)} %get-tuple-element.64.own_ref, ...), custom_call_target="tpu_custom_call" | custom-call | flops 300000000 | bytes 8000000 | tf_op jit(solution)/shard_map/back/pallas_call | solution.py:581
  24.9 1.5 %collective-permute-start.4 = (bf16[1280,128]{1,0:T(8,128)(2,1)S(1)}, bf16[1280,128]{1,0:T(8,128)(2,1)S(1)}, u32[]{:S(2)}, u32[]{:S(2)}) collective-permute-start(bf16[1280,128]{1,0:T(8,128)(2,1)S(1)} %get-tuple-element.75.refs_3_), channel_id=1, source_target_pairs={{0,1},{1,0},{2,3},{3,2},{4,5},{5,4},{6,7},{7,6},{8,9},{9,8},{10,11... | collective-permute-start | bytes 983048 | tf_op jit(solution)/shard_map/ppermute | solution.py:785
  26.4 4.7 %weigh.1 = (f32[4,184,128]{2,1,0:T(8,128)S(1)}, bf16[4,184,128]{2,1,0:T(8,128)(2,1)S(1)}) custom-call(s32[1]{0:T(128)} %bitcast.rank_ref.refs_0_.refs_2_, bf16[18,16,16,128]{3,2,1,0:T(8,128)(2,1)S(1)} %get-tuple-element.52.zero_ref.refs_1_, bf16[18,16,16,128]{3,2,1,0:T(8,128)(2,1)S(1)} %get-tuple-element.53.one_ref.refs_2_, ...), custom_call_target="tpu_custom_call" | custom-call | flops 4000000000 | bytes 10000000 | tf_op jit(solution)/shard_map/weigh/pallas_call | solution.py:602
  31.1 1.9 %collective-permute-start.3 = (bf16[4,184,128]{2,1,0:T(8,128)(2,1)S(1)}, bf16[4,184,128]{2,1,0:T(8,128)(2,1)S(1)}, u32[]{:S(2)}, u32[]{:S(2)}) collective-permute-start(bf16[4,184,128]{2,1,0:T(8,128)(2,1)S(1)} %get-tuple-element.72), channel_id=1, source_target_pairs={{0,32},{32,0},{1,33},{33,1},{2,34},{34,2},{3,35},{35,3},{4,36},{36... | collective-permute-start | bytes 565256 | tf_op jit(solution)/shard_map/ppermute | solution.py:778
  33.3 0.7 collective-permute-done.3.came_ref
  34.1 1.4 %collective-permute-start.6 = (bf16[184,128]{1,0:T(8,128)(2,1)S(1)}, bf16[184,128]{1,0:T(8,128)(2,1)S(1)}, u32[]{:S(2)}, u32[]{:S(2)}) collective-permute-start(bf16[184,128]{1,0:T(8,128)(2,1)S(1)} %get-tuple-element.78), channel_id=1, source_target_pairs={{0,64},{64,0},{128,192},{192,128},{1,65},{65,1},{129,193},{193,129... | collective-permute-start | bytes 141320 | tf_op jit(solution)/shard_map/ppermute | solution.py:809
  35.5 2.6 %collective-permute-start.7 = (bf16[184,128]{1,0:T(8,128)(2,1)S(1)}, bf16[184,128]{1,0:T(8,128)(2,1)S(1)}, u32[]{:S(2)}, u32[]{:S(2)}) collective-permute-start(bf16[184,128]{1,0:T(8,128)(2,1)S(1)} %get-tuple-element.79), channel_id=1, source_target_pairs={{0,128},{64,192},{128,0},{192,64},{1,129},{65,193},{129,1},{193,65... | collective-permute-start | bytes 141320 | tf_op jit(solution)/shard_map/ppermute | solution.py:809
  38.1 1.8 %collective-permute-done.5.other_ref = bf16[256,128]{1,0:T(8,128)(2,1)S(1)} collective-permute-done((bf16[256,128]{1,0:T(8,128)(2,1)S(1)}, bf16[256,128]{1,0:T(8,128)(2,1)S(1)}, u32[]{:S(2)}, u32[]{:S(2)}) %collective-permute-start.5) | collective-permute-done | bytes 65568 | tf_op jit(solution)/shard_map/ppermute | solution.py:786
  40.0 2.7 %input_taps.1 = (bf16[18,16,16,128]{3,2,1,0:T(8,128)(2,1)S(1)}, bf16[18,16,16,128]{3,2,1,0:T(8,128)(2,1)S(1)}, bf16[18,16,16,128]{3,2,1,0:T(8,128)(2,1)S(1)}, bf...) custom-call(f32[184,128]{1,0:T(8,128)S(1)} %get-tuple-element.73.aft, ...), custom_call_target="tpu_custom_call" | custom-call | flops 1000000000 | bytes 8000000 | tf_op jit(solution)/shard_map/input_taps/pallas_call | solution.py:635
  42.8 1.1 %collective-permute-start.10 = (f32[184,128]{1,0:T(8,128)S(1)}, f32[184,128]{1,0:T(8,128)S(1)}, u32[]{:S(2)}, u32[]{:S(2)}) collective-permute-start(f32[184,128]{1,0:T(8,128)S(1)} %add.16.refs_0_), channel_id=1, source_target_pairs={{0,2},{1,3},{2,0},{3,1},{4,6},{5,7},{6,4},{7,5},{8,10},{9,11},{10,... | collective-permute-start | bytes 282632 | tf_op jit(solution)/shard_map/ppermute | solution.py:778
  43.9 2.2 %collective-permute-start.9 = (f32[184,128]{1,0:T(8,128)S(1)}, f32[184,128]{1,0:T(8,128)S(1)}, u32[]{:S(2)}, u32[]{:S(2)}) collective-permute-start(f32[184,128]{1,0:T(8,128)S(1)} %add.16.refs_0_), channel_id=1, source_target_pairs={{0,1},{1,0},{2,3},{3,2},{4,5},{5,4},{6,7},{7,6},{8,9},{9,8},{10,11... | collective-permute-start | bytes 282632 | tf_op jit(solution)/shard_map/ppermute | solution.py:778
  46.1 3.6 %input_half.2 = (bf16[128,4096]{1,0:T(8,128)(2,1)}, f32[8,128]{1,0:T(8,128)S(1)}) custom-call(f32[184,128]{1,0:T(8,128)S(1)} %add.16.refs_0_, bf16[18,16,16,128]{3,2,1,0:T(8,128)(2,1)S(1)} %get-tuple-element.81.refs_1_, bf16[18,16,16,128]{3,2,1,0:T(8,128)(2,1)S(1)} %get-tuple-element.82.refs_2_, bf16[18,16,16,128]{3,2,1,0:T(8,128)(2,1)S(1)} %get-tuple-element.83.refs_3_, ...), custom_call_target="tpu_custom_call" | custom-call | flops 2500000000 | bytes 6000000 | tf_op jit(solution)/shard_map/input_half/pallas_call | solution.py:660
  49.8 0.7 collective-permute-start.14
  50.5 2.9 %collective-permute-start.12 = (bf16[184,128]{1,0:T(8,128)(2,1)S(1)}, bf16[184,128]{1,0:T(8,128)(2,1)S(1)}, u32[]{:S(2)}, u32[]{:S(2)}) collective-permute-start(bf16[184,128]{1,0:T(8,128)(2,1)S(1)} %add.17.refs_0_), channel_id=1, source_target_pairs={{0,4},{4,0},{8,12},{12,8},{16,20},{20,16},{24,28},{28,24},{1,5},{5... | collective-permute-start | bytes 141320 | tf_op jit(solution)/shard_map/ppermute | solution.py:778
  53.4 3.6 %input_half.3 = (bf16[128,4096]{1,0:T(8,128)(2,1)}, f32[8,128]{1,0:T(8,128)S(1)}) custom-call(bf16[184,128]{1,0:T(8,128)(2,1)S(1)} %add.17.refs_0_, bf16[18,16,16,128]{3,2,1,0:T(8,128)(2,1)S(1)} %get-tuple-element.81.refs_1_, bf16[18,16,16,128]{3,2,1,0:T(8,128)(2,1)S(1)} %get-tuple-element.82.refs_2_, ...), custom_call_target="tpu_custom_call", output_to_operand_aliasing={{0}: (8, {})} | custom-call | flops 2500000000 | bytes 6000000 | tf_op jit(solution)/shard_map/input_half/pallas_call | solution.py:660
  57.1 3.2 %collective-permute-start.15 = (bf16[184,128]{1,0:T(8,128)(2,1)S(1)}, bf16[184,128]{1,0:T(8,128)(2,1)S(1)}, u32[]{:S(2)}, u32[]{:S(2)}) collective-permute-start(bf16[184,128]{1,0:T(8,128)(2,1)S(1)} %add.18.refs_0_), channel_id=1, source_target_pairs={{0,16},{4,20},{8,24},{12,28},{16,0},{20,4},{24,8},{28,12},{1,17},{... | collective-permute-start | bytes 141320 | tf_op jit(solution)/shard_map/ppermute | solution.py:778
  60.3 1.6 %coarse_half.2 = (bf16[128,4096]{1,0:T(8,128)(2,1)}, f32[8,128]{1,0:T(8,128)S(1)}) custom-call(bf16[184,128]{1,0:T(8,128)(2,1)S(1)} %add.18.refs_0_, s32[1,8]{1,0:T(1,128)S(1)} %copy-done.5, s32[1]{0:T(128)} %bitcast.rank_ref.refs_0_.refs_2_, bf16[1280,128]{1,0:T(8,128)(2,1)S(1)} %get-tuple-element.75.refs_3_, ...), custom_call_target="tpu_custom_call" | custom-call | bytes 4000000 | tf_op jit(solution)/shard_map/coarse_half/pallas_call | solution.py:188
  61.8 2.2 %collective-permute-done.15.refs_1_ = bf16[184,128]{1,0:T(8,128)(2,1)S(1)} collective-permute-done((bf16[184,128]{1,0:T(8,128)(2,1)S(1)}, bf16[184,128]{1,0:T(8,128)(2,1)S(1)}, u32[]{:S(2)}, u32[]{:S(2)}) %collective-permute-start.15) | collective-permute-done | bytes 47136 | tf_op jit(solution)/shard_map/ppermute | solution.py:778
  64.0 2.9 %collective-permute-start.18 = (bf16[184,128]{1,0:T(8,128)(2,1)S(1)}, bf16[184,128]{1,0:T(8,128)(2,1)S(1)}, u32[]{:S(2)}, u32[]{:S(2)}) collective-permute-start(bf16[184,128]{1,0:T(8,128)(2,1)S(1)} %add.19.refs_0_), channel_id=1, source_target_pairs={{0,192},{64,128},{128,64},{192,0},{1,193},{65,129},{129,65},{193,1... | collective-permute-start | bytes 141320 | tf_op jit(solution)/shard_map/ppermute | solution.py:778
  67.6 1.6 %coarse_half.3 = (bf16[128,4096]{1,0:T(8,128)(2,1)}, f32[8,128]{1,0:T(8,128)S(1)}) custom-call(bf16[184,128]{1,0:T(8,128)(2,1)S(1)} %add.19.refs_0_, s32[1,8]{1,0:T(1,128)S(1)} %copy-done.5, s32[1]{0:T(128)} %bitcast.rank_ref.refs_0_.refs_2_, bf16[1280,128]{1,0:T(8,128)(2,1)S(1)} %get-tuple-element.75.refs_3_, ...), custom_call_target="tpu_custom_call", output_to_operand_aliasing={{0}: (5, {})} | custom-call | bytes 4000000 | tf_op jit(solution)/shard_map/coarse_half/pallas_call | solution.py:188
  69.2 2.2 %collective-permute-done.17.refs_2_ = bf16[184,128]{1,0:T(8,128)(2,1)S(1)} collective-permute-done((bf16[184,128]{1,0:T(8,128)(2,1)S(1)}, bf16[184,128]{1,0:T(8,128)(2,1)S(1)}, u32[]{:S(2)}, u32[]{:S(2)}) %collective-permute-start.17) | collective-permute-done | bytes 47136 | tf_op jit(solution)/shard_map/ppermute | solution.py:778
  71.4 5.4 %collective-permute-start.19 = (bf16[4,184,128]{2,1,0:T(8,128)(2,1)S(1)}, bf16[4,184,128]{2,1,0:T(8,128)(2,1)S(1)}, u32[]{:S(2)}, u32[]{:S(2)}) collective-permute-start(bf16[4,184,128]{2,1,0:T(8,128)(2,1)S(1)} %collect.1.mine_ref), channel_id=1, source_target_pairs={{0,32},{32,0},{1,33},{33,1},{2,34},{34,2},{3,35},{35,3},{4,36},{36... | collective-permute-start | bytes 565256 | tf_op jit(solution)/shard_map/ppermute | solution.py:778
  76.8 1.1 %collective-permute-done.19.theirs_ref = bf16[4,184,128]{2,1,0:T(8,128)(2,1)S(1)} collective-permute-done((bf16[4,184,128]{2,1,0:T(8,128)(2,1)S(1)}, bf16[4,184,128]{2,1,0:T(8,128)(2,1)S(1)}, u32[]{:S(2)}, u32[]{:S(2)}) %collective-permute-start.19) | collective-permute-done | bytes 188448 | tf_op jit(solution)/shard_map/ppermute | solution.py:778
  77.9 1.3 %split.1 = (f32[27,64,64]{2,1,0:T(8,128)}, f32[8,64,128]{2,1,0:T(8,128)}) custom-call(s32[1]{0:T(128)} %bitcast.rank_ref.refs_0_.refs_2_, bf16[4,184,128]{2,1,0:T(8,128)(2,1)S(1)} %collect.1.mine_ref, bf16[4,184,128]{2,1,0:T(8,128)(2,1)S(1)} %collective-permute-done.19.theirs_ref), custom_call_target="tpu_custom_call" | custom-call | tf_op jit(solution)/shard_map/split/pallas_call | solution.py:759
  (41 shorter events, 2.0 us)
Async XLA Ops:
  0.6 11.1 %copy-start = (bf16[1,128,4096]{2,1,0:T(8,128)(2,1)S(1)}, bf16[1,128,4096]{2,1,0:T(8,128)(2,1)}, u32[]{:S(2)}) copy-start(bf16[1,128,4096]{2,1,0:T(8,128)(2,1)} %param.9) | copy-start | bytes 3145732
  0.7 1.3 %copy-start.1 = (bf16[2,64,4096]{2,1,0:T(8,128)(2,1)S(1)}, bf16[2,64,4096]{2,1,0:T(8,128)(2,1)}, u32[]{:S(2)}) copy-start(bf16[2,64,4096]{2,1,0:T(8,128)(2,1)} %param.6) | copy-start | bytes 3145732
  2.0 11.9 %copy-start.2 = (bf16[27,64,64]{2,1,0:T(8,128)(2,1)S(1)}, bf16[27,64,64]{2,1,0:T(8,128)(2,1)}, u32[]{:S(2)}) copy-start(bf16[27,64,64]{2,1,0:T(8,128)(2,1)} %conv_ref.1) | copy-start | bytes 663556
  2.0 11.9 %copy-start.3 = (bf16[8,128,64]{1,2,0:T(8,128)(2,1)S(1)}, bf16[8,128,64]{1,2,0:T(8,128)(2,1)}, u32[]{:S(2)}) copy-start(bf16[8,128,64]{1,2,0:T(8,128)(2,1)} %param.8) | copy-start | bytes 393220
  2.5 14.2 %collective-permute-start = (bf16[256,128]{1,0:T(8,128)(2,1)S(1)}, bf16[256,128]{1,0:T(8,128)(2,1)S(1)}, u32[]{:S(2)}, u32[]{:S(2)}) collective-permute-start(bf16[256,128]{1,0:T(8,128)(2,1)S(1)} %get-tuple-element.55), channel_id=1, source_target_pairs={{0,1},{1,0},{2,3},{3,2},{4,5},{5,4},{6,7},{7,6},{8,9},{9,8},{10,11... | collective-permute-start | bytes 196616 | tf_op jit(solution)/shard_map/ppermute | solution.py:785
  4.7 12.1 %collective-permute-start.1 = (bf16[256,128]{1,0:T(8,128)(2,1)S(1)}, bf16[256,128]{1,0:T(8,128)(2,1)S(1)}, u32[]{:S(2)}, u32[]{:S(2)}) collective-permute-start(bf16[256,128]{1,0:T(8,128)(2,1)S(1)} %get-tuple-element.56), channel_id=1, source_target_pairs={{1,2},{3,4},{5,6},{7,8},{9,10},{11,12},{13,14},{15,16},{17,18},{19... | collective-permute-start | bytes 196616 | tf_op jit(solution)/shard_map/ppermute | solution.py:786
  11.8 0.7 copy-start.4
  12.4 2.1 %copy-start.6 = (s32[2,26]{1,0:T(2,128)S(1)}, s32[2,26]{1,0:T(2,128)}, u32[]{:S(2)}) copy-start(s32[2,26]{1,0:T(2,128)} %near_ref.5) | copy-start | bytes 628
  13.7 10.0 %collective-permute-start.2 = (bf16[1024,128]{1,0:T(8,128)(2,1)S(1)}, bf16[1024,128]{1,0:T(8,128)(2,1)S(1)}, u32[]{:S(2)}, u32[]{:S(2)}) collective-permute-start(bf16[1024,128]{1,0:T(8,128)(2,1)S(1)} %get-tuple-element.65), channel_id=1, source_target_pairs={{0,1},{1,0},{2,3},{3,2},{4,5},{5,4},{6,7},{7,6},{8,9},{9,8},{10,11... | collective-permute-start | bytes 786440 | tf_op jit(solution)/shard_map/ppermute | solution.py:797
  24.9 15.1 %collective-permute-start.4 = (bf16[1280,128]{1,0:T(8,128)(2,1)S(1)}, bf16[1280,128]{1,0:T(8,128)(2,1)S(1)}, u32[]{:S(2)}, u32[]{:S(2)}) collective-permute-start(bf16[1280,128]{1,0:T(8,128)(2,1)S(1)} %get-tuple-element.75.refs_3_), channel_id=1, source_target_pairs={{0,1},{1,0},{2,3},{3,2},{4,5},{5,4},{6,7},{7,6},{8,9},{9,8},{10,11... | collective-permute-start | bytes 983048 | tf_op jit(solution)/shard_map/ppermute | solution.py:785
  31.1 2.9 %collective-permute-start.3 = (bf16[4,184,128]{2,1,0:T(8,128)(2,1)S(1)}, bf16[4,184,128]{2,1,0:T(8,128)(2,1)S(1)}, u32[]{:S(2)}, u32[]{:S(2)}) collective-permute-start(bf16[4,184,128]{2,1,0:T(8,128)(2,1)S(1)} %get-tuple-element.72), channel_id=1, source_target_pairs={{0,32},{32,0},{1,33},{33,1},{2,34},{34,2},{3,35},{35,3},{4,36},{36... | collective-permute-start | bytes 565256 | tf_op jit(solution)/shard_map/ppermute | solution.py:778
  33.0 7.0 %collective-permute-start.5 = (bf16[256,128]{1,0:T(8,128)(2,1)S(1)}, bf16[256,128]{1,0:T(8,128)(2,1)S(1)}, u32[]{:S(2)}, u32[]{:S(2)}) collective-permute-start(bf16[256,128]{1,0:T(8,128)(2,1)S(1)} %get-tuple-element.76), channel_id=1, source_target_pairs={{1,2},{3,4},{5,6},{7,8},{9,10},{11,12},{13,14},{15,16},{17,18},{19... | collective-permute-start | bytes 196616 | tf_op jit(solution)/shard_map/ppermute | solution.py:786
  34.1 8.6 %collective-permute-start.6 = (bf16[184,128]{1,0:T(8,128)(2,1)S(1)}, bf16[184,128]{1,0:T(8,128)(2,1)S(1)}, u32[]{:S(2)}, u32[]{:S(2)}) collective-permute-start(bf16[184,128]{1,0:T(8,128)(2,1)S(1)} %get-tuple-element.78), channel_id=1, source_target_pairs={{0,64},{64,0},{128,192},{192,128},{1,65},{65,1},{129,193},{193,129... | collective-permute-start | bytes 141320 | tf_op jit(solution)/shard_map/ppermute | solution.py:809
  35.5 7.2 %collective-permute-start.7 = (bf16[184,128]{1,0:T(8,128)(2,1)S(1)}, bf16[184,128]{1,0:T(8,128)(2,1)S(1)}, u32[]{:S(2)}, u32[]{:S(2)}) collective-permute-start(bf16[184,128]{1,0:T(8,128)(2,1)S(1)} %get-tuple-element.79), channel_id=1, source_target_pairs={{0,128},{64,192},{128,0},{192,64},{1,129},{65,193},{129,1},{193,65... | collective-permute-start | bytes 141320 | tf_op jit(solution)/shard_map/ppermute | solution.py:809
  38.1 4.6 %collective-permute-start.8 = (bf16[184,128]{1,0:T(8,128)(2,1)S(1)}, bf16[184,128]{1,0:T(8,128)(2,1)S(1)}, u32[]{:S(2)}, u32[]{:S(2)}) collective-permute-start(bf16[184,128]{1,0:T(8,128)(2,1)S(1)} %get-tuple-element.80), channel_id=1, source_target_pairs={{0,192},{64,128},{128,64},{192,0},{1,193},{65,129},{129,65},{193,1... | collective-permute-start | bytes 141320 | tf_op jit(solution)/shard_map/ppermute | solution.py:809
  42.7 7.0 %collective-permute-start.11 = (f32[184,128]{1,0:T(8,128)S(1)}, f32[184,128]{1,0:T(8,128)S(1)}, u32[]{:S(2)}, u32[]{:S(2)}) collective-permute-start(f32[184,128]{1,0:T(8,128)S(1)} %add.16.refs_0_), channel_id=1, source_target_pairs={{0,3},{1,2},{2,1},{3,0},{4,7},{5,6},{6,5},{7,4},{8,11},{9,10},{10,... | collective-permute-start | bytes 282632 | tf_op jit(solution)/shard_map/ppermute | solution.py:778
  42.8 6.9 %collective-permute-start.10 = (f32[184,128]{1,0:T(8,128)S(1)}, f32[184,128]{1,0:T(8,128)S(1)}, u32[]{:S(2)}, u32[]{:S(2)}) collective-permute-start(f32[184,128]{1,0:T(8,128)S(1)} %add.16.refs_0_), channel_id=1, source_target_pairs={{0,2},{1,3},{2,0},{3,1},{4,6},{5,7},{6,4},{7,5},{8,10},{9,11},{10,... | collective-permute-start | bytes 282632 | tf_op jit(solution)/shard_map/ppermute | solution.py:778
  43.9 5.8 %collective-permute-start.9 = (f32[184,128]{1,0:T(8,128)S(1)}, f32[184,128]{1,0:T(8,128)S(1)}, u32[]{:S(2)}, u32[]{:S(2)}) collective-permute-start(f32[184,128]{1,0:T(8,128)S(1)} %add.16.refs_0_), channel_id=1, source_target_pairs={{0,1},{1,0},{2,3},{3,2},{4,5},{5,4},{6,7},{7,6},{8,9},{9,8},{10,11... | collective-permute-start | bytes 282632 | tf_op jit(solution)/shard_map/ppermute | solution.py:778
  49.8 7.3 %collective-permute-start.14 = (bf16[184,128]{1,0:T(8,128)(2,1)S(1)}, bf16[184,128]{1,0:T(8,128)(2,1)S(1)}, u32[]{:S(2)}, u32[]{:S(2)}) collective-permute-start(bf16[184,128]{1,0:T(8,128)(2,1)S(1)} %add.17.refs_0_), channel_id=1, source_target_pairs={{0,12},{4,8},{8,4},{12,0},{16,28},{20,24},{24,20},{28,16},{1,13},{... | collective-permute-start | bytes 141320 | tf_op jit(solution)/shard_map/ppermute | solution.py:778
  50.5 6.6 %collective-permute-start.13 = (bf16[184,128]{1,0:T(8,128)(2,1)S(1)}, bf16[184,128]{1,0:T(8,128)(2,1)S(1)}, u32[]{:S(2)}, u32[]{:S(2)}) collective-permute-start(bf16[184,128]{1,0:T(8,128)(2,1)S(1)} %add.17.refs_0_), channel_id=1, source_target_pairs={{0,8},{4,12},{8,0},{12,4},{16,24},{20,28},{24,16},{28,20},{1,9},{5... | collective-permute-start | bytes 141320 | tf_op jit(solution)/shard_map/ppermute | solution.py:778
  50.5 6.6 %collective-permute-start.12 = (bf16[184,128]{1,0:T(8,128)(2,1)S(1)}, bf16[184,128]{1,0:T(8,128)(2,1)S(1)}, u32[]{:S(2)}, u32[]{:S(2)}) collective-permute-start(bf16[184,128]{1,0:T(8,128)(2,1)S(1)} %add.17.refs_0_), channel_id=1, source_target_pairs={{0,4},{4,0},{8,12},{12,8},{16,20},{20,16},{24,28},{28,24},{1,5},{5... | collective-permute-start | bytes 141320 | tf_op jit(solution)/shard_map/ppermute | solution.py:778
  53.4 6.8 %copy-start.5 = (s32[1,8]{1,0:T(1,128)S(1)}, s32[1,8]{1,0:T(1,128)}, u32[]{:S(2)}) copy-start(s32[1,8]{1,0:T(1,128)} %refs_1_.3) | copy-start | bytes 100
  57.1 6.9 %collective-permute-start.15 = (bf16[184,128]{1,0:T(8,128)(2,1)S(1)}, bf16[184,128]{1,0:T(8,128)(2,1)S(1)}, u32[]{:S(2)}, u32[]{:S(2)}) collective-permute-start(bf16[184,128]{1,0:T(8,128)(2,1)S(1)} %add.18.refs_0_), channel_id=1, source_target_pairs={{0,16},{4,20},{8,24},{12,28},{16,0},{20,4},{24,8},{28,12},{1,17},{... | collective-permute-start | bytes 141320 | tf_op jit(solution)/shard_map/ppermute | solution.py:778
  64.0 5.2 %collective-permute-start.18 = (bf16[184,128]{1,0:T(8,128)(2,1)S(1)}, bf16[184,128]{1,0:T(8,128)(2,1)S(1)}, u32[]{:S(2)}, u32[]{:S(2)}) collective-permute-start(bf16[184,128]{1,0:T(8,128)(2,1)S(1)} %add.19.refs_0_), channel_id=1, source_target_pairs={{0,192},{64,128},{128,64},{192,0},{1,193},{65,129},{129,65},{193,1... | collective-permute-start | bytes 141320 | tf_op jit(solution)/shard_map/ppermute | solution.py:778
  66.9 4.4 %collective-permute-start.17 = (bf16[184,128]{1,0:T(8,128)(2,1)S(1)}, bf16[184,128]{1,0:T(8,128)(2,1)S(1)}, u32[]{:S(2)}, u32[]{:S(2)}) collective-permute-start(bf16[184,128]{1,0:T(8,128)(2,1)S(1)} %add.19.refs_0_), channel_id=1, source_target_pairs={{0,128},{64,192},{128,0},{192,64},{1,129},{65,193},{129,1},{193,65... | collective-permute-start | bytes 141320 | tf_op jit(solution)/shard_map/ppermute | solution.py:778
  67.2 4.2 %collective-permute-start.16 = (bf16[184,128]{1,0:T(8,128)(2,1)S(1)}, bf16[184,128]{1,0:T(8,128)(2,1)S(1)}, u32[]{:S(2)}, u32[]{:S(2)}) collective-permute-start(bf16[184,128]{1,0:T(8,128)(2,1)S(1)} %add.19.refs_0_), channel_id=1, source_target_pairs={{0,64},{64,0},{128,192},{192,128},{1,65},{65,1},{129,193},{193,129... | collective-permute-start | bytes 141320 | tf_op jit(solution)/shard_map/ppermute | solution.py:778
  71.4 6.5 %collective-permute-start.19 = (bf16[4,184,128]{2,1,0:T(8,128)(2,1)S(1)}, bf16[4,184,128]{2,1,0:T(8,128)(2,1)S(1)}, u32[]{:S(2)}, u32[]{:S(2)}) collective-permute-start(bf16[4,184,128]{2,1,0:T(8,128)(2,1)S(1)} %collect.1.mine_ref), channel_id=1, source_target_pairs={{0,32},{32,0},{1,33},{33,1},{2,34},{34,2},{3,35},{35,3},{4,36},{36... | collective-permute-start | bytes 565256 | tf_op jit(solution)/shard_map/ppermute | solution.py:778

commit v6 on v5

--- a/solution.py
+++ b/solution.py
@@ -52,7 +52,7 @@
     other_ref[pl.ds(pl.multiple_of(i * SIDE, SIDE), SIDE)] = jnp.where(even, low, high)
 
 
-def faces_kernel(rank_ref, x_ref, v_ref, pair_ref, other_ref, token_ref):
+def faces_kernel(rank_ref, x_ref, v_ref, pair_ref, other_ref):
     def plane(i):
         columns = pl.ds(pl.multiple_of(i * 256, 256), 256)
         voxels = x_ref[:, columns].astype(F32).T.astype(BF16).reshape(SIDE, SIDE, LANES)
@@ -60,16 +60,15 @@
         place_faces(rank_ref, i, voxels, pair_ref, other_ref)
 
     loop(SIDE, plane, 4)
-    token_ref[...] = jnp.zeros_like(token_ref)
 
 
 def faces_call(rank, x):
     face = jax.ShapeDtypeStruct((256, LANES), BF16)
     return pl.pallas_call(
         faces_kernel,
-        out_shape=(jax.ShapeDtypeStruct((SIDE, SIDE, SIDE, LANES), BF16), face, face, TOKEN),
+        out_shape=(jax.ShapeDtypeStruct((SIDE, SIDE, SIDE, LANES), BF16), face, face),
         in_specs=[SMEM_SPEC, VMEM_SPEC],
-        out_specs=(VMEM_SPEC,) * 4,
+        out_specs=(VMEM_SPEC,) * 3,
         compiler_params=params(16),
         cost_estimate=pl.CostEstimate(flops=0, bytes_accessed=4_000_000, transcendentals=0),
         name="faces",
@@ -86,7 +85,9 @@
     return place, found
 
 
-def cot_kernel(after_ref, child_ref, rank_ref, cot_ref, own_ref, send_ref, turned_ref):
+def cot_kernel(face_ref, child_ref, rank_ref, cot_ref, own_ref, send_ref, turned_ref):
+    send_ref[1024:1280] = face_ref[...]
+
     def plane(i):
         columns = pl.ds(pl.multiple_of(i * 256, 256), 256)
         turned = cot_ref[:, columns].astype(F32).T
@@ -102,18 +103,20 @@
             out_ref[slot * 512 : (slot + 1) * 512] = block.reshape(512, LANES).astype(BF16)
 
 
-def cot_call(after, children, rank, cot):
-    blocks = jax.ShapeDtypeStruct((1024, LANES), BF16)
+def cot_call(face, children, rank, cot):
     return pl.pallas_call(
         cot_kernel,
-        out_shape=(blocks, blocks),
-        in_specs=[ANY_SPEC, SMEM_SPEC, SMEM_SPEC, VMEM_SPEC],
+        out_shape=(
+            jax.ShapeDtypeStruct((1024, LANES), BF16),
+            jax.ShapeDtypeStruct((1280, LANES), BF16),
+        ),
+        in_specs=[VMEM_SPEC, SMEM_SPEC, SMEM_SPEC, VMEM_SPEC],
         out_specs=(VMEM_SPEC,) * 2,
         scratch_shapes=[pltpu.VMEM((2, HALF, 2, HALF, 2, HALF, LANES), F32)],
         compiler_params=params(20),
         cost_estimate=pl.CostEstimate(flops=0, bytes_accessed=8_000_000, transcendentals=0),
         name="cot",
-    )(after, children, rank, cot)
+    )(face, children, rank, cot)
 
 
 def weights_kernel(
@@ -676,6 +679,22 @@
     )(after, *taps, weights, *begun)
 
 
+def stamp_kernel(sent_ref, other_ref, out_ref):
+    pass
+
+
+def stamp_call(sent, other):
+    return pl.pallas_call(
+        stamp_kernel,
+        out_shape=jax.ShapeDtypeStruct(sent.shape, sent.dtype),
+        in_specs=[ANY_SPEC] * 2,
+        out_specs=ANY_SPEC,
+        input_output_aliases={0: 0},
+        compiler_params=params(16),
+        name="stamp",
+    )(sent, other)
+
+
 def deal_kernel(rank_ref, kept_ref, came_ref, own_ref, *refs):
     share_refs, total_ref = refs[:-1], refs[-1]
     total_ref[...] = kept_ref[...] + came_ref[...].astype(F32)
@@ -779,8 +798,7 @@
 
 
 def exchange(pair, other, axis):
-    peers = lax.axis_size(axis)
-    across = [(i, (i + 1) % peers) for i in range(1, peers, 2)]
+    across = [(i, i + 1) for i in range(1, lax.axis_size(axis) - 1, 2)]
     return (
         lax.ppermute(pair, axis, swaps(axis)),
         lax.ppermute(other, axis, across + [(j, i) for i, j in across]),
@@ -791,20 +809,19 @@
     dev = ("z", "x")
     rank = lax.axis_index(("y", "core", "z", "x")).reshape(1).astype(jnp.int32)
 
-    voxels, pair, other, token = faces_call(rank, fine_input.reshape(LANES, SIDE**3))
-    own, send = cot_call(token, children, rank, coarse_cot.reshape(LANES, SIDE**3))
+    voxels, pair, other = faces_call(rank, fine_input.reshape(LANES, SIDE**3))
+    own, pair = cot_call(pair, children, rank, coarse_cot.reshape(LANES, SIDE**3))
     pair, other = exchange(pair, other, dev)
-    came = lax.ppermute(send, dev, swaps(dev))
     forward, backward, down, down_t = weights_call(conv_weight, down_weight.transpose(0, 2, 1))
     inner = inner_call(neighbours, voxels)
     octants, slope, act, *edges = forward_call(
         neighbours, rank, pair, other, inner, forward, down
     )
-    mine, other_out, grads, turned, spun = back_call(rank, own, came, down_t, slope, octants)
+    mine, other_out, grads, turned, spun = back_call(rank, own, pair, down_t, slope, octants)
     theirs, grad_other = exchange(mine, other_out, dev)
 
     kept, sent = weigh_call(rank, inner, edges, act, turned, spun)
-    (came,) = swapped(sent, "core", (1,))
+    (came,) = swapped(stamp_call(sent, grad_other), "core", (1,))
     own, *shares = deal_call(rank, kept, came)
     came = [lax.ppermute(share, "y", swaps("y", s + 1)) for s, share in enumerate(shares)]
     *taps_in, token = input_taps_call(own, neighbours, rank, grads, theirs, grad_other)
@@ -813,10 +830,10 @@
     input_grad, token = input_half_call(part, taps_in, backward, 0)
     part = add_call(token, [part, *came])
     came = swapped(part, "z", (1, 2, 3))
-    input_grad, token = input_half_call(part, taps_in, backward, 1, (input_grad,))
+    coarse, token = coarse_half_call(part, children, rank, mine, theirs, 0)
     part = add_call(token, [part, *came])
     came = swapped(part, "z", (4,))
-    coarse, token = coarse_half_call(part, children, rank, mine, theirs, 0)
+    input_grad, token = input_half_call(part, taps_in, backward, 1, (input_grad,))
     part = add_call(token, [part, *came])
     came = swapped(part, "y", (1, 2, 3))
     coarse, token = coarse_half_call(part, children, rank, mine, theirs, 1, (coarse,))

time: 79.3 us -> 83 us (1.047)
  starting transfers between devices: 36.2 us -> 38.4 us
  waiting for transfers between devices: 8.04 us -> 9.52 us
    ppermute x2, starting transfers between devices: 7.42 us -> 1.32 us  [exchange(): lax.ppermute(other, axis, across + [(j, i) for i, j in across])]
    ppermute x12, starting transfers between devices: 21 us -> 25.9 us  [swapped(): return [lax.ppermute(array, axis, swaps(axis, step)) for step in steps]]
    ppermute x2, starting transfers between devices: 3.65 us -> 7.16 us  [exchange(): lax.ppermute(pair, axis, swaps(axis))]
    ppermute x2, waiting for transfers between devices: 0.01 us -> 2.48 us  [exchange(): lax.ppermute(pair, axis, swaps(axis))]
    ppermute x2, waiting for transfers between devices: 1.85 us -> 0.01 us  [exchange(): lax.ppermute(other, axis, across + [(j, i) for i, j in across])]
    ppermute x3, waiting for transfers between devices: 0.01 us -> 1.39 us  [body(): lax.ppermute(share, 'y', swaps('y', s + 1))]
  transfers between devices with their start and end apart: 20 -> 19, of which waited for: 5 -> 7; matrix products, arithmetic and copies ran while one was open for 0% -> 0% of each run, Pallas kernels for 37% -> 25%
where the time goes in v6:
time: 83 us; the launch traced here: 82.8 us
  starting transfers between devices  38.4 us (46%)
  Pallas kernels  32 us (39%)
  waiting for transfers between devices  9.52 us (11%)
  local copies, waits for them, and re-layouts  1.97 us (2%)
  between operations  0.85 us (1%)
    ppermute x12, starting transfers between devices, swapped(): return [lax.ppermute(array, axis, swaps(axis, step)) for step in steps]  25.9 us
    pallas_call x2, Pallas kernels, input_half_call(): pl.pallas_call(functools.partial(input_half_kernel, half), grid=(1,), out...  7.27 us
    ppermute x2, starting transfers between devices, exchange(): lax.ppermute(pair, axis, swaps(axis))  7.16 us
    pallas_call x1, Pallas kernels, forward_call(): pl.pallas_call(forward_kernel, out_shape=(jax.ShapeDtypeStruct((1024, LAN...  6.87 us
    ppermute x12, waiting for transfers between devices, swapped(): return [lax.ppermute(array, axis, swaps(axis, step)) for step in steps]  5.64 us
    pallas_call x1, Pallas kernels, weigh_call(): pl.pallas_call(weigh_kernel, out_shape=(jax.ShapeDtypeStruct((GROUPS // 2...  4.69 us
    ppermute x3, starting transfers between devices, body(): lax.ppermute(share, 'y', swaps('y', s + 1))  4.01 us
    pallas_call x2, Pallas kernels, coarse_half_call(): pl.pallas_call(functools.partial(coarse_half_kernel, half), grid=(1,), ou...  3.14 us
  transfers between devices with their start and end apart: 19, of which 7 were waited for; matrix products, arithmetic and copies ran while one was open for 0% of the time, Pallas kernels for 25%

profile of v6, /device:TPU:1, one launch (start us, length us, event | category | flops | bytes accessed | tf_op | source)
XLA Modules:
  0.0 82.8 jit_solution(4623141954366211248)
XLA Ops:
  0.7 1.3 %copy-done.1 = bf16[2,64,4096]{2,1,0:T(8,128)(2,1)S(1)} copy-done((bf16[2,64,4096]{2,1,0:T(8,128)(2,1)S(1)}, bf16[2,64,4096]{2,1,0:T(8,128)(2,1)}, u32[]{:S(2)}) %copy-start.1) | copy-done | bytes 1048600
  3.2 1.3 %cot.1 = (bf16[1024,128]{1,0:T(8,128)(2,1)S(1)}, bf16[1280,128]{1,0:T(8,128)(2,1)S(1)}) custom-call(bf16[256,128]{1,0:T(8,128)(2,1)S(1)} %get-tuple-element.54.face_ref, s32[1,8]{1,0:T(1,128)S(1)} %copy-done.4, s32[1]{0:T(128)} %bitcast.rank_ref.refs_0_.refs_2_, bf16[128,4096]{1,0:T(8,128)(2,1)S(1)} %bitcast.7), custom_call_target="tpu_custom_call" | custom-call | bytes 8000000 | tf_op jit(solution)/shard_map/cot/pallas_call | solution.py:107
  4.5 2.1 %collective-permute-start = (bf16[1280,128]{1,0:T(8,128)(2,1)S(1)}, bf16[1280,128]{1,0:T(8,128)(2,1)S(1)}, u32[]{:S(2)}, u32[]{:S(2)}) collective-permute-start(bf16[1280,128]{1,0:T(8,128)(2,1)S(1)} %get-tuple-element.55), channel_id=1, source_target_pairs={{0,1},{1,0},{2,3},{3,2},{4,5},{5,4},{6,7},{7,6},{8,9},{9,8},{10,11... | collective-permute-start | bytes 983048 | tf_op jit(solution)/shard_map/ppermute | solution.py:803
  6.6 0.7 collective-permute-start.1
  8.0 2.3 %inner.1 = (bf16[18,16,16,128]{3,2,1,0:T(8,128)(2,1)S(1)}, bf16[18,16,16,128]{3,2,1,0:T(8,128)(2,1)S(1)}, bf16[18,16,16,128]{3,2,1,0:T(8,128)(2,1)S(1)}) custom-call(s32[2,26]{1,0:T(2,128)S(1)} %copy-done.6, bf16[16,16,16,128]{3,2,1,0:T(8,128)(2,1)S(1)} %get-tuple-element.50.v_ref), custom_call_target="tpu_custom_call" | custom-call | flops 1000000000 | bytes 8000000 | tf_op jit(solution)/shard_map/inner/pallas_call | solution.py:549
  10.3 2.5 %collective-permute-done.pair_ref.came_ref = bf16[1280,128]{1,0:T(8,128)(2,1)S(1)} collective-permute-done((bf16[1280,128]{1,0:T(8,128)(2,1)S(1)}, bf16[1280,128]{1,0:T(8,128)(2,1)S(1)}, u32[]{:S(2)}, u32[]{:S(2)}) %collective-permute-start) | collective-permute-done | bytes 327712 | tf_op jit(solution)/shard_map/ppermute | solution.py:803
  12.7 6.9 %forward.1 = (bf16[1024,128]{1,0:T(8,128)(2,1)S(1)}, f32[16,256,128]{2,1,0:T(8,128)S(1)}, bf16[512,1024]{1,0:T(8,128)(2,1)S(1)}, bf16[18,2,16,128]{3,2,1,0:T(8,1...) custom-call(s32[2,26]{1,0:T(2,128)S(1)} %copy-done.6, ...), custom_call_target="tpu_custom_call" | custom-call | flops 4000000000 | bytes 16000000 | tf_op jit(solution)/shard_map/forward/pallas_call | solution.py:564
  19.6 1.2 %back.1 = (bf16[1280,128]{1,0:T(8,128)(2,1)S(1)}, bf16[256,128]{1,0:T(8,128)(2,1)S(1)}, bf16[16,16,16,128]{3,2,1,0:T(8,128)(2,1)S(1)}, bf16[20,128,256]{2,1,0:T(8,128)(2,1)S(1)}, bf16[2,128,512]{2,1,0:T(8,128)(2,1)S(1)}) custom-call(s32[1]{0:T(128)} %bitcast.rank_ref.refs_0_.refs_2_, bf16[1024,128]{1,0:T(8,128)(2,1)S(1)} %get-tuple-element.63.own_ref, ...), custom_call_target="tpu_custom_call" | custom-call | flops 300000000 | bytes 8000000 | tf_op jit(solution)/shard_map/back/pallas_call | solution.py:584
  20.8 0.7 collective-permute-start.2
  21.4 5.0 %collective-permute-start.4 = (bf16[1280,128]{1,0:T(8,128)(2,1)S(1)}, bf16[1280,128]{1,0:T(8,128)(2,1)S(1)}, u32[]{:S(2)}, u32[]{:S(2)}) collective-permute-start(bf16[1280,128]{1,0:T(8,128)(2,1)S(1)} %get-tuple-element.74.refs_3_), channel_id=1, source_target_pairs={{0,1},{1,0},{2,3},{3,2},{4,5},{5,4},{6,7},{7,6},{8,9},{9,8},{10,11... | collective-permute-start | bytes 983048 | tf_op jit(solution)/shard_map/ppermute | solution.py:803
  26.5 4.7 %weigh.1 = (f32[4,184,128]{2,1,0:T(8,128)S(1)}, bf16[4,184,128]{2,1,0:T(8,128)(2,1)S(1)}) custom-call(s32[1]{0:T(128)} %bitcast.rank_ref.refs_0_.refs_2_, bf16[18,16,16,128]{3,2,1,0:T(8,128)(2,1)S(1)} %get-tuple-element.51.zero_ref.refs_1_, bf16[18,16,16,128]{3,2,1,0:T(8,128)(2,1)S(1)} %get-tuple-element.52.one_ref.refs_2_, ...), custom_call_target="tpu_custom_call" | custom-call | flops 4000000000 | bytes 10000000 | tf_op jit(solution)/shard_map/weigh/pallas_call | solution.py:605
  31.2 2.2 %collective-permute-start.3 = (bf16[4,184,128]{2,1,0:T(8,128)(2,1)S(1)}, bf16[4,184,128]{2,1,0:T(8,128)(2,1)S(1)}, u32[]{:S(2)}, u32[]{:S(2)}) collective-permute-start(bf16[4,184,128]{2,1,0:T(8,128)(2,1)S(1)} %stamp.1), channel_id=1, source_target_pairs={{0,32},{32,0},{1,33},{33,1},{2,34},{34,2},{3,35},{35,3},{4,36},{36... | collective-permute-start | bytes 565256 | tf_op jit(solution)/shard_map/ppermute | solution.py:797
  33.4 1.1 %collective-permute-done.3.came_ref = bf16[4,184,128]{2,1,0:T(8,128)(2,1)S(1)} collective-permute-done((bf16[4,184,128]{2,1,0:T(8,128)(2,1)S(1)}, bf16[4,184,128]{2,1,0:T(8,128)(2,1)S(1)}, u32[]{:S(2)}, u32[]{:S(2)}) %collective-permute-start.3) | collective-permute-done | bytes 188448 | tf_op jit(solution)/shard_map/ppermute | solution.py:797
  34.5 1.4 %collective-permute-start.5 = (bf16[184,128]{1,0:T(8,128)(2,1)S(1)}, bf16[184,128]{1,0:T(8,128)(2,1)S(1)}, u32[]{:S(2)}, u32[]{:S(2)}) collective-permute-start(bf16[184,128]{1,0:T(8,128)(2,1)S(1)} %get-tuple-element.76), channel_id=1, source_target_pairs={{0,64},{64,0},{128,192},{192,128},{1,65},{65,1},{129,193},{193,129... | collective-permute-start | bytes 141320 | tf_op jit(solution)/shard_map/ppermute | solution.py:826
  35.9 2.6 %collective-permute-start.6 = (bf16[184,128]{1,0:T(8,128)(2,1)S(1)}, bf16[184,128]{1,0:T(8,128)(2,1)S(1)}, u32[]{:S(2)}, u32[]{:S(2)}) collective-permute-start(bf16[184,128]{1,0:T(8,128)(2,1)S(1)} %get-tuple-element.77), channel_id=1, source_target_pairs={{0,128},{64,192},{128,0},{192,64},{1,129},{65,193},{129,1},{193,65... | collective-permute-start | bytes 141320 | tf_op jit(solution)/shard_map/ppermute | solution.py:826
  38.5 2.7 %input_taps.1 = (bf16[18,16,16,128]{3,2,1,0:T(8,128)(2,1)S(1)}, bf16[18,16,16,128]{3,2,1,0:T(8,128)(2,1)S(1)}, bf16[18,16,16,128]{3,2,1,0:T(8,128)(2,1)S(1)}, bf...) custom-call(f32[184,128]{1,0:T(8,128)S(1)} %get-tuple-element.72.aft, ...), custom_call_target="tpu_custom_call" | custom-call | flops 1000000000 | bytes 8000000 | tf_op jit(solution)/shard_map/input_taps/pallas_call | solution.py:638
  41.3 1.4 %collective-permute-done.7.refs_3_ = bf16[184,128]{1,0:T(8,128)(2,1)S(1)} collective-permute-done((bf16[184,128]{1,0:T(8,128)(2,1)S(1)}, bf16[184,128]{1,0:T(8,128)(2,1)S(1)}, u32[]{:S(2)}, u32[]{:S(2)}) %collective-permute-start.7) | collective-permute-done | bytes 47136 | tf_op jit(solution)/shard_map/ppermute | solution.py:826
  42.7 1.7 %collective-permute-start.10 = (f32[184,128]{1,0:T(8,128)S(1)}, f32[184,128]{1,0:T(8,128)S(1)}, u32[]{:S(2)}, u32[]{:S(2)}) collective-permute-start(f32[184,128]{1,0:T(8,128)S(1)} %add.16.refs_0_), channel_id=1, source_target_pairs={{0,3},{1,2},{2,1},{3,0},{4,7},{5,6},{6,5},{7,4},{8,11},{9,10},{10,... | collective-permute-start | bytes 282632 | tf_op jit(solution)/shard_map/ppermute | solution.py:797
  44.4 1.6 %collective-permute-start.9 = (f32[184,128]{1,0:T(8,128)S(1)}, f32[184,128]{1,0:T(8,128)S(1)}, u32[]{:S(2)}, u32[]{:S(2)}) collective-permute-start(f32[184,128]{1,0:T(8,128)S(1)} %add.16.refs_0_), channel_id=1, source_target_pairs={{0,2},{1,3},{2,0},{3,1},{4,6},{5,7},{6,4},{7,5},{8,10},{9,11},{10,... | collective-permute-start | bytes 282632 | tf_op jit(solution)/shard_map/ppermute | solution.py:797
  46.0 3.6 %input_half.2 = (bf16[128,4096]{1,0:T(8,128)(2,1)}, f32[8,128]{1,0:T(8,128)S(1)}) custom-call(f32[184,128]{1,0:T(8,128)S(1)} %add.16.refs_0_, bf16[18,16,16,128]{3,2,1,0:T(8,128)(2,1)S(1)} %get-tuple-element.79.refs_1_, bf16[18,16,16,128]{3,2,1,0:T(8,128)(2,1)S(1)} %get-tuple-element.80.refs_2_, bf16[18,16,16,128]{3,2,1,0:T(8,128)(2,1)S(1)} %get-tuple-element.81.refs_3_, ...), custom_call_target="tpu_custom_call" | custom-call | flops 2500000000 | bytes 6000000 | tf_op jit(solution)/shard_map/input_half/pallas_call | solution.py:663
  49.7 7.1 %collective-permute-start.13 = (bf16[184,128]{1,0:T(8,128)(2,1)S(1)}, bf16[184,128]{1,0:T(8,128)(2,1)S(1)}, u32[]{:S(2)}, u32[]{:S(2)}) collective-permute-start(bf16[184,128]{1,0:T(8,128)(2,1)S(1)} %add.17.refs_0_), channel_id=1, source_target_pairs={{0,12},{4,8},{8,4},{12,0},{16,28},{20,24},{24,20},{28,16},{1,13},{... | collective-permute-start | bytes 141320 | tf_op jit(solution)/shard_map/ppermute | solution.py:797
  57.2 1.6 %coarse_half.2 = (bf16[128,4096]{1,0:T(8,128)(2,1)}, f32[8,128]{1,0:T(8,128)S(1)}) custom-call(bf16[184,128]{1,0:T(8,128)(2,1)S(1)} %add.17.refs_0_, s32[1,8]{1,0:T(1,128)S(1)} %copy-done.5, s32[1]{0:T(128)} %bitcast.rank_ref.refs_0_.refs_2_, bf16[1280,128]{1,0:T(8,128)(2,1)S(1)} %get-tuple-element.74.refs_3_, ...), custom_call_target="tpu_custom_call" | custom-call | bytes 4000000 | tf_op jit(solution)/shard_map/coarse_half/pallas_call | solution.py:191
  58.8 1.9 %collective-permute-done.12.refs_2_ = bf16[184,128]{1,0:T(8,128)(2,1)S(1)} collective-permute-done((bf16[184,128]{1,0:T(8,128)(2,1)S(1)}, bf16[184,128]{1,0:T(8,128)(2,1)S(1)}, u32[]{:S(2)}, u32[]{:S(2)}) %collective-permute-start.12) | collective-permute-done | bytes 47136 | tf_op jit(solution)/shard_map/ppermute | solution.py:797
  60.7 3.1 %collective-permute-start.14 = (bf16[184,128]{1,0:T(8,128)(2,1)S(1)}, bf16[184,128]{1,0:T(8,128)(2,1)S(1)}, u32[]{:S(2)}, u32[]{:S(2)}) collective-permute-start(bf16[184,128]{1,0:T(8,128)(2,1)S(1)} %add.18.refs_0_), channel_id=1, source_target_pairs={{0,16},{4,20},{8,24},{12,28},{16,0},{20,4},{24,8},{28,12},{1,17},{... | collective-permute-start | bytes 141320 | tf_op jit(solution)/shard_map/ppermute | solution.py:797
  63.8 3.6 %input_half.3 = (bf16[128,4096]{1,0:T(8,128)(2,1)}, f32[8,128]{1,0:T(8,128)S(1)}) custom-call(bf16[184,128]{1,0:T(8,128)(2,1)S(1)} %add.18.refs_0_, bf16[18,16,16,128]{3,2,1,0:T(8,128)(2,1)S(1)} %get-tuple-element.79.refs_1_, bf16[18,16,16,128]{3,2,1,0:T(8,128)(2,1)S(1)} %get-tuple-element.80.refs_2_, ...), custom_call_target="tpu_custom_call", output_to_operand_aliasing={{0}: (8, {})} | custom-call | flops 2500000000 | bytes 6000000 | tf_op jit(solution)/shard_map/input_half/pallas_call | solution.py:663
  67.7 1.8 %collective-permute-start.17 = (bf16[184,128]{1,0:T(8,128)(2,1)S(1)}, bf16[184,128]{1,0:T(8,128)(2,1)S(1)}, u32[]{:S(2)}, u32[]{:S(2)}) collective-permute-start(bf16[184,128]{1,0:T(8,128)(2,1)S(1)} %add.19.refs_0_), channel_id=1, source_target_pairs={{0,192},{64,128},{128,64},{192,0},{1,193},{65,129},{129,65},{193,1... | collective-permute-start | bytes 141320 | tf_op jit(solution)/shard_map/ppermute | solution.py:797
  70.1 0.9 %collective-permute-start.15 = (bf16[184,128]{1,0:T(8,128)(2,1)S(1)}, bf16[184,128]{1,0:T(8,128)(2,1)S(1)}, u32[]{:S(2)}, u32[]{:S(2)}) collective-permute-start(bf16[184,128]{1,0:T(8,128)(2,1)S(1)} %add.19.refs_0_), channel_id=1, source_target_pairs={{0,64},{64,0},{128,192},{192,128},{1,65},{65,1},{129,193},{193,129... | collective-permute-start | bytes 141320 | tf_op jit(solution)/shard_map/ppermute | solution.py:797
  71.0 1.6 %coarse_half.3 = (bf16[128,4096]{1,0:T(8,128)(2,1)}, f32[8,128]{1,0:T(8,128)S(1)}) custom-call(bf16[184,128]{1,0:T(8,128)(2,1)S(1)} %add.19.refs_0_, s32[1,8]{1,0:T(1,128)S(1)} %copy-done.5, s32[1]{0:T(128)} %bitcast.rank_ref.refs_0_.refs_2_, bf16[1280,128]{1,0:T(8,128)(2,1)S(1)} %get-tuple-element.74.refs_3_, ...), custom_call_target="tpu_custom_call", output_to_operand_aliasing={{0}: (5, {})} | custom-call | bytes 4000000 | tf_op jit(solution)/shard_map/coarse_half/pallas_call | solution.py:191
  72.6 1.3 %collective-permute-done.16.refs_2_ = bf16[184,128]{1,0:T(8,128)(2,1)S(1)} collective-permute-done((bf16[184,128]{1,0:T(8,128)(2,1)S(1)}, bf16[184,128]{1,0:T(8,128)(2,1)S(1)}, u32[]{:S(2)}, u32[]{:S(2)}) %collective-permute-start.16) | collective-permute-done | bytes 47136 | tf_op jit(solution)/shard_map/ppermute | solution.py:797
  74.0 6.5 %collective-permute-start.18 = (bf16[4,184,128]{2,1,0:T(8,128)(2,1)S(1)}, bf16[4,184,128]{2,1,0:T(8,128)(2,1)S(1)}, u32[]{:S(2)}, u32[]{:S(2)}) collective-permute-start(bf16[4,184,128]{2,1,0:T(8,128)(2,1)S(1)} %collect.1.mine_ref), channel_id=1, source_target_pairs={{0,32},{32,0},{1,33},{33,1},{2,34},{34,2},{3,35},{35,3},{4,36},{36... | collective-permute-start | bytes 565256 | tf_op jit(solution)/shard_map/ppermute | solution.py:797
  80.5 1.1 %collective-permute-done.18.theirs_ref = bf16[4,184,128]{2,1,0:T(8,128)(2,1)S(1)} collective-permute-done((bf16[4,184,128]{2,1,0:T(8,128)(2,1)S(1)}, bf16[4,184,128]{2,1,0:T(8,128)(2,1)S(1)}, u32[]{:S(2)}, u32[]{:S(2)}) %collective-permute-start.18) | collective-permute-done | bytes 188448 | tf_op jit(solution)/shard_map/ppermute | solution.py:797
  81.5 1.3 %split.1 = (f32[27,64,64]{2,1,0:T(8,128)}, f32[8,64,128]{2,1,0:T(8,128)}) custom-call(s32[1]{0:T(128)} %bitcast.rank_ref.refs_0_.refs_2_, bf16[4,184,128]{2,1,0:T(8,128)(2,1)S(1)} %collect.1.mine_ref, bf16[4,184,128]{2,1,0:T(8,128)(2,1)S(1)} %collective-permute-done.18.theirs_ref), custom_call_target="tpu_custom_call" | custom-call | tf_op jit(solution)/shard_map/split/pallas_call | solution.py:778
  (40 shorter events, 3.4 us)
Async XLA Ops:
  0.6 1.9 %copy-start = (bf16[1,128,4096]{2,1,0:T(8,128)(2,1)S(1)}, bf16[1,128,4096]{2,1,0:T(8,128)(2,1)}, u32[]{:S(2)}) copy-start(bf16[1,128,4096]{2,1,0:T(8,128)(2,1)} %param.9) | copy-start | bytes 3145732
  0.7 1.3 %copy-start.1 = (bf16[2,64,4096]{2,1,0:T(8,128)(2,1)S(1)}, bf16[2,64,4096]{2,1,0:T(8,128)(2,1)}, u32[]{:S(2)}) copy-start(bf16[2,64,4096]{2,1,0:T(8,128)(2,1)} %param.6) | copy-start | bytes 3145732
  2.0 5.3 %copy-start.2 = (bf16[27,64,64]{2,1,0:T(8,128)(2,1)S(1)}, bf16[27,64,64]{2,1,0:T(8,128)(2,1)}, u32[]{:S(2)}) copy-start(bf16[27,64,64]{2,1,0:T(8,128)(2,1)} %conv_ref.1) | copy-start | bytes 663556
  2.0 5.4 %copy-start.3 = (bf16[8,128,64]{1,2,0:T(8,128)(2,1)S(1)}, bf16[8,128,64]{1,2,0:T(8,128)(2,1)}, u32[]{:S(2)}) copy-start(bf16[8,128,64]{1,2,0:T(8,128)(2,1)} %param.8) | copy-start | bytes 393220
  2.5 0.7 copy-start.4
  3.2 4.8 %copy-start.6 = (s32[2,26]{1,0:T(2,128)S(1)}, s32[2,26]{1,0:T(2,128)}, u32[]{:S(2)}) copy-start(s32[2,26]{1,0:T(2,128)} %near_ref.5) | copy-start | bytes 628
  4.5 8.2 %collective-permute-start = (bf16[1280,128]{1,0:T(8,128)(2,1)S(1)}, bf16[1280,128]{1,0:T(8,128)(2,1)S(1)}, u32[]{:S(2)}, u32[]{:S(2)}) collective-permute-start(bf16[1280,128]{1,0:T(8,128)(2,1)S(1)} %get-tuple-element.55), channel_id=1, source_target_pairs={{0,1},{1,0},{2,3},{3,2},{4,5},{5,4},{6,7},{7,6},{8,9},{9,8},{10,11... | collective-permute-start | bytes 983048 | tf_op jit(solution)/shard_map/ppermute | solution.py:803
  6.6 3.6 %collective-permute-start.1 = (bf16[256,128]{1,0:T(8,128)(2,1)S(1)}, bf16[256,128]{1,0:T(8,128)(2,1)S(1)}, u32[]{:S(2)}, u32[]{:S(2)}) collective-permute-start(bf16[256,128]{1,0:T(8,128)(2,1)S(1)} %get-tuple-element.56), channel_id=1, source_target_pairs={{1,2},{3,4},{5,6},{7,8},{9,10},{11,12},{13,14},{15,16},{17,18},{19... | collective-permute-start | bytes 196616 | tf_op jit(solution)/shard_map/ppermute | solution.py:804
  20.8 10.4 %collective-permute-start.2 = (bf16[256,128]{1,0:T(8,128)(2,1)S(1)}, bf16[256,128]{1,0:T(8,128)(2,1)S(1)}, u32[]{:S(2)}, u32[]{:S(2)}) collective-permute-start(bf16[256,128]{1,0:T(8,128)(2,1)S(1)} %get-tuple-element.71), channel_id=1, source_target_pairs={{1,2},{3,4},{5,6},{7,8},{9,10},{11,12},{13,14},{15,16},{17,18},{19... | collective-permute-start | bytes 196616 | tf_op jit(solution)/shard_map/ppermute | solution.py:804
  21.4 17.1 %collective-permute-start.4 = (bf16[1280,128]{1,0:T(8,128)(2,1)S(1)}, bf16[1280,128]{1,0:T(8,128)(2,1)S(1)}, u32[]{:S(2)}, u32[]{:S(2)}) collective-permute-start(bf16[1280,128]{1,0:T(8,128)(2,1)S(1)} %get-tuple-element.74.refs_3_), channel_id=1, source_target_pairs={{0,1},{1,0},{2,3},{3,2},{4,5},{5,4},{6,7},{7,6},{8,9},{9,8},{10,11... | collective-permute-start | bytes 983048 | tf_op jit(solution)/shard_map/ppermute | solution.py:803
  31.2 3.3 %collective-permute-start.3 = (bf16[4,184,128]{2,1,0:T(8,128)(2,1)S(1)}, bf16[4,184,128]{2,1,0:T(8,128)(2,1)S(1)}, u32[]{:S(2)}, u32[]{:S(2)}) collective-permute-start(bf16[4,184,128]{2,1,0:T(8,128)(2,1)S(1)} %stamp.1), channel_id=1, source_target_pairs={{0,32},{32,0},{1,33},{33,1},{2,34},{34,2},{3,35},{35,3},{4,36},{36... | collective-permute-start | bytes 565256 | tf_op jit(solution)/shard_map/ppermute | solution.py:797
  34.5 6.7 %collective-permute-start.5 = (bf16[184,128]{1,0:T(8,128)(2,1)S(1)}, bf16[184,128]{1,0:T(8,128)(2,1)S(1)}, u32[]{:S(2)}, u32[]{:S(2)}) collective-permute-start(bf16[184,128]{1,0:T(8,128)(2,1)S(1)} %get-tuple-element.76), channel_id=1, source_target_pairs={{0,64},{64,0},{128,192},{192,128},{1,65},{65,1},{129,193},{193,129... | collective-permute-start | bytes 141320 | tf_op jit(solution)/shard_map/ppermute | solution.py:826
  35.9 5.4 %collective-permute-start.6 = (bf16[184,128]{1,0:T(8,128)(2,1)S(1)}, bf16[184,128]{1,0:T(8,128)(2,1)S(1)}, u32[]{:S(2)}, u32[]{:S(2)}) collective-permute-start(bf16[184,128]{1,0:T(8,128)(2,1)S(1)} %get-tuple-element.77), channel_id=1, source_target_pairs={{0,128},{64,192},{128,0},{192,64},{1,129},{65,193},{129,1},{193,65... | collective-permute-start | bytes 141320 | tf_op jit(solution)/shard_map/ppermute | solution.py:826
  38.5 4.1 %collective-permute-start.7 = (bf16[184,128]{1,0:T(8,128)(2,1)S(1)}, bf16[184,128]{1,0:T(8,128)(2,1)S(1)}, u32[]{:S(2)}, u32[]{:S(2)}) collective-permute-start(bf16[184,128]{1,0:T(8,128)(2,1)S(1)} %get-tuple-element.78), channel_id=1, source_target_pairs={{0,192},{64,128},{128,64},{192,0},{1,193},{65,129},{129,65},{193,1... | collective-permute-start | bytes 141320 | tf_op jit(solution)/shard_map/ppermute | solution.py:826
  42.7 7.0 %collective-permute-start.10 = (f32[184,128]{1,0:T(8,128)S(1)}, f32[184,128]{1,0:T(8,128)S(1)}, u32[]{:S(2)}, u32[]{:S(2)}) collective-permute-start(f32[184,128]{1,0:T(8,128)S(1)} %add.16.refs_0_), channel_id=1, source_target_pairs={{0,3},{1,2},{2,1},{3,0},{4,7},{5,6},{6,5},{7,4},{8,11},{9,10},{10,... | collective-permute-start | bytes 282632 | tf_op jit(solution)/shard_map/ppermute | solution.py:797
  44.4 5.3 %collective-permute-start.9 = (f32[184,128]{1,0:T(8,128)S(1)}, f32[184,128]{1,0:T(8,128)S(1)}, u32[]{:S(2)}, u32[]{:S(2)}) collective-permute-start(f32[184,128]{1,0:T(8,128)S(1)} %add.16.refs_0_), channel_id=1, source_target_pairs={{0,2},{1,3},{2,0},{3,1},{4,6},{5,7},{6,4},{7,5},{8,10},{9,11},{10,... | collective-permute-start | bytes 282632 | tf_op jit(solution)/shard_map/ppermute | solution.py:797
  46.0 3.7 %collective-permute-start.8 = (f32[184,128]{1,0:T(8,128)S(1)}, f32[184,128]{1,0:T(8,128)S(1)}, u32[]{:S(2)}, u32[]{:S(2)}) collective-permute-start(f32[184,128]{1,0:T(8,128)S(1)} %add.16.refs_0_), channel_id=1, source_target_pairs={{0,1},{1,0},{2,3},{3,2},{4,5},{5,4},{6,7},{7,6},{8,9},{9,8},{10,11... | collective-permute-start | bytes 282632 | tf_op jit(solution)/shard_map/ppermute | solution.py:797
  46.0 11.2 %copy-start.5 = (s32[1,8]{1,0:T(1,128)S(1)}, s32[1,8]{1,0:T(1,128)}, u32[]{:S(2)}) copy-start(s32[1,8]{1,0:T(1,128)} %refs_1_.3) | copy-start | bytes 100
  49.7 9.1 %collective-permute-start.13 = (bf16[184,128]{1,0:T(8,128)(2,1)S(1)}, bf16[184,128]{1,0:T(8,128)(2,1)S(1)}, u32[]{:S(2)}, u32[]{:S(2)}) collective-permute-start(bf16[184,128]{1,0:T(8,128)(2,1)S(1)} %add.17.refs_0_), channel_id=1, source_target_pairs={{0,12},{4,8},{8,4},{12,0},{16,28},{20,24},{24,20},{28,16},{1,13},{... | collective-permute-start | bytes 141320 | tf_op jit(solution)/shard_map/ppermute | solution.py:797
  56.8 3.8 %collective-permute-start.12 = (bf16[184,128]{1,0:T(8,128)(2,1)S(1)}, bf16[184,128]{1,0:T(8,128)(2,1)S(1)}, u32[]{:S(2)}, u32[]{:S(2)}) collective-permute-start(bf16[184,128]{1,0:T(8,128)(2,1)S(1)} %add.17.refs_0_), channel_id=1, source_target_pairs={{0,8},{4,12},{8,0},{12,4},{16,24},{20,28},{24,16},{28,20},{1,9},{5... | collective-permute-start | bytes 141320 | tf_op jit(solution)/shard_map/ppermute | solution.py:797
  56.8 3.8 %collective-permute-start.11 = (bf16[184,128]{1,0:T(8,128)(2,1)S(1)}, bf16[184,128]{1,0:T(8,128)(2,1)S(1)}, u32[]{:S(2)}, u32[]{:S(2)}) collective-permute-start(bf16[184,128]{1,0:T(8,128)(2,1)S(1)} %add.17.refs_0_), channel_id=1, source_target_pairs={{0,4},{4,0},{8,12},{12,8},{16,20},{20,16},{24,28},{28,24},{1,5},{5... | collective-permute-start | bytes 141320 | tf_op jit(solution)/shard_map/ppermute | solution.py:797
  60.7 7.0 %collective-permute-start.14 = (bf16[184,128]{1,0:T(8,128)(2,1)S(1)}, bf16[184,128]{1,0:T(8,128)(2,1)S(1)}, u32[]{:S(2)}, u32[]{:S(2)}) collective-permute-start(bf16[184,128]{1,0:T(8,128)(2,1)S(1)} %add.18.refs_0_), channel_id=1, source_target_pairs={{0,16},{4,20},{8,24},{12,28},{16,0},{20,4},{24,8},{28,12},{1,17},{... | collective-permute-start | bytes 141320 | tf_op jit(solution)/shard_map/ppermute | solution.py:797
  67.7 4.9 %collective-permute-start.17 = (bf16[184,128]{1,0:T(8,128)(2,1)S(1)}, bf16[184,128]{1,0:T(8,128)(2,1)S(1)}, u32[]{:S(2)}, u32[]{:S(2)}) collective-permute-start(bf16[184,128]{1,0:T(8,128)(2,1)S(1)} %add.19.refs_0_), channel_id=1, source_target_pairs={{0,192},{64,128},{128,64},{192,0},{1,193},{65,129},{129,65},{193,1... | collective-permute-start | bytes 141320 | tf_op jit(solution)/shard_map/ppermute | solution.py:797
  69.5 4.4 %collective-permute-start.16 = (bf16[184,128]{1,0:T(8,128)(2,1)S(1)}, bf16[184,128]{1,0:T(8,128)(2,1)S(1)}, u32[]{:S(2)}, u32[]{:S(2)}) collective-permute-start(bf16[184,128]{1,0:T(8,128)(2,1)S(1)} %add.19.refs_0_), channel_id=1, source_target_pairs={{0,128},{64,192},{128,0},{192,64},{1,129},{65,193},{129,1},{193,65... | collective-permute-start | bytes 141320 | tf_op jit(solution)/shard_map/ppermute | solution.py:797
  70.1 3.8 %collective-permute-start.15 = (bf16[184,128]{1,0:T(8,128)(2,1)S(1)}, bf16[184,128]{1,0:T(8,128)(2,1)S(1)}, u32[]{:S(2)}, u32[]{:S(2)}) collective-permute-start(bf16[184,128]{1,0:T(8,128)(2,1)S(1)} %add.19.refs_0_), channel_id=1, source_target_pairs={{0,64},{64,0},{128,192},{192,128},{1,65},{65,1},{129,193},{193,129... | collective-permute-start | bytes 141320 | tf_op jit(solution)/shard_map/ppermute | solution.py:797
  74.0 7.5 %collective-permute-start.18 = (bf16[4,184,128]{2,1,0:T(8,128)(2,1)S(1)}, bf16[4,184,128]{2,1,0:T(8,128)(2,1)S(1)}, u32[]{:S(2)}, u32[]{:S(2)}) collective-permute-start(bf16[4,184,128]{2,1,0:T(8,128)(2,1)S(1)} %collect.1.mine_ref), channel_id=1, source_target_pairs={{0,32},{32,0},{1,33},{33,1},{2,34},{34,2},{3,35},{35,3},{4,36},{36... | collective-permute-start | bytes 565256 | tf_op jit(solution)/shard_map/ppermute | solution.py:797

commit v7 on v5

--- a/solution.py
+++ b/solution.py
@@ -472,7 +472,7 @@
     total_ref[...] = jnp.zeros_like(total_ref)
 
     def weigh(g, carry):
-        planes = [3 * g + p for p in range(3)]
+        planes = [6 * g + p for p in range(6)]
         for n, brick in enumerate((zero, one)):
             lhs = [
                 jnp.concatenate(
@@ -498,7 +498,7 @@
             )
         return carry
 
-    lax.fori_loop(0, (SIDE + 2) // 3, weigh, 0)
+    lax.fori_loop(0, (SIDE + 2) // 6, weigh, 0)
     lower = low_half((192, LANES))
     last = []
     for b in range(3):
@@ -778,13 +778,17 @@
     return [lax.ppermute(array, axis, swaps(axis, step)) for step in steps]
 
 
-def exchange(pair, other, axis):
-    peers = lax.axis_size(axis)
-    across = [(i, (i + 1) % peers) for i in range(1, peers, 2)]
-    return (
-        lax.ppermute(pair, axis, swaps(axis)),
-        lax.ppermute(other, axis, across + [(j, i) for i, j in across]),
-    )
+def exchange(pair, other):
+    bricks = ("y", "core", "z", "x")
+    rows = lax.axis_size(("z", "x"))
+    across = []
+    for device in range(lax.axis_size(bricks)):
+        row = device % rows
+        if row in (0, rows - 1):
+            across.append((device, device ^ rows))
+        else:
+            across.append((device, device + 1 if row % 2 else device - 1))
+    return lax.ppermute(pair, ("z", "x"), swaps(("z", "x"))), lax.ppermute(other, bricks, across)
 
 
 def body(fine_input, conv_weight, down_weight, coarse_cot, neighbours, children):
@@ -793,7 +797,7 @@
 
     voxels, pair, other, token = faces_call(rank, fine_input.reshape(LANES, SIDE**3))
     own, send = cot_call(token, children, rank, coarse_cot.reshape(LANES, SIDE**3))
-    pair, other = exchange(pair, other, dev)
+    pair, other = exchange(pair, other)
     came = lax.ppermute(send, dev, swaps(dev))
     forward, backward, down, down_t = weights_call(conv_weight, down_weight.transpose(0, 2, 1))
     inner = inner_call(neighbours, voxels)
@@ -801,7 +805,7 @@
         neighbours, rank, pair, other, inner, forward, down
     )
     mine, other_out, grads, turned, spun = back_call(rank, own, came, down_t, slope, octants)
-    theirs, grad_other = exchange(mine, other_out, dev)
+    theirs, grad_other = exchange(mine, other_out)
 
     kept, sent = weigh_call(rank, inner, edges, act, turned, spun)
     (came,) = swapped(sent, "core", (1,))
@@ -813,10 +817,10 @@
     input_grad, token = input_half_call(part, taps_in, backward, 0)
     part = add_call(token, [part, *came])
     came = swapped(part, "z", (1, 2, 3))
-    input_grad, token = input_half_call(part, taps_in, backward, 1, (input_grad,))
+    coarse, token = coarse_half_call(part, children, rank, mine, theirs, 0)
     part = add_call(token, [part, *came])
     came = swapped(part, "z", (4,))
-    coarse, token = coarse_half_call(part, children, rank, mine, theirs, 0)
+    input_grad, token = input_half_call(part, taps_in, backward, 1, (input_grad,))
     part = add_call(token, [part, *came])
     came = swapped(part, "y", (1, 2, 3))
     coarse, token = coarse_half_call(part, children, rank, mine, theirs, 1, (coarse,))

time: 79.3 us -> 77.4 us (0.976)
  starting transfers between devices: 36.2 us -> 35.1 us
    ppermute x4, starting transfers between devices: 11.1 us -> 4.25 us  [the longest x2 2.85 us: exchange(): lax.ppermute(pair, ('z', 'x'), swaps(('z', 'x')))]
    ppermute x12, starting transfers between devices: 21 us -> 25.9 us  [swapped(): return [lax.ppermute(array, axis, swaps(axis, step)) for step in steps]]
    ppermute x4, waiting for transfers between devices: 1.86 us -> 0.01 us  [the longest x2 0.01 us: exchange(): lax.ppermute(pair, ('z', 'x'), swaps(('z', 'x')))]
    ppermute x3, waiting for transfers between devices: 0.01 us -> 1.38 us  [body(): lax.ppermute(share, 'y', swaps('y', s + 1))]
    ppermute x1, starting transfers between devices: 0.09 us -> 0.91 us  [body(): came = lax.ppermute(send, dev, swaps(dev))]
  transfers between devices with their start and end apart: 20 -> 20, of which waited for: 5 -> 6; matrix products, arithmetic and copies ran while one was open for 0% -> 0% of each run, Pallas kernels for 37% -> 37%
where the time goes in v7:
time: 77.4 us; the launch traced here: 77.3 us
  starting transfers between devices  35.1 us (45%)
  Pallas kernels  31.5 us (41%)
  waiting for transfers between devices  7.86 us (10%)
  local copies, waits for them, and re-layouts  1.98 us (3%)
  between operations  0.81 us (1%)
    ppermute x12, starting transfers between devices, swapped(): return [lax.ppermute(array, axis, swaps(axis, step)) for step in steps]  25.9 us
    pallas_call x2, Pallas kernels, input_half_call(): pl.pallas_call(functools.partial(input_half_kernel, half), grid=(1,), out...  7.28 us
    pallas_call x1, Pallas kernels, forward_call(): pl.pallas_call(forward_kernel, out_shape=(jax.ShapeDtypeStruct((1024, LAN...  6.88 us
    ppermute x12, waiting for transfers between devices, swapped(): return [lax.ppermute(array, axis, swaps(axis, step)) for step in steps]  6.47 us
    pallas_call x1, Pallas kernels, weigh_call(): pl.pallas_call(weigh_kernel, out_shape=(jax.ShapeDtypeStruct((GROUPS // 2...  4.17 us
    ppermute x3, starting transfers between devices, body(): lax.ppermute(share, 'y', swaps('y', s + 1))  4 us
    pallas_call x2, Pallas kernels, coarse_half_call(): pl.pallas_call(functools.partial(coarse_half_kernel, half), grid=(1,), ou...  3.15 us
    ppermute x2, starting transfers between devices, exchange(): lax.ppermute(pair, ('z', 'x'), swaps(('z', 'x')))  2.85 us
  transfers between devices with their start and end apart: 20, of which 6 were waited for; matrix products, arithmetic and copies ran while one was open for 0% of the time, Pallas kernels for 37%

profile of v7, /device:TPU:1, one launch (start us, length us, event | category | flops | bytes accessed | tf_op | source)
XLA Modules:
  0.0 77.3 jit_solution(6673326385003916565)
XLA Ops:
  0.7 1.3 %copy-done.1 = bf16[2,64,4096]{2,1,0:T(8,128)(2,1)S(1)} copy-done((bf16[2,64,4096]{2,1,0:T(8,128)(2,1)S(1)}, bf16[2,64,4096]{2,1,0:T(8,128)(2,1)}, u32[]{:S(2)}) %copy-start.1) | copy-done | bytes 1048600
  2.5 2.1 %collective-permute-start = (bf16[256,128]{1,0:T(8,128)(2,1)S(1)}, bf16[256,128]{1,0:T(8,128)(2,1)S(1)}, u32[]{:S(2)}, u32[]{:S(2)}) collective-permute-start(bf16[256,128]{1,0:T(8,128)(2,1)S(1)} %get-tuple-element.55), channel_id=1, source_target_pairs={{0,1},{1,0},{2,3},{3,2},{4,5},{5,4},{6,7},{7,6},{8,9},{9,8},{10,11... | collective-permute-start | bytes 196616 | tf_op jit(solution)/shard_map/ppermute | solution.py:791
  4.7 1.3 %collective-permute-start.1 = (bf16[256,128]{1,0:T(8,128)(2,1)S(1)}, bf16[256,128]{1,0:T(8,128)(2,1)S(1)}, u32[]{:S(2)}, u32[]{:S(2)}) collective-permute-start(bf16[256,128]{1,0:T(8,128)(2,1)S(1)} %get-tuple-element.56), channel_id=1, source_target_pairs={{0,32},{1,2},{2,1},{3,4},{4,3},{5,6},{6,5},{7,8},{8,7},{9,10},{10,... | collective-permute-start | bytes 196616 | tf_op jit(solution)/shard_map/ppermute | solution.py:791
  6.6 1.3 %cot.1 = (bf16[1024,128]{1,0:T(8,128)(2,1)S(1)}, bf16[1024,128]{1,0:T(8,128)(2,1)S(1)}) custom-call(f32[8,128]{1,0:T(8,128)S(1)} %get-tuple-element.63.after_ref, s32[1,8]{1,0:T(1,128)S(1)} %copy-done.4, s32[1]{0:T(128)} %bitcast.rank_ref.refs_0_.refs_2_, bf16[128,4096]{1,0:T(8,128)(2,1)S(1)} %bitcast.7), custom_call_target="tpu_custom_call" | custom-call | bytes 8000000 | tf_op jit(solution)/shard_map/cot/pallas_call | solution.py:107
  7.9 0.9 %collective-permute-start.2 = (bf16[1024,128]{1,0:T(8,128)(2,1)S(1)}, bf16[1024,128]{1,0:T(8,128)(2,1)S(1)}, u32[]{:S(2)}, u32[]{:S(2)}) collective-permute-start(bf16[1024,128]{1,0:T(8,128)(2,1)S(1)} %get-tuple-element.65), channel_id=1, source_target_pairs={{0,1},{1,0},{2,3},{3,2},{4,5},{5,4},{6,7},{7,6},{8,9},{9,8},{10,11... | collective-permute-start | bytes 786440 | tf_op jit(solution)/shard_map/ppermute | solution.py:801
  9.5 2.3 %inner.1 = (bf16[18,16,16,128]{3,2,1,0:T(8,128)(2,1)S(1)}, bf16[18,16,16,128]{3,2,1,0:T(8,128)(2,1)S(1)}, bf16[18,16,16,128]{3,2,1,0:T(8,128)(2,1)S(1)}) custom-call(s32[2,26]{1,0:T(2,128)S(1)} %copy-done.6, bf16[16,16,16,128]{3,2,1,0:T(8,128)(2,1)S(1)} %get-tuple-element.51.v_ref), custom_call_target="tpu_custom_call" | custom-call | flops 1000000000 | bytes 8000000 | tf_op jit(solution)/shard_map/inner/pallas_call | solution.py:546
  11.8 6.9 %forward.1 = (bf16[1024,128]{1,0:T(8,128)(2,1)S(1)}, f32[16,256,128]{2,1,0:T(8,128)S(1)}, bf16[512,1024]{1,0:T(8,128)(2,1)S(1)}, bf16[18,2,16,128]{3,2,1,0:T(8,1...) custom-call(s32[2,26]{1,0:T(2,128)S(1)} %copy-done.6, ...), custom_call_target="tpu_custom_call" | custom-call | flops 4000000000 | bytes 16000000 | tf_op jit(solution)/shard_map/forward/pallas_call | solution.py:561
  18.7 1.2 %back.1 = (bf16[1280,128]{1,0:T(8,128)(2,1)S(1)}, bf16[256,128]{1,0:T(8,128)(2,1)S(1)}, bf16[16,16,16,128]{3,2,1,0:T(8,128)(2,1)S(1)}, bf16[20,128,256]{2,1,0:T(8,128)(2,1)S(1)}, bf16[2,128,512]{2,1,0:T(8,128)(2,1)S(1)}) custom-call(s32[1]{0:T(128)} %bitcast.rank_ref.refs_0_.refs_2_, bf16[1024,128]{1,0:T(8,128)(2,1)S(1)} %get-tuple-element.64.own_ref, ...), custom_call_target="tpu_custom_call" | custom-call | flops 300000000 | bytes 8000000 | tf_op jit(solution)/shard_map/back/pallas_call | solution.py:581
  19.9 0.7 collective-permute-start.4
  20.6 4.2 %weigh.1 = (f32[4,184,128]{2,1,0:T(8,128)S(1)}, bf16[4,184,128]{2,1,0:T(8,128)(2,1)S(1)}) custom-call(s32[1]{0:T(128)} %bitcast.rank_ref.refs_0_.refs_2_, bf16[18,16,16,128]{3,2,1,0:T(8,128)(2,1)S(1)} %get-tuple-element.52.zero_ref.refs_1_, bf16[18,16,16,128]{3,2,1,0:T(8,128)(2,1)S(1)} %get-tuple-element.53.one_ref.refs_2_, ...), custom_call_target="tpu_custom_call" | custom-call | flops 4000000000 | bytes 10000000 | tf_op jit(solution)/shard_map/weigh/pallas_call | solution.py:602
  24.8 1.0 %collective-permute-start.3 = (bf16[4,184,128]{2,1,0:T(8,128)(2,1)S(1)}, bf16[4,184,128]{2,1,0:T(8,128)(2,1)S(1)}, u32[]{:S(2)}, u32[]{:S(2)}) collective-permute-start(bf16[4,184,128]{2,1,0:T(8,128)(2,1)S(1)} %get-tuple-element.72), channel_id=1, source_target_pairs={{0,32},{32,0},{1,33},{33,1},{2,34},{34,2},{3,35},{35,3},{4,36},{36... | collective-permute-start | bytes 565256 | tf_op jit(solution)/shard_map/ppermute | solution.py:778
  25.8 1.0 %collective-permute-done.3.came_ref = bf16[4,184,128]{2,1,0:T(8,128)(2,1)S(1)} collective-permute-done((bf16[4,184,128]{2,1,0:T(8,128)(2,1)S(1)}, bf16[4,184,128]{2,1,0:T(8,128)(2,1)S(1)}, u32[]{:S(2)}, u32[]{:S(2)}) %collective-permute-start.3) | collective-permute-done | bytes 188448 | tf_op jit(solution)/shard_map/ppermute | solution.py:778
  26.9 1.4 %collective-permute-start.6 = (bf16[184,128]{1,0:T(8,128)(2,1)S(1)}, bf16[184,128]{1,0:T(8,128)(2,1)S(1)}, u32[]{:S(2)}, u32[]{:S(2)}) collective-permute-start(bf16[184,128]{1,0:T(8,128)(2,1)S(1)} %get-tuple-element.78), channel_id=1, source_target_pairs={{0,64},{64,0},{128,192},{192,128},{1,65},{65,1},{129,193},{193,129... | collective-permute-start | bytes 141320 | tf_op jit(solution)/shard_map/ppermute | solution.py:813
  28.2 2.6 %collective-permute-start.7 = (bf16[184,128]{1,0:T(8,128)(2,1)S(1)}, bf16[184,128]{1,0:T(8,128)(2,1)S(1)}, u32[]{:S(2)}, u32[]{:S(2)}) collective-permute-start(bf16[184,128]{1,0:T(8,128)(2,1)S(1)} %get-tuple-element.79), channel_id=1, source_target_pairs={{0,128},{64,192},{128,0},{192,64},{1,129},{65,193},{129,1},{193,65... | collective-permute-start | bytes 141320 | tf_op jit(solution)/shard_map/ppermute | solution.py:813
  30.9 2.7 %input_taps.1 = (bf16[18,16,16,128]{3,2,1,0:T(8,128)(2,1)S(1)}, bf16[18,16,16,128]{3,2,1,0:T(8,128)(2,1)S(1)}, bf16[18,16,16,128]{3,2,1,0:T(8,128)(2,1)S(1)}, bf...) custom-call(f32[184,128]{1,0:T(8,128)S(1)} %get-tuple-element.73.aft, ...), custom_call_target="tpu_custom_call" | custom-call | flops 1000000000 | bytes 8000000 | tf_op jit(solution)/shard_map/input_taps/pallas_call | solution.py:635
  33.6 1.4 %collective-permute-done.8.refs_3_ = bf16[184,128]{1,0:T(8,128)(2,1)S(1)} collective-permute-done((bf16[184,128]{1,0:T(8,128)(2,1)S(1)}, bf16[184,128]{1,0:T(8,128)(2,1)S(1)}, u32[]{:S(2)}, u32[]{:S(2)}) %collective-permute-start.8) | collective-permute-done | bytes 47136 | tf_op jit(solution)/shard_map/ppermute | solution.py:813
  35.0 4.2 %collective-permute-start.11 = (f32[184,128]{1,0:T(8,128)S(1)}, f32[184,128]{1,0:T(8,128)S(1)}, u32[]{:S(2)}, u32[]{:S(2)}) collective-permute-start(f32[184,128]{1,0:T(8,128)S(1)} %add.16.refs_0_), channel_id=1, source_target_pairs={{0,3},{1,2},{2,1},{3,0},{4,7},{5,6},{6,5},{7,4},{8,11},{9,10},{10,... | collective-permute-start | bytes 282632 | tf_op jit(solution)/shard_map/ppermute | solution.py:778
  39.2 0.7 collective-permute-start.9
  39.9 3.6 %input_half.2 = (bf16[128,4096]{1,0:T(8,128)(2,1)}, f32[8,128]{1,0:T(8,128)S(1)}) custom-call(f32[184,128]{1,0:T(8,128)S(1)} %add.16.refs_0_, bf16[18,16,16,128]{3,2,1,0:T(8,128)(2,1)S(1)} %get-tuple-element.81.refs_1_, bf16[18,16,16,128]{3,2,1,0:T(8,128)(2,1)S(1)} %get-tuple-element.82.refs_2_, bf16[18,16,16,128]{3,2,1,0:T(8,128)(2,1)S(1)} %get-tuple-element.83.refs_3_, ...), custom_call_target="tpu_custom_call" | custom-call | flops 2500000000 | bytes 6000000 | tf_op jit(solution)/shard_map/input_half/pallas_call | solution.py:660
  43.6 0.7 collective-permute-done.10.refs_2_
  44.3 5.8 %collective-permute-start.14 = (bf16[184,128]{1,0:T(8,128)(2,1)S(1)}, bf16[184,128]{1,0:T(8,128)(2,1)S(1)}, u32[]{:S(2)}, u32[]{:S(2)}) collective-permute-start(bf16[184,128]{1,0:T(8,128)(2,1)S(1)} %add.17.refs_0_), channel_id=1, source_target_pairs={{0,12},{4,8},{8,4},{12,0},{16,28},{20,24},{24,20},{28,16},{1,13},{... | collective-permute-start | bytes 141320 | tf_op jit(solution)/shard_map/ppermute | solution.py:778
  50.5 1.6 %coarse_half.2 = (bf16[128,4096]{1,0:T(8,128)(2,1)}, f32[8,128]{1,0:T(8,128)S(1)}) custom-call(bf16[184,128]{1,0:T(8,128)(2,1)S(1)} %add.17.refs_0_, s32[1,8]{1,0:T(1,128)S(1)} %copy-done.5, s32[1]{0:T(128)} %bitcast.rank_ref.refs_0_.refs_2_, bf16[1280,128]{1,0:T(8,128)(2,1)S(1)} %get-tuple-element.75.refs_3_, ...), custom_call_target="tpu_custom_call" | custom-call | bytes 4000000 | tf_op jit(solution)/shard_map/coarse_half/pallas_call | solution.py:188
  52.0 1.9 %collective-permute-done.13.refs_2_ = bf16[184,128]{1,0:T(8,128)(2,1)S(1)} collective-permute-done((bf16[184,128]{1,0:T(8,128)(2,1)S(1)}, bf16[184,128]{1,0:T(8,128)(2,1)S(1)}, u32[]{:S(2)}, u32[]{:S(2)}) %collective-permute-start.13) | collective-permute-done | bytes 47136 | tf_op jit(solution)/shard_map/ppermute | solution.py:778
  53.9 4.0 %collective-permute-start.15 = (bf16[184,128]{1,0:T(8,128)(2,1)S(1)}, bf16[184,128]{1,0:T(8,128)(2,1)S(1)}, u32[]{:S(2)}, u32[]{:S(2)}) collective-permute-start(bf16[184,128]{1,0:T(8,128)(2,1)S(1)} %add.18.refs_0_), channel_id=1, source_target_pairs={{0,16},{4,20},{8,24},{12,28},{16,0},{20,4},{24,8},{28,12},{1,17},{... | collective-permute-start | bytes 141320 | tf_op jit(solution)/shard_map/ppermute | solution.py:778
  57.9 3.6 %input_half.3 = (bf16[128,4096]{1,0:T(8,128)(2,1)}, f32[8,128]{1,0:T(8,128)S(1)}) custom-call(bf16[184,128]{1,0:T(8,128)(2,1)S(1)} %add.18.refs_0_, bf16[18,16,16,128]{3,2,1,0:T(8,128)(2,1)S(1)} %get-tuple-element.81.refs_1_, bf16[18,16,16,128]{3,2,1,0:T(8,128)(2,1)S(1)} %get-tuple-element.82.refs_2_, ...), custom_call_target="tpu_custom_call", output_to_operand_aliasing={{0}: (8, {})} | custom-call | flops 2500000000 | bytes 6000000 | tf_op jit(solution)/shard_map/input_half/pallas_call | solution.py:660
  61.6 2.4 %collective-permute-start.18 = (bf16[184,128]{1,0:T(8,128)(2,1)S(1)}, bf16[184,128]{1,0:T(8,128)(2,1)S(1)}, u32[]{:S(2)}, u32[]{:S(2)}) collective-permute-start(bf16[184,128]{1,0:T(8,128)(2,1)S(1)} %add.19.refs_0_), channel_id=1, source_target_pairs={{0,192},{64,128},{128,64},{192,0},{1,193},{65,129},{129,65},{193,1... | collective-permute-start | bytes 141320 | tf_op jit(solution)/shard_map/ppermute | solution.py:778
  64.0 0.9 %collective-permute-start.16 = (bf16[184,128]{1,0:T(8,128)(2,1)S(1)}, bf16[184,128]{1,0:T(8,128)(2,1)S(1)}, u32[]{:S(2)}, u32[]{:S(2)}) collective-permute-start(bf16[184,128]{1,0:T(8,128)(2,1)S(1)} %add.19.refs_0_), channel_id=1, source_target_pairs={{0,64},{64,0},{128,192},{192,128},{1,65},{65,1},{129,193},{193,129... | collective-permute-start | bytes 141320 | tf_op jit(solution)/shard_map/ppermute | solution.py:778
  65.0 1.6 %coarse_half.3 = (bf16[128,4096]{1,0:T(8,128)(2,1)}, f32[8,128]{1,0:T(8,128)S(1)}) custom-call(bf16[184,128]{1,0:T(8,128)(2,1)S(1)} %add.19.refs_0_, s32[1,8]{1,0:T(1,128)S(1)} %copy-done.5, s32[1]{0:T(128)} %bitcast.rank_ref.refs_0_.refs_2_, bf16[1280,128]{1,0:T(8,128)(2,1)S(1)} %get-tuple-element.75.refs_3_, ...), custom_call_target="tpu_custom_call", output_to_operand_aliasing={{0}: (5, {})} | custom-call | bytes 4000000 | tf_op jit(solution)/shard_map/coarse_half/pallas_call | solution.py:188
  66.5 1.9 %collective-permute-done.17.refs_2_ = bf16[184,128]{1,0:T(8,128)(2,1)S(1)} collective-permute-done((bf16[184,128]{1,0:T(8,128)(2,1)S(1)}, bf16[184,128]{1,0:T(8,128)(2,1)S(1)}, u32[]{:S(2)}, u32[]{:S(2)}) %collective-permute-start.17) | collective-permute-done | bytes 47136 | tf_op jit(solution)/shard_map/ppermute | solution.py:778
  68.4 6.5 %collective-permute-start.19 = (bf16[4,184,128]{2,1,0:T(8,128)(2,1)S(1)}, bf16[4,184,128]{2,1,0:T(8,128)(2,1)S(1)}, u32[]{:S(2)}, u32[]{:S(2)}) collective-permute-start(bf16[4,184,128]{2,1,0:T(8,128)(2,1)S(1)} %collect.1.mine_ref), channel_id=1, source_target_pairs={{0,32},{32,0},{1,33},{33,1},{2,34},{34,2},{3,35},{35,3},{4,36},{36... | collective-permute-start | bytes 565256 | tf_op jit(solution)/shard_map/ppermute | solution.py:778
  74.9 1.1 %collective-permute-done.19.theirs_ref = bf16[4,184,128]{2,1,0:T(8,128)(2,1)S(1)} collective-permute-done((bf16[4,184,128]{2,1,0:T(8,128)(2,1)S(1)}, bf16[4,184,128]{2,1,0:T(8,128)(2,1)S(1)}, u32[]{:S(2)}, u32[]{:S(2)}) %collective-permute-start.19) | collective-permute-done | bytes 188448 | tf_op jit(solution)/shard_map/ppermute | solution.py:778
  76.0 1.3 %split.1 = (f32[27,64,64]{2,1,0:T(8,128)}, f32[8,64,128]{2,1,0:T(8,128)}) custom-call(s32[1]{0:T(128)} %bitcast.rank_ref.refs_0_.refs_2_, bf16[4,184,128]{2,1,0:T(8,128)(2,1)S(1)} %collect.1.mine_ref, bf16[4,184,128]{2,1,0:T(8,128)(2,1)S(1)} %collective-permute-done.19.theirs_ref), custom_call_target="tpu_custom_call" | custom-call | tf_op jit(solution)/shard_map/split/pallas_call | solution.py:759
  (41 shorter events, 2.7 us)
Async XLA Ops:
  0.6 5.3 %copy-start = (bf16[1,128,4096]{2,1,0:T(8,128)(2,1)S(1)}, bf16[1,128,4096]{2,1,0:T(8,128)(2,1)}, u32[]{:S(2)}) copy-start(bf16[1,128,4096]{2,1,0:T(8,128)(2,1)} %param.9) | copy-start | bytes 3145732
  0.7 1.3 %copy-start.1 = (bf16[2,64,4096]{2,1,0:T(8,128)(2,1)S(1)}, bf16[2,64,4096]{2,1,0:T(8,128)(2,1)}, u32[]{:S(2)}) copy-start(bf16[2,64,4096]{2,1,0:T(8,128)(2,1)} %param.6) | copy-start | bytes 3145732
  2.0 6.9 %copy-start.2 = (bf16[27,64,64]{2,1,0:T(8,128)(2,1)S(1)}, bf16[27,64,64]{2,1,0:T(8,128)(2,1)}, u32[]{:S(2)}) copy-start(bf16[27,64,64]{2,1,0:T(8,128)(2,1)} %conv_ref.1) | copy-start | bytes 663556
  2.0 6.9 %copy-start.3 = (bf16[8,128,64]{1,2,0:T(8,128)(2,1)S(1)}, bf16[8,128,64]{1,2,0:T(8,128)(2,1)}, u32[]{:S(2)}) copy-start(bf16[8,128,64]{1,2,0:T(8,128)(2,1)} %param.8) | copy-start | bytes 393220
  2.5 9.2 %collective-permute-start = (bf16[256,128]{1,0:T(8,128)(2,1)S(1)}, bf16[256,128]{1,0:T(8,128)(2,1)S(1)}, u32[]{:S(2)}, u32[]{:S(2)}) collective-permute-start(bf16[256,128]{1,0:T(8,128)(2,1)S(1)} %get-tuple-element.55), channel_id=1, source_target_pairs={{0,1},{1,0},{2,3},{3,2},{4,5},{5,4},{6,7},{7,6},{8,9},{9,8},{10,11... | collective-permute-start | bytes 196616 | tf_op jit(solution)/shard_map/ppermute | solution.py:791
  4.7 7.1 %collective-permute-start.1 = (bf16[256,128]{1,0:T(8,128)(2,1)S(1)}, bf16[256,128]{1,0:T(8,128)(2,1)S(1)}, u32[]{:S(2)}, u32[]{:S(2)}) collective-permute-start(bf16[256,128]{1,0:T(8,128)(2,1)S(1)} %get-tuple-element.56), channel_id=1, source_target_pairs={{0,32},{1,2},{2,1},{3,4},{4,3},{5,6},{6,5},{7,8},{8,7},{9,10},{10,... | collective-permute-start | bytes 196616 | tf_op jit(solution)/shard_map/ppermute | solution.py:791
  6.0 0.7 copy-start.4
  6.6 2.9 %copy-start.6 = (s32[2,26]{1,0:T(2,128)S(1)}, s32[2,26]{1,0:T(2,128)}, u32[]{:S(2)}) copy-start(s32[2,26]{1,0:T(2,128)} %near_ref.5) | copy-start | bytes 628
  7.9 10.8 %collective-permute-start.2 = (bf16[1024,128]{1,0:T(8,128)(2,1)S(1)}, bf16[1024,128]{1,0:T(8,128)(2,1)S(1)}, u32[]{:S(2)}, u32[]{:S(2)}) collective-permute-start(bf16[1024,128]{1,0:T(8,128)(2,1)S(1)} %get-tuple-element.65), channel_id=1, source_target_pairs={{0,1},{1,0},{2,3},{3,2},{4,5},{5,4},{6,7},{7,6},{8,9},{9,8},{10,11... | collective-permute-start | bytes 786440 | tf_op jit(solution)/shard_map/ppermute | solution.py:801
  19.9 11.0 %collective-permute-start.4 = (bf16[1280,128]{1,0:T(8,128)(2,1)S(1)}, bf16[1280,128]{1,0:T(8,128)(2,1)S(1)}, u32[]{:S(2)}, u32[]{:S(2)}) collective-permute-start(bf16[1280,128]{1,0:T(8,128)(2,1)S(1)} %get-tuple-element.75.refs_3_), channel_id=1, source_target_pairs={{0,1},{1,0},{2,3},{3,2},{4,5},{5,4},{6,7},{7,6},{8,9},{9,8},{10,11... | collective-permute-start | bytes 983048 | tf_op jit(solution)/shard_map/ppermute | solution.py:791
  24.8 2.0 %collective-permute-start.3 = (bf16[4,184,128]{2,1,0:T(8,128)(2,1)S(1)}, bf16[4,184,128]{2,1,0:T(8,128)(2,1)S(1)}, u32[]{:S(2)}, u32[]{:S(2)}) collective-permute-start(bf16[4,184,128]{2,1,0:T(8,128)(2,1)S(1)} %get-tuple-element.72), channel_id=1, source_target_pairs={{0,32},{32,0},{1,33},{33,1},{2,34},{34,2},{3,35},{35,3},{4,36},{36... | collective-permute-start | bytes 565256 | tf_op jit(solution)/shard_map/ppermute | solution.py:778
  25.7 5.1 %collective-permute-start.5 = (bf16[256,128]{1,0:T(8,128)(2,1)S(1)}, bf16[256,128]{1,0:T(8,128)(2,1)S(1)}, u32[]{:S(2)}, u32[]{:S(2)}) collective-permute-start(bf16[256,128]{1,0:T(8,128)(2,1)S(1)} %get-tuple-element.76), channel_id=1, source_target_pairs={{0,32},{1,2},{2,1},{3,4},{4,3},{5,6},{6,5},{7,8},{8,7},{9,10},{10,... | collective-permute-start | bytes 196616 | tf_op jit(solution)/shard_map/ppermute | solution.py:791
  26.9 6.7 %collective-permute-start.6 = (bf16[184,128]{1,0:T(8,128)(2,1)S(1)}, bf16[184,128]{1,0:T(8,128)(2,1)S(1)}, u32[]{:S(2)}, u32[]{:S(2)}) collective-permute-start(bf16[184,128]{1,0:T(8,128)(2,1)S(1)} %get-tuple-element.78), channel_id=1, source_target_pairs={{0,64},{64,0},{128,192},{192,128},{1,65},{65,1},{129,193},{193,129... | collective-permute-start | bytes 141320 | tf_op jit(solution)/shard_map/ppermute | solution.py:813
  28.2 5.4 %collective-permute-start.7 = (bf16[184,128]{1,0:T(8,128)(2,1)S(1)}, bf16[184,128]{1,0:T(8,128)(2,1)S(1)}, u32[]{:S(2)}, u32[]{:S(2)}) collective-permute-start(bf16[184,128]{1,0:T(8,128)(2,1)S(1)} %get-tuple-element.79), channel_id=1, source_target_pairs={{0,128},{64,192},{128,0},{192,64},{1,129},{65,193},{129,1},{193,65... | collective-permute-start | bytes 141320 | tf_op jit(solution)/shard_map/ppermute | solution.py:813
  30.9 4.1 %collective-permute-start.8 = (bf16[184,128]{1,0:T(8,128)(2,1)S(1)}, bf16[184,128]{1,0:T(8,128)(2,1)S(1)}, u32[]{:S(2)}, u32[]{:S(2)}) collective-permute-start(bf16[184,128]{1,0:T(8,128)(2,1)S(1)} %get-tuple-element.80), channel_id=1, source_target_pairs={{0,192},{64,128},{128,64},{192,0},{1,193},{65,129},{129,65},{193,1... | collective-permute-start | bytes 141320 | tf_op jit(solution)/shard_map/ppermute | solution.py:813
  35.0 8.5 %collective-permute-start.11 = (f32[184,128]{1,0:T(8,128)S(1)}, f32[184,128]{1,0:T(8,128)S(1)}, u32[]{:S(2)}, u32[]{:S(2)}) collective-permute-start(f32[184,128]{1,0:T(8,128)S(1)} %add.16.refs_0_), channel_id=1, source_target_pairs={{0,3},{1,2},{2,1},{3,0},{4,7},{5,6},{6,5},{7,4},{8,11},{9,10},{10,... | collective-permute-start | bytes 282632 | tf_op jit(solution)/shard_map/ppermute | solution.py:778
  39.2 5.0 %collective-permute-start.10 = (f32[184,128]{1,0:T(8,128)S(1)}, f32[184,128]{1,0:T(8,128)S(1)}, u32[]{:S(2)}, u32[]{:S(2)}) collective-permute-start(f32[184,128]{1,0:T(8,128)S(1)} %add.16.refs_0_), channel_id=1, source_target_pairs={{0,2},{1,3},{2,0},{3,1},{4,6},{5,7},{6,4},{7,5},{8,10},{9,11},{10,... | collective-permute-start | bytes 282632 | tf_op jit(solution)/shard_map/ppermute | solution.py:778
  39.2 5.0 %collective-permute-start.9 = (f32[184,128]{1,0:T(8,128)S(1)}, f32[184,128]{1,0:T(8,128)S(1)}, u32[]{:S(2)}, u32[]{:S(2)}) collective-permute-start(f32[184,128]{1,0:T(8,128)S(1)} %add.16.refs_0_), channel_id=1, source_target_pairs={{0,1},{1,0},{2,3},{3,2},{4,5},{5,4},{6,7},{7,6},{8,9},{9,8},{10,11... | collective-permute-start | bytes 282632 | tf_op jit(solution)/shard_map/ppermute | solution.py:778
  39.9 10.6 %copy-start.5 = (s32[1,8]{1,0:T(1,128)S(1)}, s32[1,8]{1,0:T(1,128)}, u32[]{:S(2)}) copy-start(s32[1,8]{1,0:T(1,128)} %refs_1_.3) | copy-start | bytes 100
  44.3 7.7 %collective-permute-start.14 = (bf16[184,128]{1,0:T(8,128)(2,1)S(1)}, bf16[184,128]{1,0:T(8,128)(2,1)S(1)}, u32[]{:S(2)}, u32[]{:S(2)}) collective-permute-start(bf16[184,128]{1,0:T(8,128)(2,1)S(1)} %add.17.refs_0_), channel_id=1, source_target_pairs={{0,12},{4,8},{8,4},{12,0},{16,28},{20,24},{24,20},{28,16},{1,13},{... | collective-permute-start | bytes 141320 | tf_op jit(solution)/shard_map/ppermute | solution.py:778
  50.1 3.8 %collective-permute-start.13 = (bf16[184,128]{1,0:T(8,128)(2,1)S(1)}, bf16[184,128]{1,0:T(8,128)(2,1)S(1)}, u32[]{:S(2)}, u32[]{:S(2)}) collective-permute-start(bf16[184,128]{1,0:T(8,128)(2,1)S(1)} %add.17.refs_0_), channel_id=1, source_target_pairs={{0,8},{4,12},{8,0},{12,4},{16,24},{20,28},{24,16},{28,20},{1,9},{5... | collective-permute-start | bytes 141320 | tf_op jit(solution)/shard_map/ppermute | solution.py:778
  50.1 3.8 %collective-permute-start.12 = (bf16[184,128]{1,0:T(8,128)(2,1)S(1)}, bf16[184,128]{1,0:T(8,128)(2,1)S(1)}, u32[]{:S(2)}, u32[]{:S(2)}) collective-permute-start(bf16[184,128]{1,0:T(8,128)(2,1)S(1)} %add.17.refs_0_), channel_id=1, source_target_pairs={{0,4},{4,0},{8,12},{12,8},{16,20},{20,16},{24,28},{28,24},{1,5},{5... | collective-permute-start | bytes 141320 | tf_op jit(solution)/shard_map/ppermute | solution.py:778
  53.9 7.7 %collective-permute-start.15 = (bf16[184,128]{1,0:T(8,128)(2,1)S(1)}, bf16[184,128]{1,0:T(8,128)(2,1)S(1)}, u32[]{:S(2)}, u32[]{:S(2)}) collective-permute-start(bf16[184,128]{1,0:T(8,128)(2,1)S(1)} %add.18.refs_0_), channel_id=1, source_target_pairs={{0,16},{4,20},{8,24},{12,28},{16,0},{20,4},{24,8},{28,12},{1,17},{... | collective-permute-start | bytes 141320 | tf_op jit(solution)/shard_map/ppermute | solution.py:778
  61.6 4.9 %collective-permute-start.18 = (bf16[184,128]{1,0:T(8,128)(2,1)S(1)}, bf16[184,128]{1,0:T(8,128)(2,1)S(1)}, u32[]{:S(2)}, u32[]{:S(2)}) collective-permute-start(bf16[184,128]{1,0:T(8,128)(2,1)S(1)} %add.19.refs_0_), channel_id=1, source_target_pairs={{0,192},{64,128},{128,64},{192,0},{1,193},{65,129},{129,65},{193,1... | collective-permute-start | bytes 141320 | tf_op jit(solution)/shard_map/ppermute | solution.py:778
  64.0 4.4 %collective-permute-start.17 = (bf16[184,128]{1,0:T(8,128)(2,1)S(1)}, bf16[184,128]{1,0:T(8,128)(2,1)S(1)}, u32[]{:S(2)}, u32[]{:S(2)}) collective-permute-start(bf16[184,128]{1,0:T(8,128)(2,1)S(1)} %add.19.refs_0_), channel_id=1, source_target_pairs={{0,128},{64,192},{128,0},{192,64},{1,129},{65,193},{129,1},{193,65... | collective-permute-start | bytes 141320 | tf_op jit(solution)/shard_map/ppermute | solution.py:778
  64.0 4.4 %collective-permute-start.16 = (bf16[184,128]{1,0:T(8,128)(2,1)S(1)}, bf16[184,128]{1,0:T(8,128)(2,1)S(1)}, u32[]{:S(2)}, u32[]{:S(2)}) collective-permute-start(bf16[184,128]{1,0:T(8,128)(2,1)S(1)} %add.19.refs_0_), channel_id=1, source_target_pairs={{0,64},{64,0},{128,192},{192,128},{1,65},{65,1},{129,193},{193,129... | collective-permute-start | bytes 141320 | tf_op jit(solution)/shard_map/ppermute | solution.py:778
  68.4 7.6 %collective-permute-start.19 = (bf16[4,184,128]{2,1,0:T(8,128)(2,1)S(1)}, bf16[4,184,128]{2,1,0:T(8,128)(2,1)S(1)}, u32[]{:S(2)}, u32[]{:S(2)}) collective-permute-start(bf16[4,184,128]{2,1,0:T(8,128)(2,1)S(1)} %collect.1.mine_ref), channel_id=1, source_target_pairs={{0,32},{32,0},{1,33},{33,1},{2,34},{34,2},{3,35},{35,3},{4,36},{36... | collective-permute-start | bytes 565256 | tf_op jit(solution)/shard_map/ppermute | solution.py:778

commit v8 on v7

--- a/solution.py
+++ b/solution.py
@@ -329,7 +329,7 @@
     return jnp.concatenate(parts, axis=1).reshape(-1, LANES)
 
 
-def convolve(tap_refs, w_ref, acc_ref, first=0, planes=SIDE + 2, group=6):
+def convolve(tap_refs, w_ref, acc_ref, first=0, planes=SIDE + 2, group=9):
     rows = group * 256
 
     def clear(i):
@@ -367,7 +367,7 @@
 
 def inner_kernel(near_ref, v_ref, zero_ref, one_ref, both_ref, core_ref, ends_ref):
     assemble_inner(near_ref, v_ref, core_ref, ends_ref)
-    gather_taps(core_ref, ends_ref, (zero_ref, one_ref, both_ref), 3)
+    gather_taps(core_ref, ends_ref, (zero_ref, one_ref, both_ref), 6)
 
 
 def forward_kernel(
@@ -394,7 +394,7 @@
 ):
     edges = (zero_edge_ref, one_edge_ref, both_edge_ref)
     assemble_edges(near_ref, rank_ref, pair_ref, other_ref, face_ref, core_ref, ends_ref)
-    gather_taps(core_ref, ends_ref, edges, 9)
+    gather_taps(core_ref, ends_ref, edges, 18)
     convolve(tuple(zip((zero_ref, one_ref, both_ref), edges)), w_ref, acc_ref)
 
     def activate(i):
@@ -403,7 +403,7 @@
         fine_ref[i // 2, i % 2] = (preact * gate).reshape(HALF, 2, SIDE, LANES)
         slope_ref[i] = gate * (1.0 + preact * (1.0 - gate))
 
-    loop(SIDE, activate, 4)
+    loop(SIDE, activate, 8)
     for t, a, b, c in taps():
         picked = fine_ref[:, a, :, b, pl.ds(c, HALF, stride=2), :]
         act_ref[:, t * LANES : (t + 1) * LANES] = picked.reshape(512, LANES).astype(BF16)
@@ -451,7 +451,7 @@
         g_ref[i] = rounded
         place_faces(rank_ref, i, rounded, pair_ref, other_ref, 1024)
 
-    loop(SIDE, back, 4)
+    loop(SIDE, back, 8)
 
 
 def weigh_kernel(*refs):
@@ -472,7 +472,7 @@
     total_ref[...] = jnp.zeros_like(total_ref)
 
     def weigh(g, carry):
-        planes = [6 * g + p for p in range(6)]
+        planes = [9 * g + p for p in range(9)]
         for n, brick in enumerate((zero, one)):
             lhs = [
                 jnp.concatenate(
@@ -498,7 +498,7 @@
             )
         return carry
 
-    lax.fori_loop(0, (SIDE + 2) // 6, weigh, 0)
+    lax.fori_loop(0, (SIDE + 2) // 9, weigh, 0)
     lower = low_half((192, LANES))
     last = []
     for b in range(3):
@@ -623,11 +623,11 @@
     inner, edges, token_ref = refs[:3], refs[3:6], refs[6]
     core_ref, ends_ref, face_ref, edge_core_ref, edge_ends_ref = refs[7:]
     assemble_inner(near_ref, g_ref, core_ref, ends_ref)
-    gather_taps(core_ref, ends_ref, inner, 3)
+    gather_taps(core_ref, ends_ref, inner, 6)
     assemble_edges(
         near_ref, rank_ref, pair_ref, other_ref, face_ref, edge_core_ref, edge_ends_ref
     )
-    gather_taps(edge_core_ref, edge_ends_ref, edges, 9)
+    gather_taps(edge_core_ref, edge_ends_ref, edges, 18)
     token_ref[...] = jnp.zeros_like(token_ref)
 
 
@@ -649,7 +649,7 @@
 def input_half_kernel(half, *refs):
     inner, edges, w_ref = refs[1:4], refs[4:7], refs[7]
     out_ref, token_ref, acc_ref = refs[-3:]
-    convolve(tuple(zip(inner, edges)), w_ref, acc_ref, half * HALF, HALF + 2, 5)
+    convolve(tuple(zip(inner, edges)), w_ref, acc_ref, half * HALF, HALF + 2, 10)
 
     for i in range(HALF):
         out_ref[:, i * 256 : (i + 1) * 256] = acc_ref[i + 2].T.astype(BF16)

time: 77.4 us -> 76.3 us (0.986)
  Pallas kernels: 31.5 us -> 29.9 us
  waiting for transfers between devices: 7.86 us -> 8.68 us
  transfers between devices with their start and end apart: 20 -> 20, of which waited for: 6 -> 6; matrix products, arithmetic and copies ran while one was open for 0% -> 0% of each run, Pallas kernels for 37% -> 35%
where the time goes in v8:
time: 76.3 us; the launch traced here: 76.2 us
  starting transfers between devices  34.8 us (46%)
  Pallas kernels  29.9 us (39%)
  waiting for transfers between devices  8.68 us (11%)
  local copies, waits for them, and re-layouts  1.98 us (3%)
  between operations  0.81 us (1%)
    ppermute x12, starting transfers between devices, swapped(): return [lax.ppermute(array, axis, swaps(axis, step)) for step in steps]  25.7 us
    ppermute x12, waiting for transfers between devices, swapped(): return [lax.ppermute(array, axis, swaps(axis, step)) for step in steps]  7.08 us
    pallas_call x1, Pallas kernels, forward_call(): pl.pallas_call(forward_kernel, out_shape=(jax.ShapeDtypeStruct((1024, LAN...  6.66 us
    pallas_call x2, Pallas kernels, input_half_call(): pl.pallas_call(functools.partial(input_half_kernel, half), grid=(1,), out...  6.54 us
    ppermute x3, starting transfers between devices, body(): lax.ppermute(share, 'y', swaps('y', s + 1))  4 us
    pallas_call x1, Pallas kernels, weigh_call(): pl.pallas_call(weigh_kernel, out_shape=(jax.ShapeDtypeStruct((GROUPS // 2...  3.97 us
    pallas_call x2, Pallas kernels, coarse_half_call(): pl.pallas_call(functools.partial(coarse_half_kernel, half), grid=(1,), ou...  3.15 us
    ppermute x2, starting transfers between devices, exchange(): lax.ppermute(pair, ('z', 'x'), swaps(('z', 'x')))  2.85 us
  transfers between devices with their start and end apart: 20, of which 6 were waited for; matrix products, arithmetic and copies ran while one was open for 0% of the time, Pallas kernels for 35%

profile of v8, /device:TPU:1, one launch (start us, length us, event | category | flops | bytes accessed | tf_op | source)
XLA Modules:
  0.0 76.2 jit_solution(16732437175380108800)
XLA Ops:
  0.7 1.3 %copy-done.1 = bf16[2,64,4096]{2,1,0:T(8,128)(2,1)S(1)} copy-done((bf16[2,64,4096]{2,1,0:T(8,128)(2,1)S(1)}, bf16[2,64,4096]{2,1,0:T(8,128)(2,1)}, u32[]{:S(2)}) %copy-start.1) | copy-done | bytes 1048600
  2.5 2.1 %collective-permute-start = (bf16[256,128]{1,0:T(8,128)(2,1)S(1)}, bf16[256,128]{1,0:T(8,128)(2,1)S(1)}, u32[]{:S(2)}, u32[]{:S(2)}) collective-permute-start(bf16[256,128]{1,0:T(8,128)(2,1)S(1)} %get-tuple-element.55), channel_id=1, source_target_pairs={{0,1},{1,0},{2,3},{3,2},{4,5},{5,4},{6,7},{7,6},{8,9},{9,8},{10,11... | collective-permute-start | bytes 196616 | tf_op jit(solution)/shard_map/ppermute | solution.py:791
  4.7 1.3 %collective-permute-start.1 = (bf16[256,128]{1,0:T(8,128)(2,1)S(1)}, bf16[256,128]{1,0:T(8,128)(2,1)S(1)}, u32[]{:S(2)}, u32[]{:S(2)}) collective-permute-start(bf16[256,128]{1,0:T(8,128)(2,1)S(1)} %get-tuple-element.56), channel_id=1, source_target_pairs={{0,32},{1,2},{2,1},{3,4},{4,3},{5,6},{6,5},{7,8},{8,7},{9,10},{10,... | collective-permute-start | bytes 196616 | tf_op jit(solution)/shard_map/ppermute | solution.py:791
  6.0 0.7 copy-done.4
  6.6 1.3 %cot.1 = (bf16[1024,128]{1,0:T(8,128)(2,1)S(1)}, bf16[1024,128]{1,0:T(8,128)(2,1)S(1)}) custom-call(f32[8,128]{1,0:T(8,128)S(1)} %get-tuple-element.63.after_ref, s32[1,8]{1,0:T(1,128)S(1)} %copy-done.4, s32[1]{0:T(128)} %bitcast.rank_ref.refs_0_.refs_2_, bf16[128,4096]{1,0:T(8,128)(2,1)S(1)} %bitcast.7), custom_call_target="tpu_custom_call" | custom-call | bytes 8000000 | tf_op jit(solution)/shard_map/cot/pallas_call | solution.py:107
  7.9 0.9 %collective-permute-start.2 = (bf16[1024,128]{1,0:T(8,128)(2,1)S(1)}, bf16[1024,128]{1,0:T(8,128)(2,1)S(1)}, u32[]{:S(2)}, u32[]{:S(2)}) collective-permute-start(bf16[1024,128]{1,0:T(8,128)(2,1)S(1)} %get-tuple-element.65), channel_id=1, source_target_pairs={{0,1},{1,0},{2,3},{3,2},{4,5},{5,4},{6,7},{7,6},{8,9},{9,8},{10,11... | collective-permute-start | bytes 786440 | tf_op jit(solution)/shard_map/ppermute | solution.py:801
  9.5 2.1 %inner.1 = (bf16[18,16,16,128]{3,2,1,0:T(8,128)(2,1)S(1)}, bf16[18,16,16,128]{3,2,1,0:T(8,128)(2,1)S(1)}, bf16[18,16,16,128]{3,2,1,0:T(8,128)(2,1)S(1)}) custom-call(s32[2,26]{1,0:T(2,128)S(1)} %copy-done.6, bf16[16,16,16,128]{3,2,1,0:T(8,128)(2,1)S(1)} %get-tuple-element.51.v_ref), custom_call_target="tpu_custom_call" | custom-call | flops 1000000000 | bytes 8000000 | tf_op jit(solution)/shard_map/inner/pallas_call | solution.py:546
  11.6 6.7 %forward.1 = (bf16[1024,128]{1,0:T(8,128)(2,1)S(1)}, f32[16,256,128]{2,1,0:T(8,128)S(1)}, bf16[512,1024]{1,0:T(8,128)(2,1)S(1)}, bf16[18,2,16,128]{3,2,1,0:T(8,1...) custom-call(s32[2,26]{1,0:T(2,128)S(1)} %copy-done.6, ...), custom_call_target="tpu_custom_call" | custom-call | flops 4000000000 | bytes 16000000 | tf_op jit(solution)/shard_map/forward/pallas_call | solution.py:561
  18.3 1.0 %back.1 = (bf16[1280,128]{1,0:T(8,128)(2,1)S(1)}, bf16[256,128]{1,0:T(8,128)(2,1)S(1)}, bf16[16,16,16,128]{3,2,1,0:T(8,128)(2,1)S(1)}, bf16[20,128,256]{2,1,0:T(8,128)(2,1)S(1)}, bf16[2,128,512]{2,1,0:T(8,128)(2,1)S(1)}) custom-call(s32[1]{0:T(128)} %bitcast.rank_ref.refs_0_.refs_2_, bf16[1024,128]{1,0:T(8,128)(2,1)S(1)} %get-tuple-element.64.own_ref, ...), custom_call_target="tpu_custom_call" | custom-call | flops 300000000 | bytes 8000000 | tf_op jit(solution)/shard_map/back/pallas_call | solution.py:581
  19.3 0.7 collective-permute-start.4
  20.0 4.0 %weigh.1 = (f32[4,184,128]{2,1,0:T(8,128)S(1)}, bf16[4,184,128]{2,1,0:T(8,128)(2,1)S(1)}) custom-call(s32[1]{0:T(128)} %bitcast.rank_ref.refs_0_.refs_2_, bf16[18,16,16,128]{3,2,1,0:T(8,128)(2,1)S(1)} %get-tuple-element.52.zero_ref.refs_1_, bf16[18,16,16,128]{3,2,1,0:T(8,128)(2,1)S(1)} %get-tuple-element.53.one_ref.refs_2_, ...), custom_call_target="tpu_custom_call" | custom-call | flops 4000000000 | bytes 10000000 | tf_op jit(solution)/shard_map/weigh/pallas_call | solution.py:602
  24.0 1.0 %collective-permute-start.3 = (bf16[4,184,128]{2,1,0:T(8,128)(2,1)S(1)}, bf16[4,184,128]{2,1,0:T(8,128)(2,1)S(1)}, u32[]{:S(2)}, u32[]{:S(2)}) collective-permute-start(bf16[4,184,128]{2,1,0:T(8,128)(2,1)S(1)} %get-tuple-element.72), channel_id=1, source_target_pairs={{0,32},{32,0},{1,33},{33,1},{2,34},{34,2},{3,35},{35,3},{4,36},{36... | collective-permute-start | bytes 565256 | tf_op jit(solution)/shard_map/ppermute | solution.py:778
  25.1 1.0 %collective-permute-done.3.came_ref = bf16[4,184,128]{2,1,0:T(8,128)(2,1)S(1)} collective-permute-done((bf16[4,184,128]{2,1,0:T(8,128)(2,1)S(1)}, bf16[4,184,128]{2,1,0:T(8,128)(2,1)S(1)}, u32[]{:S(2)}, u32[]{:S(2)}) %collective-permute-start.3) | collective-permute-done | bytes 188448 | tf_op jit(solution)/shard_map/ppermute | solution.py:778
  26.1 1.4 %collective-permute-start.6 = (bf16[184,128]{1,0:T(8,128)(2,1)S(1)}, bf16[184,128]{1,0:T(8,128)(2,1)S(1)}, u32[]{:S(2)}, u32[]{:S(2)}) collective-permute-start(bf16[184,128]{1,0:T(8,128)(2,1)S(1)} %get-tuple-element.78), channel_id=1, source_target_pairs={{0,64},{64,0},{128,192},{192,128},{1,65},{65,1},{129,193},{193,129... | collective-permute-start | bytes 141320 | tf_op jit(solution)/shard_map/ppermute | solution.py:813
  27.5 2.6 %collective-permute-start.7 = (bf16[184,128]{1,0:T(8,128)(2,1)S(1)}, bf16[184,128]{1,0:T(8,128)(2,1)S(1)}, u32[]{:S(2)}, u32[]{:S(2)}) collective-permute-start(bf16[184,128]{1,0:T(8,128)(2,1)S(1)} %get-tuple-element.79), channel_id=1, source_target_pairs={{0,128},{64,192},{128,0},{192,64},{1,129},{65,193},{129,1},{193,65... | collective-permute-start | bytes 141320 | tf_op jit(solution)/shard_map/ppermute | solution.py:813
  30.2 2.5 %input_taps.1 = (bf16[18,16,16,128]{3,2,1,0:T(8,128)(2,1)S(1)}, bf16[18,16,16,128]{3,2,1,0:T(8,128)(2,1)S(1)}, bf16[18,16,16,128]{3,2,1,0:T(8,128)(2,1)S(1)}, bf...) custom-call(f32[184,128]{1,0:T(8,128)S(1)} %get-tuple-element.73.aft, ...), custom_call_target="tpu_custom_call" | custom-call | flops 1000000000 | bytes 8000000 | tf_op jit(solution)/shard_map/input_taps/pallas_call | solution.py:635
  32.7 1.6 %collective-permute-done.8.refs_3_ = bf16[184,128]{1,0:T(8,128)(2,1)S(1)} collective-permute-done((bf16[184,128]{1,0:T(8,128)(2,1)S(1)}, bf16[184,128]{1,0:T(8,128)(2,1)S(1)}, u32[]{:S(2)}, u32[]{:S(2)}) %collective-permute-start.8) | collective-permute-done | bytes 47136 | tf_op jit(solution)/shard_map/ppermute | solution.py:813
  34.3 4.0 %collective-permute-start.11 = (f32[184,128]{1,0:T(8,128)S(1)}, f32[184,128]{1,0:T(8,128)S(1)}, u32[]{:S(2)}, u32[]{:S(2)}) collective-permute-start(f32[184,128]{1,0:T(8,128)S(1)} %add.16.refs_0_), channel_id=1, source_target_pairs={{0,3},{1,2},{2,1},{3,0},{4,7},{5,6},{6,5},{7,4},{8,11},{9,10},{10,... | collective-permute-start | bytes 282632 | tf_op jit(solution)/shard_map/ppermute | solution.py:778
  38.3 0.7 collective-permute-start.9
  39.0 3.3 %input_half.2 = (bf16[128,4096]{1,0:T(8,128)(2,1)}, f32[8,128]{1,0:T(8,128)S(1)}) custom-call(f32[184,128]{1,0:T(8,128)S(1)} %add.16.refs_0_, bf16[18,16,16,128]{3,2,1,0:T(8,128)(2,1)S(1)} %get-tuple-element.81.refs_1_, bf16[18,16,16,128]{3,2,1,0:T(8,128)(2,1)S(1)} %get-tuple-element.82.refs_2_, bf16[18,16,16,128]{3,2,1,0:T(8,128)(2,1)S(1)} %get-tuple-element.83.refs_3_, ...), custom_call_target="tpu_custom_call" | custom-call | flops 2500000000 | bytes 6000000 | tf_op jit(solution)/shard_map/input_half/pallas_call | solution.py:660
  42.3 1.1 %collective-permute-done.10.refs_2_ = f32[184,128]{1,0:T(8,128)S(1)} collective-permute-done((f32[184,128]{1,0:T(8,128)S(1)}, f32[184,128]{1,0:T(8,128)S(1)}, u32[]{:S(2)}, u32[]{:S(2)}) %collective-permute-start.10) | collective-permute-done | bytes 94240 | tf_op jit(solution)/shard_map/ppermute | solution.py:778
  43.4 5.6 %collective-permute-start.14 = (bf16[184,128]{1,0:T(8,128)(2,1)S(1)}, bf16[184,128]{1,0:T(8,128)(2,1)S(1)}, u32[]{:S(2)}, u32[]{:S(2)}) collective-permute-start(bf16[184,128]{1,0:T(8,128)(2,1)S(1)} %add.17.refs_0_), channel_id=1, source_target_pairs={{0,12},{4,8},{8,4},{12,0},{16,28},{20,24},{24,20},{28,16},{1,13},{... | collective-permute-start | bytes 141320 | tf_op jit(solution)/shard_map/ppermute | solution.py:778
  49.4 1.6 %coarse_half.2 = (bf16[128,4096]{1,0:T(8,128)(2,1)}, f32[8,128]{1,0:T(8,128)S(1)}) custom-call(bf16[184,128]{1,0:T(8,128)(2,1)S(1)} %add.17.refs_0_, s32[1,8]{1,0:T(1,128)S(1)} %copy-done.5, s32[1]{0:T(128)} %bitcast.rank_ref.refs_0_.refs_2_, bf16[1280,128]{1,0:T(8,128)(2,1)S(1)} %get-tuple-element.75.refs_3_, ...), custom_call_target="tpu_custom_call" | custom-call | bytes 4000000 | tf_op jit(solution)/shard_map/coarse_half/pallas_call | solution.py:188
  51.0 1.9 %collective-permute-done.13.refs_2_ = bf16[184,128]{1,0:T(8,128)(2,1)S(1)} collective-permute-done((bf16[184,128]{1,0:T(8,128)(2,1)S(1)}, bf16[184,128]{1,0:T(8,128)(2,1)S(1)}, u32[]{:S(2)}, u32[]{:S(2)}) %collective-permute-start.13) | collective-permute-done | bytes 47136 | tf_op jit(solution)/shard_map/ppermute | solution.py:778
  52.9 3.8 %collective-permute-start.15 = (bf16[184,128]{1,0:T(8,128)(2,1)S(1)}, bf16[184,128]{1,0:T(8,128)(2,1)S(1)}, u32[]{:S(2)}, u32[]{:S(2)}) collective-permute-start(bf16[184,128]{1,0:T(8,128)(2,1)S(1)} %add.18.refs_0_), channel_id=1, source_target_pairs={{0,16},{4,20},{8,24},{12,28},{16,0},{20,4},{24,8},{28,12},{1,17},{... | collective-permute-start | bytes 141320 | tf_op jit(solution)/shard_map/ppermute | solution.py:778
  56.7 3.3 %input_half.3 = (bf16[128,4096]{1,0:T(8,128)(2,1)}, f32[8,128]{1,0:T(8,128)S(1)}) custom-call(bf16[184,128]{1,0:T(8,128)(2,1)S(1)} %add.18.refs_0_, bf16[18,16,16,128]{3,2,1,0:T(8,128)(2,1)S(1)} %get-tuple-element.81.refs_1_, bf16[18,16,16,128]{3,2,1,0:T(8,128)(2,1)S(1)} %get-tuple-element.82.refs_2_, ...), custom_call_target="tpu_custom_call", output_to_operand_aliasing={{0}: (8, {})} | custom-call | flops 2500000000 | bytes 6000000 | tf_op jit(solution)/shard_map/input_half/pallas_call | solution.py:660
  60.0 2.6 %collective-permute-start.18 = (bf16[184,128]{1,0:T(8,128)(2,1)S(1)}, bf16[184,128]{1,0:T(8,128)(2,1)S(1)}, u32[]{:S(2)}, u32[]{:S(2)}) collective-permute-start(bf16[184,128]{1,0:T(8,128)(2,1)S(1)} %add.19.refs_0_), channel_id=1, source_target_pairs={{0,192},{64,128},{128,64},{192,0},{1,193},{65,129},{129,65},{193,1... | collective-permute-start | bytes 141320 | tf_op jit(solution)/shard_map/ppermute | solution.py:778
  63.3 1.6 %coarse_half.3 = (bf16[128,4096]{1,0:T(8,128)(2,1)}, f32[8,128]{1,0:T(8,128)S(1)}) custom-call(bf16[184,128]{1,0:T(8,128)(2,1)S(1)} %add.19.refs_0_, s32[1,8]{1,0:T(1,128)S(1)} %copy-done.5, s32[1]{0:T(128)} %bitcast.rank_ref.refs_0_.refs_2_, bf16[1280,128]{1,0:T(8,128)(2,1)S(1)} %get-tuple-element.75.refs_3_, ...), custom_call_target="tpu_custom_call", output_to_operand_aliasing={{0}: (5, {})} | custom-call | bytes 4000000 | tf_op jit(solution)/shard_map/coarse_half/pallas_call | solution.py:188
  64.9 2.1 %collective-permute-done.17.refs_2_ = bf16[184,128]{1,0:T(8,128)(2,1)S(1)} collective-permute-done((bf16[184,128]{1,0:T(8,128)(2,1)S(1)}, bf16[184,128]{1,0:T(8,128)(2,1)S(1)}, u32[]{:S(2)}, u32[]{:S(2)}) %collective-permute-start.17) | collective-permute-done | bytes 47136 | tf_op jit(solution)/shard_map/ppermute | solution.py:778
  67.1 6.8 %collective-permute-start.19 = (bf16[4,184,128]{2,1,0:T(8,128)(2,1)S(1)}, bf16[4,184,128]{2,1,0:T(8,128)(2,1)S(1)}, u32[]{:S(2)}, u32[]{:S(2)}) collective-permute-start(bf16[4,184,128]{2,1,0:T(8,128)(2,1)S(1)} %collect.1.mine_ref), channel_id=1, source_target_pairs={{0,32},{32,0},{1,33},{33,1},{2,34},{34,2},{3,35},{35,3},{4,36},{36... | collective-permute-start | bytes 565256 | tf_op jit(solution)/shard_map/ppermute | solution.py:778
  73.9 1.1 %collective-permute-done.19.theirs_ref = bf16[4,184,128]{2,1,0:T(8,128)(2,1)S(1)} collective-permute-done((bf16[4,184,128]{2,1,0:T(8,128)(2,1)S(1)}, bf16[4,184,128]{2,1,0:T(8,128)(2,1)S(1)}, u32[]{:S(2)}, u32[]{:S(2)}) %collective-permute-start.19) | collective-permute-done | bytes 188448 | tf_op jit(solution)/shard_map/ppermute | solution.py:778
  74.9 1.3 %split.1 = (f32[27,64,64]{2,1,0:T(8,128)}, f32[8,64,128]{2,1,0:T(8,128)}) custom-call(s32[1]{0:T(128)} %bitcast.rank_ref.refs_0_.refs_2_, bf16[4,184,128]{2,1,0:T(8,128)(2,1)S(1)} %collect.1.mine_ref, bf16[4,184,128]{2,1,0:T(8,128)(2,1)S(1)} %collective-permute-done.19.theirs_ref), custom_call_target="tpu_custom_call" | custom-call | tf_op jit(solution)/shard_map/split/pallas_call | solution.py:759
  (41 shorter events, 2.7 us)
Async XLA Ops:
  0.6 5.3 %copy-start = (bf16[1,128,4096]{2,1,0:T(8,128)(2,1)S(1)}, bf16[1,128,4096]{2,1,0:T(8,128)(2,1)}, u32[]{:S(2)}) copy-start(bf16[1,128,4096]{2,1,0:T(8,128)(2,1)} %param.9) | copy-start | bytes 3145732
  0.7 1.3 %copy-start.1 = (bf16[2,64,4096]{2,1,0:T(8,128)(2,1)S(1)}, bf16[2,64,4096]{2,1,0:T(8,128)(2,1)}, u32[]{:S(2)}) copy-start(bf16[2,64,4096]{2,1,0:T(8,128)(2,1)} %param.6) | copy-start | bytes 3145732
  2.0 6.9 %copy-start.2 = (bf16[27,64,64]{2,1,0:T(8,128)(2,1)S(1)}, bf16[27,64,64]{2,1,0:T(8,128)(2,1)}, u32[]{:S(2)}) copy-start(bf16[27,64,64]{2,1,0:T(8,128)(2,1)} %conv_ref.1) | copy-start | bytes 663556
  2.0 6.9 %copy-start.3 = (bf16[8,128,64]{1,2,0:T(8,128)(2,1)S(1)}, bf16[8,128,64]{1,2,0:T(8,128)(2,1)}, u32[]{:S(2)}) copy-start(bf16[8,128,64]{1,2,0:T(8,128)(2,1)} %param.8) | copy-start | bytes 393220
  2.5 9.1 %collective-permute-start = (bf16[256,128]{1,0:T(8,128)(2,1)S(1)}, bf16[256,128]{1,0:T(8,128)(2,1)S(1)}, u32[]{:S(2)}, u32[]{:S(2)}) collective-permute-start(bf16[256,128]{1,0:T(8,128)(2,1)S(1)} %get-tuple-element.55), channel_id=1, source_target_pairs={{0,1},{1,0},{2,3},{3,2},{4,5},{5,4},{6,7},{7,6},{8,9},{9,8},{10,11... | collective-permute-start | bytes 196616 | tf_op jit(solution)/shard_map/ppermute | solution.py:791
  4.7 7.0 %collective-permute-start.1 = (bf16[256,128]{1,0:T(8,128)(2,1)S(1)}, bf16[256,128]{1,0:T(8,128)(2,1)S(1)}, u32[]{:S(2)}, u32[]{:S(2)}) collective-permute-start(bf16[256,128]{1,0:T(8,128)(2,1)S(1)} %get-tuple-element.56), channel_id=1, source_target_pairs={{0,32},{1,2},{2,1},{3,4},{4,3},{5,6},{6,5},{7,8},{8,7},{9,10},{10,... | collective-permute-start | bytes 196616 | tf_op jit(solution)/shard_map/ppermute | solution.py:791
  6.0 0.7 copy-start.4
  6.6 2.9 %copy-start.6 = (s32[2,26]{1,0:T(2,128)S(1)}, s32[2,26]{1,0:T(2,128)}, u32[]{:S(2)}) copy-start(s32[2,26]{1,0:T(2,128)} %near_ref.5) | copy-start | bytes 628
  7.9 10.4 %collective-permute-start.2 = (bf16[1024,128]{1,0:T(8,128)(2,1)S(1)}, bf16[1024,128]{1,0:T(8,128)(2,1)S(1)}, u32[]{:S(2)}, u32[]{:S(2)}) collective-permute-start(bf16[1024,128]{1,0:T(8,128)(2,1)S(1)} %get-tuple-element.65), channel_id=1, source_target_pairs={{0,1},{1,0},{2,3},{3,2},{4,5},{5,4},{6,7},{7,6},{8,9},{9,8},{10,11... | collective-permute-start | bytes 786440 | tf_op jit(solution)/shard_map/ppermute | solution.py:801
  19.3 10.8 %collective-permute-start.4 = (bf16[1280,128]{1,0:T(8,128)(2,1)S(1)}, bf16[1280,128]{1,0:T(8,128)(2,1)S(1)}, u32[]{:S(2)}, u32[]{:S(2)}) collective-permute-start(bf16[1280,128]{1,0:T(8,128)(2,1)S(1)} %get-tuple-element.75.refs_3_), channel_id=1, source_target_pairs={{0,1},{1,0},{2,3},{3,2},{4,5},{5,4},{6,7},{7,6},{8,9},{9,8},{10,11... | collective-permute-start | bytes 983048 | tf_op jit(solution)/shard_map/ppermute | solution.py:791
  24.0 2.1 %collective-permute-start.3 = (bf16[4,184,128]{2,1,0:T(8,128)(2,1)S(1)}, bf16[4,184,128]{2,1,0:T(8,128)(2,1)S(1)}, u32[]{:S(2)}, u32[]{:S(2)}) collective-permute-start(bf16[4,184,128]{2,1,0:T(8,128)(2,1)S(1)} %get-tuple-element.72), channel_id=1, source_target_pairs={{0,32},{32,0},{1,33},{33,1},{2,34},{34,2},{3,35},{35,3},{4,36},{36... | collective-permute-start | bytes 565256 | tf_op jit(solution)/shard_map/ppermute | solution.py:778
  25.0 5.1 %collective-permute-start.5 = (bf16[256,128]{1,0:T(8,128)(2,1)S(1)}, bf16[256,128]{1,0:T(8,128)(2,1)S(1)}, u32[]{:S(2)}, u32[]{:S(2)}) collective-permute-start(bf16[256,128]{1,0:T(8,128)(2,1)S(1)} %get-tuple-element.76), channel_id=1, source_target_pairs={{0,32},{1,2},{2,1},{3,4},{4,3},{5,6},{6,5},{7,8},{8,7},{9,10},{10,... | collective-permute-start | bytes 196616 | tf_op jit(solution)/shard_map/ppermute | solution.py:791
  26.1 6.5 %collective-permute-start.6 = (bf16[184,128]{1,0:T(8,128)(2,1)S(1)}, bf16[184,128]{1,0:T(8,128)(2,1)S(1)}, u32[]{:S(2)}, u32[]{:S(2)}) collective-permute-start(bf16[184,128]{1,0:T(8,128)(2,1)S(1)} %get-tuple-element.78), channel_id=1, source_target_pairs={{0,64},{64,0},{128,192},{192,128},{1,65},{65,1},{129,193},{193,129... | collective-permute-start | bytes 141320 | tf_op jit(solution)/shard_map/ppermute | solution.py:813
  27.5 5.2 %collective-permute-start.7 = (bf16[184,128]{1,0:T(8,128)(2,1)S(1)}, bf16[184,128]{1,0:T(8,128)(2,1)S(1)}, u32[]{:S(2)}, u32[]{:S(2)}) collective-permute-start(bf16[184,128]{1,0:T(8,128)(2,1)S(1)} %get-tuple-element.79), channel_id=1, source_target_pairs={{0,128},{64,192},{128,0},{192,64},{1,129},{65,193},{129,1},{193,65... | collective-permute-start | bytes 141320 | tf_op jit(solution)/shard_map/ppermute | solution.py:813
  30.1 4.1 %collective-permute-start.8 = (bf16[184,128]{1,0:T(8,128)(2,1)S(1)}, bf16[184,128]{1,0:T(8,128)(2,1)S(1)}, u32[]{:S(2)}, u32[]{:S(2)}) collective-permute-start(bf16[184,128]{1,0:T(8,128)(2,1)S(1)} %get-tuple-element.80), channel_id=1, source_target_pairs={{0,192},{64,128},{128,64},{192,0},{1,193},{65,129},{129,65},{193,1... | collective-permute-start | bytes 141320 | tf_op jit(solution)/shard_map/ppermute | solution.py:813
  34.3 8.0 %collective-permute-start.11 = (f32[184,128]{1,0:T(8,128)S(1)}, f32[184,128]{1,0:T(8,128)S(1)}, u32[]{:S(2)}, u32[]{:S(2)}) collective-permute-start(f32[184,128]{1,0:T(8,128)S(1)} %add.16.refs_0_), channel_id=1, source_target_pairs={{0,3},{1,2},{2,1},{3,0},{4,7},{5,6},{6,5},{7,4},{8,11},{9,10},{10,... | collective-permute-start | bytes 282632 | tf_op jit(solution)/shard_map/ppermute | solution.py:778
  38.3 5.0 %collective-permute-start.10 = (f32[184,128]{1,0:T(8,128)S(1)}, f32[184,128]{1,0:T(8,128)S(1)}, u32[]{:S(2)}, u32[]{:S(2)}) collective-permute-start(f32[184,128]{1,0:T(8,128)S(1)} %add.16.refs_0_), channel_id=1, source_target_pairs={{0,2},{1,3},{2,0},{3,1},{4,6},{5,7},{6,4},{7,5},{8,10},{9,11},{10,... | collective-permute-start | bytes 282632 | tf_op jit(solution)/shard_map/ppermute | solution.py:778
  38.3 5.0 %collective-permute-start.9 = (f32[184,128]{1,0:T(8,128)S(1)}, f32[184,128]{1,0:T(8,128)S(1)}, u32[]{:S(2)}, u32[]{:S(2)}) collective-permute-start(f32[184,128]{1,0:T(8,128)S(1)} %add.16.refs_0_), channel_id=1, source_target_pairs={{0,1},{1,0},{2,3},{3,2},{4,5},{5,4},{6,7},{7,6},{8,9},{9,8},{10,11... | collective-permute-start | bytes 282632 | tf_op jit(solution)/shard_map/ppermute | solution.py:778
  39.0 10.4 %copy-start.5 = (s32[1,8]{1,0:T(1,128)S(1)}, s32[1,8]{1,0:T(1,128)}, u32[]{:S(2)}) copy-start(s32[1,8]{1,0:T(1,128)} %refs_1_.3) | copy-start | bytes 100
  43.4 7.6 %collective-permute-start.14 = (bf16[184,128]{1,0:T(8,128)(2,1)S(1)}, bf16[184,128]{1,0:T(8,128)(2,1)S(1)}, u32[]{:S(2)}, u32[]{:S(2)}) collective-permute-start(bf16[184,128]{1,0:T(8,128)(2,1)S(1)} %add.17.refs_0_), channel_id=1, source_target_pairs={{0,12},{4,8},{8,4},{12,0},{16,28},{20,24},{24,20},{28,16},{1,13},{... | collective-permute-start | bytes 141320 | tf_op jit(solution)/shard_map/ppermute | solution.py:778
  49.0 3.8 %collective-permute-start.13 = (bf16[184,128]{1,0:T(8,128)(2,1)S(1)}, bf16[184,128]{1,0:T(8,128)(2,1)S(1)}, u32[]{:S(2)}, u32[]{:S(2)}) collective-permute-start(bf16[184,128]{1,0:T(8,128)(2,1)S(1)} %add.17.refs_0_), channel_id=1, source_target_pairs={{0,8},{4,12},{8,0},{12,4},{16,24},{20,28},{24,16},{28,20},{1,9},{5... | collective-permute-start | bytes 141320 | tf_op jit(solution)/shard_map/ppermute | solution.py:778
  49.1 3.8 %collective-permute-start.12 = (bf16[184,128]{1,0:T(8,128)(2,1)S(1)}, bf16[184,128]{1,0:T(8,128)(2,1)S(1)}, u32[]{:S(2)}, u32[]{:S(2)}) collective-permute-start(bf16[184,128]{1,0:T(8,128)(2,1)S(1)} %add.17.refs_0_), channel_id=1, source_target_pairs={{0,4},{4,0},{8,12},{12,8},{16,20},{20,16},{24,28},{28,24},{1,5},{5... | collective-permute-start | bytes 141320 | tf_op jit(solution)/shard_map/ppermute | solution.py:778
  52.9 7.1 %collective-permute-start.15 = (bf16[184,128]{1,0:T(8,128)(2,1)S(1)}, bf16[184,128]{1,0:T(8,128)(2,1)S(1)}, u32[]{:S(2)}, u32[]{:S(2)}) collective-permute-start(bf16[184,128]{1,0:T(8,128)(2,1)S(1)} %add.18.refs_0_), channel_id=1, source_target_pairs={{0,16},{4,20},{8,24},{12,28},{16,0},{20,4},{24,8},{28,12},{1,17},{... | collective-permute-start | bytes 141320 | tf_op jit(solution)/shard_map/ppermute | solution.py:778
  60.0 4.9 %collective-permute-start.18 = (bf16[184,128]{1,0:T(8,128)(2,1)S(1)}, bf16[184,128]{1,0:T(8,128)(2,1)S(1)}, u32[]{:S(2)}, u32[]{:S(2)}) collective-permute-start(bf16[184,128]{1,0:T(8,128)(2,1)S(1)} %add.19.refs_0_), channel_id=1, source_target_pairs={{0,192},{64,128},{128,64},{192,0},{1,193},{65,129},{129,65},{193,1... | collective-permute-start | bytes 141320 | tf_op jit(solution)/shard_map/ppermute | solution.py:778
  62.6 4.4 %collective-permute-start.17 = (bf16[184,128]{1,0:T(8,128)(2,1)S(1)}, bf16[184,128]{1,0:T(8,128)(2,1)S(1)}, u32[]{:S(2)}, u32[]{:S(2)}) collective-permute-start(bf16[184,128]{1,0:T(8,128)(2,1)S(1)} %add.19.refs_0_), channel_id=1, source_target_pairs={{0,128},{64,192},{128,0},{192,64},{1,129},{65,193},{129,1},{193,65... | collective-permute-start | bytes 141320 | tf_op jit(solution)/shard_map/ppermute | solution.py:778
  62.9 4.1 %collective-permute-start.16 = (bf16[184,128]{1,0:T(8,128)(2,1)S(1)}, bf16[184,128]{1,0:T(8,128)(2,1)S(1)}, u32[]{:S(2)}, u32[]{:S(2)}) collective-permute-start(bf16[184,128]{1,0:T(8,128)(2,1)S(1)} %add.19.refs_0_), channel_id=1, source_target_pairs={{0,64},{64,0},{128,192},{192,128},{1,65},{65,1},{129,193},{193,129... | collective-permute-start | bytes 141320 | tf_op jit(solution)/shard_map/ppermute | solution.py:778
  67.1 7.9 %collective-permute-start.19 = (bf16[4,184,128]{2,1,0:T(8,128)(2,1)S(1)}, bf16[4,184,128]{2,1,0:T(8,128)(2,1)S(1)}, u32[]{:S(2)}, u32[]{:S(2)}) collective-permute-start(bf16[4,184,128]{2,1,0:T(8,128)(2,1)S(1)} %collect.1.mine_ref), channel_id=1, source_target_pairs={{0,32},{32,0},{1,33},{33,1},{2,34},{34,2},{3,35},{35,3},{4,36},{36... | collective-permute-start | bytes 565256 | tf_op jit(solution)/shard_map/ppermute | solution.py:778

commit v9 on v8

--- a/solution.py
+++ b/solution.py
@@ -59,7 +59,7 @@
         v_ref[i] = voxels
         place_faces(rank_ref, i, voxels, pair_ref, other_ref)
 
-    loop(SIDE, plane, 4)
+    loop(SIDE, plane, 8)
     token_ref[...] = jnp.zeros_like(token_ref)
 
 
@@ -92,7 +92,7 @@
         turned = cot_ref[:, columns].astype(F32).T
         turned_ref[i // HALF, i % HALF] = turned.reshape(2, HALF, 2, HALF, LANES)
 
-    loop(SIDE, plane, 4)
+    loop(SIDE, plane, 8)
     rank = rank_ref[0]
     for out_ref, holder in ((own_ref, rank), (send_ref, rank ^ 1)):
         for slot in range(2):
@@ -329,7 +329,7 @@
     return jnp.concatenate(parts, axis=1).reshape(-1, LANES)
 
 
-def convolve(tap_refs, w_ref, acc_ref, first=0, planes=SIDE + 2, group=9):
+def convolve(tap_refs, w_ref, acc_ref, first=0, planes=SIDE + 2, group=18):
     rows = group * 256
 
     def clear(i):
@@ -367,7 +367,7 @@
 
 def inner_kernel(near_ref, v_ref, zero_ref, one_ref, both_ref, core_ref, ends_ref):
     assemble_inner(near_ref, v_ref, core_ref, ends_ref)
-    gather_taps(core_ref, ends_ref, (zero_ref, one_ref, both_ref), 6)
+    gather_taps(core_ref, ends_ref, (zero_ref, one_ref, both_ref), 9)
 
 
 def forward_kernel(
@@ -403,7 +403,7 @@
         fine_ref[i // 2, i % 2] = (preact * gate).reshape(HALF, 2, SIDE, LANES)
         slope_ref[i] = gate * (1.0 + preact * (1.0 - gate))
 
-    loop(SIDE, activate, 8)
+    loop(SIDE, activate, 16)
     for t, a, b, c in taps():
         picked = fine_ref[:, a, :, b, pl.ds(c, HALF, stride=2), :]
         act_ref[:, t * LANES : (t + 1) * LANES] = picked.reshape(512, LANES).astype(BF16)
@@ -451,7 +451,7 @@
         g_ref[i] = rounded
         place_faces(rank_ref, i, rounded, pair_ref, other_ref, 1024)
 
-    loop(SIDE, back, 8)
+    loop(SIDE, back, 16)
 
 
 def weigh_kernel(*refs):
@@ -472,7 +472,7 @@
     total_ref[...] = jnp.zeros_like(total_ref)
 
     def weigh(g, carry):
-        planes = [9 * g + p for p in range(9)]
+        planes = [18 * g + p for p in range(18)]
         for n, brick in enumerate((zero, one)):
             lhs = [
                 jnp.concatenate(
@@ -498,7 +498,7 @@
             )
         return carry
 
-    lax.fori_loop(0, (SIDE + 2) // 9, weigh, 0)
+    lax.fori_loop(0, (SIDE + 2) // 18, weigh, 0)
     lower = low_half((192, LANES))
     last = []
     for b in range(3):
@@ -623,7 +623,7 @@
     inner, edges, token_ref = refs[:3], refs[3:6], refs[6]
     core_ref, ends_ref, face_ref, edge_core_ref, edge_ends_ref = refs[7:]
     assemble_inner(near_ref, g_ref, core_ref, ends_ref)
-    gather_taps(core_ref, ends_ref, inner, 6)
+    gather_taps(core_ref, ends_ref, inner, 9)
     assemble_edges(
         near_ref, rank_ref, pair_ref, other_ref, face_ref, edge_core_ref, edge_ends_ref
     )

time: 76.3 us -> 75.4 us (0.988)
  Pallas kernels: 29.9 us -> 28.8 us
where the time goes in v9:
time: 75.4 us; the launch traced here: 75.3 us
  starting transfers between devices  35 us (46%)
  Pallas kernels  28.8 us (38%)
  waiting for transfers between devices  8.67 us (11%)
  local copies, waits for them, and re-layouts  1.98 us (3%)
  between operations  0.81 us (1%)
    ppermute x12, starting transfers between devices, swapped(): return [lax.ppermute(array, axis, swaps(axis, step)) for step in steps]  25.7 us
    ppermute x12, waiting for transfers between devices, swapped(): return [lax.ppermute(array, axis, swaps(axis, step)) for step in steps]  7.06 us
    pallas_call x1, Pallas kernels, forward_call(): pl.pallas_call(forward_kernel, out_shape=(jax.ShapeDtypeStruct((1024, LAN...  6.64 us
    pallas_call x2, Pallas kernels, input_half_call(): pl.pallas_call(functools.partial(input_half_kernel, half), grid=(1,), out...  6.54 us
    ppermute x3, starting transfers between devices, body(): lax.ppermute(share, 'y', swaps('y', s + 1))  4 us
    pallas_call x1, Pallas kernels, weigh_call(): pl.pallas_call(weigh_kernel, out_shape=(jax.ShapeDtypeStruct((GROUPS // 2...  3.4 us
    pallas_call x2, Pallas kernels, coarse_half_call(): pl.pallas_call(functools.partial(coarse_half_kernel, half), grid=(1,), ou...  3.15 us
    ppermute x2, starting transfers between devices, exchange(): lax.ppermute(pair, ('z', 'x'), swaps(('z', 'x')))  3.03 us
  transfers between devices with their start and end apart: 20, of which 6 were waited for; matrix products, arithmetic and copies ran while one was open for 0% of the time, Pallas kernels for 35%

profile of v9, /device:TPU:1, one launch (start us, length us, event | category | flops | bytes accessed | tf_op | source)
XLA Modules:
  0.0 75.3 jit_solution(11657309058552018902)
XLA Ops:
  0.7 1.3 %copy-done.1 = bf16[2,64,4096]{2,1,0:T(8,128)(2,1)S(1)} copy-done((bf16[2,64,4096]{2,1,0:T(8,128)(2,1)S(1)}, bf16[2,64,4096]{2,1,0:T(8,128)(2,1)}, u32[]{:S(2)}) %copy-start.1) | copy-done | bytes 1048600
  2.4 2.1 %collective-permute-start = (bf16[256,128]{1,0:T(8,128)(2,1)S(1)}, bf16[256,128]{1,0:T(8,128)(2,1)S(1)}, u32[]{:S(2)}, u32[]{:S(2)}) collective-permute-start(bf16[256,128]{1,0:T(8,128)(2,1)S(1)} %get-tuple-element.55), channel_id=1, source_target_pairs={{0,1},{1,0},{2,3},{3,2},{4,5},{5,4},{6,7},{7,6},{8,9},{9,8},{10,11... | collective-permute-start | bytes 196616 | tf_op jit(solution)/shard_map/ppermute | solution.py:791
  4.5 1.3 %collective-permute-start.1 = (bf16[256,128]{1,0:T(8,128)(2,1)S(1)}, bf16[256,128]{1,0:T(8,128)(2,1)S(1)}, u32[]{:S(2)}, u32[]{:S(2)}) collective-permute-start(bf16[256,128]{1,0:T(8,128)(2,1)S(1)} %get-tuple-element.56), channel_id=1, source_target_pairs={{0,32},{1,2},{2,1},{3,4},{4,3},{5,6},{6,5},{7,8},{8,7},{9,10},{10,... | collective-permute-start | bytes 196616 | tf_op jit(solution)/shard_map/ppermute | solution.py:791
  5.8 0.7 copy-done.4
  6.5 1.1 %cot.1 = (bf16[1024,128]{1,0:T(8,128)(2,1)S(1)}, bf16[1024,128]{1,0:T(8,128)(2,1)S(1)}) custom-call(f32[8,128]{1,0:T(8,128)S(1)} %get-tuple-element.63.after_ref, s32[1,8]{1,0:T(1,128)S(1)} %copy-done.4, s32[1]{0:T(128)} %bitcast.rank_ref.refs_0_.refs_2_, bf16[128,4096]{1,0:T(8,128)(2,1)S(1)} %bitcast.7), custom_call_target="tpu_custom_call" | custom-call | bytes 8000000 | tf_op jit(solution)/shard_map/cot/pallas_call | solution.py:107
  7.6 0.9 %collective-permute-start.2 = (bf16[1024,128]{1,0:T(8,128)(2,1)S(1)}, bf16[1024,128]{1,0:T(8,128)(2,1)S(1)}, u32[]{:S(2)}, u32[]{:S(2)}) collective-permute-start(bf16[1024,128]{1,0:T(8,128)(2,1)S(1)} %get-tuple-element.65), channel_id=1, source_target_pairs={{0,1},{1,0},{2,3},{3,2},{4,5},{5,4},{6,7},{7,6},{8,9},{9,8},{10,11... | collective-permute-start | bytes 786440 | tf_op jit(solution)/shard_map/ppermute | solution.py:801
  9.2 2.1 %inner.1 = (bf16[18,16,16,128]{3,2,1,0:T(8,128)(2,1)S(1)}, bf16[18,16,16,128]{3,2,1,0:T(8,128)(2,1)S(1)}, bf16[18,16,16,128]{3,2,1,0:T(8,128)(2,1)S(1)}) custom-call(s32[2,26]{1,0:T(2,128)S(1)} %copy-done.6, bf16[16,16,16,128]{3,2,1,0:T(8,128)(2,1)S(1)} %get-tuple-element.51.v_ref), custom_call_target="tpu_custom_call" | custom-call | flops 1000000000 | bytes 8000000 | tf_op jit(solution)/shard_map/inner/pallas_call | solution.py:546
  11.3 6.6 %forward.1 = (bf16[1024,128]{1,0:T(8,128)(2,1)S(1)}, f32[16,256,128]{2,1,0:T(8,128)S(1)}, bf16[512,1024]{1,0:T(8,128)(2,1)S(1)}, bf16[18,2,16,128]{3,2,1,0:T(8,1...) custom-call(s32[2,26]{1,0:T(2,128)S(1)} %copy-done.6, ...), custom_call_target="tpu_custom_call" | custom-call | flops 4000000000 | bytes 16000000 | tf_op jit(solution)/shard_map/forward/pallas_call | solution.py:561
  18.0 0.8 %back.1 = (bf16[1280,128]{1,0:T(8,128)(2,1)S(1)}, bf16[256,128]{1,0:T(8,128)(2,1)S(1)}, bf16[16,16,16,128]{3,2,1,0:T(8,128)(2,1)S(1)}, bf16[20,128,256]{2,1,0:T(8,128)(2,1)S(1)}, bf16[2,128,512]{2,1,0:T(8,128)(2,1)S(1)}) custom-call(s32[1]{0:T(128)} %bitcast.rank_ref.refs_0_.refs_2_, bf16[1024,128]{1,0:T(8,128)(2,1)S(1)} %get-tuple-element.64.own_ref, ...), custom_call_target="tpu_custom_call" | custom-call | flops 300000000 | bytes 8000000 | tf_op jit(solution)/shard_map/back/pallas_call | solution.py:581
  18.8 0.9 %collective-permute-start.4 = (bf16[1280,128]{1,0:T(8,128)(2,1)S(1)}, bf16[1280,128]{1,0:T(8,128)(2,1)S(1)}, u32[]{:S(2)}, u32[]{:S(2)}) collective-permute-start(bf16[1280,128]{1,0:T(8,128)(2,1)S(1)} %get-tuple-element.75.refs_3_), channel_id=1, source_target_pairs={{0,1},{1,0},{2,3},{3,2},{4,5},{5,4},{6,7},{7,6},{8,9},{9,8},{10,11... | collective-permute-start | bytes 983048 | tf_op jit(solution)/shard_map/ppermute | solution.py:791
  19.7 3.4 %weigh.1 = (f32[4,184,128]{2,1,0:T(8,128)S(1)}, bf16[4,184,128]{2,1,0:T(8,128)(2,1)S(1)}) custom-call(s32[1]{0:T(128)} %bitcast.rank_ref.refs_0_.refs_2_, bf16[18,16,16,128]{3,2,1,0:T(8,128)(2,1)S(1)} %get-tuple-element.52.zero_ref.refs_1_, bf16[18,16,16,128]{3,2,1,0:T(8,128)(2,1)S(1)} %get-tuple-element.53.one_ref.refs_2_, ...), custom_call_target="tpu_custom_call" | custom-call | flops 4000000000 | bytes 10000000 | tf_op jit(solution)/shard_map/weigh/pallas_call | solution.py:602
  23.1 1.0 %collective-permute-start.3 = (bf16[4,184,128]{2,1,0:T(8,128)(2,1)S(1)}, bf16[4,184,128]{2,1,0:T(8,128)(2,1)S(1)}, u32[]{:S(2)}, u32[]{:S(2)}) collective-permute-start(bf16[4,184,128]{2,1,0:T(8,128)(2,1)S(1)} %get-tuple-element.72), channel_id=1, source_target_pairs={{0,32},{32,0},{1,33},{33,1},{2,34},{34,2},{3,35},{35,3},{4,36},{36... | collective-permute-start | bytes 565256 | tf_op jit(solution)/shard_map/ppermute | solution.py:778
  24.3 1.0 %collective-permute-done.3.came_ref = bf16[4,184,128]{2,1,0:T(8,128)(2,1)S(1)} collective-permute-done((bf16[4,184,128]{2,1,0:T(8,128)(2,1)S(1)}, bf16[4,184,128]{2,1,0:T(8,128)(2,1)S(1)}, u32[]{:S(2)}, u32[]{:S(2)}) %collective-permute-start.3) | collective-permute-done | bytes 188448 | tf_op jit(solution)/shard_map/ppermute | solution.py:778
  25.3 1.4 %collective-permute-start.6 = (bf16[184,128]{1,0:T(8,128)(2,1)S(1)}, bf16[184,128]{1,0:T(8,128)(2,1)S(1)}, u32[]{:S(2)}, u32[]{:S(2)}) collective-permute-start(bf16[184,128]{1,0:T(8,128)(2,1)S(1)} %get-tuple-element.78), channel_id=1, source_target_pairs={{0,64},{64,0},{128,192},{192,128},{1,65},{65,1},{129,193},{193,129... | collective-permute-start | bytes 141320 | tf_op jit(solution)/shard_map/ppermute | solution.py:813
  26.6 2.6 %collective-permute-start.7 = (bf16[184,128]{1,0:T(8,128)(2,1)S(1)}, bf16[184,128]{1,0:T(8,128)(2,1)S(1)}, u32[]{:S(2)}, u32[]{:S(2)}) collective-permute-start(bf16[184,128]{1,0:T(8,128)(2,1)S(1)} %get-tuple-element.79), channel_id=1, source_target_pairs={{0,128},{64,192},{128,0},{192,64},{1,129},{65,193},{129,1},{193,65... | collective-permute-start | bytes 141320 | tf_op jit(solution)/shard_map/ppermute | solution.py:813
  29.3 2.5 %input_taps.1 = (bf16[18,16,16,128]{3,2,1,0:T(8,128)(2,1)S(1)}, bf16[18,16,16,128]{3,2,1,0:T(8,128)(2,1)S(1)}, bf16[18,16,16,128]{3,2,1,0:T(8,128)(2,1)S(1)}, bf...) custom-call(f32[184,128]{1,0:T(8,128)S(1)} %get-tuple-element.73.aft, ...), custom_call_target="tpu_custom_call" | custom-call | flops 1000000000 | bytes 8000000 | tf_op jit(solution)/shard_map/input_taps/pallas_call | solution.py:635
  31.8 1.6 %collective-permute-done.8.refs_3_ = bf16[184,128]{1,0:T(8,128)(2,1)S(1)} collective-permute-done((bf16[184,128]{1,0:T(8,128)(2,1)S(1)}, bf16[184,128]{1,0:T(8,128)(2,1)S(1)}, u32[]{:S(2)}, u32[]{:S(2)}) %collective-permute-start.8) | collective-permute-done | bytes 47136 | tf_op jit(solution)/shard_map/ppermute | solution.py:813
  33.4 4.0 %collective-permute-start.11 = (f32[184,128]{1,0:T(8,128)S(1)}, f32[184,128]{1,0:T(8,128)S(1)}, u32[]{:S(2)}, u32[]{:S(2)}) collective-permute-start(f32[184,128]{1,0:T(8,128)S(1)} %add.16.refs_0_), channel_id=1, source_target_pairs={{0,3},{1,2},{2,1},{3,0},{4,7},{5,6},{6,5},{7,4},{8,11},{9,10},{10,... | collective-permute-start | bytes 282632 | tf_op jit(solution)/shard_map/ppermute | solution.py:778
  37.5 0.7 collective-permute-start.9
  38.2 3.3 %input_half.2 = (bf16[128,4096]{1,0:T(8,128)(2,1)}, f32[8,128]{1,0:T(8,128)S(1)}) custom-call(f32[184,128]{1,0:T(8,128)S(1)} %add.16.refs_0_, bf16[18,16,16,128]{3,2,1,0:T(8,128)(2,1)S(1)} %get-tuple-element.81.refs_1_, bf16[18,16,16,128]{3,2,1,0:T(8,128)(2,1)S(1)} %get-tuple-element.82.refs_2_, bf16[18,16,16,128]{3,2,1,0:T(8,128)(2,1)S(1)} %get-tuple-element.83.refs_3_, ...), custom_call_target="tpu_custom_call" | custom-call | flops 2500000000 | bytes 6000000 | tf_op jit(solution)/shard_map/input_half/pallas_call | solution.py:660
  41.4 1.1 %collective-permute-done.10.refs_2_ = f32[184,128]{1,0:T(8,128)S(1)} collective-permute-done((f32[184,128]{1,0:T(8,128)S(1)}, f32[184,128]{1,0:T(8,128)S(1)}, u32[]{:S(2)}, u32[]{:S(2)}) %collective-permute-start.10) | collective-permute-done | bytes 94240 | tf_op jit(solution)/shard_map/ppermute | solution.py:778
  42.5 5.6 %collective-permute-start.14 = (bf16[184,128]{1,0:T(8,128)(2,1)S(1)}, bf16[184,128]{1,0:T(8,128)(2,1)S(1)}, u32[]{:S(2)}, u32[]{:S(2)}) collective-permute-start(bf16[184,128]{1,0:T(8,128)(2,1)S(1)} %add.17.refs_0_), channel_id=1, source_target_pairs={{0,12},{4,8},{8,4},{12,0},{16,28},{20,24},{24,20},{28,16},{1,13},{... | collective-permute-start | bytes 141320 | tf_op jit(solution)/shard_map/ppermute | solution.py:778
  48.6 1.6 %coarse_half.2 = (bf16[128,4096]{1,0:T(8,128)(2,1)}, f32[8,128]{1,0:T(8,128)S(1)}) custom-call(bf16[184,128]{1,0:T(8,128)(2,1)S(1)} %add.17.refs_0_, s32[1,8]{1,0:T(1,128)S(1)} %copy-done.5, s32[1]{0:T(128)} %bitcast.rank_ref.refs_0_.refs_2_, bf16[1280,128]{1,0:T(8,128)(2,1)S(1)} %get-tuple-element.75.refs_3_, ...), custom_call_target="tpu_custom_call" | custom-call | bytes 4000000 | tf_op jit(solution)/shard_map/coarse_half/pallas_call | solution.py:188
  50.2 1.9 %collective-permute-done.13.refs_2_ = bf16[184,128]{1,0:T(8,128)(2,1)S(1)} collective-permute-done((bf16[184,128]{1,0:T(8,128)(2,1)S(1)}, bf16[184,128]{1,0:T(8,128)(2,1)S(1)}, u32[]{:S(2)}, u32[]{:S(2)}) %collective-permute-start.13) | collective-permute-done | bytes 47136 | tf_op jit(solution)/shard_map/ppermute | solution.py:778
  52.0 3.8 %collective-permute-start.15 = (bf16[184,128]{1,0:T(8,128)(2,1)S(1)}, bf16[184,128]{1,0:T(8,128)(2,1)S(1)}, u32[]{:S(2)}, u32[]{:S(2)}) collective-permute-start(bf16[184,128]{1,0:T(8,128)(2,1)S(1)} %add.18.refs_0_), channel_id=1, source_target_pairs={{0,16},{4,20},{8,24},{12,28},{16,0},{20,4},{24,8},{28,12},{1,17},{... | collective-permute-start | bytes 141320 | tf_op jit(solution)/shard_map/ppermute | solution.py:778
  55.8 3.3 %input_half.3 = (bf16[128,4096]{1,0:T(8,128)(2,1)}, f32[8,128]{1,0:T(8,128)S(1)}) custom-call(bf16[184,128]{1,0:T(8,128)(2,1)S(1)} %add.18.refs_0_, bf16[18,16,16,128]{3,2,1,0:T(8,128)(2,1)S(1)} %get-tuple-element.81.refs_1_, bf16[18,16,16,128]{3,2,1,0:T(8,128)(2,1)S(1)} %get-tuple-element.82.refs_2_, ...), custom_call_target="tpu_custom_call", output_to_operand_aliasing={{0}: (8, {})} | custom-call | flops 2500000000 | bytes 6000000 | tf_op jit(solution)/shard_map/input_half/pallas_call | solution.py:660
  59.1 2.6 %collective-permute-start.18 = (bf16[184,128]{1,0:T(8,128)(2,1)S(1)}, bf16[184,128]{1,0:T(8,128)(2,1)S(1)}, u32[]{:S(2)}, u32[]{:S(2)}) collective-permute-start(bf16[184,128]{1,0:T(8,128)(2,1)S(1)} %add.19.refs_0_), channel_id=1, source_target_pairs={{0,192},{64,128},{128,64},{192,0},{1,193},{65,129},{129,65},{193,1... | collective-permute-start | bytes 141320 | tf_op jit(solution)/shard_map/ppermute | solution.py:778
  62.5 1.6 %coarse_half.3 = (bf16[128,4096]{1,0:T(8,128)(2,1)}, f32[8,128]{1,0:T(8,128)S(1)}) custom-call(bf16[184,128]{1,0:T(8,128)(2,1)S(1)} %add.19.refs_0_, s32[1,8]{1,0:T(1,128)S(1)} %copy-done.5, s32[1]{0:T(128)} %bitcast.rank_ref.refs_0_.refs_2_, bf16[1280,128]{1,0:T(8,128)(2,1)S(1)} %get-tuple-element.75.refs_3_, ...), custom_call_target="tpu_custom_call", output_to_operand_aliasing={{0}: (5, {})} | custom-call | bytes 4000000 | tf_op jit(solution)/shard_map/coarse_half/pallas_call | solution.py:188
  64.0 2.1 %collective-permute-done.17.refs_2_ = bf16[184,128]{1,0:T(8,128)(2,1)S(1)} collective-permute-done((bf16[184,128]{1,0:T(8,128)(2,1)S(1)}, bf16[184,128]{1,0:T(8,128)(2,1)S(1)}, u32[]{:S(2)}, u32[]{:S(2)}) %collective-permute-start.17) | collective-permute-done | bytes 47136 | tf_op jit(solution)/shard_map/ppermute | solution.py:778
  66.2 6.8 %collective-permute-start.19 = (bf16[4,184,128]{2,1,0:T(8,128)(2,1)S(1)}, bf16[4,184,128]{2,1,0:T(8,128)(2,1)S(1)}, u32[]{:S(2)}, u32[]{:S(2)}) collective-permute-start(bf16[4,184,128]{2,1,0:T(8,128)(2,1)S(1)} %collect.1.mine_ref), channel_id=1, source_target_pairs={{0,32},{32,0},{1,33},{33,1},{2,34},{34,2},{3,35},{35,3},{4,36},{36... | collective-permute-start | bytes 565256 | tf_op jit(solution)/shard_map/ppermute | solution.py:778
  73.0 1.1 %collective-permute-done.19.theirs_ref = bf16[4,184,128]{2,1,0:T(8,128)(2,1)S(1)} collective-permute-done((bf16[4,184,128]{2,1,0:T(8,128)(2,1)S(1)}, bf16[4,184,128]{2,1,0:T(8,128)(2,1)S(1)}, u32[]{:S(2)}, u32[]{:S(2)}) %collective-permute-start.19) | collective-permute-done | bytes 188448 | tf_op jit(solution)/shard_map/ppermute | solution.py:778
  74.0 1.3 %split.1 = (f32[27,64,64]{2,1,0:T(8,128)}, f32[8,64,128]{2,1,0:T(8,128)}) custom-call(s32[1]{0:T(128)} %bitcast.rank_ref.refs_0_.refs_2_, bf16[4,184,128]{2,1,0:T(8,128)(2,1)S(1)} %collect.1.mine_ref, bf16[4,184,128]{2,1,0:T(8,128)(2,1)S(1)} %collective-permute-done.19.theirs_ref), custom_call_target="tpu_custom_call" | custom-call | tf_op jit(solution)/shard_map/split/pallas_call | solution.py:759
  (41 shorter events, 2.5 us)
Async XLA Ops:
  0.6 5.2 %copy-start = (bf16[1,128,4096]{2,1,0:T(8,128)(2,1)S(1)}, bf16[1,128,4096]{2,1,0:T(8,128)(2,1)}, u32[]{:S(2)}) copy-start(bf16[1,128,4096]{2,1,0:T(8,128)(2,1)} %param.9) | copy-start | bytes 3145732
  0.7 1.3 %copy-start.1 = (bf16[2,64,4096]{2,1,0:T(8,128)(2,1)S(1)}, bf16[2,64,4096]{2,1,0:T(8,128)(2,1)}, u32[]{:S(2)}) copy-start(bf16[2,64,4096]{2,1,0:T(8,128)(2,1)} %param.6) | copy-start | bytes 3145732
  2.0 6.6 %copy-start.2 = (bf16[27,64,64]{2,1,0:T(8,128)(2,1)S(1)}, bf16[27,64,64]{2,1,0:T(8,128)(2,1)}, u32[]{:S(2)}) copy-start(bf16[27,64,64]{2,1,0:T(8,128)(2,1)} %conv_ref.1) | copy-start | bytes 663556
  2.0 6.6 %copy-start.3 = (bf16[8,128,64]{1,2,0:T(8,128)(2,1)S(1)}, bf16[8,128,64]{1,2,0:T(8,128)(2,1)}, u32[]{:S(2)}) copy-start(bf16[8,128,64]{1,2,0:T(8,128)(2,1)} %param.8) | copy-start | bytes 393220
  2.4 8.9 %collective-permute-start = (bf16[256,128]{1,0:T(8,128)(2,1)S(1)}, bf16[256,128]{1,0:T(8,128)(2,1)S(1)}, u32[]{:S(2)}, u32[]{:S(2)}) collective-permute-start(bf16[256,128]{1,0:T(8,128)(2,1)S(1)} %get-tuple-element.55), channel_id=1, source_target_pairs={{0,1},{1,0},{2,3},{3,2},{4,5},{5,4},{6,7},{7,6},{8,9},{9,8},{10,11... | collective-permute-start | bytes 196616 | tf_op jit(solution)/shard_map/ppermute | solution.py:791
  4.5 6.8 %collective-permute-start.1 = (bf16[256,128]{1,0:T(8,128)(2,1)S(1)}, bf16[256,128]{1,0:T(8,128)(2,1)S(1)}, u32[]{:S(2)}, u32[]{:S(2)}) collective-permute-start(bf16[256,128]{1,0:T(8,128)(2,1)S(1)} %get-tuple-element.56), channel_id=1, source_target_pairs={{0,32},{1,2},{2,1},{3,4},{4,3},{5,6},{6,5},{7,8},{8,7},{9,10},{10,... | collective-permute-start | bytes 196616 | tf_op jit(solution)/shard_map/ppermute | solution.py:791
  5.8 0.7 copy-start.4
  6.5 2.7 %copy-start.6 = (s32[2,26]{1,0:T(2,128)S(1)}, s32[2,26]{1,0:T(2,128)}, u32[]{:S(2)}) copy-start(s32[2,26]{1,0:T(2,128)} %near_ref.5) | copy-start | bytes 628
  7.6 10.4 %collective-permute-start.2 = (bf16[1024,128]{1,0:T(8,128)(2,1)S(1)}, bf16[1024,128]{1,0:T(8,128)(2,1)S(1)}, u32[]{:S(2)}, u32[]{:S(2)}) collective-permute-start(bf16[1024,128]{1,0:T(8,128)(2,1)S(1)} %get-tuple-element.65), channel_id=1, source_target_pairs={{0,1},{1,0},{2,3},{3,2},{4,5},{5,4},{6,7},{7,6},{8,9},{9,8},{10,11... | collective-permute-start | bytes 786440 | tf_op jit(solution)/shard_map/ppermute | solution.py:801
  18.8 10.4 %collective-permute-start.4 = (bf16[1280,128]{1,0:T(8,128)(2,1)S(1)}, bf16[1280,128]{1,0:T(8,128)(2,1)S(1)}, u32[]{:S(2)}, u32[]{:S(2)}) collective-permute-start(bf16[1280,128]{1,0:T(8,128)(2,1)S(1)} %get-tuple-element.75.refs_3_), channel_id=1, source_target_pairs={{0,1},{1,0},{2,3},{3,2},{4,5},{5,4},{6,7},{7,6},{8,9},{9,8},{10,11... | collective-permute-start | bytes 983048 | tf_op jit(solution)/shard_map/ppermute | solution.py:791
  23.1 2.1 %collective-permute-start.3 = (bf16[4,184,128]{2,1,0:T(8,128)(2,1)S(1)}, bf16[4,184,128]{2,1,0:T(8,128)(2,1)S(1)}, u32[]{:S(2)}, u32[]{:S(2)}) collective-permute-start(bf16[4,184,128]{2,1,0:T(8,128)(2,1)S(1)} %get-tuple-element.72), channel_id=1, source_target_pairs={{0,32},{32,0},{1,33},{33,1},{2,34},{34,2},{3,35},{35,3},{4,36},{36... | collective-permute-start | bytes 565256 | tf_op jit(solution)/shard_map/ppermute | solution.py:778
  24.2 5.1 %collective-permute-start.5 = (bf16[256,128]{1,0:T(8,128)(2,1)S(1)}, bf16[256,128]{1,0:T(8,128)(2,1)S(1)}, u32[]{:S(2)}, u32[]{:S(2)}) collective-permute-start(bf16[256,128]{1,0:T(8,128)(2,1)S(1)} %get-tuple-element.76), channel_id=1, source_target_pairs={{0,32},{1,2},{2,1},{3,4},{4,3},{5,6},{6,5},{7,8},{8,7},{9,10},{10,... | collective-permute-start | bytes 196616 | tf_op jit(solution)/shard_map/ppermute | solution.py:791
  25.3 6.5 %collective-permute-start.6 = (bf16[184,128]{1,0:T(8,128)(2,1)S(1)}, bf16[184,128]{1,0:T(8,128)(2,1)S(1)}, u32[]{:S(2)}, u32[]{:S(2)}) collective-permute-start(bf16[184,128]{1,0:T(8,128)(2,1)S(1)} %get-tuple-element.78), channel_id=1, source_target_pairs={{0,64},{64,0},{128,192},{192,128},{1,65},{65,1},{129,193},{193,129... | collective-permute-start | bytes 141320 | tf_op jit(solution)/shard_map/ppermute | solution.py:813
  26.6 5.2 %collective-permute-start.7 = (bf16[184,128]{1,0:T(8,128)(2,1)S(1)}, bf16[184,128]{1,0:T(8,128)(2,1)S(1)}, u32[]{:S(2)}, u32[]{:S(2)}) collective-permute-start(bf16[184,128]{1,0:T(8,128)(2,1)S(1)} %get-tuple-element.79), channel_id=1, source_target_pairs={{0,128},{64,192},{128,0},{192,64},{1,129},{65,193},{129,1},{193,65... | collective-permute-start | bytes 141320 | tf_op jit(solution)/shard_map/ppermute | solution.py:813
  29.3 4.1 %collective-permute-start.8 = (bf16[184,128]{1,0:T(8,128)(2,1)S(1)}, bf16[184,128]{1,0:T(8,128)(2,1)S(1)}, u32[]{:S(2)}, u32[]{:S(2)}) collective-permute-start(bf16[184,128]{1,0:T(8,128)(2,1)S(1)} %get-tuple-element.80), channel_id=1, source_target_pairs={{0,192},{64,128},{128,64},{192,0},{1,193},{65,129},{129,65},{193,1... | collective-permute-start | bytes 141320 | tf_op jit(solution)/shard_map/ppermute | solution.py:813
  33.4 8.0 %collective-permute-start.11 = (f32[184,128]{1,0:T(8,128)S(1)}, f32[184,128]{1,0:T(8,128)S(1)}, u32[]{:S(2)}, u32[]{:S(2)}) collective-permute-start(f32[184,128]{1,0:T(8,128)S(1)} %add.16.refs_0_), channel_id=1, source_target_pairs={{0,3},{1,2},{2,1},{3,0},{4,7},{5,6},{6,5},{7,4},{8,11},{9,10},{10,... | collective-permute-start | bytes 282632 | tf_op jit(solution)/shard_map/ppermute | solution.py:778
  37.5 5.0 %collective-permute-start.10 = (f32[184,128]{1,0:T(8,128)S(1)}, f32[184,128]{1,0:T(8,128)S(1)}, u32[]{:S(2)}, u32[]{:S(2)}) collective-permute-start(f32[184,128]{1,0:T(8,128)S(1)} %add.16.refs_0_), channel_id=1, source_target_pairs={{0,2},{1,3},{2,0},{3,1},{4,6},{5,7},{6,4},{7,5},{8,10},{9,11},{10,... | collective-permute-start | bytes 282632 | tf_op jit(solution)/shard_map/ppermute | solution.py:778
  37.5 5.0 %collective-permute-start.9 = (f32[184,128]{1,0:T(8,128)S(1)}, f32[184,128]{1,0:T(8,128)S(1)}, u32[]{:S(2)}, u32[]{:S(2)}) collective-permute-start(f32[184,128]{1,0:T(8,128)S(1)} %add.16.refs_0_), channel_id=1, source_target_pairs={{0,1},{1,0},{2,3},{3,2},{4,5},{5,4},{6,7},{7,6},{8,9},{9,8},{10,11... | collective-permute-start | bytes 282632 | tf_op jit(solution)/shard_map/ppermute | solution.py:778
  38.2 10.4 %copy-start.5 = (s32[1,8]{1,0:T(1,128)S(1)}, s32[1,8]{1,0:T(1,128)}, u32[]{:S(2)}) copy-start(s32[1,8]{1,0:T(1,128)} %refs_1_.3) | copy-start | bytes 100
  42.5 7.6 %collective-permute-start.14 = (bf16[184,128]{1,0:T(8,128)(2,1)S(1)}, bf16[184,128]{1,0:T(8,128)(2,1)S(1)}, u32[]{:S(2)}, u32[]{:S(2)}) collective-permute-start(bf16[184,128]{1,0:T(8,128)(2,1)S(1)} %add.17.refs_0_), channel_id=1, source_target_pairs={{0,12},{4,8},{8,4},{12,0},{16,28},{20,24},{24,20},{28,16},{1,13},{... | collective-permute-start | bytes 141320 | tf_op jit(solution)/shard_map/ppermute | solution.py:778
  48.2 3.8 %collective-permute-start.13 = (bf16[184,128]{1,0:T(8,128)(2,1)S(1)}, bf16[184,128]{1,0:T(8,128)(2,1)S(1)}, u32[]{:S(2)}, u32[]{:S(2)}) collective-permute-start(bf16[184,128]{1,0:T(8,128)(2,1)S(1)} %add.17.refs_0_), channel_id=1, source_target_pairs={{0,8},{4,12},{8,0},{12,4},{16,24},{20,28},{24,16},{28,20},{1,9},{5... | collective-permute-start | bytes 141320 | tf_op jit(solution)/shard_map/ppermute | solution.py:778
  48.2 3.8 %collective-permute-start.12 = (bf16[184,128]{1,0:T(8,128)(2,1)S(1)}, bf16[184,128]{1,0:T(8,128)(2,1)S(1)}, u32[]{:S(2)}, u32[]{:S(2)}) collective-permute-start(bf16[184,128]{1,0:T(8,128)(2,1)S(1)} %add.17.refs_0_), channel_id=1, source_target_pairs={{0,4},{4,0},{8,12},{12,8},{16,20},{20,16},{24,28},{28,24},{1,5},{5... | collective-permute-start | bytes 141320 | tf_op jit(solution)/shard_map/ppermute | solution.py:778
  52.0 7.1 %collective-permute-start.15 = (bf16[184,128]{1,0:T(8,128)(2,1)S(1)}, bf16[184,128]{1,0:T(8,128)(2,1)S(1)}, u32[]{:S(2)}, u32[]{:S(2)}) collective-permute-start(bf16[184,128]{1,0:T(8,128)(2,1)S(1)} %add.18.refs_0_), channel_id=1, source_target_pairs={{0,16},{4,20},{8,24},{12,28},{16,0},{20,4},{24,8},{28,12},{1,17},{... | collective-permute-start | bytes 141320 | tf_op jit(solution)/shard_map/ppermute | solution.py:778
  59.1 4.9 %collective-permute-start.18 = (bf16[184,128]{1,0:T(8,128)(2,1)S(1)}, bf16[184,128]{1,0:T(8,128)(2,1)S(1)}, u32[]{:S(2)}, u32[]{:S(2)}) collective-permute-start(bf16[184,128]{1,0:T(8,128)(2,1)S(1)} %add.19.refs_0_), channel_id=1, source_target_pairs={{0,192},{64,128},{128,64},{192,0},{1,193},{65,129},{129,65},{193,1... | collective-permute-start | bytes 141320 | tf_op jit(solution)/shard_map/ppermute | solution.py:778
  61.7 4.4 %collective-permute-start.17 = (bf16[184,128]{1,0:T(8,128)(2,1)S(1)}, bf16[184,128]{1,0:T(8,128)(2,1)S(1)}, u32[]{:S(2)}, u32[]{:S(2)}) collective-permute-start(bf16[184,128]{1,0:T(8,128)(2,1)S(1)} %add.19.refs_0_), channel_id=1, source_target_pairs={{0,128},{64,192},{128,0},{192,64},{1,129},{65,193},{129,1},{193,65... | collective-permute-start | bytes 141320 | tf_op jit(solution)/shard_map/ppermute | solution.py:778
  62.1 4.1 %collective-permute-start.16 = (bf16[184,128]{1,0:T(8,128)(2,1)S(1)}, bf16[184,128]{1,0:T(8,128)(2,1)S(1)}, u32[]{:S(2)}, u32[]{:S(2)}) collective-permute-start(bf16[184,128]{1,0:T(8,128)(2,1)S(1)} %add.19.refs_0_), channel_id=1, source_target_pairs={{0,64},{64,0},{128,192},{192,128},{1,65},{65,1},{129,193},{193,129... | collective-permute-start | bytes 141320 | tf_op jit(solution)/shard_map/ppermute | solution.py:778
  66.2 7.9 %collective-permute-start.19 = (bf16[4,184,128]{2,1,0:T(8,128)(2,1)S(1)}, bf16[4,184,128]{2,1,0:T(8,128)(2,1)S(1)}, u32[]{:S(2)}, u32[]{:S(2)}) collective-permute-start(bf16[4,184,128]{2,1,0:T(8,128)(2,1)S(1)} %collect.1.mine_ref), channel_id=1, source_target_pairs={{0,32},{32,0},{1,33},{33,1},{2,34},{34,2},{3,35},{35,3},{4,36},{36... | collective-permute-start | bytes 565256 | tf_op jit(solution)/shard_map/ppermute | solution.py:778
